TPU v7x, 256 devices: a whole 4x4x8 slice. The times are simulated.
256 devices in a mesh: dp: 32 (over y, z), tensor: 8 (over x, core).
Axes of the slice: x: 4, y: 4, z: 8, core: 2. Of those that a mesh axis runs over, the one named last changes fastest.
Arguments:
- queries: bfloat16 [16384, 8192], P('dp', 'tensor'), may hold values from -70 to 70
- features: bfloat16 [64, 128, 8192], P('dp'), may hold values from -6 to 6
- k_weight: bfloat16 [8192, 1024], P('dp', 'tensor'), may hold values from -0.0625 to 0.0625
- v_weight: bfloat16 [8192, 1024], P('dp', 'tensor'), may hold values from -0.0625 to 0.0625
- k_gain: float32 [128], replicated, may hold values from 0.1 to 1.9
- block_image: int32 [1024], replicated, may hold values from 0 to 63, as said below
- image_slot: int32 [64], replicated, may hold values from 0 to 63, as said below
- image_tiles: int32 [64], replicated, may hold values from 1 to 4, as said below
- cotangent: bfloat16 [16384, 8192], P('dp', 'tensor'), may hold values from -6 to 6
Outputs:
- attended: bfloat16 [16384, 8192], P('dp', 'tensor')
- grad_queries: bfloat16 [16384, 8192], P('dp', 'tensor')
- grad_features: bfloat16 [64, 128, 8192], P('dp', 'tensor')
- grad_k_weight: float32 [8192, 1024], P('dp', 'tensor')
- grad_v_weight: float32 [8192, 1024], P('dp', 'tensor')
Inputs may be any that keep to these rules, and one draw needn't show every extreme that they name: `block_image`: the blocks of one index of dp cite exactly 16 distinct images, whose slots lie on 16 distinct owners (at most one cited slot of each owner); each cited image is cited by one run of consecutive blocks. A permutation: image i lives in slot image_slot[i], that is on index image_slot[i] // 2 of dp, at position image_slot[i] % 2 of its features. `image_tiles`: both ends are taken in every draw.
All inputs are finite; a program needn't handle non-finite values.
Results may differ from a plain program's by a relative error of at most 0.03.
The roundings to bfloat16 on the way count: a program that leaves them out, or rounds other values in their place, can miss the bound.
Values may be sent and summed in bfloat16 or wider, within the bound.
No kernel may reach another device: no remote copies, remote signals or barrier semaphores. Data moves between devices by JAX's collectives and lax.ppermute only.
A program may use at most 128 MiB of HBM per device.

v0:
```python
import jax
import jax.numpy as jnp
from jax import lax
from jax.sharding import PartitionSpec as P

TILES = 4


EPS = 1e-05
MASKED_SCORE = -1e30


def key_norm(raw_keys, gain):
    mean_square = jnp.mean(raw_keys * raw_keys, axis=-1, keepdims=True)
    return raw_keys * lax.rsqrt(mean_square + EPS) * gain


def group_total(match_half, block_terms):
    high_part = block_terms.astype(jnp.bfloat16)
    low_part = (block_terms - high_part.astype(jnp.float32)).astype(jnp.bfloat16)
    total = jnp.einsum("bo,bjkd->ojkd", match_half, high_part, preferred_element_type=jnp.float32)
    return total + jnp.einsum(
        "bo,bjkd->ojkd", match_half, low_part, preferred_element_type=jnp.float32
    )


def local(
    queries, features, k_weight, v_weight, k_gain, block_image, image_slot, image_tiles, cotangent
):
    dp_count = lax.axis_size("dp")
    tensor_count = lax.axis_size("tensor")
    my_index = lax.axis_index("dp")
    images_here, vision_tokens, vision_width = features.shape
    head_dim = k_gain.shape[0]
    kv_cols = k_weight.shape[1]
    kv_heads = kv_cols // head_dim
    tok_rows = queries.shape[0]
    q_heads = queries.shape[1] // head_dim
    group_size = q_heads // kv_heads
    images_total = image_slot.shape[0]
    blocks_here = block_image.shape[0] // dp_count
    block_rows = tok_rows // blocks_here
    score_scale = head_dim ** (-0.5)
    flat_rows = features.reshape(images_here * vision_tokens, vision_width)
    k_full, v_full = (
        lax.all_gather(k_weight, "dp", axis=0, tiled=True),
        lax.all_gather(v_weight, "dp", axis=0, tiled=True),
    )
    keys_raw = jnp.dot(flat_rows, k_full, preferred_element_type=jnp.float32)
    values_raw = jnp.dot(flat_rows, v_full, preferred_element_type=jnp.float32)
    keys_shaped = keys_raw.reshape(images_here * vision_tokens, kv_heads, head_dim)
    keys_local = (
        key_norm(keys_shaped, k_gain)
        .astype(jnp.bfloat16)
        .reshape(images_here, vision_tokens, kv_cols)
    )
    values_local = values_raw.astype(jnp.bfloat16).reshape(images_here, vision_tokens, kv_cols)
    image_ids = lax.broadcasted_iota(jnp.int32, (1, images_total), 1)
    id_match = block_image[:, None] == image_ids
    slot_grid = jnp.sum(jnp.where(id_match, image_slot[None, :], 0), axis=1).reshape(
        dp_count, blocks_here
    )
    tile_grid = jnp.sum(jnp.where(id_match, image_tiles[None, :], 0), axis=1).reshape(
        dp_count, blocks_here
    )
    my_slots = lax.dynamic_index_in_dim(slot_grid, my_index, 0, keepdims=False)
    my_tiles = lax.dynamic_index_in_dim(tile_grid, my_index, 0, keepdims=False)
    token_index = lax.broadcasted_iota(jnp.int32, (blocks_here, vision_tokens), 1)
    valid_keys = token_index < (my_tiles * (vision_tokens // TILES))[:, None]
    all_keys, all_values = (
        lax.all_gather(keys_local, "dp", axis=0, tiled=True),
        lax.all_gather(values_local, "dp", axis=0, tiled=True),
    )
    block_keys = all_keys[my_slots].reshape(blocks_here, vision_tokens, kv_heads, head_dim)
    block_values = all_values[my_slots].reshape(blocks_here, vision_tokens, kv_heads, head_dim)
    query_blocks = queries.reshape(blocks_here, block_rows, kv_heads, group_size, head_dim)
    grad_blocks = cotangent.reshape(blocks_here, block_rows, kv_heads, group_size, head_dim)
    scores = (
        jnp.einsum(
            "brkgd,bjkd->bkgrj", query_blocks, block_keys, preferred_element_type=jnp.float32
        )
        * score_scale
    )
    scores = jnp.where(valid_keys[:, None, None, None, :], scores, MASKED_SCORE)
    row_max = jnp.max(scores, axis=-1, keepdims=True)
    exp_scores = jnp.exp(scores - row_max)
    attn_probs = exp_scores / jnp.sum(exp_scores, axis=-1, keepdims=True)
    probs_half = attn_probs.astype(jnp.bfloat16)
    attended = jnp.einsum(
        "bkgrj,bjkd->brkgd", probs_half, block_values, preferred_element_type=jnp.float32
    )
    attended = attended.astype(jnp.bfloat16).reshape(tok_rows, q_heads * head_dim)
    grad_probs = jnp.einsum(
        "brkgd,bjkd->bkgrj", grad_blocks, block_values, preferred_element_type=jnp.float32
    )
    row_delta = jnp.sum(attn_probs * grad_probs, axis=-1, keepdims=True)
    grad_scores = (attn_probs * (grad_probs - row_delta) * score_scale).astype(jnp.bfloat16)
    grad_queries = jnp.einsum(
        "bkgrj,bjkd->brkgd", grad_scores, block_keys, preferred_element_type=jnp.float32
    )
    grad_queries = grad_queries.astype(jnp.bfloat16).reshape(tok_rows, q_heads * head_dim)
    key_blocks = jnp.einsum(
        "bkgrj,brkgd->bjkd", grad_scores, query_blocks, preferred_element_type=jnp.float32
    )
    value_blocks = jnp.einsum(
        "bkgrj,brkgd->bjkd", probs_half, grad_blocks, preferred_element_type=jnp.float32
    )
    group_match = (
        my_slots[:, None] == lax.broadcasted_iota(jnp.int32, (1, images_total), 1)
    ).astype(jnp.bfloat16)
    key_groups = group_total(group_match, key_blocks).reshape(images_total, vision_tokens, kv_cols)
    value_groups = group_total(group_match, value_blocks).reshape(
        images_total, vision_tokens, kv_cols
    )
    key_groups_half = key_groups.astype(jnp.bfloat16)
    value_groups_half = value_groups.astype(jnp.bfloat16)
    grad_keys, grad_values = (
        lax.psum_scatter(key_groups_half, "dp", scatter_dimension=0, tiled=True).astype(
            jnp.float32
        ),
        lax.psum_scatter(value_groups_half, "dp", scatter_dimension=0, tiled=True).astype(
            jnp.float32
        ),
    )
    _, pull_back = jax.vjp(lambda raw_keys: key_norm(raw_keys, k_gain), keys_shaped)
    grad_keys_raw = pull_back(grad_keys.reshape(images_here * vision_tokens, kv_heads, head_dim))[0]
    grad_keys_half = grad_keys_raw.reshape(images_here * vision_tokens, kv_cols).astype(
        jnp.bfloat16
    )
    grad_values_half = grad_values.reshape(images_here * vision_tokens, kv_cols).astype(
        jnp.bfloat16
    )
    both_grads = jnp.concatenate([grad_keys_half, grad_values_half], axis=1)
    weight_shares = lax.psum_scatter(
        lax.dot_general(
            flat_rows, both_grads, (((0,), (0,)), ((), ())), preferred_element_type=jnp.float32
        ).astype(jnp.bfloat16),
        "dp",
        scatter_dimension=0,
        tiled=True,
    ).astype(jnp.float32)
    key_by_token = jnp.transpose(
        grad_keys_half.reshape(images_here, vision_tokens, kv_cols), (1, 0, 2)
    )
    value_by_token = jnp.transpose(
        grad_values_half.reshape(images_here, vision_tokens, kv_cols), (1, 0, 2)
    )
    partial_term = jnp.einsum(
        "ric,vc->riv", key_by_token, k_full, preferred_element_type=jnp.float32
    )
    partial_term = partial_term + jnp.einsum(
        "ric,vc->riv", value_by_token, v_full, preferred_element_type=jnp.float32
    )
    row_shares = lax.psum_scatter(
        partial_term.reshape(
            vision_tokens // tensor_count * lax.axis_size("tensor"), images_here * vision_width
        ).astype(jnp.bfloat16),
        "tensor",
        scatter_dimension=0,
        tiled=True,
    ).astype(jnp.float32)
    grad_features = jnp.transpose(
        row_shares.reshape(-1, images_here, vision_width), (1, 0, 2)
    ).astype(jnp.bfloat16)
    return (
        attended,
        grad_queries,
        grad_features,
        weight_shares[:, :kv_cols],
        weight_shares[:, kv_cols:],
    )


def solution(mesh):
    in_specs = (
        P("dp", "tensor"),
        P("dp", None, None),
        P("dp", "tensor"),
        P("dp", "tensor"),
        P(),
        P(),
        P(),
        P(),
        P("dp", "tensor"),
    )
    out_specs = (
        P("dp", "tensor"),
        P("dp", "tensor"),
        P("dp", "tensor", None),
        P("dp", "tensor"),
        P("dp", "tensor"),
    )
    return jax.shard_map(local, mesh=mesh, in_specs=in_specs, out_specs=out_specs, check_vma=False)
```

profile of v0, /device:TPU:32, one launch (start us, length us, event | category | flops | bytes accessed | tf_op | source)
XLA Modules:
  0.0 1056.4 jit_solution(7131254541868180377)
XLA Ops:
  7.2 0.7 all-gather.9.cloned.1.call-update
  7.9 0.7 all-gather.5.cloned.1.call-update
  8.7 81.5 %all-gather.9.cloned.1.call-done = bf16[8192,128]{1,0:T(8,128)(2,1)} async-done(((bf16[256,128]{1,0:T(8,128)(2,1)}), bf16[8192,128]{1,0:T(8,128)(2,1)}) %all-gather.9.cloned.1.call-update) | async-done | bytes 2097168 | tf_op jit(solution)/shard_map/all_gather | solution.py:46
  90.2 4.2 multiply_reduce_fusion
  94.4 0.7 multiply_convert_fusion
  95.3 72.7 %all-gather.5.cloned.1.call-done = bf16[8192,128]{1,0:T(8,128)(2,1)} async-done(((bf16[256,128]{1,0:T(8,128)(2,1)}), bf16[8192,128]{1,0:T(8,128)(2,1)}) %all-gather.5.cloned.1.call-update) | async-done | bytes 2097168 | tf_op jit(solution)/shard_map/all_gather | solution.py:47
  168.0 4.7 convolution_convert_fusion.3
  173.1 1.3 copy.86
  174.3 1.2 copy.88
  175.7 70.6 %all-gather.11.cloned.1.call-done = bf16[64,128,128]{2,1,0:T(8,128)(2,1)} async-done(((bf16[2,128,128]{2,1,0:T(8,128)(2,1)}), bf16[64,128,128]{2,1,0:T(8,128)(2,1)}) %all-gather.11.cloned.1.call-update) | async-done | bytes 2097168 | tf_op jit(solution)/shard_map/all_gather | solution.py:71
  246.3 2.3 gather_fusion.1
  248.7 2.2 bitcast_reduce_fusion
  250.8 1.3 fusion.13
  252.2 72.3 %all-gather.7.cloned.1.call-done = bf16[64,128,128]{2,1,0:T(8,128)(2,1)} async-done(((bf16[2,128,128]{2,1,0:T(8,128)(2,1)}), bf16[64,128,128]{2,1,0:T(8,128)(2,1)}) %all-gather.7.cloned.1.call-update) | async-done | bytes 2097168 | tf_op jit(solution)/shard_map/all_gather | solution.py:72
  324.5 3.5 gather_fusion
  328.0 3.2 fusion.7
  331.1 1.9 fusion.16
  333.1 0.5 fusion.36
  333.6 0.4 copy-done.2
  334.5 0.9 fusion.32
  335.4 1.2 add_convert_fusion.1
  336.7 2.7 copy.69
  339.6 3.8 fusion.25
  343.8 0.9 fusion.29
  344.7 1.2 add_convert_fusion
  346.0 2.7 copy.73
  348.7 204.5 %reduce-scatter.7.cloned.1.call-done = bf16[2,128,128]{2,1,0:T(8,128)(2,1)} async-done(((bf16[64,128,128]{2,1,0:T(8,128)(2,1)}), bf16[2,128,128]{2,1,0:T(8,128)(2,1)}) %reduce-scatter.7.cloned.1.call-update) | async-done | bytes 65552 | tf_op jit(solution)/shard_map/reduce_scatter | solution.py:118
  553.2 1.0 fusion.48
  554.2 1.0 fusion.42
  555.1 216.9 %reduce-scatter.9.cloned.1.call-done = bf16[2,128,128]{2,1,0:T(8,128)(2,1)} async-done(((bf16[64,128,128]{2,1,0:T(8,128)(2,1)}), bf16[2,128,128]{2,1,0:T(8,128)(2,1)}) %reduce-scatter.9.cloned.1.call-update) | async-done | bytes 65552 | tf_op jit(solution)/shard_map/reduce_scatter | solution.py:121
  772.1 5.5 fusion.1
  777.6 3.0 fusion.4
  780.6 3.2 fusion
  783.9 6.4 copy.74
  790.2 6.5 copy.84
  796.8 0.9 copy-done.7
  797.6 2.5 fusion.14
  800.5 0.9 copy-done.3
  801.4 0.4 fusion.15
  802.1 1.8 copy_bitcast_fusion
  804.0 194.0 %reduce-scatter.11.cloned.1.call-done = bf16[256,256]{0,1:T(8,128)(2,1)} async-done(((bf16[8192,256]{0,1:T(8,128)(2,1)}), bf16[256,256]{0,1:T(8,128)(2,1)}) %reduce-scatter.11.cloned.1.call-update) | async-done | bytes 131088 | tf_op jit(solution)/shard_map/reduce_scatter | solution.py:134
  998.0 0.9 fusion.65
  998.9 0.8 copy.78
  999.6 0.8 copy.77
  1000.4 40.0 %reduce-scatter.13.cloned.1.call-done = bf16[16,16384]{1,0:T(8,128)(2,1)} async-done(((bf16[128,16384]{1,0:T(8,128)(2,1)}), bf16[16,16384]{1,0:T(8,128)(2,1)}) %reduce-scatter.13.cloned.1.call-update) | async-done | bytes 524304
  1040.3 4.5 copy.85
  1044.8 3.6 copy.83
  1048.4 1.1 copy.76
  (57 shorter events, 2.5 us)
Async XLA Ops:
  7.2 83.0 %all-gather.9.cloned.1.call-start = ((), (), s32[]{:S(2)}) async-start(), calls=%async_computation.6 | async-start | bytes 2162688 | tf_op jit(solution)/shard_map/all_gather | solution.py:46
  7.9 160.1 %all-gather.5.cloned.1.call-start = ((), (), s32[]{:S(2)}) async-start(), calls=%async_computation.4 | async-start | bytes 2162688 | tf_op jit(solution)/shard_map/all_gather | solution.py:47
  8.6 237.7 %all-gather.11.cloned.1.call-start = ((), (), s32[]{:S(2)}) async-start(), calls=%async_computation.7 | async-start | bytes 2162688 | tf_op jit(solution)/shard_map/all_gather | solution.py:71
  90.2 4.2 copy-start.10
  95.2 77.6 %copy-start.12 = (s32[1024]{0:T(1024)S(1)}, s32[1024]{0:T(1024)}, u32[]{:S(2)}) copy-start(s32[1024]{0:T(1024)} %param.14) | copy-start | bytes 12292
  95.2 77.6 %copy-start.13 = (s32[64]{0:T(128)S(1)}, s32[64]{0:T(128)}, u32[]{:S(2)}) copy-start(s32[64]{0:T(128)} %param.16) | copy-start | bytes 772
  95.2 77.6 %copy-start.14 = (s32[64]{0:T(128)S(1)}, s32[64]{0:T(128)}, u32[]{:S(2)}) copy-start(s32[64]{0:T(128)} %param.15) | copy-start | bytes 772
  95.2 77.9 %copy-start.4 = (bf16[512,1024]{1,0:T(8,128)(2,1)S(1)}, bf16[512,1024]{1,0:T(8,128)(2,1)}, u32[]{:S(2)}) copy-start(bf16[512,1024]{1,0:T(8,128)(2,1)} %param.9) | copy-start | bytes 3145732
  95.2 229.3 %all-gather.7.cloned.1.call-start = ((), (), s32[]{:S(2)}) async-start(), calls=%async_computation.5 | async-start | bytes 2162688 | tf_op jit(solution)/shard_map/all_gather | solution.py:72
  172.7 1.6 copy-start.5
  172.7 380.5 %reduce-scatter.7.cloned.1.call-start = ((), (), s32[]{:S(2)}) async-start(), calls=%async_computation.8 | async-start | bytes 2162688 | tf_op jit(solution)/shard_map/reduce_scatter | solution.py:118
  175.6 73.0 %copy-start.9 = (s32[1024]{0:T(1024)}, s32[1024]{0:T(1024)S(1)}, u32[]{:S(2)}) copy-start(s32[1024]{0:T(1024)S(1)} %pad_clamp_fusion) | copy-start | bytes 12292
  252.2 87.4 %copy-start.6 = (f32[32,8,16]{2,1,0:T(8,128)}, f32[32,8,16]{2,1,0:T(8,128)S(1)}, u32[]{:S(2)}) copy-start(f32[32,8,16]{2,1,0:T(8,128)S(1)} %fusion.13) | copy-start | bytes 49156
  331.1 2.0 copy-start.1
  333.1 1.0 copy-start.2
  339.4 432.7 %reduce-scatter.9.cloned.1.call-start = ((), (), s32[]{:S(2)}) async-start(), calls=%async_computation.9 | async-start | bytes 2162688 | tf_op jit(solution)/shard_map/reduce_scatter | solution.py:121
  348.6 204.6 %copy-start.11 = (f32[128]{0:T(128)S(1)}, f32[128]{0:T(128)}, u32[]{:S(2)}) copy-start(f32[128]{0:T(128)} %param.13) | copy-start | bytes 1540
  348.6 649.3 %reduce-scatter.11.cloned.1.call-start = ((), (), s32[]{:S(2)}) async-start(), calls=%async_computation.10 | async-start | bytes 4325376 | tf_op jit(solution)/shard_map/reduce_scatter | solution.py:134
  777.5 262.8 %reduce-scatter.13.cloned.1.call-start = ((), (), s32[]{:S(2)}) async-start(), calls=%async_computation.11 | async-start | bytes 4718592
  777.6 3.0 copy-start
  777.6 3.0 copy-start.8
  796.7 0.9 copy-start.7
  800.2 1.2 copy-start.3
Sparse Core Ops, SparseCore 0:
  10.6 79.5 all-gather.8
  92.8 75.1 all-gather.4
  171.1 75.1 all-gather.10
  249.3 75.1 all-gather.6
  339.5 213.6 reduce-scatter.6
  557.4 214.6 reduce-scatter.8
  777.7 220.2 reduce-scatter.10
  1000.7 39.6 reduce-scatter.12
where the time goes:
time: 1060 us
  waiting for transfers between devices  954 us (90%)
  local copies, waits for them, and re-layouts  42.9 us (4%)
  matrix products  37.4 us (4%)
  between operations  14.5 us (1%)
    reduce_scatter x1, waiting for transfers between devices, local(): lax.psum_scatter(value_groups_half, 'dp', scatter_dimension=0, tiled=True)  217 us
    reduce_scatter x1, waiting for transfers between devices, local(): lax.psum_scatter(key_groups_half, 'dp', scatter_dimension=0, tiled=True)  204 us
    reduce_scatter x1, waiting for transfers between devices, local(): lax.psum_scatter(lax.dot_general(flat_rows, both_grads, (((0,), (0,)), ((...  194 us
    all_gather x1, waiting for transfers between devices, local(): lax.all_gather(k_weight, 'dp', axis=0, tiled=True)  81.5 us
    all_gather x1, waiting for transfers between devices, local(): lax.all_gather(v_weight, 'dp', axis=0, tiled=True)  72.7 us
    all_gather x1, waiting for transfers between devices, local(): lax.all_gather(values_local, 'dp', axis=0, tiled=True)  72.3 us
    all_gather x1, waiting for transfers between devices, local(): lax.all_gather(keys_local, 'dp', axis=0, tiled=True)  70.6 us
    unnamed x9, waiting for transfers between devices  41.4 us
  transfers between devices with their start and end apart: 8, of which 8 were waited for; matrix products, arithmetic and copies ran while one was open for 5% of the time, Pallas kernels for 0%

commit v1 on v0

v1 whole, which is shorter than its diff:
```python
import functools

import jax
import jax.numpy as jnp
from jax import lax
from jax.experimental import pallas as pl
from jax.experimental.pallas import tpu as pltpu
from jax.sharding import PartitionSpec as P

TILES = 4
EPS = 1e-05
MASKED_SCORE = -1e30
NY, NZ = 4, 8
Y_GROUPS = [[y * NZ + z for y in range(NY)] for z in range(NZ)]
Z_GROUPS = [[y * NZ + z for z in range(NZ)] for y in range(NY)]
BF16, F32 = jnp.bfloat16, jnp.float32
VMEM_BYTES = 48 * 1024 * 1024


def dot_dims(a, b, a_dim, b_dim):
    return lax.dot_general(
        a, b, (((a_dim,), (b_dim,)), ((), ())), preferred_element_type=F32
    )


def project_kernel(pos_ref, f_ref, w_ref, gain_ref, send_ref, raw_ref, acc, kv):
    step = pl.program_id(0)
    part = jnp.dot(f_ref[...], w_ref[...], preferred_element_type=F32)

    @pl.when(step == 0)
    def _():
        acc[...] = part

    @pl.when(step > 0)
    def _():
        acc[...] += part

    @pl.when(step == pl.num_programs(0) - 1)
    def _():
        head_dim = gain_ref.shape[1]
        tokens = send_ref.shape[1]
        raw = acc[:, :head_dim]
        raw_ref[...] = raw
        scale = lax.rsqrt(jnp.mean(raw * raw, axis=-1, keepdims=True) + EPS)
        keys = (raw * scale * gain_ref[...]).astype(BF16)
        values = acc[:, head_dim:].astype(BF16)
        for i in range(kv.shape[0]):
            kv[i, :, :head_dim] = keys[i * tokens : (i + 1) * tokens]
            kv[i, :, head_dim:] = values[i * tokens : (i + 1) * tokens]

        def put(d, carry):
            send_ref[d] = kv[jnp.maximum(pos_ref[d], 0)]
            return carry

        lax.fori_loop(0, send_ref.shape[0], put, 0)


def project(pos, rows, weights, gain, images, tokens):
    depth = rows.shape[1]
    cols = weights.shape[1]
    dp = pos.shape[0]
    tile = 1024
    return pl.pallas_call(
        project_kernel,
        grid_spec=pltpu.PrefetchScalarGridSpec(
            num_scalar_prefetch=1,
            grid=(depth // tile,),
            in_specs=[
                pl.BlockSpec((rows.shape[0], tile), lambda i, s: (0, i)),
                pl.BlockSpec((tile, cols), lambda i, s: (i, 0)),
                pl.BlockSpec((1, gain.shape[1]), lambda i, s: (0, 0)),
            ],
            out_specs=[
                pl.BlockSpec((dp, tokens, cols), lambda i, s: (0, 0, 0)),
                pl.BlockSpec((rows.shape[0], cols // 2), lambda i, s: (0, 0)),
            ],
            scratch_shapes=[
                pltpu.VMEM((rows.shape[0], cols), F32),
                pltpu.VMEM((images, tokens, cols), BF16),
            ],
        ),
        out_shape=[
            jax.ShapeDtypeStruct((dp, tokens, cols), BF16),
            jax.ShapeDtypeStruct((rows.shape[0], cols // 2), F32),
        ],
        compiler_params=pltpu.CompilerParams(vmem_limit_bytes=VMEM_BYTES),
        name="project",
    )(pos, rows, weights, gain)


def attend_kernel(
    owner_ref, valid_ref, first_ref, q_ref, ct_ref, kv_ref, out_ref, gq_ref, part_ref, acc
):
    blocks = owner_ref.shape[0]
    rows = q_ref.shape[0] // blocks
    head_dim = kv_ref.shape[2] // 2
    heads = q_ref.shape[1] // head_dim
    tokens = kv_ref.shape[1]
    scale = head_dim**-0.5
    part_ref[...] = jnp.zeros_like(part_ref)

    def one_block(b, carry):
        start = pl.multiple_of(b * rows, rows)
        owner = owner_ref[b]

        def load(ref):
            return jnp.concatenate(
                [
                    ref[pl.ds(start, rows), g * head_dim : (g + 1) * head_dim]
                    for g in range(heads)
                ],
                axis=0,
            )

        def store(ref, full):
            for g in range(heads):
                ref[pl.ds(start, rows), g * head_dim : (g + 1) * head_dim] = full[
                    g * rows : (g + 1) * rows
                ]

        queries, grads = load(q_ref), load(ct_ref)
        keys = kv_ref[owner, :, :head_dim]
        values = kv_ref[owner, :, head_dim:]
        scores = dot_dims(keys, queries, 1, 1) * scale
        token = lax.broadcasted_iota(jnp.int32, (tokens, 1), 0)
        scores = jnp.where(token < valid_ref[b], scores, MASKED_SCORE)
        weights = jnp.exp(scores - jnp.max(scores, axis=0, keepdims=True))
        probs = weights / jnp.sum(weights, axis=0, keepdims=True)
        probs_half = probs.astype(BF16)
        d_probs = dot_dims(values, grads, 1, 1)
        delta = jnp.sum(probs * d_probs, axis=0, keepdims=True)
        d_scores = (probs * (d_probs - delta) * scale).astype(BF16)
        store(out_ref, dot_dims(probs_half, values, 0, 0).astype(BF16))
        store(gq_ref, dot_dims(d_scores, keys, 0, 0).astype(BF16))
        key_part = jnp.dot(d_scores, queries, preferred_element_type=F32)
        value_part = jnp.dot(probs_half, grads, preferred_element_type=F32)
        keep = first_ref[b] == 0
        key_part = key_part + jnp.where(keep, acc[:, :head_dim], 0.0)
        value_part = value_part + jnp.where(keep, acc[:, head_dim:], 0.0)
        acc[:, :head_dim] = key_part
        acc[:, head_dim:] = value_part
        part_ref[owner, :, :head_dim] = key_part.astype(BF16)
        part_ref[owner, :, head_dim:] = value_part.astype(BF16)
        return carry

    acc[...] = jnp.zeros_like(acc)
    lax.fori_loop(0, blocks, one_block, 0, unroll=2)


def attend(owner, valid, first, queries, cotangent, kv):
    smem = pl.BlockSpec(memory_space=pltpu.SMEM)
    vmem = pl.BlockSpec(memory_space=pltpu.VMEM)
    return pl.pallas_call(
        attend_kernel,
        in_specs=[smem] * 3 + [vmem] * 3,
        out_specs=[vmem] * 3,
        out_shape=[
            jax.ShapeDtypeStruct(queries.shape, BF16),
            jax.ShapeDtypeStruct(queries.shape, BF16),
            jax.ShapeDtypeStruct(kv.shape, BF16),
        ],
        scratch_shapes=[pltpu.VMEM(kv.shape[1:], F32)],
        compiler_params=pltpu.CompilerParams(vmem_limit_bytes=VMEM_BYTES),
        name="attend",
    )(owner, valid, first, queries, cotangent, kv)


def owner_kernel(pos_ref, part_ref, raw_ref, gain_ref, grad_ref, acc):
    head_dim = gain_ref.shape[1]
    tokens = part_ref.shape[1]
    acc[...] = jnp.zeros_like(acc)

    def add(d, carry):
        @pl.when(pos_ref[d] >= 0)
        def _():
            acc[pos_ref[d]] += part_ref[d].astype(F32)

        return carry

    lax.fori_loop(0, part_ref.shape[0], add, 0)
    gain = gain_ref[...]
    for i in range(acc.shape[0]):
        here = slice(i * tokens, (i + 1) * tokens)
        raw = raw_ref[here]
        scale = lax.rsqrt(jnp.mean(raw * raw, axis=-1, keepdims=True) + EPS)
        scaled = acc[i, :, :head_dim] * gain
        pull = jnp.mean(raw * scaled, axis=-1, keepdims=True)
        grad = scale * scaled - raw * (scale * scale * scale * pull)
        grad_ref[here, :head_dim] = grad.astype(BF16)
        grad_ref[here, head_dim:] = acc[i, :, head_dim:].astype(BF16)


def owner_grads(pos, parts, raw, gain, images):
    smem = pl.BlockSpec(memory_space=pltpu.SMEM)
    vmem = pl.BlockSpec(memory_space=pltpu.VMEM)
    return pl.pallas_call(
        owner_kernel,
        in_specs=[smem] + [vmem] * 3,
        out_specs=vmem,
        out_shape=jax.ShapeDtypeStruct((raw.shape[0], parts.shape[2]), BF16),
        scratch_shapes=[pltpu.VMEM((images,) + parts.shape[1:], F32)],
        compiler_params=pltpu.CompilerParams(vmem_limit_bytes=VMEM_BYTES),
        name="owner_grads",
    )(pos, parts, raw, gain)


def local(
    queries, features, k_weight, v_weight, k_gain, block_image, image_slot, image_tiles, cotangent
):
    dp_count = lax.axis_size("dp")
    tensor_count = lax.axis_size("tensor")
    me = lax.axis_index("dp")
    images, tokens, width = features.shape
    head_dim = k_gain.shape[0]
    cols = 2 * head_dim
    rows = features.reshape(images * tokens, width)
    gain = k_gain.reshape(1, head_dim)

    image_ids = lax.broadcasted_iota(jnp.int32, (1, image_slot.shape[0]), 1)
    id_match = block_image[:, None] == image_ids
    slots = jnp.sum(jnp.where(id_match, image_slot[None, :], 0), axis=1).reshape(dp_count, -1)
    tiles = jnp.sum(jnp.where(id_match, image_tiles[None, :], 0), axis=1).reshape(dp_count, -1)
    my_slots = lax.dynamic_index_in_dim(slots, me, 0, keepdims=False)
    my_tiles = lax.dynamic_index_in_dim(tiles, me, 0, keepdims=False)
    owner = my_slots // images
    valid = my_tiles * (tokens // TILES)
    first = jnp.concatenate(
        [jnp.ones((1,), jnp.int32), (my_slots[1:] != my_slots[:-1]).astype(jnp.int32)]
    )
    pos = jnp.max(jnp.where(slots // images == me, slots % images, -1), axis=1)

    weights = lax.all_gather(
        jnp.concatenate([k_weight, v_weight], axis=1), "dp", axis=0, tiled=True
    )
    feature_cols = lax.all_to_all(
        rows, "dp", 1, 0, tiled=True, axis_index_groups=Y_GROUPS
    )
    send, raw = project(pos, rows, weights, gain, images, tokens)
    kv = lax.all_to_all(send, "dp", 0, 0, tiled=True)
    attended, grad_queries, parts = attend(owner, valid, first, queries, cotangent, kv)
    parts = lax.all_to_all(parts, "dp", 0, 0, tiled=True)
    grads = owner_grads(pos, parts, raw, gain, images)

    line = lax.all_gather(grads, "dp", axis=0, tiled=True, axis_index_groups=Y_GROUPS)
    shares = dot_dims(feature_cols, line, 0, 0).astype(BF16)
    shares = lax.all_to_all(
        shares.reshape(NZ, -1, cols), "dp", 0, 0, tiled=True, axis_index_groups=Z_GROUPS
    )
    weight_grads = jnp.sum(shares.astype(F32), axis=0)

    by_target = jnp.transpose(
        grads.reshape(images, tensor_count, tokens // tensor_count, cols), (1, 0, 2, 3)
    ).reshape(images * tokens, cols)
    partial = dot_dims(by_target, weights, 1, 1).astype(BF16)
    partial = lax.all_to_all(
        partial.reshape(tensor_count, -1, width), "tensor", 0, 0, tiled=True
    )
    grad_features = jnp.sum(partial.astype(F32), axis=0).astype(BF16)
    grad_features = grad_features.reshape(images, tokens // tensor_count, width)
    return (
        attended,
        grad_queries,
        grad_features,
        weight_grads[:, :head_dim],
        weight_grads[:, head_dim:],
    )


def solution(mesh):
    in_specs = (
        P("dp", "tensor"),
        P("dp", None, None),
        P("dp", "tensor"),
        P("dp", "tensor"),
        P(),
        P(),
        P(),
        P(),
        P("dp", "tensor"),
    )
    out_specs = (
        P("dp", "tensor"),
        P("dp", "tensor"),
        P("dp", "tensor", None),
        P("dp", "tensor"),
        P("dp", "tensor"),
    )
    return jax.shard_map(local, mesh=mesh, in_specs=in_specs, out_specs=out_specs, check_vma=False)
```

time: 1060 us -> 387 us (0.37)
  waiting for transfers between devices: 954 us -> 233 us
  blocking collectives: 0 us -> 50.6 us
  matrix products: 37.4 us -> 8.92 us
  starting transfers between devices: 0.5 us -> 26.4 us
  Pallas kernels: 0 us -> 25.4 us
  local copies, waits for them, and re-layouts: 42.9 us -> 19.1 us
    reduce_scatter x3 -> x0, waiting for transfers between devices: 615 us -> none  [the longest x1 217 us: local(): lax.psum_scatter(value_groups_half, 'dp', scatter_dimension=0, tiled=True)]
    all_gather x4 -> x1, waiting for transfers between devices: 297 us -> 86 us  [local(): lax.all_gather(jnp.concatenate([k_weight, v_weight], axis=1), 'dp', axis=...]
    all_to_all x0 -> x5, waiting for transfers between devices: none -> 147 us  [the longest x1 48 us: local(): kv = lax.all_to_all(send, 'dp', 0, 0, tiled=True)]
    all_gather x0 -> x1, blocking collectives: none -> 50.6 us  [local(): lax.all_gather(grads, 'dp', axis=0, tiled=True, axis_index_groups=Y_GROUPS)]
    unnamed x9 -> x1, waiting for transfers between devices: 41.4 us -> 0.02 us
    dot_general x15 -> x2, matrix products: 37.4 us -> 8.92 us  [dot_dims(): lax.dot_general(a, b, (((a_dim,), (b_dim,)), ((), ())), preferred_element...]
    all_to_all x0 -> x5, starting transfers between devices: none -> 26.3 us  [the longest x1 6.03 us: local(): kv = lax.all_to_all(send, 'dp', 0, 0, tiled=True)]
    pallas_call x0 -> x3, Pallas kernels: none -> 25.4 us  [the longest x1 15 us: attend(): pl.pallas_call(attend_kernel, in_specs=[smem] * 3 + [vmem] * 3, out_specs...]
  transfers between devices with their start and end apart: 8 -> 6, of which waited for: 8 -> 5; matrix products, arithmetic and copies ran while one was open for 5% -> 4% of each run, Pallas kernels for 0% -> 0%
where the time goes in v1:
time: 387 us; the launch traced here: 384 us
  waiting for transfers between devices  233 us (60%)
  blocking collectives  50.6 us (13%)
  starting transfers between devices  26.4 us (7%)
  Pallas kernels  25.4 us (7%)
  local copies, waits for them, and re-layouts  19.1 us (5%)
  between operations  14.1 us (4%)
  matrix products  8.92 us (2%)
  other arithmetic  6.54 us (2%)
    all_gather x1, waiting for transfers between devices, local(): lax.all_gather(jnp.concatenate([k_weight, v_weight], axis=1), 'dp', axis=...  86 us
    all_gather x1, blocking collectives, local(): lax.all_gather(grads, 'dp', axis=0, tiled=True, axis_index_groups=Y_GROUPS)  50.6 us
    all_to_all x1, waiting for transfers between devices, local(): kv = lax.all_to_all(send, 'dp', 0, 0, tiled=True)  48 us
    all_to_all x1, waiting for transfers between devices, local(): lax.all_to_all(partial.reshape(tensor_count, -1, width), 'tensor', 0, 0,...  48 us
    all_to_all x1, waiting for transfers between devices, local(): parts = lax.all_to_all(parts, 'dp', 0, 0, tiled=True)  33.9 us
    all_to_all x1, waiting for transfers between devices, local(): lax.all_to_all(shares.reshape(NZ, -1, cols), 'dp', 0, 0, tiled=True, axis...  17.2 us
    pallas_call x1, Pallas kernels, attend(): pl.pallas_call(attend_kernel, in_specs=[smem] * 3 + [vmem] * 3, out_specs...  15 us
    all_to_all x2, local copies, waits for them, and re-layouts, local(): lax.all_to_all(rows, 'dp', 1, 0, tiled=True, axis_index_groups=Y_GROUPS)  14.3 us
  transfers between devices with their start and end apart: 6, of which 5 were waited for; matrix products, arithmetic and copies ran while one was open for 4% of the time, Pallas kernels for 0%

profile of v1, /device:TPU:32, one launch (start us, length us, event | category | flops | bytes accessed | tf_op | source)
XLA Modules:
  0.0 384.2 jit_solution(4395993874152428801)
XLA Ops:
  7.2 0.0 all-gather.2.cloned.1.call-start
  7.2 1.5 pad_maximum_fusion
  8.8 0.0 all-gather.2.cloned.1.call-update
  8.8 0.8 select_reduce_fusion
  9.6 0.1 reshape.51
  9.7 0.1 fusion.2.pos_ref
  9.8 86.0 %all-gather.2.cloned.1.call-done.w_ref = bf16[8192,256]{1,0:T(8,128)(2,1)} async-done(((bf16[256,256]{1,0:T(8,128)(2,1)}), bf16[8192,256]{1,0:T(8,128)(2,1)}) %all-gather.2.cloned.1.call-update) | async-done | bytes 4194320 | tf_op jit(solution)/shard_map/all_gather | solution.py:232
  95.8 0.0 copy-start.3
  95.8 0.7 copy-done.3
  96.5 9.1 %project.1 = (bf16[32,128,256]{2,1,0:T(8,128)(2,1)}, f32[256,128]{1,0:T(8,128)S(1)}) custom-call(s32[32]{0:T(128)S(1)} %fusion.2.pos_ref, bf16[256,8192]{1,0:T(8,128)(2,1)} %bitcast.35, bf16[8192,256]{1,0:T(8,128)(2,1)} %all-gather.2.cloned.1.call-done.w_ref, f32[1,128]{1,0:T(1,128)S(1)} %bitcast.33), custom_call_target="tpu_custom_call" | custom-call | tf_op jit(solution)/shard_map/project/pallas_call | solution.py:63
  105.5 0.0 copy-start.1
  105.5 0.0 copy-start.2
  105.5 6.0 %all-to-all-start = ((bf16[32,128,256]{2,1,0:T(8,128)(2,1)}), bf16[32,128,256]{2,1,0:T(8,128)(2,1)}, u32[]{:S(2)}, u32[]{:S(2)}) async-start(bf16[32,128,256]{2,1,0:T(8,128)(2,1)} %get-tuple-element.10), calls=%async_computation | async-start | bytes 4194304 | tf_op jit(solution)/shard_map/all_to_all | solution.py:239
  111.6 0.1 reshape.52
  111.7 0.1 compare_bitcast_fusion
  111.8 0.1 add_convert_fusion.first_ref
  111.8 48.0 %all-to-all-done.kv_ref = bf16[32,128,256]{2,1,0:T(8,128)(2,1)} async-done(((bf16[32,128,256]{2,1,0:T(8,128)(2,1)}), bf16[32,128,256]{2,1,0:T(8,128)(2,1)}, u32[]{:S(2)}, u32[]{:S(2)}) %all-to-all-start) | async-done | bytes 2097184 | tf_op jit(solution)/shard_map/all_to_all | solution.py:239
  159.9 0.0 copy-done.1
  159.9 0.0 copy-done.2
  159.9 15.0 %attend.1 = (bf16[512,1024]{1,0:T(8,128)(2,1)}, bf16[512,1024]{1,0:T(8,128)(2,1)}, bf16[32,128,256]{2,1,0:T(8,128)(2,1)S(1)}) custom-call(s32[32]{0:T(128)S(1)} %get-tuple-element.27.owner_ref, s32[32]{0:T(128)S(1)} %multiply_bitcast_fusion.valid_ref, s32[32]{0:T(128)S(1)} %add_convert_fusion.first_ref, bf16[512,1024]{1,0:T(8,128)(2,1)S(1)} %copy-done.1, ...), custom_call_target="tpu_custom_call" | custom-call | tf_op jit(solution)/shard_map/attend/pallas_call | solution.py:153
  174.9 0.0 copy-start
  174.9 1.3 copy-done
  176.2 5.4 %all-to-all-start.1 = ((bf16[32,128,256]{2,1,0:T(8,128)(2,1)}), bf16[32,128,256]{2,1,0:T(8,128)(2,1)S(1)}, u32[]{:S(2)}, u32[]{:S(2)}) async-start(bf16[32,128,256]{2,1,0:T(8,128)(2,1)} %copy-done), calls=%async_computation.1 | async-start | bytes 4194304 | tf_op jit(solution)/shard_map/all_to_all | solution.py:241
  181.6 7.9 %all_to_all.29 = bf16[256,4,2048]{2,1,0:T(4,128)(2,1)} reshape(bf16[2,128,8192]{2,1,0:T(8,128)(2,1)} %param.10) | data formatting | bytes 8388608 | tf_op jit(solution)/shard_map/all_to_all | solution.py:235
  189.5 6.5 %copy.24 = bf16[256,4,2048]{2,0,1:T(8,128)(2,1)} copy(bf16[256,4,2048]{2,1,0:T(4,128)(2,1)} %all_to_all.29) | data formatting | bytes 8388608 | tf_op jit(solution)/shard_map/all_to_all | solution.py:235
  195.9 0.0 copy-start.4
  195.9 33.9 %all-to-all-done.1.part_ref = bf16[32,128,256]{2,1,0:T(8,128)(2,1)S(1)} async-done(((bf16[32,128,256]{2,1,0:T(8,128)(2,1)}), bf16[32,128,256]{2,1,0:T(8,128)(2,1)S(1)}, u32[]{:S(2)}, u32[]{:S(2)}) %all-to-all-start.1) | async-done | bytes 2097184 | tf_op jit(solution)/shard_map/all_to_all | solution.py:241
  229.9 4.9 %all-to-all-start.3 = ((bf16[256,4,2048]{2,0,1:T(8,128)(2,1)}), bf16[256,4,2048]{2,0,1:T(8,128)(2,1)}, u32[]{:S(2)}, u32[]{:S(2)}) async-start(bf16[256,4,2048]{2,0,1:T(8,128)(2,1)} %copy.24), calls=%async_computation.3 | async-start | bytes 8388608 | tf_op jit(solution)/shard_map/all_to_all | solution.py:235
  234.8 0.0 copy-done.4
  234.8 1.3 owner_grads.1
  236.2 50.6 %all_gather.7 = bf16[1024,256]{1,0:T(8,128)(2,1)S(1)} all-gather(bf16[256,256]{1,0:T(8,128)(2,1)S(1)} %owner_grads.1), channel_id=1, replica_groups={{0,64,128,192},{8,72,136,200},{16,80,144,208},{24,88,152,216},{32,96,16..., dimensions={0}, use_global_device_ids=true | all-gather | bytes 655360 | tf_op jit(solution)/shard_map/all_gather | solution.py:244
  286.8 0.0 all-to-all-done.3
  286.8 3.5 convolution_convert_fusion.1
  290.2 1.1 copy.34
  291.4 5.4 %all-to-all-start.4 = ((bf16[8,256,256]{1,2,0:T(8,128)(2,1)}), bf16[8,256,256]{1,2,0:T(8,128)(2,1)S(1)}, u32[]{:S(2)}, u32[]{:S(2)}) async-start(bf16[8,256,256]{1,2,0:T(8,128)(2,1)} %bitcast.31), calls=%async_computation.4 | async-start | bytes 2097152 | tf_op jit(solution)/shard_map/all_to_all | solution.py:246
  296.8 5.5 %convolution_convert_fusion = bf16[256,8192]{1,0:T(8,128)(2,1)} fusion(bf16[256,256]{1,0:T(8,128)(2,1)S(1)} %bitcast.38, bf16[8192,256]{1,0:T(8,128)(2,1)} %all-gather.2.cloned.1.call-done.w_ref), kind=kOutput, calls=%fused_computation | convolution fusion | flops 1075838976 | bytes 8519680 | tf_op jit(solution)/shard_map/dot_general | solution.py:21
  302.3 17.2 %all-to-all-done.4 = bf16[8,256,256]{1,2,0:T(8,128)(2,1)S(1)} async-done(((bf16[8,256,256]{1,2,0:T(8,128)(2,1)}), bf16[8,256,256]{1,2,0:T(8,128)(2,1)S(1)}, u32[]{:S(2)}, u32[]{:S(2)}) %all-to-all-start.4) | async-done | bytes 1048608 | tf_op jit(solution)/shard_map/all_to_all | solution.py:246
  319.4 4.6 %all-to-all-start.2 = ((bf16[8,32,8192]{2,1,0:T(8,128)(2,1)}), bf16[8,32,8192]{2,1,0:T(8,128)(2,1)}, u32[]{:S(2)}, u32[]{:S(2)}) async-start(bf16[8,32,8192]{2,1,0:T(8,128)(2,1)} %bitcast.36), calls=%async_computation.2 | async-start | bytes 8388608 | tf_op jit(solution)/shard_map/all_to_all | solution.py:255
  324.0 0.1 convert_reduce_fusion
  324.2 0.8 copy.28
  324.9 0.8 copy.27
  325.7 48.0 %all-to-all-done.2 = bf16[8,32,8192]{2,1,0:T(8,128)(2,1)} async-done(((bf16[8,32,8192]{2,1,0:T(8,128)(2,1)}), bf16[8,32,8192]{2,1,0:T(8,128)(2,1)}, u32[]{:S(2)}, u32[]{:S(2)}) %all-to-all-start.2) | async-done | bytes 4194336 | tf_op jit(solution)/shard_map/all_to_all | solution.py:255
  373.6 3.7 reduce_sum.41
  (4 shorter events, 0.1 us)
Async XLA Ops:
  7.2 88.6 %all-gather.2.cloned.1.call-start = ((), (), s32[]{:S(2)}) async-start(), calls=%async_computation.5 | async-start | bytes 4325376 | tf_op jit(solution)/shard_map/all_gather | solution.py:232
  95.8 0.7 copy-start.3
  105.5 54.3 %copy-start.1 = (bf16[512,1024]{1,0:T(8,128)(2,1)S(1)}, bf16[512,1024]{1,0:T(8,128)(2,1)}, u32[]{:S(2)}) copy-start(bf16[512,1024]{1,0:T(8,128)(2,1)} %q_ref.1) | copy-start | bytes 3145732
  105.5 54.3 %copy-start.2 = (bf16[512,1024]{1,0:T(8,128)(2,1)S(1)}, bf16[512,1024]{1,0:T(8,128)(2,1)}, u32[]{:S(2)}) copy-start(bf16[512,1024]{1,0:T(8,128)(2,1)} %ct_ref.1) | copy-start | bytes 3145732
  105.5 54.3 %all-to-all-start = ((bf16[32,128,256]{2,1,0:T(8,128)(2,1)}), bf16[32,128,256]{2,1,0:T(8,128)(2,1)}, u32[]{:S(2)}, u32[]{:S(2)}) async-start(bf16[32,128,256]{2,1,0:T(8,128)(2,1)} %get-tuple-element.10), calls=%async_computation | async-start | bytes 4194304 | tf_op jit(solution)/shard_map/all_to_all | solution.py:239
  174.9 1.3 copy-start
  176.2 53.7 %all-to-all-start.1 = ((bf16[32,128,256]{2,1,0:T(8,128)(2,1)}), bf16[32,128,256]{2,1,0:T(8,128)(2,1)S(1)}, u32[]{:S(2)}, u32[]{:S(2)}) async-start(bf16[32,128,256]{2,1,0:T(8,128)(2,1)} %copy-done), calls=%async_computation.1 | async-start | bytes 4194304 | tf_op jit(solution)/shard_map/all_to_all | solution.py:241
  195.9 38.9 %copy-start.4 = (f32[128]{0:T(128)S(1)}, f32[128]{0:T(128)}, u32[]{:S(2)}) copy-start(f32[128]{0:T(128)} %param.13) | copy-start | bytes 1540
  229.9 56.9 %all-to-all-start.3 = ((bf16[256,4,2048]{2,0,1:T(8,128)(2,1)}), bf16[256,4,2048]{2,0,1:T(8,128)(2,1)}, u32[]{:S(2)}, u32[]{:S(2)}) async-start(bf16[256,4,2048]{2,0,1:T(8,128)(2,1)} %copy.24), calls=%async_computation.3 | async-start | bytes 8388608 | tf_op jit(solution)/shard_map/all_to_all | solution.py:235
  291.4 28.1 %all-to-all-start.4 = ((bf16[8,256,256]{1,2,0:T(8,128)(2,1)}), bf16[8,256,256]{1,2,0:T(8,128)(2,1)S(1)}, u32[]{:S(2)}, u32[]{:S(2)}) async-start(bf16[8,256,256]{1,2,0:T(8,128)(2,1)} %bitcast.31), calls=%async_computation.4 | async-start | bytes 2097152 | tf_op jit(solution)/shard_map/all_to_all | solution.py:246
  319.4 54.2 %all-to-all-start.2 = ((bf16[8,32,8192]{2,1,0:T(8,128)(2,1)}), bf16[8,32,8192]{2,1,0:T(8,128)(2,1)}, u32[]{:S(2)}, u32[]{:S(2)}) async-start(bf16[8,32,8192]{2,1,0:T(8,128)(2,1)} %bitcast.36), calls=%async_computation.2 | async-start | bytes 8388608 | tf_op jit(solution)/shard_map/all_to_all | solution.py:255
Sparse Core Ops, SparseCore 0:
  11.2 84.5 all-gather.1

commit v2 on v1

v2 whole, which is shorter than its diff:
```python
import functools

import jax
import jax.numpy as jnp
from jax import lax
from jax.experimental import pallas as pl
from jax.experimental.pallas import tpu as pltpu
from jax.sharding import PartitionSpec as P

TILES = 4
EPS = 1e-05
MASKED_SCORE = -1e30
NY, NZ = 4, 8
Y_GROUPS = [[y * NZ + z for y in range(NY)] for z in range(NZ)]
Z_GROUPS = [[y * NZ + z for z in range(NZ)] for y in range(NY)]
BF16, F32 = jnp.bfloat16, jnp.float32
VMEM_BYTES = 32 * 1024 * 1024
GROUP = 4


def dot_dims(a, b, a_dim, b_dim):
    return lax.dot_general(
        a, b, (((a_dim,), (b_dim,)), ((), ())), preferred_element_type=F32
    )


def project_kernel(
    pos_ref, place_ref, f_ref, kw_ref, *refs, zones
):
    vw_refs, (gain_ref, send_ref, raw_ref, kv) = refs[: len(zones)], refs[len(zones) :]
    head_dim = gain_ref.shape[1]
    tokens = send_ref.shape[1]
    total = jnp.zeros((f_ref.shape[0], 2 * head_dim), F32)
    for cols, w in weight_blocks(place_ref, kw_ref, vw_refs, zones):
        total = total + jnp.dot(f_ref[:, cols], w, preferred_element_type=F32)
    raw = total[:, :head_dim]
    raw_ref[...] = raw
    scale = lax.rsqrt(jnp.mean(raw * raw, axis=-1, keepdims=True) + EPS)
    keys = (raw * scale * gain_ref[...]).astype(BF16)
    values = total[:, head_dim:].astype(BF16)
    for i in range(kv.shape[0]):
        kv[i, :, :head_dim] = keys[i * tokens : (i + 1) * tokens]
        kv[i, :, head_dim:] = values[i * tokens : (i + 1) * tokens]

    def put(d, carry):
        send_ref[d] = kv[jnp.maximum(pos_ref[d], 0)]
        return carry

    lax.fori_loop(0, send_ref.shape[0], put, 0)


def weight_blocks(place_ref, kw_ref, vw_refs, zones):
    for ref, (offset, y_from, y_count) in zip(vw_refs, zones):
        z = lax.rem(place_ref[1] + offset + NZ, NZ)
        block = ref.shape[0] // y_count
        for i in range(y_count):
            y = lax.rem(place_ref[0] + y_from + i, NY)
            at = pl.multiple_of((y * NZ + z) * block, block)
            here = pl.ds(at, block)
            yield here, jnp.concatenate(
                [kw_ref[here, :], ref[i * block : (i + 1) * block, :]], axis=1
            )


def project(pos, place, rows, k_full, v_pieces, zones, gain, images, tokens):
    smem = pl.BlockSpec(memory_space=pltpu.SMEM)
    vmem = pl.BlockSpec(memory_space=pltpu.VMEM)
    dp, cols = pos.shape[0], 2 * k_full.shape[1]
    return pl.pallas_call(
        functools.partial(project_kernel, zones=zones),
        in_specs=[smem] * 2 + [vmem] * (3 + len(v_pieces)),
        out_specs=[vmem] * 2,
        out_shape=[
            jax.ShapeDtypeStruct((dp, tokens, cols), BF16),
            jax.ShapeDtypeStruct((rows.shape[0], cols // 2), F32),
        ],
        scratch_shapes=[pltpu.VMEM((images, tokens, cols), BF16)],
        compiler_params=pltpu.CompilerParams(vmem_limit_bytes=VMEM_BYTES),
        cost_estimate=pl.CostEstimate(
            flops=2 * rows.size * cols, bytes_accessed=12 * 2**20, transcendentals=0
        ),
        name="project",
    )(pos, place, rows, k_full, *v_pieces, gain)


def feature_kernel(place_ref, grad_ref, kw_ref, *refs, zones, targets):
    vw_refs, (own_ref, other_ref, lhs) = refs[: len(zones)], refs[len(zones) :]
    half = own_ref.shape[0]
    chips = targets // 2
    tokens = grad_ref.shape[0] // 2
    share = tokens // targets
    for core in range(2):
        for chip in range(chips):
            x = lax.rem(place_ref[2] + chip, chips)
            target = x * 2 + lax.rem(place_ref[3] + core, 2)
            for i in range(2):
                at = pl.multiple_of(i * tokens + target * share, share)
                to = ((core * chips + chip) * 2 + i) * share
                lhs[to : to + share, :] = grad_ref[pl.ds(at, share), :]
    for cols, w in weight_blocks(place_ref, kw_ref, vw_refs, zones):
        part = dot_dims(lhs[...], w, 1, 1).astype(BF16)
        own_ref[:, cols] = part[:half]
        other_ref[:, cols] = part[half:]


def feature_terms(place, grads, k_full, v_pieces, zones, targets):
    smem = pl.BlockSpec(memory_space=pltpu.SMEM)
    vmem = pl.BlockSpec(memory_space=pltpu.VMEM)
    half = jax.ShapeDtypeStruct((grads.shape[0] // 2, k_full.shape[0]), BF16)
    return pl.pallas_call(
        functools.partial(feature_kernel, zones=zones, targets=targets),
        in_specs=[smem] + [vmem] * (2 + len(v_pieces)),
        out_specs=[vmem] * 2,
        out_shape=[half, half],
        scratch_shapes=[pltpu.VMEM(grads.shape, BF16)],
        compiler_params=pltpu.CompilerParams(vmem_limit_bytes=VMEM_BYTES),
        cost_estimate=pl.CostEstimate(
            flops=4 * half.size * grads.shape[1], bytes_accessed=8 * 2**20, transcendentals=0
        ),
        name="feature_terms",
    )(place, grads, k_full, *v_pieces)


def load_heads(ref, start, rows, head_dim):
    heads = ref.shape[1] // head_dim
    return jnp.concatenate(
        [ref[pl.ds(start, rows), g * head_dim : (g + 1) * head_dim] for g in range(heads)],
        axis=0,
    )


def store_heads(ref, start, rows, head_dim, full):
    for g in range(ref.shape[1] // head_dim):
        ref[pl.ds(start, rows), g * head_dim : (g + 1) * head_dim] = full[
            g * rows : (g + 1) * rows
        ]


def attend_kernel(
    owner_ref, valid_ref, first_ref, q_ref, ct_ref, kv_ref, part_ref, probs_ref, ds_ref, acc
):
    blocks = owner_ref.shape[0]
    rows = q_ref.shape[0] // blocks
    head_dim = kv_ref.shape[2] // 2
    tokens = kv_ref.shape[1]
    scale = head_dim**-0.5
    part_ref[...] = jnp.zeros_like(part_ref)
    acc[...] = jnp.zeros_like(acc)

    def some_blocks(step, carry):
        at = [step * GROUP + i for i in range(GROUP)]
        owners = [owner_ref[b] for b in at]
        starts = [pl.multiple_of(b * rows, rows) for b in at]
        queries = [load_heads(q_ref, s, rows, head_dim) for s in starts]
        grads = [load_heads(ct_ref, s, rows, head_dim) for s in starts]
        scores = [
            dot_dims(kv_ref[o, :, :head_dim], q, 1, 1) * scale for o, q in zip(owners, queries)
        ]
        d_probs = [dot_dims(kv_ref[o, :, head_dim:], g, 1, 1) for o, g in zip(owners, grads)]
        token = lax.broadcasted_iota(jnp.int32, (tokens, 1), 0)
        scores = [
            jnp.where(token < valid_ref[b], s, MASKED_SCORE) for b, s in zip(at, scores)
        ]
        weights = [jnp.exp(s - jnp.max(s, axis=0, keepdims=True)) for s in scores]
        probs = [w * (1.0 / jnp.sum(w, axis=0, keepdims=True)) for w in weights]
        halves = [p.astype(BF16) for p in probs]
        deltas = [jnp.sum(p * d, axis=0, keepdims=True) for p, d in zip(probs, d_probs)]
        d_scores = [
            (p * (d - x) * scale).astype(BF16) for p, d, x in zip(probs, d_probs, deltas)
        ]
        key_parts = [
            jnp.dot(d, q, preferred_element_type=F32) for d, q in zip(d_scores, queries)
        ]
        value_parts = [
            jnp.dot(p, g, preferred_element_type=F32) for p, g in zip(halves, grads)
        ]
        key_run, value_run = acc[:, :head_dim], acc[:, head_dim:]
        for i, b in enumerate(at):
            keep = first_ref[b] == 0
            key_run = key_parts[i] + jnp.where(keep, key_run, 0.0)
            value_run = value_parts[i] + jnp.where(keep, value_run, 0.0)
            part_ref[owners[i], :, :head_dim] = key_run.astype(BF16)
            part_ref[owners[i], :, head_dim:] = value_run.astype(BF16)
            probs_ref[b] = halves[i]
            ds_ref[b] = d_scores[i]
        acc[:, :head_dim] = key_run
        acc[:, head_dim:] = value_run
        return carry

    lax.fori_loop(0, blocks // GROUP, some_blocks, 0)


def attend(owner, valid, first, queries, cotangent, kv):
    smem = pl.BlockSpec(memory_space=pltpu.SMEM)
    vmem = pl.BlockSpec(memory_space=pltpu.VMEM)
    blocks, (_, tokens, cols) = owner.shape[0], kv.shape
    rows = queries.size * 2 // (blocks * cols)
    stash = jax.ShapeDtypeStruct((blocks, tokens, rows), BF16)
    return pl.pallas_call(
        attend_kernel,
        in_specs=[smem] * 3 + [vmem] * 3,
        out_specs=[vmem] * 3,
        out_shape=[jax.ShapeDtypeStruct(kv.shape, BF16), stash, stash],
        scratch_shapes=[pltpu.VMEM(kv.shape[1:], F32)],
        compiler_params=pltpu.CompilerParams(vmem_limit_bytes=VMEM_BYTES),
        cost_estimate=pl.CostEstimate(
            flops=8 * queries.size * tokens, bytes_accessed=8 * 2**20, transcendentals=0
        ),
        name="attend",
    )(owner, valid, first, queries, cotangent, kv)


def apply_kernel(owner_ref, kv_ref, probs_ref, ds_ref, out_ref, gq_ref):
    blocks = owner_ref.shape[0]
    rows = out_ref.shape[0] // blocks
    head_dim = kv_ref.shape[2] // 2

    def some_blocks(step, carry):
        at = [step * GROUP + i for i in range(GROUP)]
        owners = [owner_ref[b] for b in at]
        outs = [
            dot_dims(probs_ref[b], kv_ref[o, :, head_dim:], 0, 0) for b, o in zip(at, owners)
        ]
        gqs = [dot_dims(ds_ref[b], kv_ref[o, :, :head_dim], 0, 0) for b, o in zip(at, owners)]
        for i, b in enumerate(at):
            start = pl.multiple_of(b * rows, rows)
            store_heads(out_ref, start, rows, head_dim, outs[i].astype(BF16))
            store_heads(gq_ref, start, rows, head_dim, gqs[i].astype(BF16))
        return carry

    lax.fori_loop(0, blocks // GROUP, some_blocks, 0)


def apply(owner, kv, probs, d_scores, shape):
    smem = pl.BlockSpec(memory_space=pltpu.SMEM)
    vmem = pl.BlockSpec(memory_space=pltpu.VMEM)
    out = jax.ShapeDtypeStruct(shape, BF16)
    return pl.pallas_call(
        apply_kernel,
        in_specs=[smem] + [vmem] * 3,
        out_specs=[vmem] * 2,
        out_shape=[out, out],
        compiler_params=pltpu.CompilerParams(vmem_limit_bytes=VMEM_BYTES),
        cost_estimate=pl.CostEstimate(
            flops=4 * out.size * kv.shape[1], bytes_accessed=6 * 2**20, transcendentals=0
        ),
        name="apply",
    )(owner, kv, probs, d_scores)


def owner_kernel(
    pos_ref, place_ref, part_ref, raw_ref, gain_ref, grad_ref, by_core_ref, acc
):
    head_dim = gain_ref.shape[1]
    tokens = part_ref.shape[1]
    acc[...] = jnp.zeros_like(acc)

    def add(d, carry):
        @pl.when(pos_ref[d] >= 0)
        def _():
            acc[pos_ref[d]] += part_ref[d].astype(F32)

        return carry

    lax.fori_loop(0, part_ref.shape[0], add, 0)
    gain = gain_ref[...]
    for i in range(acc.shape[0]):
        here = slice(i * tokens, (i + 1) * tokens)
        raw = raw_ref[here]
        scale = lax.rsqrt(jnp.mean(raw * raw, axis=-1, keepdims=True) + EPS)
        scaled = acc[i, :, :head_dim] * gain
        pull = jnp.mean(raw * scaled, axis=-1, keepdims=True)
        grad = scale * scaled - raw * (scale * scale * scale * pull)
        grad_ref[here, :head_dim] = grad.astype(BF16)
        grad_ref[here, head_dim:] = acc[i, :, head_dim:].astype(BF16)
    for i in range(2):
        at = pl.multiple_of(lax.rem(place_ref[3] + i, 2) * tokens, tokens)
        by_core_ref[i * tokens : (i + 1) * tokens, :] = grad_ref[pl.ds(at, tokens), :]


def owner_grads(pos, place, parts, raw, gain, images):
    smem = pl.BlockSpec(memory_space=pltpu.SMEM)
    vmem = pl.BlockSpec(memory_space=pltpu.VMEM)
    return pl.pallas_call(
        owner_kernel,
        in_specs=[smem] * 2 + [vmem] * 3,
        out_specs=[vmem] * 2,
        out_shape=[jax.ShapeDtypeStruct((raw.shape[0], parts.shape[2]), BF16)] * 2,
        scratch_shapes=[pltpu.VMEM((images,) + parts.shape[1:], F32)],
        compiler_params=pltpu.CompilerParams(vmem_limit_bytes=VMEM_BYTES),
        name="owner_grads",
    )(pos, place, parts, raw, gain)


def transpose_kernel(*refs):
    pieces, out_ref = refs[:-1], refs[-1]
    tokens = pieces[0].shape[0]
    for i, ref in enumerate(pieces):
        out_ref[:, i * tokens : (i + 1) * tokens] = ref[...].T


def transpose_pieces(pieces):
    vmem = pl.BlockSpec(memory_space=pltpu.VMEM)
    tokens, width = pieces[0].shape
    return pl.pallas_call(
        transpose_kernel,
        in_specs=[vmem] * len(pieces),
        out_specs=vmem,
        out_shape=jax.ShapeDtypeStruct((width, tokens * len(pieces)), BF16),
        compiler_params=pltpu.CompilerParams(vmem_limit_bytes=VMEM_BYTES),
        cost_estimate=pl.CostEstimate(
            flops=0, bytes_accessed=8 * tokens * width * len(pieces), transcendentals=0
        ),
        name="transpose_pieces",
    )(*pieces)


def weight_kernel(own_ref, other_ref, *refs):
    lines, out_ref = refs[:-1], refs[-1]
    half = lines[0].shape[0] // 2
    first = jnp.concatenate([ref[:half, :] for ref in lines], axis=0)
    second = jnp.concatenate([ref[half:, :] for ref in lines], axis=0)
    block = out_ref.shape[1]
    for i in range(out_ref.shape[0]):
        here = slice(i * block, (i + 1) * block)
        total = jnp.dot(own_ref[here, :], first, preferred_element_type=F32)
        total = total + jnp.dot(other_ref[here, :], second, preferred_element_type=F32)
        out_ref[i] = total.astype(BF16)


def weight_terms(own_cols, other_cols, lines):
    vmem = pl.BlockSpec(memory_space=pltpu.VMEM)
    width, cols = own_cols.shape[0], lines[0].shape[1]
    return pl.pallas_call(
        weight_kernel,
        in_specs=[vmem] * (2 + len(lines)),
        out_specs=vmem,
        out_shape=jax.ShapeDtypeStruct((NZ, width // NZ, cols), BF16),
        compiler_params=pltpu.CompilerParams(vmem_limit_bytes=VMEM_BYTES),
        cost_estimate=pl.CostEstimate(
            flops=4 * own_cols.size * cols, bytes_accessed=6 * 2**20, transcendentals=0
        ),
        name="weight_terms",
    )(own_cols, other_cols, *lines)


def shift_y(x, by):
    if by == 0:
        return x
    pairs = [(y * NZ + z, (y + by) % NY * NZ + z) for y in range(NY) for z in range(NZ)]
    return lax.ppermute(x, "dp", pairs)


def shift_z(x, by):
    pairs = [(y * NZ + z, y * NZ + (z + by) % NZ) for y in range(NY) for z in range(NZ)]
    return lax.ppermute(x, "dp", pairs)


def swap_cores(x, count):
    return lax.ppermute(x, "tensor", [(t, t ^ 1) for t in range(count)])


def local(
    queries, features, k_weight, v_weight, k_gain, block_image, image_slot, image_tiles, cotangent
):
    dp_count = lax.axis_size("dp")
    tensor_count = lax.axis_size("tensor")
    me = lax.axis_index("dp")
    images, tokens, width = features.shape
    head_dim = k_gain.shape[0]
    cols = 2 * head_dim
    rows = features.reshape(images * tokens, width)
    gain = k_gain.reshape(1, head_dim)

    image_ids = lax.broadcasted_iota(jnp.int32, (1, image_slot.shape[0]), 1)
    id_match = block_image[:, None] == image_ids
    slots = jnp.sum(jnp.where(id_match, image_slot[None, :], 0), axis=1).reshape(dp_count, -1)
    tiles = jnp.sum(jnp.where(id_match, image_tiles[None, :], 0), axis=1).reshape(dp_count, -1)
    my_slots = lax.dynamic_index_in_dim(slots, me, 0, keepdims=False)
    my_tiles = lax.dynamic_index_in_dim(tiles, me, 0, keepdims=False)
    owner = my_slots // images
    valid = my_tiles * (tokens // TILES)
    first = jnp.concatenate(
        [jnp.ones((1,), jnp.int32), (my_slots[1:] != my_slots[:-1]).astype(jnp.int32)]
    )
    pos = jnp.max(jnp.where(slots // images == me, slots % images, -1), axis=1)

    pos, owner, valid, first = lax.optimization_barrier((pos, owner, valid, first))
    my_y, my_z = me // NZ, lax.rem(me, NZ)
    tensor = lax.axis_index("tensor")
    place = jnp.stack([my_y, my_z, tensor // 2, lax.rem(tensor, 2)])

    block = k_weight.shape[0]
    k_line = lax.all_to_all(
        jnp.broadcast_to(k_weight, (NZ,) + k_weight.shape),
        "dp", 0, 0, tiled=True, axis_index_groups=Z_GROUPS,
    )
    v_line = jnp.concatenate([shift_y(v_weight, (NY - i) % NY) for i in range(NY)])
    below, above = shift_z(v_line, 1), shift_z(v_line, -1)
    k_line, below, above = lax.optimization_barrier((k_line, below, above))
    k_full = lax.all_to_all(
        jnp.broadcast_to(k_line, (NY,) + k_line.shape),
        "dp", 0, 0, tiled=True, axis_index_groups=Y_GROUPS,
    ).reshape(width, head_dim)
    v_pieces, zones = [v_line], [(0, 0, NY)]
    for hop in range(1, NZ // 2):
        if hop > 1:
            below, above = shift_z(below, 1), shift_z(above, -1)
        v_pieces += [below, above]
        zones += [(-hop, 0, NY), (hop, 0, NY)]
    half = NY // 2 * block
    v_pieces += [shift_z(below[:half], 1), shift_z(above[half:], -1)]
    zones += [(NZ // 2, 0, NY // 2), (NZ // 2, NY // 2, NY // 2)]

    send, raw = project(pos, place, rows, k_full, v_pieces, zones, gain, images, tokens)
    kv = lax.all_to_all(send, "dp", 0, 0, tiled=True)

    rows_later, _ = lax.optimization_barrier((features, raw))
    core = place[3]
    span = width // NY
    col_pieces = [
        shift_y(
            lax.dynamic_slice(
                rows_later, (core, 0, (my_y + s) % NY * span), (1, tokens, span)
            )[0],
            s,
        )
        for s in range(NY)
    ]

    parts, probs, d_scores = attend(owner, valid, first, queries, cotangent, kv)
    parts, col_pieces = lax.optimization_barrier((parts, col_pieces))
    parts = lax.all_to_all(parts, "dp", 0, 0, tiled=True)
    own_cols = transpose_pieces(col_pieces)
    other_cols = swap_cores(own_cols, tensor_count)
    attended, grad_queries = apply(owner, kv, probs, d_scores, queries.shape)
    parts, other_cols, attended, grad_queries = lax.optimization_barrier(
        (parts, other_cols, attended, grad_queries)
    )
    grads, by_core = owner_grads(pos, place, parts, raw, gain, images)

    lines = [shift_y(by_core, s) for s in range(NY)]
    shares = weight_terms(own_cols, other_cols, lines)
    shares = lax.all_to_all(
        shares, "dp", 0, 0, tiled=True, axis_index_groups=Z_GROUPS
    )
    weight_grads = jnp.sum(shares.astype(F32), axis=0)

    own, other = feature_terms(place, grads, k_full, v_pieces, zones, tensor_count)
    other = swap_cores(other, tensor_count)
    share = own.shape[0] * 2 // tensor_count
    pairs = [
        own[s * share : (s + 1) * share].astype(F32)
        + other[s * share : (s + 1) * share].astype(F32)
        for s in range(tensor_count // 2)
    ]
    grad_features = pairs[0]
    for s in range(1, tensor_count // 2):
        grad_features = grad_features + lax.ppermute(
            pairs[s].astype(BF16),
            "tensor",
            [(t, (t + 2 * s) % tensor_count) for t in range(tensor_count)],
        ).astype(F32)
    grad_features = grad_features.astype(BF16).reshape(images, tokens // tensor_count, width)
    return (
        attended,
        grad_queries,
        grad_features,
        weight_grads[:, :head_dim],
        weight_grads[:, head_dim:],
    )


def solution(mesh):
    in_specs = (
        P("dp", "tensor"),
        P("dp", None, None),
        P("dp", "tensor"),
        P("dp", "tensor"),
        P(),
        P(),
        P(),
        P(),
        P("dp", "tensor"),
    )
    out_specs = (
        P("dp", "tensor"),
        P("dp", "tensor"),
        P("dp", "tensor", None),
        P("dp", "tensor"),
        P("dp", "tensor"),
    )
    return jax.shard_map(local, mesh=mesh, in_specs=in_specs, out_specs=out_specs, check_vma=False)
```

time: 387 us -> 253 us (0.65)
  waiting for transfers between devices: 233 us -> 127 us
  blocking collectives: 50.6 us -> 0 us
  starting transfers between devices: 26.4 us -> 64.9 us
  between operations: 14.1 us -> 0.98 us
  matrix products: 8.92 us -> 0 us
  local copies, waits for them, and re-layouts: 19.1 us -> 24.2 us
    all_gather x1 -> x0, waiting for transfers between devices: 86 us -> none  [local(): lax.all_gather(jnp.concatenate([k_weight, v_weight], axis=1), 'dp', axis=...]
    all_gather x1 -> x0, blocking collectives: 50.6 us -> none  [local(): lax.all_gather(grads, 'dp', axis=0, tiled=True, axis_index_groups=Y_GROUPS)]
    all_to_all x3, waiting for transfers between devices: 65.1 us -> 20.5 us  [the longest x1 19.1 us: local(): lax.all_to_all(shares, 'dp', 0, 0, tiled=True, axis_index_groups=Z_GROUPS)]
    ppermute x0 -> x22, starting transfers between devices: none -> 30.5 us  [the longest x9 15.5 us: shift_y(): return lax.ppermute(x, 'dp', pairs)]
    ppermute x0 -> x22, waiting for transfers between devices: none -> 30.5 us  [the longest x8 21.1 us: shift_z(): return lax.ppermute(x, 'dp', pairs)]
    all_to_all x2 -> x0, local copies, waits for them, and re-layouts: 14.3 us -> none  [local(): lax.all_to_all(rows, 'dp', 1, 0, tiled=True, axis_index_groups=Y_GROUPS)]
    unnamed x12 -> x57, local copies, waits for them, and re-layouts: 3.5 us -> 15.8 us
    all_to_all x1, waiting for transfers between devices: 48 us -> 38.5 us  [local(): kv = lax.all_to_all(send, 'dp', 0, 0, tiled=True)]
  transfers between devices with their start and end apart: 6 -> 27, of which waited for: 5 -> 14; matrix products, arithmetic and copies ran while one was open for 4% -> 5% of each run, Pallas kernels for 0% -> 6%
where the time goes in v2:
time: 253 us; the launch traced here: 251 us
  waiting for transfers between devices  127 us (50%)
  starting transfers between devices  64.9 us (26%)
  Pallas kernels  24.9 us (10%)
  local copies, waits for them, and re-layouts  24.2 us (10%)
  other arithmetic  8.16 us (3%)
    all_to_all x1, waiting for transfers between devices, local(): kv = lax.all_to_all(send, 'dp', 0, 0, tiled=True)  38.5 us
    all_to_all x1, waiting for transfers between devices, local(): parts = lax.all_to_all(parts, 'dp', 0, 0, tiled=True)  37.9 us
    ppermute x8, waiting for transfers between devices, shift_z(): return lax.ppermute(x, 'dp', pairs)  21.1 us
    all_to_all x1, waiting for transfers between devices, local(): lax.all_to_all(shares, 'dp', 0, 0, tiled=True, axis_index_groups=Z_GROUPS)  19.1 us
    unnamed x57, local copies, waits for them, and re-layouts  15.8 us
    ppermute x9, starting transfers between devices, shift_y(): return lax.ppermute(x, 'dp', pairs)  15.5 us
    all_to_all x1, starting transfers between devices, local(): kv = lax.all_to_all(send, 'dp', 0, 0, tiled=True)  10.3 us
    ppermute x9, waiting for transfers between devices, shift_y(): return lax.ppermute(x, 'dp', pairs)  9.4 us
  transfers between devices with their start and end apart: 27, of which 14 were waited for; matrix products, arithmetic and copies ran while one was open for 5% of the time, Pallas kernels for 6%

profile of v2, /device:TPU:32, one launch (start us, length us, event | category | flops | bytes accessed | tf_op | source)
XLA Modules:
  0.0 250.6 jit_solution(17685840544116093319)
XLA Ops:
  0.6 1.7 broadcast_in_dim.32
  2.3 8.6 %all-to-all-start = ((bf16[8,256,128]{2,1,0:T(8,128)(2,1)}), bf16[8,256,128]{2,1,0:T(8,128)(2,1)S(1)}, u32[]{:S(2)}, u32[]{:S(2)}) async-start(bf16[8,256,128]{2,1,0:T(8,128)(2,1)} %broadcast_in_dim.32), calls=%async_computation | async-start | bytes 1048576 | tf_op jit(solution)/shard_map/all_to_all | solution.py:394
  10.9 3.0 %collective-permute-start = (bf16[256,128]{1,0:T(8,128)(2,1)}, bf16[256,128]{1,0:T(8,128)(2,1)S(1)}, u32[]{:S(2)}, u32[]{:S(2)}) collective-permute-start(bf16[256,128]{1,0:T(8,128)(2,1)} %param.12), channel_id=1, source_target_pairs={{0,192},{8,200},{16,208},{24,216},{32,224},{40,232},{48,240},{56,2... | collective-permute-start | bytes 196616 | tf_op jit(solution)/shard_map/ppermute | solution.py:351
  16.4 3.5 %collective-permute-done.1 = bf16[256,128]{1,0:T(8,128)(2,1)S(1)} collective-permute-done((bf16[256,128]{1,0:T(8,128)(2,1)}, bf16[256,128]{1,0:T(8,128)(2,1)S(1)}, u32[]{:S(2)}, u32[]{:S(2)}) %collective-permute-start.1) | collective-permute-done | bytes 65568 | tf_op jit(solution)/shard_map/ppermute | solution.py:351
  20.6 1.5 collective-permute-start.3
  22.7 5.7 %collective-permute-done.3.refs_1_ = bf16[1024,128]{1,0:T(8,128)(2,1)S(1)} collective-permute-done((bf16[1024,128]{1,0:T(8,128)(2,1)S(1)}, bf16[1024,128]{1,0:T(8,128)(2,1)S(1)}, u32[]{:S(2)}, u32[]{:S(2)}) %collective-permute-start.3) | collective-permute-done | bytes 262176 | tf_op jit(solution)/shard_map/ppermute | solution.py:356
  28.4 1.4 collective-permute-done.4.refs_2_
  29.9 1.8 broadcast_in_dim.33
  31.7 4.3 %all-to-all-start.1 = ((bf16[4,8,256,128]{3,2,1,0:T(8,128)(2,1)}), bf16[4,8,256,128]{3,2,1,0:T(8,128)(2,1)S(1)}, u32[]{:S(2)}, u32[]{:S(2)}) async-start(bf16[4,8,256,128]{3,2,1,0:T(8,128)(2,1)} %broadcast_in_dim.33), calls=%async_computation.1 | async-start | bytes 4194304 | tf_op jit(solution)/shard_map/all_to_all | solution.py:401
  36.0 1.8 collective-permute-start.6
  38.5 4.7 %collective-permute-done.6.refs_4_ = bf16[1024,128]{1,0:T(8,128)(2,1)} collective-permute-done((bf16[1024,128]{1,0:T(8,128)(2,1)S(1)}, bf16[1024,128]{1,0:T(8,128)(2,1)}, u32[]{:S(2)}, u32[]{:S(2)}) %collective-permute-start.6) | collective-permute-done | bytes 262176 | tf_op jit(solution)/shard_map/ppermute | solution.py:356
  43.1 2.1 collective-permute-start.8
  46.2 4.3 %collective-permute-done.8.refs_6_ = bf16[1024,128]{1,0:T(8,128)(2,1)S(1)} collective-permute-done((bf16[1024,128]{1,0:T(8,128)(2,1)}, bf16[1024,128]{1,0:T(8,128)(2,1)S(1)}, u32[]{:S(2)}, u32[]{:S(2)}) %collective-permute-start.8) | collective-permute-done | bytes 262176 | tf_op jit(solution)/shard_map/ppermute | solution.py:356
  51.2 1.5 collective-permute-start.10
  55.3 1.7 collective-permute-done.10.refs_8_
  57.0 3.2 %collective-permute-done.9.refs_7_ = bf16[512,128]{1,0:T(8,128)(2,1)} collective-permute-done((bf16[512,128]{1,0:T(8,128)(2,1)}, bf16[512,128]{1,0:T(8,128)(2,1)}, u32[]{:S(2)}, u32[]{:S(2)}) %collective-permute-start.9) | collective-permute-done | bytes 131104 | tf_op jit(solution)/shard_map/ppermute | solution.py:356
  60.2 1.4 all-to-all-done.1
  61.6 2.2 copy-done
  63.8 2.8 %project.1 = (bf16[32,128,256]{2,1,0:T(8,128)(2,1)S(1)}, f32[256,128]{1,0:T(8,128)S(1)}) custom-call(s32[32]{0:T(128)S(1)} %fusion.2.pos_ref, s32[4]{0:T(128)S(1)} %pad_add_fusion.place_ref, bf16[256,8192]{1,0:T(8,128)(2,1)S(1)} %bitcast.30, bf16[8192,128]{1,0:T(8,128)(2,1)S(1)} %bitcast.28, bf16[1024,128]{1,0:T(8,128)(2,1)S(1)} %constant_dynamic-update-slice_fusion.refs_0_, ...), custom_call_target="tpu_custom_call" | custom-call | flops 1073741824 | bytes 12582912 | tf_op jit(solution)/shard_map/project/pallas_call | solution.py:69
  66.6 1.4 copy-done.3
  68.6 10.3 %all-to-all-start.2 = ((bf16[32,128,256]{2,1,0:T(8,128)(2,1)}), bf16[32,128,256]{2,1,0:T(8,128)(2,1)}, u32[]{:S(2)}, u32[]{:S(2)}) async-start(bf16[32,128,256]{2,1,0:T(8,128)(2,1)} %copy-done.3), calls=%async_computation.2 | async-start | bytes 4194304 | tf_op jit(solution)/shard_map/all_to_all | solution.py:416
  79.0 2.7 %dynamic-slice_bitcast_fusion = (bf16[128,2048]{1,0:T(8,128)(2,1)}, bf16[128,2048]{1,0:T(8,128)(2,1)}, bf16[128,2048]{1,0:T(8,128)(2,1)}, bf16[128,2048]{1,0:T(8,128)(2,1)S(1)}) fusion(bf16[2,128,8192]{2,1,0:T(8,128)(2,1)} %param.10, s32[]{:T(128)S(6)} %select_n.85, s32[]{:T(128)S(6)} %select_n.93, s32[]{:T(128)S(6)} %select_n.91, s32[]{:T(128)S(6)} %select_n.89, ...), kind=kLoop, calls=%fused_computation.5 | loop fusion | bytes 4194324 | tf_op jit(solution)/shard_map/squeeze | solution.py:423
  81.8 1.5 collective-permute-start.11
  83.2 2.7 %collective-permute-start.12 = (bf16[128,2048]{1,0:T(8,128)(2,1)}, bf16[128,2048]{1,0:T(8,128)(2,1)}, u32[]{:S(2)}, u32[]{:S(2)}) collective-permute-start(bf16[128,2048]{1,0:T(8,128)(2,1)} %get-tuple-element.69), channel_id=1, source_target_pairs={{0,128},{8,136},{16,144},{24,152},{32,160},{40,168},{48,176},{56,1... | collective-permute-start | bytes 1572872 | tf_op jit(solution)/shard_map/ppermute | solution.py:351
  86.0 1.4 collective-permute-start.13
  87.4 38.5 %all-to-all-done.2.kv_ref = bf16[32,128,256]{2,1,0:T(8,128)(2,1)} async-done(((bf16[32,128,256]{2,1,0:T(8,128)(2,1)}), bf16[32,128,256]{2,1,0:T(8,128)(2,1)}, u32[]{:S(2)}, u32[]{:S(2)}) %all-to-all-start.2) | async-done | bytes 2097184 | tf_op jit(solution)/shard_map/all_to_all | solution.py:416
  129.7 5.7 %attend.1 = (bf16[32,128,256]{2,1,0:T(8,128)(2,1)S(1)}, bf16[32,128,128]{2,1,0:T(8,128)(2,1)S(1)}, bf16[32,128,128]{2,1,0:T(8,128)(2,1)S(1)}) custom-call(s32[32]{0:T(128)S(1)} %get-tuple-element.33.owner_ref, s32[32]{0:T(128)S(1)} %copy-done.22, s32[32]{0:T(128)S(1)} %copy-done.23, bf16[512,1024]{1,0:T(8,128)(2,1)S(1)} %copy-done.9, ...), custom_call_target="tpu_custom_call" | custom-call | flops 536870912 | bytes 8388608 | tf_op jit(solution)/shard_map/attend/pallas_call | solution.py:199
  135.4 1.4 copy-done.4
  138.7 6.1 %all-to-all-start.3 = ((bf16[32,128,256]{2,1,0:T(8,128)(2,1)}), bf16[32,128,256]{2,1,0:T(8,128)(2,1)}, u32[]{:S(2)}, u32[]{:S(2)}) async-start(bf16[32,128,256]{2,1,0:T(8,128)(2,1)} %copy-done.4), calls=%async_computation.3 | async-start | bytes 4194304 | tf_op jit(solution)/shard_map/all_to_all | solution.py:433
  144.9 2.1 transpose_pieces.1.own_ref
  147.1 5.6 %apply.1 = (bf16[512,1024]{1,0:T(8,128)(2,1)}, bf16[512,1024]{1,0:T(8,128)(2,1)}) custom-call(s32[32]{0:T(128)S(1)} %get-tuple-element.33.owner_ref, bf16[32,128,256]{2,1,0:T(8,128)(2,1)} %all-to-all-done.2.kv_ref, bf16[32,128,128]{2,1,0:T(8,128)(2,1)S(1)} %copy-done.12, bf16[32,128,128]{2,1,0:T(8,128)(2,1)S(1)} %copy-done.14), custom_call_target="tpu_custom_call" | custom-call | flops 268435456 | bytes 6291456 | tf_op jit(solution)/shard_map/apply/pallas_call | solution.py:238
  152.8 1.3 copy-done.7
  154.1 37.9 %all-to-all-done.3.part_ref = bf16[32,128,256]{2,1,0:T(8,128)(2,1)} async-done(((bf16[32,128,256]{2,1,0:T(8,128)(2,1)}), bf16[32,128,256]{2,1,0:T(8,128)(2,1)}, u32[]{:S(2)}, u32[]{:S(2)}) %all-to-all-start.3) | async-done | bytes 2097184 | tf_op jit(solution)/shard_map/all_to_all | solution.py:433
  192.9 2.4 owner_grads.1
  195.4 4.0 %feature_terms.1 = (bf16[128,8192]{1,0:T(8,128)(2,1)S(1)}, bf16[128,8192]{1,0:T(8,128)(2,1)}) custom-call(s32[4]{0:T(128)S(1)} %pad_add_fusion.place_ref, bf16[256,256]{1,0:T(8,128)(2,1)S(1)} %get-tuple-element.56.grad_ref, bf16[8192,128]{1,0:T(8,128)(2,1)S(1)} %bitcast.29, bf16[1024,128]{1,0:T(8,128)(2,1)S(1)} %constant_dynamic-update-slice_fusion.refs_0_, ...), custom_call_target="tpu_custom_call" | custom-call | flops 1073741824 | bytes 8388608 | tf_op jit(solution)/shard_map/feature_terms/pallas_call | solution.py:110
  200.7 1.4 collective-permute-start.19
  202.2 1.6 collective-permute-start.20
  203.8 2.3 collective-permute-start.21
  206.0 4.6 %collective-permute-done.19.refs_1_ = bf16[256,256]{1,0:T(8,128)(2,1)S(1)} collective-permute-done((bf16[256,256]{1,0:T(8,128)(2,1)S(1)}, bf16[256,256]{1,0:T(8,128)(2,1)S(1)}, u32[]{:S(2)}, u32[]{:S(2)}) %collective-permute-start.19) | collective-permute-done | bytes 131104 | tf_op jit(solution)/shard_map/ppermute | solution.py:351
  211.2 2.2 weight_terms.1
  213.5 5.1 %all-to-all-start.4 = ((bf16[8,256,256]{2,1,0:T(8,128)(2,1)}), bf16[8,256,256]{2,1,0:T(8,128)(2,1)}, u32[]{:S(2)}, u32[]{:S(2)}) async-start(bf16[8,256,256]{2,1,0:T(8,128)(2,1)} %weight_terms.1), calls=%async_computation.4 | async-start | bytes 2097152 | tf_op jit(solution)/shard_map/all_to_all | solution.py:444
  218.6 2.5 %add_convert_fusion.3 = (bf16[32,8192]{1,0:T(8,128)(2,1)}, bf16[32,8192]{1,0:T(8,128)(2,1)S(1)}, bf16[32,8192]{1,0:T(8,128)(2,1)S(1)}) fusion(bf16[128,8192]{1,0:T(8,128)(2,1)} %collective-permute-done.15, bf16[128,8192]{1,0:T(8,128)(2,1)S(1)} %copy-done.6), kind=kLoop, calls=%fused_computation.4 | loop fusion | flops 3145728 | bytes 4718592 | tf_op jit(solution)/shard_map/convert_element_type | solution.py:460
  221.1 1.5 collective-permute-start.16
  222.6 2.7 %collective-permute-start.17 = (bf16[32,8192]{1,0:T(8,128)(2,1)S(1)}, bf16[32,8192]{1,0:T(8,128)(2,1)}, u32[]{:S(2)}, u32[]{:S(2)}) collective-permute-start(bf16[32,8192]{1,0:T(8,128)(2,1)S(1)} %get-tuple-element.67), channel_id=1, source_target_pairs={{0,4},{1,5},{2,6},{3,7},{4,0},{5,1},{6,2},{7,3},{8,12},{9,13},{10,... | collective-permute-start | bytes 1572872 | tf_op jit(solution)/shard_map/ppermute | solution.py:459
  225.3 1.4 collective-permute-start.18
  226.7 19.1 %all-to-all-done.4 = bf16[8,256,256]{2,1,0:T(8,128)(2,1)} async-done(((bf16[8,256,256]{2,1,0:T(8,128)(2,1)}), bf16[8,256,256]{2,1,0:T(8,128)(2,1)}, u32[]{:S(2)}, u32[]{:S(2)}) %all-to-all-start.4) | async-done | bytes 1048608 | tf_op jit(solution)/shard_map/all_to_all | solution.py:444
  245.8 1.4 convert_reduce_fusion
  247.9 2.6 %add_convert_fusion = bf16[32,8192]{1,0:T(8,128)(2,1)} fusion(bf16[32,8192]{1,0:T(8,128)(2,1)} %collective-permute-done.18, bf16[32,8192]{1,0:T(8,128)(2,1)} %collective-permute-done.17, bf16[32,8192]{1,0:T(8,128)(2,1)} %collective-permute-done.16, bf16[128,8192]{1,0:T(8,128)(2,1)} %collective-permute-done.15, bf16[128,8192]{1,0:T(8,128)(2,1)S(1)} %copy-done.6), kind=kLoop, calls=%fused_computation.1 | loop fusion | flops 2621440 | bytes 3145728 | tf_op jit(solution)/shard_map/convert_element_type | solution.py:464
  (89 shorter events, 18.6 us)
Async XLA Ops:
  2.3 27.6 %all-to-all-start = ((bf16[8,256,128]{2,1,0:T(8,128)(2,1)}), bf16[8,256,128]{2,1,0:T(8,128)(2,1)S(1)}, u32[]{:S(2)}, u32[]{:S(2)}) async-start(bf16[8,256,128]{2,1,0:T(8,128)(2,1)} %broadcast_in_dim.32), calls=%async_computation | async-start | bytes 1048576 | tf_op jit(solution)/shard_map/all_to_all | solution.py:394
  10.9 5.5 %collective-permute-start = (bf16[256,128]{1,0:T(8,128)(2,1)}, bf16[256,128]{1,0:T(8,128)(2,1)S(1)}, u32[]{:S(2)}, u32[]{:S(2)}) collective-permute-start(bf16[256,128]{1,0:T(8,128)(2,1)} %param.12), channel_id=1, source_target_pairs={{0,192},{8,200},{16,208},{24,216},{32,224},{40,232},{48,240},{56,2... | collective-permute-start | bytes 196616 | tf_op jit(solution)/shard_map/ppermute | solution.py:351
  13.9 6.0 %collective-permute-start.1 = (bf16[256,128]{1,0:T(8,128)(2,1)}, bf16[256,128]{1,0:T(8,128)(2,1)S(1)}, u32[]{:S(2)}, u32[]{:S(2)}) collective-permute-start(bf16[256,128]{1,0:T(8,128)(2,1)} %param.12), channel_id=1, source_target_pairs={{0,128},{8,136},{16,144},{24,152},{32,160},{40,168},{48,176},{56,1... | collective-permute-start | bytes 196616 | tf_op jit(solution)/shard_map/ppermute | solution.py:351
  14.5 6.1 %collective-permute-start.2 = (bf16[256,128]{1,0:T(8,128)(2,1)}, bf16[256,128]{1,0:T(8,128)(2,1)S(1)}, u32[]{:S(2)}, u32[]{:S(2)}) collective-permute-start(bf16[256,128]{1,0:T(8,128)(2,1)} %param.12), channel_id=1, source_target_pairs={{0,64},{8,72},{16,80},{24,88},{32,96},{40,104},{48,112},{56,120},{... | collective-permute-start | bytes 196616 | tf_op jit(solution)/shard_map/ppermute | solution.py:351
  20.6 7.8 %collective-permute-start.3 = (bf16[1024,128]{1,0:T(8,128)(2,1)S(1)}, bf16[1024,128]{1,0:T(8,128)(2,1)S(1)}, u32[]{:S(2)}, u32[]{:S(2)}) collective-permute-start(bf16[1024,128]{1,0:T(8,128)(2,1)S(1)} %constant_dynamic-update-slice_fusion.refs_0_), channel_id=1, source_target_pairs={{0,8},{8,16},{16,24},{24,32},{32,40},{40,48},{48,56},{56,0},{64,72... | collective-permute-start | bytes 786440 | tf_op jit(solution)/shard_map/ppermute | solution.py:356
  22.2 7.7 %collective-permute-start.4 = (bf16[1024,128]{1,0:T(8,128)(2,1)S(1)}, bf16[1024,128]{1,0:T(8,128)(2,1)S(1)}, u32[]{:S(2)}, u32[]{:S(2)}) collective-permute-start(bf16[1024,128]{1,0:T(8,128)(2,1)S(1)} %constant_dynamic-update-slice_fusion.refs_0_), channel_id=1, source_target_pairs={{0,56},{8,0},{16,8},{24,16},{32,24},{40,32},{48,40},{56,48},{64,12... | collective-permute-start | bytes 786440 | tf_op jit(solution)/shard_map/ppermute | solution.py:356
  28.4 33.2 %copy-start.15 = (bf16[1024,128]{1,0:T(8,128)(2,1)}, bf16[1024,128]{1,0:T(8,128)(2,1)S(1)}, u32[]{:S(2)}) copy-start(bf16[1024,128]{1,0:T(8,128)(2,1)S(1)} %collective-permute-done.3.refs_1_) | copy-start | bytes 786436
  29.9 31.7 %copy-start.17 = (bf16[1024,128]{1,0:T(8,128)(2,1)}, bf16[1024,128]{1,0:T(8,128)(2,1)S(1)}, u32[]{:S(2)}) copy-start(bf16[1024,128]{1,0:T(8,128)(2,1)S(1)} %collective-permute-done.4.refs_2_) | copy-start | bytes 786436
  31.7 6.3 %copy-start.24 = (s32[1024]{0:T(1024)S(1)}, s32[1024]{0:T(1024)}, u32[]{:S(2)}) copy-start(s32[1024]{0:T(1024)} %param.14) | copy-start | bytes 12292
  31.7 6.3 %copy-start.25 = (s32[64]{0:T(128)S(1)}, s32[64]{0:T(128)}, u32[]{:S(2)}) copy-start(s32[64]{0:T(128)} %param.16) | copy-start | bytes 772
  31.7 6.3 %copy-start.26 = (s32[64]{0:T(128)S(1)}, s32[64]{0:T(128)}, u32[]{:S(2)}) copy-start(s32[64]{0:T(128)} %param.15) | copy-start | bytes 772
  31.7 29.9 %copy-start.21 = (f32[128]{0:T(128)S(1)}, f32[128]{0:T(128)}, u32[]{:S(2)}) copy-start(f32[128]{0:T(128)} %param.13) | copy-start | bytes 1540
  31.7 29.9 %all-to-all-start.1 = ((bf16[4,8,256,128]{3,2,1,0:T(8,128)(2,1)}), bf16[4,8,256,128]{3,2,1,0:T(8,128)(2,1)S(1)}, u32[]{:S(2)}, u32[]{:S(2)}) async-start(bf16[4,8,256,128]{3,2,1,0:T(8,128)(2,1)} %broadcast_in_dim.33), calls=%async_computation.1 | async-start | bytes 4194304 | tf_op jit(solution)/shard_map/all_to_all | solution.py:401
  36.0 7.1 %collective-permute-start.6 = (bf16[1024,128]{1,0:T(8,128)(2,1)S(1)}, bf16[1024,128]{1,0:T(8,128)(2,1)}, u32[]{:S(2)}, u32[]{:S(2)}) collective-permute-start(bf16[1024,128]{1,0:T(8,128)(2,1)S(1)} %collective-permute-done.4.refs_2_), channel_id=1, source_target_pairs={{0,56},{8,0},{16,8},{24,16},{32,24},{40,32},{48,40},{56,48},{64,12... | collective-permute-start | bytes 786440 | tf_op jit(solution)/shard_map/ppermute | solution.py:356
  37.8 7.5 %collective-permute-start.5 = (bf16[1024,128]{1,0:T(8,128)(2,1)S(1)}, bf16[1024,128]{1,0:T(8,128)(2,1)}, u32[]{:S(2)}, u32[]{:S(2)}) collective-permute-start(bf16[1024,128]{1,0:T(8,128)(2,1)S(1)} %collective-permute-done.3.refs_1_), channel_id=1, source_target_pairs={{0,8},{8,16},{16,24},{24,32},{32,40},{40,48},{48,56},{56,0},{64,72... | collective-permute-start | bytes 786440 | tf_op jit(solution)/shard_map/ppermute | solution.py:356
  43.1 7.4 %collective-permute-start.8 = (bf16[1024,128]{1,0:T(8,128)(2,1)}, bf16[1024,128]{1,0:T(8,128)(2,1)S(1)}, u32[]{:S(2)}, u32[]{:S(2)}) collective-permute-start(bf16[1024,128]{1,0:T(8,128)(2,1)} %collective-permute-done.6.refs_4_), channel_id=1, source_target_pairs={{0,56},{8,0},{16,8},{24,16},{32,24},{40,32},{48,40},{56,48},{64,12... | collective-permute-start | bytes 786440 | tf_op jit(solution)/shard_map/ppermute | solution.py:356
  45.3 7.4 %collective-permute-start.7 = (bf16[1024,128]{1,0:T(8,128)(2,1)}, bf16[1024,128]{1,0:T(8,128)(2,1)S(1)}, u32[]{:S(2)}, u32[]{:S(2)}) collective-permute-start(bf16[1024,128]{1,0:T(8,128)(2,1)} %collective-permute-done.5.refs_3_), channel_id=1, source_target_pairs={{0,8},{8,16},{16,24},{24,32},{32,40},{40,48},{48,56},{56,0},{64,72... | collective-permute-start | bytes 786440 | tf_op jit(solution)/shard_map/ppermute | solution.py:356
  51.2 5.8 %collective-permute-start.10 = (bf16[512,128]{1,0:T(8,128)(2,1)}, bf16[512,128]{1,0:T(8,128)(2,1)S(1)}, u32[]{:S(2)}, u32[]{:S(2)}) collective-permute-start(bf16[512,128]{1,0:T(8,128)(2,1)} %slice.59), channel_id=1, source_target_pairs={{0,56},{8,0},{16,8},{24,16},{32,24},{40,32},{48,40},{56,48},{64,12... | collective-permute-start | bytes 393224 | tf_op jit(solution)/shard_map/ppermute | solution.py:356
  53.4 6.8 %collective-permute-start.9 = (bf16[512,128]{1,0:T(8,128)(2,1)}, bf16[512,128]{1,0:T(8,128)(2,1)}, u32[]{:S(2)}, u32[]{:S(2)}) collective-permute-start(bf16[512,128]{1,0:T(8,128)(2,1)} %slice.58), channel_id=1, source_target_pairs={{0,8},{8,16},{16,24},{24,32},{32,40},{40,48},{48,56},{56,0},{64,72... | collective-permute-start | bytes 393224 | tf_op jit(solution)/shard_map/ppermute | solution.py:356
  61.6 2.2 copy-start
  66.6 1.4 copy-start.3
  68.6 57.3 %all-to-all-start.2 = ((bf16[32,128,256]{2,1,0:T(8,128)(2,1)}), bf16[32,128,256]{2,1,0:T(8,128)(2,1)}, u32[]{:S(2)}, u32[]{:S(2)}) async-start(bf16[32,128,256]{2,1,0:T(8,128)(2,1)} %copy-done.3), calls=%async_computation.2 | async-start | bytes 4194304 | tf_op jit(solution)/shard_map/all_to_all | solution.py:416
  81.8 57.0 %collective-permute-start.11 = (bf16[128,2048]{1,0:T(8,128)(2,1)}, bf16[128,2048]{1,0:T(8,128)(2,1)}, u32[]{:S(2)}, u32[]{:S(2)}) collective-permute-start(bf16[128,2048]{1,0:T(8,128)(2,1)} %get-tuple-element.70), channel_id=1, source_target_pairs={{0,64},{8,72},{16,80},{24,88},{32,96},{40,104},{48,112},{56,120},{... | collective-permute-start | bytes 1572872 | tf_op jit(solution)/shard_map/ppermute | solution.py:351
  83.2 55.5 %collective-permute-start.12 = (bf16[128,2048]{1,0:T(8,128)(2,1)}, bf16[128,2048]{1,0:T(8,128)(2,1)}, u32[]{:S(2)}, u32[]{:S(2)}) collective-permute-start(bf16[128,2048]{1,0:T(8,128)(2,1)} %get-tuple-element.69), channel_id=1, source_target_pairs={{0,128},{8,136},{16,144},{24,152},{32,160},{40,168},{48,176},{56,1... | collective-permute-start | bytes 1572872 | tf_op jit(solution)/shard_map/ppermute | solution.py:351
  86.0 52.8 %collective-permute-start.13 = (bf16[128,2048]{1,0:T(8,128)(2,1)}, bf16[128,2048]{1,0:T(8,128)(2,1)}, u32[]{:S(2)}, u32[]{:S(2)}) collective-permute-start(bf16[128,2048]{1,0:T(8,128)(2,1)} %get-tuple-element.68), channel_id=1, source_target_pairs={{0,192},{8,200},{16,208},{24,216},{32,224},{40,232},{48,240},{56,2... | collective-permute-start | bytes 1572872 | tf_op jit(solution)/shard_map/ppermute | solution.py:351
  125.9 1.2 copy-start.9
  127.1 1.2 copy-start.10
  135.4 1.4 copy-start.4
  138.7 53.3 %all-to-all-start.3 = ((bf16[32,128,256]{2,1,0:T(8,128)(2,1)}), bf16[32,128,256]{2,1,0:T(8,128)(2,1)}, u32[]{:S(2)}, u32[]{:S(2)}) async-start(bf16[32,128,256]{2,1,0:T(8,128)(2,1)} %copy-done.4), calls=%async_computation.3 | async-start | bytes 4194304 | tf_op jit(solution)/shard_map/all_to_all | solution.py:433
  144.8 2.2 copy-start.12
  144.8 2.2 copy-start.14
  147.0 5.8 %copy-start.1 = (bf16[2048,512]{1,0:T(8,128)(2,1)}, bf16[2048,512]{1,0:T(8,128)(2,1)S(1)}, u32[]{:S(2)}) copy-start(bf16[2048,512]{1,0:T(8,128)(2,1)S(1)} %transpose_pieces.1.own_ref) | copy-start | bytes 6291460
  147.0 5.8 %collective-permute-start.14 = (bf16[2048,512]{1,0:T(8,128)(2,1)S(1)}, bf16[2048,512]{1,0:T(8,128)(2,1)S(1)}, u32[]{:S(2)}, u32[]{:S(2)}) collective-permute-start(bf16[2048,512]{1,0:T(8,128)(2,1)S(1)} %transpose_pieces.1.own_ref), channel_id=1, source_target_pairs={{0,1},{1,0},{2,3},{3,2},{4,5},{5,4},{6,7},{7,6},{8,9},{9,8},{10,11... | collective-permute-start | bytes 6291464 | tf_op jit(solution)/shard_map/ppermute | solution.py:360
  152.7 42.6 %copy-start.16 = (bf16[1024,128]{1,0:T(8,128)(2,1)S(1)}, bf16[1024,128]{1,0:T(8,128)(2,1)}, u32[]{:S(2)}) copy-start(bf16[1024,128]{1,0:T(8,128)(2,1)} %copy-done.15) | copy-start | bytes 786436
  152.7 42.6 %copy-start.18 = (bf16[1024,128]{1,0:T(8,128)(2,1)S(1)}, bf16[1024,128]{1,0:T(8,128)(2,1)}, u32[]{:S(2)}) copy-start(bf16[1024,128]{1,0:T(8,128)(2,1)} %copy-done.17) | copy-start | bytes 786436
  152.7 1.4 copy-start.7
  195.4 15.9 %copy-start.2 = (bf16[2048,512]{1,0:T(8,128)(2,1)S(1)}, bf16[2048,512]{1,0:T(8,128)(2,1)}, u32[]{:S(2)}) copy-start(bf16[2048,512]{1,0:T(8,128)(2,1)} %copy-done.1) | copy-start | bytes 6291460
  195.4 15.9 %copy-start.8 = (bf16[2048,512]{1,0:T(8,128)(2,1)S(1)}, bf16[2048,512]{1,0:T(8,128)(2,1)}, u32[]{:S(2)}) copy-start(bf16[2048,512]{1,0:T(8,128)(2,1)} %copy-done.7) | copy-start | bytes 6291460
  199.4 1.3 copy-start.5
  200.7 17.8 %collective-permute-start.15 = (bf16[128,8192]{1,0:T(8,128)(2,1)}, bf16[128,8192]{1,0:T(8,128)(2,1)}, u32[]{:S(2)}, u32[]{:S(2)}) collective-permute-start(bf16[128,8192]{1,0:T(8,128)(2,1)} %get-tuple-element.58), channel_id=1, source_target_pairs={{0,1},{1,0},{2,3},{3,2},{4,5},{5,4},{6,7},{7,6},{8,9},{9,8},{10,11... | collective-permute-start | bytes 6291464 | tf_op jit(solution)/shard_map/ppermute | solution.py:360
  200.7 9.9 %collective-permute-start.19 = (bf16[256,256]{1,0:T(8,128)(2,1)S(1)}, bf16[256,256]{1,0:T(8,128)(2,1)S(1)}, u32[]{:S(2)}, u32[]{:S(2)}) collective-permute-start(bf16[256,256]{1,0:T(8,128)(2,1)S(1)} %get-tuple-element.60.refs_0_), channel_id=1, source_target_pairs={{0,64},{8,72},{16,80},{24,88},{32,96},{40,104},{48,112},{56,120},{... | collective-permute-start | bytes 393224 | tf_op jit(solution)/shard_map/ppermute | solution.py:351
  202.2 8.5 %collective-permute-start.20 = (bf16[256,256]{1,0:T(8,128)(2,1)S(1)}, bf16[256,256]{1,0:T(8,128)(2,1)S(1)}, u32[]{:S(2)}, u32[]{:S(2)}) collective-permute-start(bf16[256,256]{1,0:T(8,128)(2,1)S(1)} %get-tuple-element.60.refs_0_), channel_id=1, source_target_pairs={{0,128},{8,136},{16,144},{24,152},{32,160},{40,168},{48,176},{56,1... | collective-permute-start | bytes 393224 | tf_op jit(solution)/shard_map/ppermute | solution.py:351
  203.8 7.5 %collective-permute-start.21 = (bf16[256,256]{1,0:T(8,128)(2,1)S(1)}, bf16[256,256]{1,0:T(8,128)(2,1)S(1)}, u32[]{:S(2)}, u32[]{:S(2)}) collective-permute-start(bf16[256,256]{1,0:T(8,128)(2,1)S(1)} %get-tuple-element.60.refs_0_), channel_id=1, source_target_pairs={{0,192},{8,200},{16,208},{24,216},{32,224},{40,232},{48,240},{56,2... | collective-permute-start | bytes 393224 | tf_op jit(solution)/shard_map/ppermute | solution.py:351
  213.5 5.1 %copy-start.6 = (bf16[128,8192]{1,0:T(8,128)(2,1)S(1)}, bf16[128,8192]{1,0:T(8,128)(2,1)}, u32[]{:S(2)}) copy-start(bf16[128,8192]{1,0:T(8,128)(2,1)} %copy-done.5) | copy-start | bytes 6291460
  213.5 32.4 %all-to-all-start.4 = ((bf16[8,256,256]{2,1,0:T(8,128)(2,1)}), bf16[8,256,256]{2,1,0:T(8,128)(2,1)}, u32[]{:S(2)}, u32[]{:S(2)}) async-start(bf16[8,256,256]{2,1,0:T(8,128)(2,1)} %weight_terms.1), calls=%async_computation.4 | async-start | bytes 2097152 | tf_op jit(solution)/shard_map/all_to_all | solution.py:444
  221.1 26.9 %collective-permute-start.16 = (bf16[32,8192]{1,0:T(8,128)(2,1)}, bf16[32,8192]{1,0:T(8,128)(2,1)}, u32[]{:S(2)}, u32[]{:S(2)}) collective-permute-start(bf16[32,8192]{1,0:T(8,128)(2,1)} %get-tuple-element.65), channel_id=1, source_target_pairs={{0,2},{1,3},{2,4},{3,5},{4,6},{5,7},{6,0},{7,1},{8,10},{9,11},{10,... | collective-permute-start | bytes 1572872 | tf_op jit(solution)/shard_map/ppermute | solution.py:459
  222.6 25.4 %collective-permute-start.17 = (bf16[32,8192]{1,0:T(8,128)(2,1)S(1)}, bf16[32,8192]{1,0:T(8,128)(2,1)}, u32[]{:S(2)}, u32[]{:S(2)}) collective-permute-start(bf16[32,8192]{1,0:T(8,128)(2,1)S(1)} %get-tuple-element.67), channel_id=1, source_target_pairs={{0,4},{1,5},{2,6},{3,7},{4,0},{5,1},{6,2},{7,3},{8,12},{9,13},{10,... | collective-permute-start | bytes 1572872 | tf_op jit(solution)/shard_map/ppermute | solution.py:459
  225.3 22.6 %collective-permute-start.18 = (bf16[32,8192]{1,0:T(8,128)(2,1)S(1)}, bf16[32,8192]{1,0:T(8,128)(2,1)}, u32[]{:S(2)}, u32[]{:S(2)}) collective-permute-start(bf16[32,8192]{1,0:T(8,128)(2,1)S(1)} %get-tuple-element.66), channel_id=1, source_target_pairs={{0,6},{1,7},{2,0},{3,1},{4,2},{5,3},{6,4},{7,5},{8,14},{9,15},{10,... | collective-permute-start | bytes 1572872 | tf_op jit(solution)/shard_map/ppermute | solution.py:459
  (6 other events, 4.8 us)

commit v3 on v1

v3 whole, which is shorter than its diff:
```python
import functools

import jax
import jax.numpy as jnp
from jax import lax
from jax.experimental import pallas as pl
from jax.experimental.pallas import tpu as pltpu
from jax.sharding import PartitionSpec as P

TILES = 4
EPS = 1e-05
MASKED_SCORE = -1e30
NY, NZ = 4, 8
Y_GROUPS = [[y * NZ + z for y in range(NY)] for z in range(NZ)]
Z_GROUPS = [[y * NZ + z for z in range(NZ)] for y in range(NY)]
BF16, F32 = jnp.bfloat16, jnp.float32
MIB = 1024 * 1024
GROUP = 4
POS, OWNER, VALID, FIRST, PLACE = range(5)


def dot_dims(a, b, a_dim, b_dim):
    return lax.dot_general(
        a, b, (((a_dim,), (b_dim,)), ((), ())), preferred_element_type=F32
    )


def limit(mib):
    return pltpu.CompilerParams(vmem_limit_bytes=mib * MIB)


def cost(flops, mib):
    return pl.CostEstimate(flops=flops, bytes_accessed=mib * MIB, transcendentals=0)


def in_vmem():
    return pl.BlockSpec(memory_space=pltpu.VMEM)


def in_hbm():
    return pl.BlockSpec(memory_space=pltpu.HBM)


def park_kernel(x_ref, out_ref, sem):
    copy = pltpu.make_async_copy(x_ref, out_ref, sem)
    copy.start()
    copy.wait()


def park(x):
    return pl.pallas_call(
        park_kernel,
        in_specs=[in_hbm()],
        out_specs=in_vmem(),
        out_shape=pltpu.VMEM(x.shape, x.dtype),
        scratch_shapes=[pltpu.SemaphoreType.DMA],
        compiler_params=limit(6),
        cost_estimate=cost(0, 8),
        name="park",
    )(x)


def weight_blocks(table_ref, w_refs, zones):
    for ref, (offset, y_from, y_count) in zip(w_refs, zones):
        z = lax.rem(table_ref[PLACE, 1] + offset, NZ)
        block = ref.shape[0] // y_count
        for i in range(y_count):
            y = lax.rem(table_ref[PLACE, 0] + y_from + i, NY)
            at = pl.multiple_of((y * NZ + z) * block, block)
            yield pl.ds(at, block), ref[i * block : (i + 1) * block, :]


def project_kernel(table_ref, f_ref, *refs, zones):
    w_refs, (gain_ref, send_ref, raw_ref, kv, sems) = refs[: len(zones)], refs[len(zones) :]
    head_dim = gain_ref.shape[1]
    tokens = send_ref.shape[1]
    total = jnp.zeros((f_ref.shape[0], 2 * head_dim), F32)
    for cols, w in weight_blocks(table_ref, w_refs, zones):
        total = total + jnp.dot(f_ref[:, cols], w[...], preferred_element_type=F32)
    raw = total[:, :head_dim]
    scale = lax.rsqrt(jnp.mean(raw * raw, axis=-1, keepdims=True) + EPS)
    keys = (raw * scale * gain_ref[...]).astype(BF16)
    values = total[:, head_dim:].astype(BF16)
    for i in range(kv.shape[0]):
        kv[i, :, :head_dim] = keys[i * tokens : (i + 1) * tokens]
        kv[i, :, head_dim:] = values[i * tokens : (i + 1) * tokens]
    copies = [
        pltpu.make_async_copy(
            kv.at[jnp.maximum(table_ref[POS, d], 0)], send_ref.at[d], sems.at[d]
        )
        for d in range(send_ref.shape[0])
    ]
    for copy in copies:
        copy.start()
    raw_ref[...] = raw
    for copy in copies:
        copy.wait()


def project(table, rows, pieces, zones, gain, dp, images, tokens):
    cols = 2 * gain.shape[1]
    return pl.pallas_call(
        functools.partial(project_kernel, zones=zones),
        grid_spec=pltpu.PrefetchScalarGridSpec(
            num_scalar_prefetch=1,
            grid=(),
            in_specs=[in_vmem()] * (2 + len(pieces)),
            out_specs=[in_hbm(), in_vmem()],
            scratch_shapes=[
                pltpu.VMEM((images, tokens, cols), BF16),
                pltpu.SemaphoreType.DMA((dp,)),
            ],
        ),
        out_shape=[
            pltpu.HBM((dp, tokens, cols), BF16),
            pltpu.HBM((rows.shape[0], cols // 2), F32),
        ],
        compiler_params=limit(12),
        cost_estimate=cost(2 * rows.size * cols, 10),
        name="project",
    )(table, rows, *pieces, gain)


def load_heads(ref, start, rows, head_dim):
    heads = ref.shape[1] // head_dim
    return jnp.concatenate(
        [ref[start : start + rows, g * head_dim : (g + 1) * head_dim] for g in range(heads)],
        axis=0,
    )


def store_heads(ref, start, rows, head_dim, full):
    for g in range(ref.shape[1] // head_dim):
        ref[start : start + rows, g * head_dim : (g + 1) * head_dim] = full[
            g * rows : (g + 1) * rows
        ]


def attend_kernel(table_ref, q_ref, ct_ref, kv_ref, part_ref, probs_ref, ds_ref, acc):
    step = pl.program_id(0)
    rows = q_ref.shape[0] // GROUP
    head_dim = kv_ref.shape[2] // 2
    tokens = kv_ref.shape[1]
    scale = head_dim**-0.5

    @pl.when(step == 0)
    def _():
        part_ref[...] = jnp.zeros_like(part_ref)
        acc[...] = jnp.zeros_like(acc)

    at = [step * GROUP + i for i in range(GROUP)]
    owners = [table_ref[OWNER, b] for b in at]
    queries = [load_heads(q_ref, i * rows, rows, head_dim) for i in range(GROUP)]
    grads = [load_heads(ct_ref, i * rows, rows, head_dim) for i in range(GROUP)]
    scores = [
        dot_dims(kv_ref[o, :, :head_dim], q, 1, 1) * scale for o, q in zip(owners, queries)
    ]
    d_probs = [dot_dims(kv_ref[o, :, head_dim:], g, 1, 1) for o, g in zip(owners, grads)]
    token = lax.broadcasted_iota(jnp.int32, (tokens, 1), 0)
    scores = [
        jnp.where(token < table_ref[VALID, b], s, MASKED_SCORE) for b, s in zip(at, scores)
    ]
    weights = [jnp.exp(s - jnp.max(s, axis=0, keepdims=True)) for s in scores]
    probs = [w * (1.0 / jnp.sum(w, axis=0, keepdims=True)) for w in weights]
    halves = [p.astype(BF16) for p in probs]
    deltas = [jnp.sum(p * d, axis=0, keepdims=True) for p, d in zip(probs, d_probs)]
    d_scores = [
        (p * (d - x) * scale).astype(BF16) for p, d, x in zip(probs, d_probs, deltas)
    ]
    key_parts = [jnp.dot(d, q, preferred_element_type=F32) for d, q in zip(d_scores, queries)]
    value_parts = [jnp.dot(p, g, preferred_element_type=F32) for p, g in zip(halves, grads)]
    key_run, value_run = acc[:, :head_dim], acc[:, head_dim:]
    for i, b in enumerate(at):
        keep = table_ref[FIRST, b] == 0
        key_run = key_parts[i] + jnp.where(keep, key_run, 0.0)
        value_run = value_parts[i] + jnp.where(keep, value_run, 0.0)
        part_ref[owners[i], :, :head_dim] = key_run.astype(BF16)
        part_ref[owners[i], :, head_dim:] = value_run.astype(BF16)
        probs_ref[i] = halves[i]
        ds_ref[i] = d_scores[i]
    acc[:, :head_dim] = key_run
    acc[:, head_dim:] = value_run


def attend(table, queries, cotangent, kv):
    blocks, (_, tokens, cols) = table.shape[1], kv.shape
    rows = queries.size * 2 // (blocks * cols)
    steps = blocks // GROUP
    text = pl.BlockSpec((queries.shape[0] // steps, queries.shape[1]), lambda i, t: (i, 0))
    whole = pl.BlockSpec(kv.shape, lambda i, t: (0, 0, 0))
    stash = pl.BlockSpec((GROUP, tokens, rows), lambda i, t: (i, 0, 0))
    stash_shape = pltpu.HBM((blocks, tokens, rows), BF16)
    return pl.pallas_call(
        attend_kernel,
        grid_spec=pltpu.PrefetchScalarGridSpec(
            num_scalar_prefetch=1,
            grid=(steps,),
            in_specs=[text, text, whole],
            out_specs=[whole, stash, stash],
            scratch_shapes=[pltpu.VMEM(kv.shape[1:], F32)],
        ),
        out_shape=[pltpu.HBM(kv.shape, BF16), stash_shape, stash_shape],
        compiler_params=limit(14),
        cost_estimate=cost(8 * queries.size * tokens, 8),
        name="attend",
    )(table, *hold(queries, cotangent, kv))


def hold(*arrays):
    return [pltpu.with_memory_space_constraint(x, pltpu.HBM) for x in arrays]


def apply_kernel(table_ref, kv_ref, probs_ref, ds_ref, out_ref, gq_ref):
    step = pl.program_id(0)
    rows = out_ref.shape[0] // GROUP
    head_dim = kv_ref.shape[2] // 2
    owners = [table_ref[OWNER, step * GROUP + i] for i in range(GROUP)]
    outs = [
        dot_dims(probs_ref[i], kv_ref[o, :, head_dim:], 0, 0) for i, o in enumerate(owners)
    ]
    gqs = [dot_dims(ds_ref[i], kv_ref[o, :, :head_dim], 0, 0) for i, o in enumerate(owners)]
    for i in range(GROUP):
        store_heads(out_ref, i * rows, rows, head_dim, outs[i].astype(BF16))
        store_heads(gq_ref, i * rows, rows, head_dim, gqs[i].astype(BF16))


def apply(table, kv, probs, d_scores, shape):
    steps = table.shape[1] // GROUP
    text = pl.BlockSpec((shape[0] // steps, shape[1]), lambda i, t: (i, 0))
    whole = pl.BlockSpec(kv.shape, lambda i, t: (0, 0, 0))
    stash = pl.BlockSpec((GROUP,) + probs.shape[1:], lambda i, t: (i, 0, 0))
    out = pltpu.HBM(shape, BF16)
    return pl.pallas_call(
        apply_kernel,
        grid_spec=pltpu.PrefetchScalarGridSpec(
            num_scalar_prefetch=1,
            grid=(steps,),
            in_specs=[whole, stash, stash],
            out_specs=[text, text],
        ),
        out_shape=[out, out],
        compiler_params=limit(10),
        cost_estimate=cost(4 * shape[0] * shape[1] * kv.shape[1], 6),
        name="apply",
    )(table, *hold(kv, probs, d_scores))


def owner_kernel(table_ref, part_ref, raw_ref, gain_ref, grad_ref, line_ref, acc):
    step = pl.program_id(0)
    head_dim = gain_ref.shape[1]
    count, tokens = part_ref.shape[:2]

    @pl.when(step == 0)
    def _():
        acc[...] = jnp.zeros_like(acc)

    for d in range(count):
        pos = table_ref[POS, step * count + d]

        @pl.when(pos >= 0)
        def _():
            acc[pos] += part_ref[d].astype(F32)

    @pl.when(step == pl.num_programs(0) - 1)
    def _():
        gain = gain_ref[...]
        for i in range(acc.shape[0]):
            here = slice(i * tokens, (i + 1) * tokens)
            raw = raw_ref[here]
            scale = lax.rsqrt(jnp.mean(raw * raw, axis=-1, keepdims=True) + EPS)
            scaled = acc[i, :, :head_dim] * gain
            pull = jnp.mean(raw * scaled, axis=-1, keepdims=True)
            grad = scale * scaled - raw * (scale * scale * scale * pull)
            grad_ref[here, :head_dim] = grad.astype(BF16)
            grad_ref[here, head_dim:] = acc[i, :, head_dim:].astype(BF16)
        for i in range(acc.shape[0]):
            at = pl.multiple_of(lax.rem(table_ref[PLACE, 3] + i, 2) * tokens, tokens)
            half = grad_ref[pl.ds(at, tokens), :]
            for y in range(NY):
                line_ref[y, i * tokens : (i + 1) * tokens, :] = half


def owner_grads(table, parts, raw, gain, images):
    dp, tokens, cols = parts.shape
    count = dp // 4
    return pl.pallas_call(
        owner_kernel,
        grid_spec=pltpu.PrefetchScalarGridSpec(
            num_scalar_prefetch=1,
            grid=(dp // count,),
            in_specs=[
                pl.BlockSpec((count, tokens, cols), lambda i, t: (i, 0, 0)),
                pl.BlockSpec(raw.shape, lambda i, t: (0, 0)),
                pl.BlockSpec(gain.shape, lambda i, t: (0, 0)),
            ],
            out_specs=[
                pl.BlockSpec((images * tokens, cols), lambda i, t: (0, 0)),
                pl.BlockSpec((NY, images * tokens, cols), lambda i, t: (0, 0, 0)),
            ],
            scratch_shapes=[pltpu.VMEM((images, tokens, cols), F32)],
        ),
        out_shape=[
            jax.ShapeDtypeStruct((images * tokens, cols), BF16),
            pltpu.HBM((NY, images * tokens, cols), BF16),
        ],
        compiler_params=limit(6),
        cost_estimate=cost(0, 3),
        name="owner_grads",
    )(table, *hold(parts, raw), gain)


def transpose_kernel(*refs):
    pieces, out_ref = refs[:-1], refs[-1]
    tokens = pieces[0].shape[0]
    for i, ref in enumerate(pieces):
        out_ref[:, i * tokens : (i + 1) * tokens] = ref[...].T


def transpose_pieces(pieces):
    tokens, width = pieces[0].shape
    return pl.pallas_call(
        transpose_kernel,
        in_specs=[in_vmem()] * len(pieces),
        out_specs=in_vmem(),
        out_shape=jax.ShapeDtypeStruct((width, tokens * len(pieces)), BF16),
        compiler_params=limit(7),
        cost_estimate=cost(0, 4),
        name="transpose_pieces",
    )(*pieces)


def weight_kernel(table_ref, own_ref, other_ref, line_ref, out_ref):
    half = line_ref.shape[1] // 2
    lines = [lax.rem(table_ref[PLACE, 0] + NY - s, NY) for s in range(NY)]
    first = jnp.concatenate([line_ref[y, :half, :] for y in lines], axis=0)
    second = jnp.concatenate([line_ref[y, half:, :] for y in lines], axis=0)
    block = out_ref.shape[1]
    for i in range(out_ref.shape[0]):
        here = slice(i * block, (i + 1) * block)
        total = jnp.dot(own_ref[here, :], first, preferred_element_type=F32)
        total = total + jnp.dot(other_ref[here, :], second, preferred_element_type=F32)
        out_ref[i] = total.astype(BF16)


def weight_terms(table, own_cols, other_cols, line):
    width, cols = own_cols.shape[0], line.shape[2]
    return pl.pallas_call(
        weight_kernel,
        grid_spec=pltpu.PrefetchScalarGridSpec(
            num_scalar_prefetch=1,
            grid=(),
            in_specs=[in_vmem()] * 3,
            out_specs=in_vmem(),
        ),
        out_shape=pltpu.HBM((NZ, width // NZ, cols), BF16),
        compiler_params=limit(9),
        cost_estimate=cost(4 * own_cols.size * cols, 6),
        name="weight_terms",
    )(table, own_cols, other_cols, line)


def feature_kernel(table_ref, grad_ref, *refs, zones, targets):
    w_refs, (own_ref, other_ref, lhs) = refs[: len(zones)], refs[len(zones) :]
    half = own_ref.shape[0]
    chips = targets // 2
    tokens = grad_ref.shape[0] // 2
    share = tokens // targets
    for core in range(2):
        for chip in range(chips):
            x = lax.rem(table_ref[PLACE, 2] + chip, chips)
            target = x * 2 + lax.rem(table_ref[PLACE, 3] + core, 2)
            for i in range(2):
                at = pl.multiple_of(i * tokens + target * share, share)
                to = ((core * chips + chip) * 2 + i) * share
                lhs[to : to + share, :] = grad_ref[pl.ds(at, share), :]
    for cols, w in weight_blocks(table_ref, w_refs, zones):
        part = dot_dims(lhs[...], w[...], 1, 1).astype(BF16)
        own_ref[:, cols] = part[:half]
        other_ref[:, cols] = part[half:]


def feature_terms(table, grads, pieces, zones, width, targets):
    half = jax.ShapeDtypeStruct((grads.shape[0] // 2, width), BF16)
    return pl.pallas_call(
        functools.partial(feature_kernel, zones=zones, targets=targets),
        grid_spec=pltpu.PrefetchScalarGridSpec(
            num_scalar_prefetch=1,
            grid=(),
            in_specs=[in_vmem()] * (1 + len(pieces)),
            out_specs=[in_vmem()] * 2,
            scratch_shapes=[pltpu.VMEM(grads.shape, BF16)],
        ),
        out_shape=[half, half],
        compiler_params=limit(13),
        cost_estimate=cost(4 * half.size * grads.shape[1], 8),
        name="feature_terms",
    )(table, grads, *pieces)


def shift_y(x, by):
    if by == 0:
        return x
    pairs = [(y * NZ + z, (y + by) % NY * NZ + z) for y in range(NY) for z in range(NZ)]
    return lax.ppermute(x, "dp", pairs)


def shift_z(x, by):
    pairs = [(y * NZ + z, y * NZ + (z + by) % NZ) for y in range(NY) for z in range(NZ)]
    return lax.ppermute(x, "dp", pairs)


def ring_z(x):
    half = x.shape[0] // 2
    pieces, zones = [x], [(0, 0, NY)]
    below = above = x
    for hop in range(1, NZ // 2):
        below, above = shift_z(below, 1), shift_z(above, -1)
        pieces += [below, above]
        zones += [(NZ - hop, 0, NY), (hop, 0, NY)]
    pieces += [shift_z(below[:half], 1), shift_z(above[half:], -1)]
    zones += [(NZ // 2, 0, NY // 2), (NZ // 2, NY // 2, NY // 2)]
    return pieces, zones


def swap_cores(x, count):
    return lax.ppermute(x, "tensor", [(t, t ^ 1) for t in range(count)])


def local(
    queries, features, k_weight, v_weight, k_gain, block_image, image_slot, image_tiles, cotangent
):
    dp_count = lax.axis_size("dp")
    tensor_count = lax.axis_size("tensor")
    me = lax.axis_index("dp")
    images, tokens, width = features.shape
    head_dim = k_gain.shape[0]
    rows = features.reshape(images * tokens, width)
    gain = k_gain.reshape(1, head_dim)
    my_y, my_z = me // NZ, lax.rem(me, NZ)
    tensor = lax.axis_index("tensor")
    core = lax.rem(tensor, 2)

    image_ids = lax.broadcasted_iota(jnp.int32, (1, image_slot.shape[0]), 1)
    id_match = block_image[:, None] == image_ids
    slots = jnp.sum(jnp.where(id_match, image_slot[None, :], 0), axis=1).reshape(dp_count, -1)
    tiles = jnp.sum(jnp.where(id_match, image_tiles[None, :], 0), axis=1).reshape(dp_count, -1)
    my_slots = lax.dynamic_index_in_dim(slots, me, 0, keepdims=False)
    my_tiles = lax.dynamic_index_in_dim(tiles, me, 0, keepdims=False)
    first = jnp.concatenate(
        [jnp.ones((1,), jnp.int32), (my_slots[1:] != my_slots[:-1]).astype(jnp.int32)]
    )
    pos = jnp.max(jnp.where(slots // images == me, slots % images, -1), axis=1)
    place = jnp.stack([my_y, my_z, tensor // 2, core])
    place = jnp.pad(place, (0, pos.shape[0] - place.shape[0]))
    table = jnp.stack([pos, my_slots // images, my_tiles * (tokens // TILES), first, place])

    block = jnp.concatenate([k_weight, v_weight], axis=1)
    line = jnp.concatenate([shift_y(block, (NY - i) % NY) for i in range(NY)])
    rows_near, line = lax.optimization_barrier((park(rows), line))
    pieces, zones = ring_z(line)

    send, raw = project(table, rows_near, pieces, zones, gain, dp_count, images, tokens)
    kv = lax.all_to_all(send, "dp", 0, 0, tiled=True)

    rows_later, _ = lax.optimization_barrier((features, raw))
    span = width // NY
    col_pieces = [
        shift_y(
            lax.dynamic_slice(
                rows_later, (core, 0, (my_y + s) % NY * span), (1, tokens, span)
            )[0],
            s,
        )
        for s in range(NY)
    ]

    parts, probs, d_scores = attend(table, queries, cotangent, kv)
    parts, col_pieces = lax.optimization_barrier((parts, col_pieces))
    parts = lax.all_to_all(parts, "dp", 0, 0, tiled=True)
    own_cols = transpose_pieces(col_pieces)
    other_cols = swap_cores(own_cols, tensor_count)
    attended, grad_queries = apply(table, kv, probs, d_scores, queries.shape)
    parts, other_cols, attended, grad_queries = lax.optimization_barrier(
        (parts, other_cols, attended, grad_queries)
    )
    grads, line_grads = owner_grads(table, parts, raw, gain, images)

    line_grads = lax.all_to_all(
        line_grads, "dp", 0, 0, tiled=True, axis_index_groups=Y_GROUPS
    )
    shares = weight_terms(table, own_cols, other_cols, line_grads)
    shares = lax.all_to_all(shares, "dp", 0, 0, tiled=True, axis_index_groups=Z_GROUPS)

    own, other = feature_terms(table, grads, pieces, zones, width, tensor_count)
    other = swap_cores(other, tensor_count)
    share = own.shape[0] * 2 // tensor_count
    pairs = [
        own[s * share : (s + 1) * share].astype(F32)
        + other[s * share : (s + 1) * share].astype(F32)
        for s in range(tensor_count // 2)
    ]
    grad_features = pairs[0]
    for s in range(1, tensor_count // 2):
        grad_features = grad_features + lax.ppermute(
            pairs[s].astype(BF16),
            "tensor",
            [(t, (t + 2 * s) % tensor_count) for t in range(tensor_count)],
        ).astype(F32)
    grad_features = grad_features.astype(BF16).reshape(images, tokens // tensor_count, width)
    shares, grad_features = lax.optimization_barrier((shares, grad_features))
    weight_grads = jnp.sum(shares.astype(F32), axis=0)
    return (
        attended,
        grad_queries,
        grad_features,
        weight_grads[:, :head_dim],
        weight_grads[:, head_dim:],
    )


def solution(mesh):
    in_specs = (
        P("dp", "tensor"),
        P("dp", None, None),
        P("dp", "tensor"),
        P("dp", "tensor"),
        P(),
        P(),
        P(),
        P(),
        P("dp", "tensor"),
    )
    out_specs = (
        P("dp", "tensor"),
        P("dp", "tensor"),
        P("dp", "tensor", None),
        P("dp", "tensor"),
        P("dp", "tensor"),
    )
    return jax.shard_map(local, mesh=mesh, in_specs=in_specs, out_specs=out_specs, check_vma=False)
```

time: 387 us -> 255 us (0.66)
  waiting for transfers between devices: 233 us -> 134 us
  blocking collectives: 50.6 us -> 12.7 us
  starting transfers between devices: 26.4 us -> 46.8 us
  between operations: 14.1 us -> 1 us
  matrix products: 8.92 us -> 0 us
  Pallas kernels: 25.4 us -> 33.7 us
    all_gather x1 -> x0, waiting for transfers between devices: 86 us -> none  [local(): lax.all_gather(jnp.concatenate([k_weight, v_weight], axis=1), 'dp', axis=...]
    all_gather x1 -> x0, blocking collectives: 50.6 us -> none  [local(): lax.all_gather(grads, 'dp', axis=0, tiled=True, axis_index_groups=Y_GROUPS)]
    all_to_all x3 -> x1, waiting for transfers between devices: 65.1 us -> 19.4 us  [local(): lax.all_to_all(shares, 'dp', 0, 0, tiled=True, axis_index_groups=Z_GROUPS)]
    ppermute x0 -> x19, waiting for transfers between devices: none -> 44.6 us  [the longest x8 36.7 us: shift_z(): return lax.ppermute(x, 'dp', pairs)]
    ppermute x0 -> x19, starting transfers between devices: none -> 28.1 us  [the longest x8 12.5 us: shift_z(): return lax.ppermute(x, 'dp', pairs)]
    all_to_all x2 -> x0, local copies, waits for them, and re-layouts: 14.3 us -> none  [local(): lax.all_to_all(rows, 'dp', 1, 0, tiled=True, axis_index_groups=Y_GROUPS)]
    all_to_all x0 -> x1, blocking collectives: none -> 12.7 us  [local(): lax.all_to_all(line_grads, 'dp', 0, 0, tiled=True, axis_index_groups=Y_GR...]
    all_to_all x3 -> x1, starting transfers between devices: 14.9 us -> 3.55 us  [local(): lax.all_to_all(shares, 'dp', 0, 0, tiled=True, axis_index_groups=Z_GROUPS)]
  transfers between devices with their start and end apart: 6 -> 22, of which waited for: 5 -> 13; matrix products, arithmetic and copies ran while one was open for 4% -> 3% of each run, Pallas kernels for 0% -> 8%
where the time goes in v3:
time: 255 us; the launch traced here: 253 us
  waiting for transfers between devices  134 us (53%)
  starting transfers between devices  46.8 us (18%)
  Pallas kernels  33.7 us (13%)
  local copies, waits for them, and re-layouts  20.3 us (8%)
  blocking collectives  12.7 us (5%)
  other arithmetic  4.82 us (2%)
    all_to_all x1, waiting for transfers between devices, local(): kv = lax.all_to_all(send, 'dp', 0, 0, tiled=True)  38.4 us
    ppermute x8, waiting for transfers between devices, shift_z(): return lax.ppermute(x, 'dp', pairs)  36.7 us
    all_to_all x1, waiting for transfers between devices, local(): parts = lax.all_to_all(parts, 'dp', 0, 0, tiled=True)  31.3 us
    all_to_all x1, waiting for transfers between devices, local(): lax.all_to_all(shares, 'dp', 0, 0, tiled=True, axis_index_groups=Z_GROUPS)  19.4 us
    unnamed x55, local copies, waits for them, and re-layouts  14.3 us
    all_to_all x1, blocking collectives, local(): lax.all_to_all(line_grads, 'dp', 0, 0, tiled=True, axis_index_groups=Y_GR...  12.7 us
    ppermute x8, starting transfers between devices, shift_z(): return lax.ppermute(x, 'dp', pairs)  12.5 us
    ppermute x6, starting transfers between devices, shift_y(): return lax.ppermute(x, 'dp', pairs)  10.3 us
  transfers between devices with their start and end apart: 22, of which 13 were waited for; matrix products, arithmetic and copies ran while one was open for 3% of the time, Pallas kernels for 8%

profile of v3, /device:TPU:32, one launch (start us, length us, event | category | flops | bytes accessed | tf_op | source)
XLA Modules:
  0.0 252.9 jit_solution(14208610248916398612)
XLA Ops:
  0.6 0.9 constant_dynamic-update-slice_fusion.1
  1.5 0.9 constant_dynamic-update-slice_fusion
  2.3 1.7 collective-permute-start.2
  4.0 2.9 %collective-permute-start.1 = (bf16[256,256]{1,0:T(8,128)(2,1)S(1)}, bf16[256,256]{1,0:T(8,128)(2,1)S(1)}, u32[]{:S(2)}, u32[]{:S(2)}) collective-permute-start(bf16[256,256]{1,0:T(8,128)(2,1)S(1)} %constant_dynamic-update-slice_fusion), channel_id=1, source_target_pairs={{0,128},{8,136},{16,144},{24,152},{32,160},{40,168},{48,176},{56,1... | collective-permute-start | bytes 393224 | tf_op jit(solution)/shard_map/ppermute | solution.py:404
  6.9 1.3 collective-permute-start
  8.3 2.2 copy-done.2
  10.8 1.9 copy-done
  13.4 1.7 collective-permute-start.3
  15.1 10.9 %collective-permute-done.4.refs_2_ = bf16[1024,256]{1,0:T(8,128)(2,1)S(1)} collective-permute-done((bf16[1024,256]{1,0:T(8,128)(2,1)S(1)}, bf16[1024,256]{1,0:T(8,128)(2,1)S(1)}, u32[]{:S(2)}, u32[]{:S(2)}) %collective-permute-start.4) | collective-permute-done | bytes 524320 | tf_op jit(solution)/shard_map/ppermute | solution.py:409
  26.0 3.3 %collective-permute-start.6 = (bf16[1024,256]{1,0:T(8,128)(2,1)S(1)}, bf16[1024,256]{1,0:T(8,128)(2,1)S(1)}, u32[]{:S(2)}, u32[]{:S(2)}) collective-permute-start(bf16[1024,256]{1,0:T(8,128)(2,1)S(1)} %collective-permute-done.4.refs_2_), channel_id=1, source_target_pairs={{0,56},{8,0},{16,8},{24,16},{32,24},{40,32},{48,40},{56,48},{64,12... | collective-permute-start | bytes 1572872 | tf_op jit(solution)/shard_map/ppermute | solution.py:409
  30.1 8.6 %collective-permute-done.6.refs_4_ = bf16[1024,256]{1,0:T(8,128)(2,1)S(1)} collective-permute-done((bf16[1024,256]{1,0:T(8,128)(2,1)S(1)}, bf16[1024,256]{1,0:T(8,128)(2,1)S(1)}, u32[]{:S(2)}, u32[]{:S(2)}) %collective-permute-start.6) | collective-permute-done | bytes 524320 | tf_op jit(solution)/shard_map/ppermute | solution.py:409
  38.7 3.7 %collective-permute-start.8 = (bf16[1024,256]{1,0:T(8,128)(2,1)S(1)}, bf16[1024,256]{1,0:T(8,128)(2,1)S(1)}, u32[]{:S(2)}, u32[]{:S(2)}) collective-permute-start(bf16[1024,256]{1,0:T(8,128)(2,1)S(1)} %collective-permute-done.6.refs_4_), channel_id=1, source_target_pairs={{0,56},{8,0},{16,8},{24,16},{32,24},{40,32},{48,40},{56,48},{64,12... | collective-permute-start | bytes 1572872 | tf_op jit(solution)/shard_map/ppermute | solution.py:409
  43.1 8.0 %collective-permute-done.8.refs_6_ = bf16[1024,256]{1,0:T(8,128)(2,1)S(1)} collective-permute-done((bf16[1024,256]{1,0:T(8,128)(2,1)S(1)}, bf16[1024,256]{1,0:T(8,128)(2,1)S(1)}, u32[]{:S(2)}, u32[]{:S(2)}) %collective-permute-start.8) | collective-permute-done | bytes 524320 | tf_op jit(solution)/shard_map/ppermute | solution.py:409
  51.9 3.4 %collective-permute-start.10 = (bf16[512,256]{1,0:T(8,128)(2,1)}, bf16[512,256]{1,0:T(8,128)(2,1)S(1)}, u32[]{:S(2)}, u32[]{:S(2)}) collective-permute-start(bf16[512,256]{1,0:T(8,128)(2,1)} %slice.59), channel_id=1, source_target_pairs={{0,56},{8,0},{16,8},{24,16},{32,24},{40,32},{48,40},{56,48},{64,12... | collective-permute-start | bytes 786440 | tf_op jit(solution)/shard_map/ppermute | solution.py:409
  55.3 0.8 slice.58
  56.3 3.2 %collective-permute-done.10.refs_8_ = bf16[512,256]{1,0:T(8,128)(2,1)S(1)} collective-permute-done((bf16[512,256]{1,0:T(8,128)(2,1)}, bf16[512,256]{1,0:T(8,128)(2,1)S(1)}, u32[]{:S(2)}, u32[]{:S(2)}) %collective-permute-start.10) | collective-permute-done | bytes 262176 | tf_op jit(solution)/shard_map/ppermute | solution.py:409
  59.5 4.9 %collective-permute-done.9.refs_7_ = bf16[512,256]{1,0:T(8,128)(2,1)} collective-permute-done((bf16[512,256]{1,0:T(8,128)(2,1)}, bf16[512,256]{1,0:T(8,128)(2,1)}, u32[]{:S(2)}, u32[]{:S(2)}) %collective-permute-start.9) | collective-permute-done | bytes 262176 | tf_op jit(solution)/shard_map/ppermute | solution.py:409
  64.4 2.2 copy-done.1
  66.6 5.4 %project.1 = (bf16[32,128,256]{2,1,0:T(8,128)(2,1)}, f32[256,128]{1,0:T(8,128)}) custom-call(s32[5,32]{1,0:T(8,128)S(1)} %stack.41.table_ref, bf16[256,8192]{1,0:T(8,128)(2,1)S(1)} %copy-done.1, bf16[1024,256]{1,0:T(8,128)(2,1)S(1)} %pad_maximum_fusion.refs_0_, bf16[1024,256]{1,0:T(8,128)(2,1)S(1)} %collective-permute-done.3.refs_1_, ...), custom_call_target="tpu_custom_call" | custom-call | flops 1073741824 | bytes 10485760 | tf_op jit(solution)/shard_map/project/pallas_call | solution.py:102
  72.0 9.1 %all-to-all-start = ((bf16[32,128,256]{2,1,0:T(8,128)(2,1)}), bf16[32,128,256]{2,1,0:T(8,128)(2,1)}, u32[]{:S(2)}, u32[]{:S(2)}) async-start(bf16[32,128,256]{2,1,0:T(8,128)(2,1)} %get-tuple-element.32), calls=%async_computation | async-start | bytes 4194304 | tf_op jit(solution)/shard_map/all_to_all | solution.py:463
  81.2 2.7 %dynamic-slice_bitcast_fusion = (bf16[128,2048]{1,0:T(8,128)(2,1)}, bf16[128,2048]{1,0:T(8,128)(2,1)}, bf16[128,2048]{1,0:T(8,128)(2,1)S(1)}, bf16[128,2048]{1,0:T(8,128)(2,1)}) fusion(bf16[2,128,8192]{2,1,0:T(8,128)(2,1)} %param.10, s32[]{:T(128)S(6)} %select_n.86, s32[]{:T(128)S(6)} %select_n.94, s32[]{:T(128)S(6)} %select_n.92, s32[]{:T(128)S(6)} %select_n.90, ...), kind=kLoop, calls=%fused_computation.6 | loop fusion | bytes 4194324 | tf_op jit(solution)/shard_map/squeeze | solution.py:469
  84.0 2.7 %collective-permute-start.13 = (bf16[128,2048]{1,0:T(8,128)(2,1)}, bf16[128,2048]{1,0:T(8,128)(2,1)S(1)}, u32[]{:S(2)}, u32[]{:S(2)}) collective-permute-start(bf16[128,2048]{1,0:T(8,128)(2,1)} %get-tuple-element.62), channel_id=1, source_target_pairs={{0,192},{8,200},{16,208},{24,216},{32,224},{40,232},{48,240},{56,2... | collective-permute-start | bytes 1572872 | tf_op jit(solution)/shard_map/ppermute | solution.py:404
  86.7 0.8 collective-permute-start.12
  87.5 0.9 collective-permute-start.11
  88.4 38.4 %all-to-all-done.kv_ref = bf16[32,128,256]{2,1,0:T(8,128)(2,1)} async-done(((bf16[32,128,256]{2,1,0:T(8,128)(2,1)}), bf16[32,128,256]{2,1,0:T(8,128)(2,1)}, u32[]{:S(2)}, u32[]{:S(2)}) %all-to-all-start) | async-done | bytes 2097184 | tf_op jit(solution)/shard_map/all_to_all | solution.py:463
  126.8 9.5 %attend.1 = (bf16[32,128,256]{2,1,0:T(8,128)(2,1)}, bf16[32,128,128]{2,1,0:T(8,128)(2,1)}, bf16[32,128,128]{2,1,0:T(8,128)(2,1)}) custom-call(s32[5,32]{1,0:T(8,128)S(1)} %stack.41.table_ref, bf16[512,1024]{1,0:T(8,128)(2,1)} %q_ref.1, bf16[512,1024]{1,0:T(8,128)(2,1)} %ct_ref.1, bf16[32,128,256]{2,1,0:T(8,128)(2,1)} %all-to-all-done.kv_ref), custom_call_target="tpu_custom_call" | custom-call | flops 536870912 | bytes 8388608 | tf_op jit(solution)/shard_map/attend/pallas_call | solution.py:193
  136.3 0.7 copy-done.15
  137.4 6.0 %all-to-all-start.1 = ((bf16[32,128,256]{2,1,0:T(8,128)(2,1)}), bf16[32,128,256]{2,1,0:T(8,128)(2,1)}, u32[]{:S(2)}, u32[]{:S(2)}) async-start(bf16[32,128,256]{2,1,0:T(8,128)(2,1)} %get-tuple-element.36), calls=%async_computation.1 | async-start | bytes 4194304 | tf_op jit(solution)/shard_map/all_to_all | solution.py:479
  143.5 1.0 copy-done.14
  144.5 1.0 copy-done.16
  145.5 1.0 copy-done.18
  146.6 1.0 copy-done.20
  148.3 7.9 %apply.1 = (bf16[512,1024]{1,0:T(8,128)(2,1)}, bf16[512,1024]{1,0:T(8,128)(2,1)}) custom-call(s32[5,32]{1,0:T(8,128)S(1)} %stack.41.table_ref, bf16[32,128,256]{2,1,0:T(8,128)(2,1)} %all-to-all-done.kv_ref, bf16[32,128,128]{2,1,0:T(8,128)(2,1)} %get-tuple-element.41.probs_ref, bf16[32,128,128]{2,1,0:T(8,128)(2,1)} %get-tuple-element.42.ds_ref), custom_call_target="tpu_custom_call" | custom-call | flops 268435456 | bytes 6291456 | tf_op jit(solution)/shard_map/apply/pallas_call | solution.py:233
  156.2 1.3 copy-done.5
  157.5 31.3 %all-to-all-done.1.part_ref = bf16[32,128,256]{2,1,0:T(8,128)(2,1)} async-done(((bf16[32,128,256]{2,1,0:T(8,128)(2,1)}), bf16[32,128,256]{2,1,0:T(8,128)(2,1)}, u32[]{:S(2)}, u32[]{:S(2)}) %all-to-all-start.1) | async-done | bytes 2097184 | tf_op jit(solution)/shard_map/all_to_all | solution.py:479
  188.8 4.2 %owner_grads.1 = (bf16[256,256]{1,0:T(8,128)(2,1)S(1)}, bf16[4,256,256]{2,1,0:T(8,128)(2,1)}) custom-call(s32[5,32]{1,0:T(8,128)S(1)} %stack.41.table_ref, bf16[32,128,256]{2,1,0:T(8,128)(2,1)} %all-to-all-done.1.part_ref, f32[256,128]{1,0:T(8,128)} %get-tuple-element.34.raw_ref, f32[1,128]{1,0:T(1,128)S(1)} %bitcast.24), custom_call_target="tpu_custom_call" | custom-call | bytes 3145728 | tf_op jit(solution)/shard_map/owner_grads/pallas_call | solution.py:286
  193.0 3.1 %feature_terms.1 = (bf16[128,8192]{1,0:T(8,128)(2,1)S(1)}, bf16[128,8192]{1,0:T(8,128)(2,1)S(1)}) custom-call(s32[5,32]{1,0:T(8,128)S(1)} %stack.41.table_ref, bf16[256,256]{1,0:T(8,128)(2,1)S(1)} %get-tuple-element.50.grad_ref, bf16[1024,256]{1,0:T(8,128)(2,1)S(1)} %pad_maximum_fusion.refs_0_, bf16[1024,256]{1,0:T(8,128)(2,1)S(1)} %copy-done.11, ...), custom_call_target="tpu_custom_call" | custom-call | flops 1073741824 | bytes 8388608 | tf_op jit(solution)/shard_map/feature_terms/pallas_call | solution.py:384
  196.2 4.1 %collective-permute-done.15 = bf16[128,8192]{1,0:T(8,128)(2,1)S(1)} collective-permute-done((bf16[128,8192]{1,0:T(8,128)(2,1)S(1)}, bf16[128,8192]{1,0:T(8,128)(2,1)S(1)}, u32[]{:S(2)}, u32[]{:S(2)}) %collective-permute-start.15) | collective-permute-done | bytes 2097184 | tf_op jit(solution)/shard_map/ppermute | solution.py:426
  200.3 1.4 add_convert_fusion.3
  202.2 1.5 collective-permute-start.16
  203.7 1.7 collective-permute-start.18
  205.4 1.8 collective-permute-start.17
  207.3 12.7 %all_to_all.20.line_ref = bf16[4,256,256]{2,1,0:T(8,128)(2,1)S(1)} all-to-all(bf16[4,256,256]{2,1,0:T(8,128)(2,1)S(1)} %copy-done.23), channel_id=1, replica_groups={{0,64,128,192},{8,72,136,200},{16,80,144,208},{24,88,152,216},{32,96,16..., dimensions={0} | all-to-all | bytes 1048576 | tf_op jit(solution)/shard_map/all_to_all | solution.py:488
  220.0 2.8 %weight_terms.1 = bf16[8,256,256]{2,1,0:T(8,128)(2,1)} custom-call(s32[5,32]{1,0:T(8,128)S(1)} %stack.41.table_ref, bf16[2048,512]{1,0:T(8,128)(2,1)S(1)} %transpose_pieces.1.own_ref, bf16[2048,512]{1,0:T(8,128)(2,1)S(1)} %copy-done.6, bf16[4,256,256]{2,1,0:T(8,128)(2,1)S(1)} %all_to_all.20.line_ref), custom_call_target="tpu_custom_call" | custom-call | flops 1073741824 | bytes 6291456 | tf_op jit(solution)/shard_map/weight_terms/pallas_call | solution.py:347
  222.9 3.5 %all-to-all-start.3 = ((bf16[8,256,256]{2,1,0:T(8,128)(2,1)}), bf16[8,256,256]{2,1,0:T(8,128)(2,1)S(1)}, u32[]{:S(2)}, u32[]{:S(2)}) async-start(bf16[8,256,256]{2,1,0:T(8,128)(2,1)} %weight_terms.1), calls=%async_computation.3 | async-start | bytes 2097152 | tf_op jit(solution)/shard_map/all_to_all | solution.py:492
  226.4 3.5 %collective-permute-done.17 = bf16[32,8192]{1,0:T(8,128)(2,1)} collective-permute-done((bf16[32,8192]{1,0:T(8,128)(2,1)}, bf16[32,8192]{1,0:T(8,128)(2,1)}, u32[]{:S(2)}, u32[]{:S(2)}) %collective-permute-start.17) | collective-permute-done | bytes 524320 | tf_op jit(solution)/shard_map/ppermute | solution.py:504
  229.9 2.8 %add_convert_fusion = bf16[32,8192]{1,0:T(8,128)(2,1)} fusion(bf16[32,8192]{1,0:T(8,128)(2,1)} %collective-permute-done.18, bf16[32,8192]{1,0:T(8,128)(2,1)} %collective-permute-done.17, bf16[32,8192]{1,0:T(8,128)(2,1)} %collective-permute-done.16, bf16[128,8192]{1,0:T(8,128)(2,1)} %copy-done.22, bf16[128,8192]{1,0:T(8,128)(2,1)} %copy-done.7), kind=kLoop, calls=%fused_computation.1 | loop fusion | flops 2621440 | bytes 3145728 | tf_op jit(solution)/shard_map/convert_element_type | solution.py:509
  232.7 19.4 %all-to-all-done.3 = bf16[8,256,256]{2,1,0:T(8,128)(2,1)S(1)} async-done(((bf16[8,256,256]{2,1,0:T(8,128)(2,1)}), bf16[8,256,256]{2,1,0:T(8,128)(2,1)S(1)}, u32[]{:S(2)}, u32[]{:S(2)}) %all-to-all-start.3) | async-done | bytes 1048608 | tf_op jit(solution)/shard_map/all_to_all | solution.py:492
  (80 shorter events, 6.0 us)
Async XLA Ops:
  2.3 10.4 %collective-permute-start.2 = (bf16[256,256]{1,0:T(8,128)(2,1)S(1)}, bf16[256,256]{1,0:T(8,128)(2,1)S(1)}, u32[]{:S(2)}, u32[]{:S(2)}) collective-permute-start(bf16[256,256]{1,0:T(8,128)(2,1)S(1)} %constant_dynamic-update-slice_fusion), channel_id=1, source_target_pairs={{0,64},{8,72},{16,80},{24,88},{32,96},{40,104},{48,112},{56,120},{... | collective-permute-start | bytes 393224 | tf_op jit(solution)/shard_map/ppermute | solution.py:404
  4.0 8.9 %collective-permute-start.1 = (bf16[256,256]{1,0:T(8,128)(2,1)S(1)}, bf16[256,256]{1,0:T(8,128)(2,1)S(1)}, u32[]{:S(2)}, u32[]{:S(2)}) collective-permute-start(bf16[256,256]{1,0:T(8,128)(2,1)S(1)} %constant_dynamic-update-slice_fusion), channel_id=1, source_target_pairs={{0,128},{8,136},{16,144},{24,152},{32,160},{40,168},{48,176},{56,1... | collective-permute-start | bytes 393224 | tf_op jit(solution)/shard_map/ppermute | solution.py:404
  6.9 6.0 %collective-permute-start = (bf16[256,256]{1,0:T(8,128)(2,1)S(1)}, bf16[256,256]{1,0:T(8,128)(2,1)S(1)}, u32[]{:S(2)}, u32[]{:S(2)}) collective-permute-start(bf16[256,256]{1,0:T(8,128)(2,1)S(1)} %constant_dynamic-update-slice_fusion), channel_id=1, source_target_pairs={{0,192},{8,200},{16,208},{24,216},{32,224},{40,232},{48,240},{56,2... | collective-permute-start | bytes 393224 | tf_op jit(solution)/shard_map/ppermute | solution.py:404
  8.3 2.2 copy-start.2
  10.4 19.3 %copy-start.24 = (s32[1024]{0:T(1024)S(1)}, s32[1024]{0:T(1024)}, u32[]{:S(2)}) copy-start(s32[1024]{0:T(1024)} %param.14) | copy-start | bytes 12292
  10.4 19.3 %copy-start.25 = (s32[64]{0:T(128)S(1)}, s32[64]{0:T(128)}, u32[]{:S(2)}) copy-start(s32[64]{0:T(128)} %param.16) | copy-start | bytes 772
  10.4 19.4 %copy-start.26 = (s32[64]{0:T(128)S(1)}, s32[64]{0:T(128)}, u32[]{:S(2)}) copy-start(s32[64]{0:T(128)} %param.15) | copy-start | bytes 772
  10.7 2.0 copy-start
  12.7 51.7 %copy-start.21 = (f32[128]{0:T(128)S(1)}, f32[128]{0:T(128)}, u32[]{:S(2)}) copy-start(f32[128]{0:T(128)} %param.13) | copy-start | bytes 1540
  13.0 13.0 %collective-permute-start.4 = (bf16[1024,256]{1,0:T(8,128)(2,1)S(1)}, bf16[1024,256]{1,0:T(8,128)(2,1)S(1)}, u32[]{:S(2)}, u32[]{:S(2)}) collective-permute-start(bf16[1024,256]{1,0:T(8,128)(2,1)S(1)} %pad_maximum_fusion.refs_0_), channel_id=1, source_target_pairs={{0,56},{8,0},{16,8},{24,16},{32,24},{40,32},{48,40},{56,48},{64,12... | collective-permute-start | bytes 1572872 | tf_op jit(solution)/shard_map/ppermute | solution.py:409
  13.4 16.4 %collective-permute-start.3 = (bf16[1024,256]{1,0:T(8,128)(2,1)S(1)}, bf16[1024,256]{1,0:T(8,128)(2,1)S(1)}, u32[]{:S(2)}, u32[]{:S(2)}) collective-permute-start(bf16[1024,256]{1,0:T(8,128)(2,1)S(1)} %pad_maximum_fusion.refs_0_), channel_id=1, source_target_pairs={{0,8},{8,16},{16,24},{24,32},{32,40},{40,48},{48,56},{56,0},{64,72... | collective-permute-start | bytes 1572872 | tf_op jit(solution)/shard_map/ppermute | solution.py:409
  26.0 46.0 %copy-start.8 = (bf16[1024,256]{1,0:T(8,128)(2,1)}, bf16[1024,256]{1,0:T(8,128)(2,1)S(1)}, u32[]{:S(2)}) copy-start(bf16[1024,256]{1,0:T(8,128)(2,1)S(1)} %collective-permute-done.4.refs_2_) | copy-start | bytes 1572868
  26.0 12.7 %collective-permute-start.6 = (bf16[1024,256]{1,0:T(8,128)(2,1)S(1)}, bf16[1024,256]{1,0:T(8,128)(2,1)S(1)}, u32[]{:S(2)}, u32[]{:S(2)}) collective-permute-start(bf16[1024,256]{1,0:T(8,128)(2,1)S(1)} %collective-permute-done.4.refs_2_), channel_id=1, source_target_pairs={{0,56},{8,0},{16,8},{24,16},{32,24},{40,32},{48,40},{56,48},{64,12... | collective-permute-start | bytes 1572872 | tf_op jit(solution)/shard_map/ppermute | solution.py:409
  29.8 42.2 %copy-start.10 = (bf16[1024,256]{1,0:T(8,128)(2,1)}, bf16[1024,256]{1,0:T(8,128)(2,1)S(1)}, u32[]{:S(2)}) copy-start(bf16[1024,256]{1,0:T(8,128)(2,1)S(1)} %collective-permute-done.3.refs_1_) | copy-start | bytes 1572868
  29.8 13.2 %collective-permute-start.5 = (bf16[1024,256]{1,0:T(8,128)(2,1)S(1)}, bf16[1024,256]{1,0:T(8,128)(2,1)}, u32[]{:S(2)}, u32[]{:S(2)}) collective-permute-start(bf16[1024,256]{1,0:T(8,128)(2,1)S(1)} %collective-permute-done.3.refs_1_), channel_id=1, source_target_pairs={{0,8},{8,16},{16,24},{24,32},{32,40},{40,48},{48,56},{56,0},{64,72... | collective-permute-start | bytes 1572872 | tf_op jit(solution)/shard_map/ppermute | solution.py:409
  38.7 33.3 %copy-start.12 = (bf16[1024,256]{1,0:T(8,128)(2,1)}, bf16[1024,256]{1,0:T(8,128)(2,1)S(1)}, u32[]{:S(2)}) copy-start(bf16[1024,256]{1,0:T(8,128)(2,1)S(1)} %collective-permute-done.6.refs_4_) | copy-start | bytes 1572868
  38.7 12.4 %collective-permute-start.8 = (bf16[1024,256]{1,0:T(8,128)(2,1)S(1)}, bf16[1024,256]{1,0:T(8,128)(2,1)S(1)}, u32[]{:S(2)}, u32[]{:S(2)}) collective-permute-start(bf16[1024,256]{1,0:T(8,128)(2,1)S(1)} %collective-permute-done.6.refs_4_), channel_id=1, source_target_pairs={{0,56},{8,0},{16,8},{24,16},{32,24},{40,32},{48,40},{56,48},{64,12... | collective-permute-start | bytes 1572872 | tf_op jit(solution)/shard_map/ppermute | solution.py:409
  43.0 12.3 %collective-permute-start.7 = (bf16[1024,256]{1,0:T(8,128)(2,1)}, bf16[1024,256]{1,0:T(8,128)(2,1)S(1)}, u32[]{:S(2)}, u32[]{:S(2)}) collective-permute-start(bf16[1024,256]{1,0:T(8,128)(2,1)} %collective-permute-done.5.refs_3_), channel_id=1, source_target_pairs={{0,8},{8,16},{16,24},{24,32},{32,40},{40,48},{48,56},{56,0},{64,72... | collective-permute-start | bytes 1572872 | tf_op jit(solution)/shard_map/ppermute | solution.py:409
  51.9 7.6 %collective-permute-start.10 = (bf16[512,256]{1,0:T(8,128)(2,1)}, bf16[512,256]{1,0:T(8,128)(2,1)S(1)}, u32[]{:S(2)}, u32[]{:S(2)}) collective-permute-start(bf16[512,256]{1,0:T(8,128)(2,1)} %slice.59), channel_id=1, source_target_pairs={{0,56},{8,0},{16,8},{24,16},{32,24},{40,32},{48,40},{56,48},{64,12... | collective-permute-start | bytes 786440 | tf_op jit(solution)/shard_map/ppermute | solution.py:409
  55.3 16.7 %copy-start.3 = (bf16[1024,256]{1,0:T(8,128)(2,1)}, bf16[1024,256]{1,0:T(8,128)(2,1)S(1)}, u32[]{:S(2)}) copy-start(bf16[1024,256]{1,0:T(8,128)(2,1)S(1)} %collective-permute-done.7.refs_5_) | copy-start | bytes 1572868
  56.0 8.4 %collective-permute-start.9 = (bf16[512,256]{1,0:T(8,128)(2,1)}, bf16[512,256]{1,0:T(8,128)(2,1)}, u32[]{:S(2)}, u32[]{:S(2)}) collective-permute-start(bf16[512,256]{1,0:T(8,128)(2,1)} %slice.58), channel_id=1, source_target_pairs={{0,8},{8,16},{16,24},{24,32},{32,40},{40,48},{48,56},{56,0},{64,72... | collective-permute-start | bytes 786440 | tf_op jit(solution)/shard_map/ppermute | solution.py:409
  64.4 2.2 copy-start.1
  72.0 54.8 %all-to-all-start = ((bf16[32,128,256]{2,1,0:T(8,128)(2,1)}), bf16[32,128,256]{2,1,0:T(8,128)(2,1)}, u32[]{:S(2)}, u32[]{:S(2)}) async-start(bf16[32,128,256]{2,1,0:T(8,128)(2,1)} %get-tuple-element.32), calls=%async_computation | async-start | bytes 4194304 | tf_op jit(solution)/shard_map/all_to_all | solution.py:463
  84.0 52.3 %collective-permute-start.13 = (bf16[128,2048]{1,0:T(8,128)(2,1)}, bf16[128,2048]{1,0:T(8,128)(2,1)S(1)}, u32[]{:S(2)}, u32[]{:S(2)}) collective-permute-start(bf16[128,2048]{1,0:T(8,128)(2,1)} %get-tuple-element.62), channel_id=1, source_target_pairs={{0,192},{8,200},{16,208},{24,216},{32,224},{40,232},{48,240},{56,2... | collective-permute-start | bytes 1572872 | tf_op jit(solution)/shard_map/ppermute | solution.py:404
  86.7 49.6 %collective-permute-start.12 = (bf16[128,2048]{1,0:T(8,128)(2,1)}, bf16[128,2048]{1,0:T(8,128)(2,1)S(1)}, u32[]{:S(2)}, u32[]{:S(2)}) collective-permute-start(bf16[128,2048]{1,0:T(8,128)(2,1)} %get-tuple-element.63), channel_id=1, source_target_pairs={{0,128},{8,136},{16,144},{24,152},{32,160},{40,168},{48,176},{56,1... | collective-permute-start | bytes 1572872 | tf_op jit(solution)/shard_map/ppermute | solution.py:404
  87.5 48.8 %collective-permute-start.11 = (bf16[128,2048]{1,0:T(8,128)(2,1)S(1)}, bf16[128,2048]{1,0:T(8,128)(2,1)S(1)}, u32[]{:S(2)}, u32[]{:S(2)}) collective-permute-start(bf16[128,2048]{1,0:T(8,128)(2,1)S(1)} %get-tuple-element.64), channel_id=1, source_target_pairs={{0,64},{8,72},{16,80},{24,88},{32,96},{40,104},{48,112},{56,120},{... | collective-permute-start | bytes 1572872 | tf_op jit(solution)/shard_map/ppermute | solution.py:404
  136.3 0.9 copy-start.17
  136.3 1.1 copy-start.19
  137.4 51.4 %all-to-all-start.1 = ((bf16[32,128,256]{2,1,0:T(8,128)(2,1)}), bf16[32,128,256]{2,1,0:T(8,128)(2,1)}, u32[]{:S(2)}, u32[]{:S(2)}) async-start(bf16[32,128,256]{2,1,0:T(8,128)(2,1)} %get-tuple-element.36), calls=%async_computation.1 | async-start | bytes 4194304 | tf_op jit(solution)/shard_map/all_to_all | solution.py:479
  143.4 1.0 copy-start.14
  144.5 1.0 copy-start.16
  145.5 1.0 copy-start.18
  146.6 1.0 copy-start.20
  148.2 8.0 %collective-permute-start.14 = (bf16[2048,512]{1,0:T(8,128)(2,1)S(1)}, bf16[2048,512]{1,0:T(8,128)(2,1)S(1)}, u32[]{:S(2)}, u32[]{:S(2)}) collective-permute-start(bf16[2048,512]{1,0:T(8,128)(2,1)S(1)} %transpose_pieces.1.own_ref), channel_id=1, source_target_pairs={{0,1},{1,0},{2,3},{3,2},{4,5},{5,4},{6,7},{7,6},{8,9},{9,8},{10,11... | collective-permute-start | bytes 6291464 | tf_op jit(solution)/shard_map/ppermute | solution.py:426
  156.2 1.3 copy-start.5
  188.8 4.2 %copy-start.4 = (bf16[1024,256]{1,0:T(8,128)(2,1)S(1)}, bf16[1024,256]{1,0:T(8,128)(2,1)}, u32[]{:S(2)}) copy-start(bf16[1024,256]{1,0:T(8,128)(2,1)} %copy-done.3) | copy-start | bytes 1572868
  188.8 4.2 %copy-start.9 = (bf16[1024,256]{1,0:T(8,128)(2,1)S(1)}, bf16[1024,256]{1,0:T(8,128)(2,1)}, u32[]{:S(2)}) copy-start(bf16[1024,256]{1,0:T(8,128)(2,1)} %copy-done.8) | copy-start | bytes 1572868
  188.8 4.2 %copy-start.11 = (bf16[1024,256]{1,0:T(8,128)(2,1)S(1)}, bf16[1024,256]{1,0:T(8,128)(2,1)}, u32[]{:S(2)}) copy-start(bf16[1024,256]{1,0:T(8,128)(2,1)} %copy-done.10) | copy-start | bytes 1572868
  188.8 4.2 %copy-start.13 = (bf16[1024,256]{1,0:T(8,128)(2,1)S(1)}, bf16[1024,256]{1,0:T(8,128)(2,1)}, u32[]{:S(2)}) copy-start(bf16[1024,256]{1,0:T(8,128)(2,1)} %copy-done.12) | copy-start | bytes 1572868
  196.1 5.6 %copy-start.7 = (bf16[128,8192]{1,0:T(8,128)(2,1)}, bf16[128,8192]{1,0:T(8,128)(2,1)S(1)}, u32[]{:S(2)}) copy-start(bf16[128,8192]{1,0:T(8,128)(2,1)S(1)} %get-tuple-element.51) | copy-start | bytes 6291460
  196.1 4.2 %collective-permute-start.15 = (bf16[128,8192]{1,0:T(8,128)(2,1)S(1)}, bf16[128,8192]{1,0:T(8,128)(2,1)S(1)}, u32[]{:S(2)}, u32[]{:S(2)}) collective-permute-start(bf16[128,8192]{1,0:T(8,128)(2,1)S(1)} %get-tuple-element.52), channel_id=1, source_target_pairs={{0,1},{1,0},{2,3},{3,2},{4,5},{5,4},{6,7},{7,6},{8,9},{9,8},{10,11... | collective-permute-start | bytes 6291464 | tf_op jit(solution)/shard_map/ppermute | solution.py:426
  200.3 1.9 copy-start.22
  200.3 6.9 %copy-start.23 = (bf16[4,256,256]{2,1,0:T(8,128)(2,1)S(1)}, bf16[4,256,256]{2,1,0:T(8,128)(2,1)}, u32[]{:S(2)}) copy-start(bf16[4,256,256]{2,1,0:T(8,128)(2,1)} %get-tuple-element.49) | copy-start | bytes 1572868
  200.3 19.7 %copy-start.6 = (bf16[2048,512]{1,0:T(8,128)(2,1)S(1)}, bf16[2048,512]{1,0:T(8,128)(2,1)}, u32[]{:S(2)}) copy-start(bf16[2048,512]{1,0:T(8,128)(2,1)} %copy-done.5) | copy-start | bytes 6291460
  202.2 24.2 %collective-permute-start.16 = (bf16[32,8192]{1,0:T(8,128)(2,1)}, bf16[32,8192]{1,0:T(8,128)(2,1)}, u32[]{:S(2)}, u32[]{:S(2)}) collective-permute-start(bf16[32,8192]{1,0:T(8,128)(2,1)} %get-tuple-element.59), channel_id=1, source_target_pairs={{0,2},{1,3},{2,4},{3,5},{4,6},{5,7},{6,0},{7,1},{8,10},{9,11},{10,... | collective-permute-start | bytes 1572872 | tf_op jit(solution)/shard_map/ppermute | solution.py:504
  203.7 22.7 %collective-permute-start.18 = (bf16[32,8192]{1,0:T(8,128)(2,1)}, bf16[32,8192]{1,0:T(8,128)(2,1)}, u32[]{:S(2)}, u32[]{:S(2)}) collective-permute-start(bf16[32,8192]{1,0:T(8,128)(2,1)} %get-tuple-element.60), channel_id=1, source_target_pairs={{0,6},{1,7},{2,0},{3,1},{4,2},{5,3},{6,4},{7,5},{8,14},{9,15},{10,... | collective-permute-start | bytes 1572872 | tf_op jit(solution)/shard_map/ppermute | solution.py:504
  205.4 24.5 %collective-permute-start.17 = (bf16[32,8192]{1,0:T(8,128)(2,1)}, bf16[32,8192]{1,0:T(8,128)(2,1)}, u32[]{:S(2)}, u32[]{:S(2)}) collective-permute-start(bf16[32,8192]{1,0:T(8,128)(2,1)} %get-tuple-element.61), channel_id=1, source_target_pairs={{0,4},{1,5},{2,6},{3,7},{4,0},{5,1},{6,2},{7,3},{8,12},{9,13},{10,... | collective-permute-start | bytes 1572872 | tf_op jit(solution)/shard_map/ppermute | solution.py:504
  222.9 29.2 %all-to-all-start.3 = ((bf16[8,256,256]{2,1,0:T(8,128)(2,1)}), bf16[8,256,256]{2,1,0:T(8,128)(2,1)S(1)}, u32[]{:S(2)}, u32[]{:S(2)}) async-start(bf16[8,256,256]{2,1,0:T(8,128)(2,1)} %weight_terms.1), calls=%async_computation.3 | async-start | bytes 2097152 | tf_op jit(solution)/shard_map/all_to_all | solution.py:492
  (1 other events, 0.8 us)

commit v4 on v2

v4 whole, which is shorter than its diff:
```python
import functools

import jax
import jax.numpy as jnp
from jax import lax
from jax.experimental import pallas as pl
from jax.experimental.pallas import tpu as pltpu
from jax.sharding import PartitionSpec as P

TILES = 4
EPS = 1e-05
MASKED_SCORE = -1e30
NY, NZ = 4, 8
Y_GROUPS = [[y * NZ + z for y in range(NY)] for z in range(NZ)]
Z_GROUPS = [[y * NZ + z for z in range(NZ)] for y in range(NY)]
BF16, F32 = jnp.bfloat16, jnp.float32
MIB = 1024 * 1024
GROUP = 4
POS, OWNER, VALID, FIRST, PLACE = range(5)


def dot_dims(a, b, a_dim, b_dim):
    return lax.dot_general(
        a, b, (((a_dim,), (b_dim,)), ((), ())), preferred_element_type=F32
    )


def limit(mib):
    return pltpu.CompilerParams(vmem_limit_bytes=mib * MIB)


def cost(flops, mib):
    return pl.CostEstimate(flops=flops, bytes_accessed=mib * MIB, transcendentals=0)


def in_vmem():
    return pl.BlockSpec(memory_space=pltpu.VMEM)


def in_hbm():
    return pl.BlockSpec(memory_space=pltpu.HBM)


def weight_blocks(table_ref, kw_ref, vw_refs, zones):
    for ref, offset in zip(vw_refs, zones):
        z = lax.rem(table_ref[PLACE, 1] + offset, NZ)
        block = ref.shape[0] // NY
        for i in range(NY):
            y = lax.rem(table_ref[PLACE, 0] + i, NY)
            here = pl.ds(pl.multiple_of((y * NZ + z) * block, block), block)
            v = ref[i * block : (i + 1) * block, :]
            yield here, jnp.concatenate([kw_ref[here, :], v], axis=1)


def project_kernel(table_ref, f_ref, kw_ref, *refs, zones):
    vw_refs, (gain_ref, send_ref, raw_ref, kv) = refs[: len(zones)], refs[len(zones) :]
    head_dim = gain_ref.shape[1]
    tokens = send_ref.shape[1]
    total = jnp.zeros((f_ref.shape[0], 2 * head_dim), F32)
    for cols, w in weight_blocks(table_ref, kw_ref, vw_refs, zones):
        total = total + jnp.dot(f_ref[:, cols], w, preferred_element_type=F32)
    raw = total[:, :head_dim]
    raw_ref[...] = raw
    scale = lax.rsqrt(jnp.mean(raw * raw, axis=-1, keepdims=True) + EPS)
    keys = (raw * scale * gain_ref[...]).astype(BF16)
    values = total[:, head_dim:].astype(BF16)
    for i in range(kv.shape[0]):
        kv[i, :, :head_dim] = keys[i * tokens : (i + 1) * tokens]
        kv[i, :, head_dim:] = values[i * tokens : (i + 1) * tokens]

    def put(d, carry):
        send_ref[d] = kv[jnp.maximum(table_ref[POS, d], 0)]
        return carry

    lax.fori_loop(0, send_ref.shape[0], put, 0, unroll=4)


def project(table, rows, k_full, v_pieces, zones, gain, dp, images, tokens):
    cols = 2 * gain.shape[1]
    return pl.pallas_call(
        functools.partial(project_kernel, zones=zones),
        grid_spec=pltpu.PrefetchScalarGridSpec(
            num_scalar_prefetch=1,
            grid=(),
            in_specs=[in_vmem()] * (3 + len(v_pieces)),
            out_specs=[in_vmem()] * 2,
            scratch_shapes=[pltpu.VMEM((images, tokens, cols), BF16)],
        ),
        out_shape=[
            pltpu.HBM((dp, tokens, cols), BF16),
            pltpu.HBM((rows.shape[0], cols // 2), F32),
        ],
        compiler_params=limit(14),
        cost_estimate=cost(2 * rows.size * cols, 10),
        name="project",
    )(table, *hold(rows), k_full, *v_pieces, gain)


def load_heads(ref, start, rows, head_dim):
    heads = ref.shape[1] // head_dim
    return jnp.concatenate(
        [ref[pl.ds(start, rows), g * head_dim : (g + 1) * head_dim] for g in range(heads)],
        axis=0,
    )


def store_heads(ref, start, rows, head_dim, full):
    for g in range(ref.shape[1] // head_dim):
        ref[pl.ds(start, rows), g * head_dim : (g + 1) * head_dim] = full[
            g * rows : (g + 1) * rows
        ]


def attend_kernel(table_ref, q_ref, ct_ref, kv_ref, part_ref, probs_ref, ds_ref, acc):
    blocks = table_ref.shape[1]
    rows = q_ref.shape[0] // blocks
    head_dim = kv_ref.shape[2] // 2
    tokens = kv_ref.shape[1]
    scale = head_dim**-0.5
    part_ref[...] = jnp.zeros_like(part_ref)
    acc[...] = jnp.zeros_like(acc)

    def some_blocks(step, carry):
        at = [step * GROUP + i for i in range(GROUP)]
        owners = [table_ref[OWNER, b] for b in at]
        starts = [pl.multiple_of(b * rows, rows) for b in at]
        queries = [load_heads(q_ref, s, rows, head_dim) for s in starts]
        grads = [load_heads(ct_ref, s, rows, head_dim) for s in starts]
        scores = [
            dot_dims(kv_ref[o, :, :head_dim], q, 1, 1) * scale for o, q in zip(owners, queries)
        ]
        d_probs = [dot_dims(kv_ref[o, :, head_dim:], g, 1, 1) for o, g in zip(owners, grads)]
        token = lax.broadcasted_iota(jnp.int32, (tokens, 1), 0)
        scores = [
            jnp.where(token < table_ref[VALID, b], s, MASKED_SCORE) for b, s in zip(at, scores)
        ]
        weights = [jnp.exp(s - jnp.max(s, axis=0, keepdims=True)) for s in scores]
        probs = [w * (1.0 / jnp.sum(w, axis=0, keepdims=True)) for w in weights]
        halves = [p.astype(BF16) for p in probs]
        deltas = [jnp.sum(p * d, axis=0, keepdims=True) for p, d in zip(probs, d_probs)]
        d_scores = [
            (p * (d - x) * scale).astype(BF16) for p, d, x in zip(probs, d_probs, deltas)
        ]
        key_parts = [
            jnp.dot(d, q, preferred_element_type=F32) for d, q in zip(d_scores, queries)
        ]
        value_parts = [
            jnp.dot(p, g, preferred_element_type=F32) for p, g in zip(halves, grads)
        ]
        key_run, value_run = acc[:, :head_dim], acc[:, head_dim:]
        for i, b in enumerate(at):
            keep = table_ref[FIRST, b] == 0
            key_run = key_parts[i] + jnp.where(keep, key_run, 0.0)
            value_run = value_parts[i] + jnp.where(keep, value_run, 0.0)
            part_ref[owners[i], :, :head_dim] = key_run.astype(BF16)
            part_ref[owners[i], :, head_dim:] = value_run.astype(BF16)
            probs_ref[b] = halves[i]
            ds_ref[b] = d_scores[i]
        acc[:, :head_dim] = key_run
        acc[:, head_dim:] = value_run
        return carry

    lax.fori_loop(0, blocks // GROUP, some_blocks, 0)


def hold(*arrays):
    return [pltpu.with_memory_space_constraint(x, pltpu.HBM) for x in arrays]


def attend(table, queries, cotangent, kv):
    blocks, (_, tokens, cols) = table.shape[1], kv.shape
    rows = queries.size * 2 // (blocks * cols)
    stash = pltpu.HBM((blocks, tokens, rows), BF16)
    return pl.pallas_call(
        attend_kernel,
        grid_spec=pltpu.PrefetchScalarGridSpec(
            num_scalar_prefetch=1,
            grid=(),
            in_specs=[in_vmem()] * 3,
            out_specs=[in_vmem()] * 3,
            scratch_shapes=[pltpu.VMEM(kv.shape[1:], F32)],
        ),
        out_shape=[pltpu.HBM(kv.shape, BF16), stash, stash],
        compiler_params=limit(13),
        cost_estimate=cost(8 * queries.size * tokens, 8),
        name="attend",
    )(table, *hold(queries, cotangent, kv))


def apply_kernel(table_ref, kv_ref, probs_ref, ds_ref, out_ref, gq_ref):
    blocks = table_ref.shape[1]
    rows = out_ref.shape[0] // blocks
    head_dim = kv_ref.shape[2] // 2

    def some_blocks(step, carry):
        at = [step * GROUP + i for i in range(GROUP)]
        owners = [table_ref[OWNER, b] for b in at]
        outs = [
            dot_dims(probs_ref[b], kv_ref[o, :, head_dim:], 0, 0) for b, o in zip(at, owners)
        ]
        gqs = [dot_dims(ds_ref[b], kv_ref[o, :, :head_dim], 0, 0) for b, o in zip(at, owners)]
        for i, b in enumerate(at):
            start = pl.multiple_of(b * rows, rows)
            store_heads(out_ref, start, rows, head_dim, outs[i].astype(BF16))
            store_heads(gq_ref, start, rows, head_dim, gqs[i].astype(BF16))
        return carry

    lax.fori_loop(0, blocks // GROUP, some_blocks, 0)


def apply(table, kv, probs, d_scores, shape):
    out = pltpu.HBM(shape, BF16)
    return pl.pallas_call(
        apply_kernel,
        grid_spec=pltpu.PrefetchScalarGridSpec(
            num_scalar_prefetch=1,
            grid=(),
            in_specs=[in_vmem()] * 3,
            out_specs=[in_vmem()] * 2,
        ),
        out_shape=[out, out],
        compiler_params=limit(9),
        cost_estimate=cost(4 * shape[0] * shape[1] * kv.shape[1], 6),
        name="apply",
    )(table, *hold(kv, probs, d_scores))


def owner_kernel(table_ref, part_ref, raw_ref, gain_ref, grad_ref, by_core_ref, acc):
    head_dim = gain_ref.shape[1]
    tokens = part_ref.shape[1]
    acc[...] = jnp.zeros_like(acc)

    def add(d, carry):
        @pl.when(table_ref[POS, d] >= 0)
        def _():
            acc[table_ref[POS, d]] += part_ref[d].astype(F32)

        return carry

    lax.fori_loop(0, part_ref.shape[0], add, 0)
    gain = gain_ref[...]
    for i in range(acc.shape[0]):
        here = slice(i * tokens, (i + 1) * tokens)
        raw = raw_ref[here]
        scale = lax.rsqrt(jnp.mean(raw * raw, axis=-1, keepdims=True) + EPS)
        scaled = acc[i, :, :head_dim] * gain
        pull = jnp.mean(raw * scaled, axis=-1, keepdims=True)
        grad = scale * scaled - raw * (scale * scale * scale * pull)
        grad_ref[here, :head_dim] = grad.astype(BF16)
        grad_ref[here, head_dim:] = acc[i, :, head_dim:].astype(BF16)
    for i in range(acc.shape[0]):
        at = pl.multiple_of(lax.rem(table_ref[PLACE, 3] + i, 2) * tokens, tokens)
        by_core_ref[i * tokens : (i + 1) * tokens, :] = grad_ref[pl.ds(at, tokens), :]


def owner_grads(table, parts, raw, gain, images):
    tokens, cols = parts.shape[1:]
    grads = jax.ShapeDtypeStruct((images * tokens, cols), BF16)
    return pl.pallas_call(
        owner_kernel,
        grid_spec=pltpu.PrefetchScalarGridSpec(
            num_scalar_prefetch=1,
            grid=(),
            in_specs=[in_vmem()] * 3,
            out_specs=[in_vmem()] * 2,
            scratch_shapes=[pltpu.VMEM((images, tokens, cols), F32)],
        ),
        out_shape=[grads, grads],
        compiler_params=limit(6),
        cost_estimate=cost(0, 3),
        name="owner_grads",
    )(table, *hold(parts, raw), gain)


def transpose_kernel(*refs):
    pieces, out_ref = refs[:-1], refs[-1]
    tokens = pieces[0].shape[0]
    for i, ref in enumerate(pieces):
        out_ref[:, i * tokens : (i + 1) * tokens] = ref[...].T


def transpose_pieces(pieces):
    tokens, width = pieces[0].shape
    return pl.pallas_call(
        transpose_kernel,
        in_specs=[in_vmem()] * len(pieces),
        out_specs=in_vmem(),
        out_shape=jax.ShapeDtypeStruct((width, tokens * len(pieces)), BF16),
        compiler_params=limit(7),
        cost_estimate=cost(0, 4),
        name="transpose_pieces",
    )(*pieces)


def weight_kernel(own_ref, other_ref, *refs):
    lines, out_ref = refs[:-1], refs[-1]
    half = lines[0].shape[0] // 2
    first = jnp.concatenate([ref[:half, :] for ref in lines], axis=0)
    second = jnp.concatenate([ref[half:, :] for ref in lines], axis=0)
    block = out_ref.shape[1]
    for i in range(out_ref.shape[0]):
        here = slice(i * block, (i + 1) * block)
        total = jnp.dot(own_ref[here, :], first, preferred_element_type=F32)
        total = total + jnp.dot(other_ref[here, :], second, preferred_element_type=F32)
        out_ref[i] = total.astype(BF16)


def weight_terms(own_cols, other_cols, lines):
    width, cols = own_cols.shape[0], lines[0].shape[1]
    return pl.pallas_call(
        weight_kernel,
        in_specs=[in_vmem()] * (2 + len(lines)),
        out_specs=in_vmem(),
        out_shape=pltpu.HBM((NZ, width // NZ, cols), BF16),
        compiler_params=limit(9),
        cost_estimate=cost(4 * own_cols.size * cols, 6),
        name="weight_terms",
    )(own_cols, other_cols, *lines)


def feature_kernel(table_ref, grad_ref, kw_ref, *refs, zones, targets):
    vw_refs, (own_ref, other_ref, lhs) = refs[: len(zones)], refs[len(zones) :]
    half = own_ref.shape[0]
    chips = targets // 2
    tokens = grad_ref.shape[0] // 2
    share = tokens // targets
    for core in range(2):
        for chip in range(chips):
            x = lax.rem(table_ref[PLACE, 2] + chip, chips)
            target = x * 2 + lax.rem(table_ref[PLACE, 3] + core, 2)
            for i in range(2):
                at = pl.multiple_of(i * tokens + target * share, share)
                to = ((core * chips + chip) * 2 + i) * share
                lhs[to : to + share, :] = grad_ref[pl.ds(at, share), :]
    for cols, w in weight_blocks(table_ref, kw_ref, vw_refs, zones):
        part = dot_dims(lhs[...], w, 1, 1).astype(BF16)
        own_ref[:, cols] = part[:half]
        other_ref[:, cols] = part[half:]


def feature_terms(table, grads, k_full, v_pieces, zones, width, targets):
    half = jax.ShapeDtypeStruct((grads.shape[0] // 2, width), BF16)
    return pl.pallas_call(
        functools.partial(feature_kernel, zones=zones, targets=targets),
        grid_spec=pltpu.PrefetchScalarGridSpec(
            num_scalar_prefetch=1,
            grid=(),
            in_specs=[in_vmem()] * (2 + len(v_pieces)),
            out_specs=[in_vmem()] * 2,
            scratch_shapes=[pltpu.VMEM(grads.shape, BF16)],
        ),
        out_shape=[half, half],
        compiler_params=limit(13),
        cost_estimate=cost(4 * half.size * grads.shape[1], 8),
        name="feature_terms",
    )(table, grads, k_full, *v_pieces)


def shift_y(x, by):
    if by == 0:
        return x
    pairs = [(y * NZ + z, (y + by) % NY * NZ + z) for y in range(NY) for z in range(NZ)]
    return lax.ppermute(x, "dp", pairs)


def shift_z(x, by):
    pairs = [(y * NZ + z, y * NZ + (z + by) % NZ) for y in range(NY) for z in range(NZ)]
    return lax.ppermute(x, "dp", pairs)


def swap_cores(x, count):
    return lax.ppermute(x, "tensor", [(t, t ^ 1) for t in range(count)])


def local(
    queries, features, k_weight, v_weight, k_gain, block_image, image_slot, image_tiles, cotangent
):
    dp_count = lax.axis_size("dp")
    tensor_count = lax.axis_size("tensor")
    me = lax.axis_index("dp")
    images, tokens, width = features.shape
    head_dim = k_gain.shape[0]
    rows = features.reshape(images * tokens, width)
    gain = k_gain.reshape(1, head_dim)
    my_y, my_z = me // NZ, lax.rem(me, NZ)
    tensor = lax.axis_index("tensor")
    core = lax.rem(tensor, 2)

    image_ids = lax.broadcasted_iota(jnp.int32, (1, image_slot.shape[0]), 1)
    id_match = block_image[:, None] == image_ids
    slots = jnp.sum(jnp.where(id_match, image_slot[None, :], 0), axis=1).reshape(dp_count, -1)
    tiles = jnp.sum(jnp.where(id_match, image_tiles[None, :], 0), axis=1).reshape(dp_count, -1)
    my_slots = lax.dynamic_index_in_dim(slots, me, 0, keepdims=False)
    my_tiles = lax.dynamic_index_in_dim(tiles, me, 0, keepdims=False)
    first = jnp.concatenate(
        [jnp.ones((1,), jnp.int32), (my_slots[1:] != my_slots[:-1]).astype(jnp.int32)]
    )
    pos = jnp.max(jnp.where(slots // images == me, slots % images, -1), axis=1)
    place = jnp.stack([my_y, my_z, tensor // 2, core])
    place = jnp.pad(place, (0, pos.shape[0] - place.shape[0]))
    table = jnp.stack([pos, my_slots // images, my_tiles * (tokens // TILES), first, place])

    k_line = lax.all_to_all(
        jnp.broadcast_to(k_weight, (NZ,) + k_weight.shape),
        "dp", 0, 0, tiled=True, axis_index_groups=Z_GROUPS,
    )
    v_line = jnp.concatenate([shift_y(v_weight, (NY - i) % NY) for i in range(NY)])
    below, above = shift_z(v_line, 1), shift_z(v_line, -1)
    k_line, below, above, table = lax.optimization_barrier((k_line, below, above, table))
    k_full = lax.all_to_all(
        jnp.broadcast_to(k_line, (NY,) + k_line.shape),
        "dp", 0, 0, tiled=True, axis_index_groups=Y_GROUPS,
    ).reshape(width, head_dim)
    v_pieces, zones = [v_line], [0]
    for hop in range(1, NZ // 2):
        if hop > 1:
            below, above = shift_z(below, 1), shift_z(above, -1)
        v_pieces += [below, above]
        zones += [NZ - hop, hop]
    v_pieces += [shift_z(below, 1)]
    zones += [NZ // 2]

    send, raw = project(
        table, rows, k_full, v_pieces, zones, gain, dp_count, images, tokens
    )
    kv = lax.all_to_all(send, "dp", 0, 0, tiled=True)

    rows_later, _ = lax.optimization_barrier((features, raw))
    span = width // NY
    col_pieces = [
        shift_y(
            lax.dynamic_slice(
                rows_later, (core, 0, (my_y + s) % NY * span), (1, tokens, span)
            )[0],
            s,
        )
        for s in range(NY)
    ]

    parts, probs, d_scores = attend(table, queries, cotangent, kv)
    parts, col_pieces = lax.optimization_barrier((parts, col_pieces))
    parts = lax.all_to_all(parts, "dp", 0, 0, tiled=True)
    own_cols = transpose_pieces(col_pieces)
    other_cols = swap_cores(own_cols, tensor_count)
    attended, grad_queries = apply(table, kv, probs, d_scores, queries.shape)
    parts, other_cols, attended, grad_queries = lax.optimization_barrier(
        (parts, other_cols, attended, grad_queries)
    )
    grads, by_core = owner_grads(table, parts, raw, gain, images)

    lines = [shift_y(by_core, s) for s in range(NY)]
    shares = weight_terms(own_cols, other_cols, lines)
    shares = lax.all_to_all(shares, "dp", 0, 0, tiled=True, axis_index_groups=Z_GROUPS)

    grads, _ = lax.optimization_barrier((grads, lines))
    own, other = feature_terms(table, grads, k_full, v_pieces, zones, width, tensor_count)
    other = swap_cores(other, tensor_count)
    share = own.shape[0] * 2 // tensor_count
    pairs = [
        own[s * share : (s + 1) * share].astype(F32)
        + other[s * share : (s + 1) * share].astype(F32)
        for s in range(tensor_count // 2)
    ]
    grad_features = pairs[0]
    for s in range(1, tensor_count // 2):
        grad_features = grad_features + lax.ppermute(
            pairs[s].astype(BF16),
            "tensor",
            [(t, (t + 2 * s) % tensor_count) for t in range(tensor_count)],
        ).astype(F32)
    grad_features = grad_features.astype(BF16).reshape(images, tokens // tensor_count, width)
    shares, grad_features = lax.optimization_barrier((shares, grad_features))
    weight_grads = jnp.sum(shares.astype(F32), axis=0)
    return (
        attended,
        grad_queries,
        grad_features,
        weight_grads[:, :head_dim],
        weight_grads[:, head_dim:],
    )


def solution(mesh):
    in_specs = (
        P("dp", "tensor"),
        P("dp", None, None),
        P("dp", "tensor"),
        P("dp", "tensor"),
        P(),
        P(),
        P(),
        P(),
        P("dp", "tensor"),
    )
    out_specs = (
        P("dp", "tensor"),
        P("dp", "tensor"),
        P("dp", "tensor", None),
        P("dp", "tensor"),
        P("dp", "tensor"),
    )
    return jax.shard_map(local, mesh=mesh, in_specs=in_specs, out_specs=out_specs, check_vma=False)
```

time: 253 us -> 256 us (1.012)
  waiting for transfers between devices: 127 us -> 145 us
  local copies, waits for them, and re-layouts: 24.2 us -> 15.3 us
  starting transfers between devices: 64.9 us -> 56.5 us
  Pallas kernels: 24.9 us -> 29.9 us
  other arithmetic: 8.16 us -> 4.38 us
    ppermute x3, waiting for transfers between devices: 0.01 us -> 16.3 us  [local(): lax.ppermute(pairs[s].astype(BF16), 'tensor', [(t, (t + 2 * s) % tensor_c...]
    all_to_all x1, waiting for transfers between devices: 19.1 us -> 7.79 us  [local(): lax.all_to_all(shares, 'dp', 0, 0, tiled=True, axis_index_groups=Z_GROUPS)]
    ppermute x8 -> x7, waiting for transfers between devices: 21.1 us -> 29.5 us  [shift_z(): return lax.ppermute(x, 'dp', pairs)]
    unnamed x57 -> x43, local copies, waits for them, and re-layouts: 15.8 us -> 8.18 us
    pallas_call x6, Pallas kernels: 20.9 us -> 27.9 us  [the longest x1 8.84 us: attend(): pl.pallas_call(attend_kernel, grid_spec=pltpu.PrefetchScalarGridSpec(num_...]
    ppermute x2, waiting for transfers between devices: 0.01 us -> 4.15 us  [swap_cores(): return lax.ppermute(x, 'tensor', [(t, t ^ 1) for t in range(count)])]
    ppermute x9, waiting for transfers between devices: 9.4 us -> 5.71 us  [shift_y(): return lax.ppermute(x, 'dp', pairs)]
    all_to_all x1, waiting for transfers between devices: 38.5 us -> 41.4 us  [local(): kv = lax.all_to_all(send, 'dp', 0, 0, tiled=True)]
  transfers between devices with their start and end apart: 27 -> 26, of which waited for: 14 -> 16; matrix products, arithmetic and copies ran while one was open for 5% -> 4% of each run, Pallas kernels for 6% -> 8%
where the time goes in v4:
time: 256 us; the launch traced here: 252 us
  waiting for transfers between devices  145 us (57%)
  starting transfers between devices  56.5 us (22%)
  Pallas kernels  29.9 us (12%)
  local copies, waits for them, and re-layouts  15.3 us (6%)
  other arithmetic  4.38 us (2%)
    all_to_all x1, waiting for transfers between devices, local(): kv = lax.all_to_all(send, 'dp', 0, 0, tiled=True)  41.4 us
    all_to_all x1, waiting for transfers between devices, local(): parts = lax.all_to_all(parts, 'dp', 0, 0, tiled=True)  39.1 us
    ppermute x7, waiting for transfers between devices, shift_z(): return lax.ppermute(x, 'dp', pairs)  29.5 us
    ppermute x3, waiting for transfers between devices, local(): lax.ppermute(pairs[s].astype(BF16), 'tensor', [(t, (t + 2 * s) % tensor_c...  16.3 us
    ppermute x9, starting transfers between devices, shift_y(): return lax.ppermute(x, 'dp', pairs)  13.3 us
    all_to_all x1, starting transfers between devices, local(): kv = lax.all_to_all(send, 'dp', 0, 0, tiled=True)  9.27 us
    pallas_call x1, Pallas kernels, attend(): pl.pallas_call(attend_kernel, grid_spec=pltpu.PrefetchScalarGridSpec(num_...  8.84 us
    all_to_all x1, starting transfers between devices, local(): lax.all_to_all(jnp.broadcast_to(k_weight, (NZ,) + k_weight.shape), 'dp',...  8.57 us
  transfers between devices with their start and end apart: 26, of which 16 were waited for; matrix products, arithmetic and copies ran while one was open for 4% of the time, Pallas kernels for 8%

profile of v4, /device:TPU:32, one launch (start us, length us, event | category | flops | bytes accessed | tf_op | source)
XLA Modules:
  0.0 252.4 jit_solution(9295161811419557311)
XLA Ops:
  0.6 3.3 %collective-permute-start.1 = (bf16[256,128]{1,0:T(8,128)(2,1)}, bf16[256,128]{1,0:T(8,128)(2,1)S(1)}, u32[]{:S(2)}, u32[]{:S(2)}) collective-permute-start(bf16[256,128]{1,0:T(8,128)(2,1)} %param.12), channel_id=1, source_target_pairs={{0,128},{8,136},{16,144},{24,152},{32,160},{40,168},{48,176},{56,1... | collective-permute-start | bytes 196616 | tf_op jit(solution)/shard_map/ppermute | solution.py:363
  3.9 1.1 collective-permute-start
  5.0 1.0 collective-permute-start.2
  5.9 1.7 broadcast_in_dim.29
  7.6 8.6 %all-to-all-start = ((bf16[8,256,128]{2,1,0:T(8,128)(2,1)}), bf16[8,256,128]{2,1,0:T(8,128)(2,1)S(1)}, u32[]{:S(2)}, u32[]{:S(2)}) async-start(bf16[8,256,128]{2,1,0:T(8,128)(2,1)} %broadcast_in_dim.29), calls=%async_computation | async-start | bytes 1048576 | tf_op jit(solution)/shard_map/all_to_all | solution.py:403
  18.4 2.0 collective-permute-start.3
  20.6 13.4 %collective-permute-done.4.refs_2_ = bf16[1024,128]{1,0:T(8,128)(2,1)S(1)} collective-permute-done((bf16[1024,128]{1,0:T(8,128)(2,1)S(1)}, bf16[1024,128]{1,0:T(8,128)(2,1)S(1)}, u32[]{:S(2)}, u32[]{:S(2)}) %collective-permute-start.4) | collective-permute-done | bytes 262176 | tf_op jit(solution)/shard_map/ppermute | solution.py:368
  34.1 1.8 broadcast_in_dim.33
  35.9 3.7 %all-to-all-start.1 = ((bf16[4,8,256,128]{3,2,1,0:T(8,128)(2,1)}), bf16[4,8,256,128]{3,2,1,0:T(8,128)(2,1)S(1)}, u32[]{:S(2)}, u32[]{:S(2)}) async-start(bf16[4,8,256,128]{3,2,1,0:T(8,128)(2,1)} %broadcast_in_dim.33), calls=%async_computation.1 | async-start | bytes 4194304 | tf_op jit(solution)/shard_map/all_to_all | solution.py:410
  39.6 1.5 collective-permute-start.5
  41.7 5.2 %collective-permute-done.5.refs_3_ = bf16[1024,128]{1,0:T(8,128)(2,1)S(1)} collective-permute-done((bf16[1024,128]{1,0:T(8,128)(2,1)S(1)}, bf16[1024,128]{1,0:T(8,128)(2,1)S(1)}, u32[]{:S(2)}, u32[]{:S(2)}) %collective-permute-start.5) | collective-permute-done | bytes 262176 | tf_op jit(solution)/shard_map/ppermute | solution.py:368
  47.0 1.2 collective-permute-start.7
  48.6 1.4 collective-permute-start.8
  50.0 4.5 %collective-permute-done.7.refs_5_ = bf16[1024,128]{1,0:T(8,128)(2,1)S(1)} collective-permute-done((bf16[1024,128]{1,0:T(8,128)(2,1)S(1)}, bf16[1024,128]{1,0:T(8,128)(2,1)S(1)}, u32[]{:S(2)}, u32[]{:S(2)}) %collective-permute-start.7) | collective-permute-done | bytes 262176 | tf_op jit(solution)/shard_map/ppermute | solution.py:368
  56.0 5.9 %collective-permute-done.9.refs_7_ = bf16[1024,128]{1,0:T(8,128)(2,1)S(1)} collective-permute-done((bf16[1024,128]{1,0:T(8,128)(2,1)S(1)}, bf16[1024,128]{1,0:T(8,128)(2,1)S(1)}, u32[]{:S(2)}, u32[]{:S(2)}) %collective-permute-start.9) | collective-permute-done | bytes 262176 | tf_op jit(solution)/shard_map/ppermute | solution.py:368
  62.6 1.6 all-to-all-done.1
  64.1 0.9 copy-done.10
  65.1 0.9 copy-done.13
  67.0 5.7 %project.1 = (bf16[32,128,256]{2,1,0:T(8,128)(2,1)}, f32[256,128]{1,0:T(8,128)}) custom-call(s32[5,32]{1,0:T(8,128)S(1)} %stack.41.table_ref, bf16[256,8192]{1,0:T(8,128)(2,1)} %bitcast.27, bf16[8192,128]{1,0:T(8,128)(2,1)S(1)} %bitcast.23, bf16[1024,128]{1,0:T(8,128)(2,1)S(1)} %constant_dynamic-update-slice_fusion.refs_0_, ...), custom_call_target="tpu_custom_call" | custom-call | flops 1073741824 | bytes 10485760 | tf_op jit(solution)/shard_map/project/pallas_call | solution.py:80
  72.7 9.3 %all-to-all-start.2 = ((bf16[32,128,256]{2,1,0:T(8,128)(2,1)}), bf16[32,128,256]{2,1,0:T(8,128)(2,1)}, u32[]{:S(2)}, u32[]{:S(2)}) async-start(bf16[32,128,256]{2,1,0:T(8,128)(2,1)} %get-tuple-element.37), calls=%async_computation.2 | async-start | bytes 4194304 | tf_op jit(solution)/shard_map/all_to_all | solution.py:426
  82.1 2.7 %dynamic-slice_bitcast_fusion = (bf16[128,2048]{1,0:T(8,128)(2,1)}, bf16[128,2048]{1,0:T(8,128)(2,1)}, bf16[128,2048]{1,0:T(8,128)(2,1)}, bf16[128,2048]{1,0:T(8,128)(2,1)S(1)}) fusion(bf16[2,128,8192]{2,1,0:T(8,128)(2,1)} %param.10, s32[]{:T(128)S(6)} %select_n.86, s32[]{:T(128)S(6)} %select_n.94, s32[]{:T(128)S(6)} %select_n.92, s32[]{:T(128)S(6)} %select_n.90, ...), kind=kLoop, calls=%fused_computation.5 | loop fusion | bytes 4194324 | tf_op jit(solution)/shard_map/squeeze | solution.py:432
  84.8 2.7 %collective-permute-start.12 = (bf16[128,2048]{1,0:T(8,128)(2,1)}, bf16[128,2048]{1,0:T(8,128)(2,1)}, u32[]{:S(2)}, u32[]{:S(2)}) collective-permute-start(bf16[128,2048]{1,0:T(8,128)(2,1)} %get-tuple-element.68), channel_id=1, source_target_pairs={{0,192},{8,200},{16,208},{24,216},{32,224},{40,232},{48,240},{56,2... | collective-permute-start | bytes 1572872 | tf_op jit(solution)/shard_map/ppermute | solution.py:363
  89.2 41.4 %all-to-all-done.2.kv_ref = bf16[32,128,256]{2,1,0:T(8,128)(2,1)} async-done(((bf16[32,128,256]{2,1,0:T(8,128)(2,1)}), bf16[32,128,256]{2,1,0:T(8,128)(2,1)}, u32[]{:S(2)}, u32[]{:S(2)}) %all-to-all-start.2) | async-done | bytes 2097184 | tf_op jit(solution)/shard_map/all_to_all | solution.py:426
  130.6 8.8 %attend.1 = (bf16[32,128,256]{2,1,0:T(8,128)(2,1)}, bf16[32,128,128]{2,1,0:T(8,128)(2,1)}, bf16[32,128,128]{2,1,0:T(8,128)(2,1)}) custom-call(s32[5,32]{1,0:T(8,128)S(1)} %stack.41.table_ref, bf16[512,1024]{1,0:T(8,128)(2,1)} %q_ref.1, bf16[512,1024]{1,0:T(8,128)(2,1)} %ct_ref.1, bf16[32,128,256]{2,1,0:T(8,128)(2,1)} %all-to-all-done.2.kv_ref), custom_call_target="tpu_custom_call" | custom-call | flops 536870912 | bytes 8388608 | tf_op jit(solution)/shard_map/attend/pallas_call | solution.py:174
  139.5 5.6 %all-to-all-start.3 = ((bf16[32,128,256]{2,1,0:T(8,128)(2,1)}), bf16[32,128,256]{2,1,0:T(8,128)(2,1)}, u32[]{:S(2)}, u32[]{:S(2)}) async-start(bf16[32,128,256]{2,1,0:T(8,128)(2,1)} %get-tuple-element.41), calls=%async_computation.3 | async-start | bytes 4194304 | tf_op jit(solution)/shard_map/all_to_all | solution.py:442
  145.1 2.0 transpose_pieces.1.own_ref
  147.2 6.2 %apply.1 = (bf16[512,1024]{1,0:T(8,128)(2,1)}, bf16[512,1024]{1,0:T(8,128)(2,1)}) custom-call(s32[5,32]{1,0:T(8,128)S(1)} %stack.41.table_ref, bf16[32,128,256]{2,1,0:T(8,128)(2,1)} %all-to-all-done.2.kv_ref, bf16[32,128,128]{2,1,0:T(8,128)(2,1)} %get-tuple-element.46.probs_ref, bf16[32,128,128]{2,1,0:T(8,128)(2,1)} %get-tuple-element.47.ds_ref), custom_call_target="tpu_custom_call" | custom-call | flops 268435456 | bytes 6291456 | tf_op jit(solution)/shard_map/apply/pallas_call | solution.py:213
  153.4 1.3 copy-done.3
  154.7 39.1 %all-to-all-done.3.part_ref = bf16[32,128,256]{2,1,0:T(8,128)(2,1)} async-done(((bf16[32,128,256]{2,1,0:T(8,128)(2,1)}), bf16[32,128,256]{2,1,0:T(8,128)(2,1)}, u32[]{:S(2)}, u32[]{:S(2)}) %all-to-all-start.3) | async-done | bytes 2097184 | tf_op jit(solution)/shard_map/all_to_all | solution.py:442
  193.7 2.9 %owner_grads.1 = (bf16[256,256]{1,0:T(8,128)(2,1)S(1)}, bf16[256,256]{1,0:T(8,128)(2,1)S(1)}) custom-call(s32[5,32]{1,0:T(8,128)S(1)} %stack.41.table_ref, bf16[32,128,256]{2,1,0:T(8,128)(2,1)} %all-to-all-done.3.part_ref, f32[256,128]{1,0:T(8,128)} %get-tuple-element.39.raw_ref, f32[1,128]{1,0:T(1,128)S(1)} %bitcast.26), custom_call_target="tpu_custom_call" | custom-call | bytes 3145728 | tf_op jit(solution)/shard_map/owner_grads/pallas_call | solution.py:259
  196.7 1.2 collective-permute-start.16
  197.9 1.8 collective-permute-start.15
  200.3 1.5 collective-permute-done.16.refs_3_
  201.7 2.7 %collective-permute-done.15.refs_2_ = bf16[256,256]{1,0:T(8,128)(2,1)S(1)} collective-permute-done((bf16[256,256]{1,0:T(8,128)(2,1)S(1)}, bf16[256,256]{1,0:T(8,128)(2,1)S(1)}, u32[]{:S(2)}, u32[]{:S(2)}) %collective-permute-start.15) | collective-permute-done | bytes 131104 | tf_op jit(solution)/shard_map/ppermute | solution.py:363
  204.4 1.6 collective-permute-done.14.refs_1_
  206.0 2.0 feature_terms.1
  208.1 4.1 %collective-permute-done.17 = bf16[128,8192]{1,0:T(8,128)(2,1)S(1)} collective-permute-done((bf16[128,8192]{1,0:T(8,128)(2,1)S(1)}, bf16[128,8192]{1,0:T(8,128)(2,1)S(1)}, u32[]{:S(2)}, u32[]{:S(2)}) %collective-permute-start.17) | collective-permute-done | bytes 2097184 | tf_op jit(solution)/shard_map/ppermute | solution.py:372
  212.6 1.0 copy-done.19
  213.6 1.5 collective-permute-start.18
  215.1 1.7 collective-permute-start.20
  216.8 1.8 collective-permute-start.19
  218.7 2.2 weight_terms.1
  220.9 3.9 %all-to-all-start.4 = ((bf16[8,256,256]{2,1,0:T(8,128)(2,1)}), bf16[8,256,256]{2,1,0:T(8,128)(2,1)S(1)}, u32[]{:S(2)}, u32[]{:S(2)}) async-start(bf16[8,256,256]{2,1,0:T(8,128)(2,1)} %weight_terms.1), calls=%async_computation.4 | async-start | bytes 2097152 | tf_op jit(solution)/shard_map/all_to_all | solution.py:453
  224.8 3.9 %collective-permute-done.18 = bf16[32,8192]{1,0:T(8,128)(2,1)S(1)} collective-permute-done((bf16[32,8192]{1,0:T(8,128)(2,1)S(1)}, bf16[32,8192]{1,0:T(8,128)(2,1)S(1)}, u32[]{:S(2)}, u32[]{:S(2)}) %collective-permute-start.18) | collective-permute-done | bytes 524320 | tf_op jit(solution)/shard_map/ppermute | solution.py:466
  228.8 1.2 collective-permute-done.20
  230.0 11.1 %collective-permute-done.19 = bf16[32,8192]{1,0:T(8,128)(2,1)} collective-permute-done((bf16[32,8192]{1,0:T(8,128)(2,1)S(1)}, bf16[32,8192]{1,0:T(8,128)(2,1)}, u32[]{:S(2)}, u32[]{:S(2)}) %collective-permute-start.19) | collective-permute-done | bytes 524320 | tf_op jit(solution)/shard_map/ppermute | solution.py:466
  241.1 2.7 %add_convert_fusion = bf16[32,8192]{1,0:T(8,128)(2,1)} fusion(bf16[32,8192]{1,0:T(8,128)(2,1)} %collective-permute-done.20, bf16[32,8192]{1,0:T(8,128)(2,1)} %collective-permute-done.19, bf16[32,8192]{1,0:T(8,128)(2,1)S(1)} %collective-permute-done.18, bf16[128,8192]{1,0:T(8,128)(2,1)} %copy-done.19, bf16[128,8192]{1,0:T(8,128)(2,1)} %copy-done.2), kind=kLoop, calls=%fused_computation.1 | loop fusion | flops 2621440 | bytes 3145728 | tf_op jit(solution)/shard_map/convert_element_type | solution.py:471
  243.8 7.8 %all-to-all-done.4 = bf16[8,256,256]{2,1,0:T(8,128)(2,1)S(1)} async-done(((bf16[8,256,256]{2,1,0:T(8,128)(2,1)}), bf16[8,256,256]{2,1,0:T(8,128)(2,1)S(1)}, u32[]{:S(2)}, u32[]{:S(2)}) %all-to-all-start.4) | async-done | bytes 1048608 | tf_op jit(solution)/shard_map/all_to_all | solution.py:453
  (73 shorter events, 10.1 us)
Async XLA Ops:
  0.6 17.6 %collective-permute-start.1 = (bf16[256,128]{1,0:T(8,128)(2,1)}, bf16[256,128]{1,0:T(8,128)(2,1)S(1)}, u32[]{:S(2)}, u32[]{:S(2)}) collective-permute-start(bf16[256,128]{1,0:T(8,128)(2,1)} %param.12), channel_id=1, source_target_pairs={{0,128},{8,136},{16,144},{24,152},{32,160},{40,168},{48,176},{56,1... | collective-permute-start | bytes 196616 | tf_op jit(solution)/shard_map/ppermute | solution.py:363
  3.9 14.3 %collective-permute-start = (bf16[256,128]{1,0:T(8,128)(2,1)}, bf16[256,128]{1,0:T(8,128)(2,1)S(1)}, u32[]{:S(2)}, u32[]{:S(2)}) collective-permute-start(bf16[256,128]{1,0:T(8,128)(2,1)} %param.12), channel_id=1, source_target_pairs={{0,192},{8,200},{16,208},{24,216},{32,224},{40,232},{48,240},{56,2... | collective-permute-start | bytes 196616 | tf_op jit(solution)/shard_map/ppermute | solution.py:363
  5.0 13.3 %collective-permute-start.2 = (bf16[256,128]{1,0:T(8,128)(2,1)}, bf16[256,128]{1,0:T(8,128)(2,1)S(1)}, u32[]{:S(2)}, u32[]{:S(2)}) collective-permute-start(bf16[256,128]{1,0:T(8,128)(2,1)} %param.12), channel_id=1, source_target_pairs={{0,64},{8,72},{16,80},{24,88},{32,96},{40,104},{48,112},{56,120},{... | collective-permute-start | bytes 196616 | tf_op jit(solution)/shard_map/ppermute | solution.py:363
  7.6 26.4 %all-to-all-start = ((bf16[8,256,128]{2,1,0:T(8,128)(2,1)}), bf16[8,256,128]{2,1,0:T(8,128)(2,1)S(1)}, u32[]{:S(2)}, u32[]{:S(2)}) async-start(bf16[8,256,128]{2,1,0:T(8,128)(2,1)} %broadcast_in_dim.29), calls=%async_computation | async-start | bytes 1048576 | tf_op jit(solution)/shard_map/all_to_all | solution.py:403
  18.3 15.8 %collective-permute-start.4 = (bf16[1024,128]{1,0:T(8,128)(2,1)S(1)}, bf16[1024,128]{1,0:T(8,128)(2,1)S(1)}, u32[]{:S(2)}, u32[]{:S(2)}) collective-permute-start(bf16[1024,128]{1,0:T(8,128)(2,1)S(1)} %constant_dynamic-update-slice_fusion.refs_0_), channel_id=1, source_target_pairs={{0,56},{8,0},{16,8},{24,16},{32,24},{40,32},{48,40},{56,48},{64,12... | collective-permute-start | bytes 786440 | tf_op jit(solution)/shard_map/ppermute | solution.py:368
  18.4 15.7 %collective-permute-start.3 = (bf16[1024,128]{1,0:T(8,128)(2,1)S(1)}, bf16[1024,128]{1,0:T(8,128)(2,1)S(1)}, u32[]{:S(2)}, u32[]{:S(2)}) collective-permute-start(bf16[1024,128]{1,0:T(8,128)(2,1)S(1)} %constant_dynamic-update-slice_fusion.refs_0_), channel_id=1, source_target_pairs={{0,8},{8,16},{16,24},{24,32},{32,40},{40,48},{48,56},{56,0},{64,72... | collective-permute-start | bytes 786440 | tf_op jit(solution)/shard_map/ppermute | solution.py:368
  35.9 28.3 %copy-start.18 = (f32[128]{0:T(128)S(1)}, f32[128]{0:T(128)}, u32[]{:S(2)}) copy-start(f32[128]{0:T(128)} %param.13) | copy-start | bytes 1540
  35.9 28.2 %all-to-all-start.1 = ((bf16[4,8,256,128]{3,2,1,0:T(8,128)(2,1)}), bf16[4,8,256,128]{3,2,1,0:T(8,128)(2,1)S(1)}, u32[]{:S(2)}, u32[]{:S(2)}) async-start(bf16[4,8,256,128]{3,2,1,0:T(8,128)(2,1)} %broadcast_in_dim.33), calls=%async_computation.1 | async-start | bytes 4194304 | tf_op jit(solution)/shard_map/all_to_all | solution.py:410
  39.6 7.3 %collective-permute-start.5 = (bf16[1024,128]{1,0:T(8,128)(2,1)S(1)}, bf16[1024,128]{1,0:T(8,128)(2,1)S(1)}, u32[]{:S(2)}, u32[]{:S(2)}) collective-permute-start(bf16[1024,128]{1,0:T(8,128)(2,1)S(1)} %collective-permute-done.3.refs_1_), channel_id=1, source_target_pairs={{0,8},{8,16},{16,24},{24,32},{32,40},{40,48},{48,56},{56,0},{64,72... | collective-permute-start | bytes 786440 | tf_op jit(solution)/shard_map/ppermute | solution.py:368
  41.2 7.5 %collective-permute-start.6 = (bf16[1024,128]{1,0:T(8,128)(2,1)S(1)}, bf16[1024,128]{1,0:T(8,128)(2,1)S(1)}, u32[]{:S(2)}, u32[]{:S(2)}) collective-permute-start(bf16[1024,128]{1,0:T(8,128)(2,1)S(1)} %collective-permute-done.4.refs_2_), channel_id=1, source_target_pairs={{0,56},{8,0},{16,8},{24,16},{32,24},{40,32},{48,40},{56,48},{64,12... | collective-permute-start | bytes 786440 | tf_op jit(solution)/shard_map/ppermute | solution.py:368
  47.0 25.7 %copy-start.5 = (bf16[1024,128]{1,0:T(8,128)(2,1)}, bf16[1024,128]{1,0:T(8,128)(2,1)S(1)}, u32[]{:S(2)}) copy-start(bf16[1024,128]{1,0:T(8,128)(2,1)S(1)} %collective-permute-done.5.refs_3_) | copy-start | bytes 786436
  47.0 7.5 %collective-permute-start.7 = (bf16[1024,128]{1,0:T(8,128)(2,1)S(1)}, bf16[1024,128]{1,0:T(8,128)(2,1)S(1)}, u32[]{:S(2)}, u32[]{:S(2)}) collective-permute-start(bf16[1024,128]{1,0:T(8,128)(2,1)S(1)} %collective-permute-done.5.refs_3_), channel_id=1, source_target_pairs={{0,8},{8,16},{16,24},{24,32},{32,40},{40,48},{48,56},{56,0},{64,72... | collective-permute-start | bytes 786440 | tf_op jit(solution)/shard_map/ppermute | solution.py:368
  48.6 24.1 %copy-start.7 = (bf16[1024,128]{1,0:T(8,128)(2,1)}, bf16[1024,128]{1,0:T(8,128)(2,1)S(1)}, u32[]{:S(2)}) copy-start(bf16[1024,128]{1,0:T(8,128)(2,1)S(1)} %collective-permute-done.6.refs_4_) | copy-start | bytes 786436
  48.6 6.6 %collective-permute-start.8 = (bf16[1024,128]{1,0:T(8,128)(2,1)S(1)}, bf16[1024,128]{1,0:T(8,128)(2,1)S(1)}, u32[]{:S(2)}, u32[]{:S(2)}) collective-permute-start(bf16[1024,128]{1,0:T(8,128)(2,1)S(1)} %collective-permute-done.6.refs_4_), channel_id=1, source_target_pairs={{0,56},{8,0},{16,8},{24,16},{32,24},{40,32},{48,40},{56,48},{64,12... | collective-permute-start | bytes 786440 | tf_op jit(solution)/shard_map/ppermute | solution.py:368
  54.5 7.3 %collective-permute-start.9 = (bf16[1024,128]{1,0:T(8,128)(2,1)S(1)}, bf16[1024,128]{1,0:T(8,128)(2,1)S(1)}, u32[]{:S(2)}, u32[]{:S(2)}) collective-permute-start(bf16[1024,128]{1,0:T(8,128)(2,1)S(1)} %collective-permute-done.7.refs_5_), channel_id=1, source_target_pairs={{0,8},{8,16},{16,24},{24,32},{32,40},{40,48},{48,56},{56,0},{64,72... | collective-permute-start | bytes 786440 | tf_op jit(solution)/shard_map/ppermute | solution.py:368
  54.6 0.7 copy-start.9
  55.3 0.7 copy-start.12
  61.9 0.7 copy-start.15
  64.1 1.0 copy-start.10
  65.1 0.9 copy-start.13
  66.0 0.9 copy-start.16
  72.7 57.9 %all-to-all-start.2 = ((bf16[32,128,256]{2,1,0:T(8,128)(2,1)}), bf16[32,128,256]{2,1,0:T(8,128)(2,1)}, u32[]{:S(2)}, u32[]{:S(2)}) async-start(bf16[32,128,256]{2,1,0:T(8,128)(2,1)} %get-tuple-element.37), calls=%async_computation.2 | async-start | bytes 4194304 | tf_op jit(solution)/shard_map/all_to_all | solution.py:426
  84.8 54.7 %collective-permute-start.12 = (bf16[128,2048]{1,0:T(8,128)(2,1)}, bf16[128,2048]{1,0:T(8,128)(2,1)}, u32[]{:S(2)}, u32[]{:S(2)}) collective-permute-start(bf16[128,2048]{1,0:T(8,128)(2,1)} %get-tuple-element.68), channel_id=1, source_target_pairs={{0,192},{8,200},{16,208},{24,216},{32,224},{40,232},{48,240},{56,2... | collective-permute-start | bytes 1572872 | tf_op jit(solution)/shard_map/ppermute | solution.py:363
  87.5 51.9 %collective-permute-start.11 = (bf16[128,2048]{1,0:T(8,128)(2,1)}, bf16[128,2048]{1,0:T(8,128)(2,1)}, u32[]{:S(2)}, u32[]{:S(2)}) collective-permute-start(bf16[128,2048]{1,0:T(8,128)(2,1)} %get-tuple-element.69), channel_id=1, source_target_pairs={{0,128},{8,136},{16,144},{24,152},{32,160},{40,168},{48,176},{56,1... | collective-permute-start | bytes 1572872 | tf_op jit(solution)/shard_map/ppermute | solution.py:363
  88.3 51.1 %collective-permute-start.10 = (bf16[128,2048]{1,0:T(8,128)(2,1)}, bf16[128,2048]{1,0:T(8,128)(2,1)}, u32[]{:S(2)}, u32[]{:S(2)}) collective-permute-start(bf16[128,2048]{1,0:T(8,128)(2,1)} %get-tuple-element.70), channel_id=1, source_target_pairs={{0,64},{8,72},{16,80},{24,88},{32,96},{40,104},{48,112},{56,120},{... | collective-permute-start | bytes 1572872 | tf_op jit(solution)/shard_map/ppermute | solution.py:363
  139.5 54.3 %all-to-all-start.3 = ((bf16[32,128,256]{2,1,0:T(8,128)(2,1)}), bf16[32,128,256]{2,1,0:T(8,128)(2,1)}, u32[]{:S(2)}, u32[]{:S(2)}) async-start(bf16[32,128,256]{2,1,0:T(8,128)(2,1)} %get-tuple-element.41), calls=%async_computation.3 | async-start | bytes 4194304 | tf_op jit(solution)/shard_map/all_to_all | solution.py:442
  147.1 6.3 %copy-start = (bf16[2048,512]{1,0:T(8,128)(2,1)}, bf16[2048,512]{1,0:T(8,128)(2,1)S(1)}, u32[]{:S(2)}) copy-start(bf16[2048,512]{1,0:T(8,128)(2,1)S(1)} %transpose_pieces.1.own_ref) | copy-start | bytes 6291460
  147.1 6.3 %collective-permute-start.13 = (bf16[2048,512]{1,0:T(8,128)(2,1)S(1)}, bf16[2048,512]{1,0:T(8,128)(2,1)S(1)}, u32[]{:S(2)}, u32[]{:S(2)}) collective-permute-start(bf16[2048,512]{1,0:T(8,128)(2,1)S(1)} %transpose_pieces.1.own_ref), channel_id=1, source_target_pairs={{0,1},{1,0},{2,3},{3,2},{4,5},{5,4},{6,7},{7,6},{8,9},{9,8},{10,11... | collective-permute-start | bytes 6291464 | tf_op jit(solution)/shard_map/ppermute | solution.py:372
  153.3 52.6 %copy-start.6 = (bf16[1024,128]{1,0:T(8,128)(2,1)S(1)}, bf16[1024,128]{1,0:T(8,128)(2,1)}, u32[]{:S(2)}) copy-start(bf16[1024,128]{1,0:T(8,128)(2,1)} %copy-done.5) | copy-start | bytes 786436
  153.3 52.6 %copy-start.8 = (bf16[1024,128]{1,0:T(8,128)(2,1)S(1)}, bf16[1024,128]{1,0:T(8,128)(2,1)}, u32[]{:S(2)}) copy-start(bf16[1024,128]{1,0:T(8,128)(2,1)} %copy-done.7) | copy-start | bytes 786436
  153.4 1.3 copy-start.3
  193.7 12.2 %copy-start.11 = (bf16[1024,128]{1,0:T(8,128)(2,1)S(1)}, bf16[1024,128]{1,0:T(8,128)(2,1)}, u32[]{:S(2)}) copy-start(bf16[1024,128]{1,0:T(8,128)(2,1)} %copy-done.9) | copy-start | bytes 786436
  193.7 12.2 %copy-start.14 = (bf16[1024,128]{1,0:T(8,128)(2,1)S(1)}, bf16[1024,128]{1,0:T(8,128)(2,1)}, u32[]{:S(2)}) copy-start(bf16[1024,128]{1,0:T(8,128)(2,1)} %copy-done.12) | copy-start | bytes 786436
  193.7 12.2 %copy-start.17 = (bf16[1024,128]{1,0:T(8,128)(2,1)S(1)}, bf16[1024,128]{1,0:T(8,128)(2,1)}, u32[]{:S(2)}) copy-start(bf16[1024,128]{1,0:T(8,128)(2,1)} %copy-done.15) | copy-start | bytes 786436
  196.7 5.0 %collective-permute-start.16 = (bf16[256,256]{1,0:T(8,128)(2,1)S(1)}, bf16[256,256]{1,0:T(8,128)(2,1)S(1)}, u32[]{:S(2)}, u32[]{:S(2)}) collective-permute-start(bf16[256,256]{1,0:T(8,128)(2,1)S(1)} %get-tuple-element.54.refs_0_), channel_id=1, source_target_pairs={{0,192},{8,200},{16,208},{24,216},{32,224},{40,232},{48,240},{56,2... | collective-permute-start | bytes 393224 | tf_op jit(solution)/shard_map/ppermute | solution.py:363
  197.9 6.5 %collective-permute-start.15 = (bf16[256,256]{1,0:T(8,128)(2,1)S(1)}, bf16[256,256]{1,0:T(8,128)(2,1)S(1)}, u32[]{:S(2)}, u32[]{:S(2)}) collective-permute-start(bf16[256,256]{1,0:T(8,128)(2,1)S(1)} %get-tuple-element.54.refs_0_), channel_id=1, source_target_pairs={{0,128},{8,136},{16,144},{24,152},{32,160},{40,168},{48,176},{56,1... | collective-permute-start | bytes 393224 | tf_op jit(solution)/shard_map/ppermute | solution.py:363
  199.8 6.2 %collective-permute-start.14 = (bf16[256,256]{1,0:T(8,128)(2,1)S(1)}, bf16[256,256]{1,0:T(8,128)(2,1)S(1)}, u32[]{:S(2)}, u32[]{:S(2)}) collective-permute-start(bf16[256,256]{1,0:T(8,128)(2,1)S(1)} %get-tuple-element.54.refs_0_), channel_id=1, source_target_pairs={{0,64},{8,72},{16,80},{24,88},{32,96},{40,104},{48,112},{56,120},{... | collective-permute-start | bytes 393224 | tf_op jit(solution)/shard_map/ppermute | solution.py:363
  208.0 4.6 %copy-start.2 = (bf16[128,8192]{1,0:T(8,128)(2,1)}, bf16[128,8192]{1,0:T(8,128)(2,1)S(1)}, u32[]{:S(2)}) copy-start(bf16[128,8192]{1,0:T(8,128)(2,1)S(1)} %get-tuple-element.57) | copy-start | bytes 6291460
  208.0 4.2 %collective-permute-start.17 = (bf16[128,8192]{1,0:T(8,128)(2,1)S(1)}, bf16[128,8192]{1,0:T(8,128)(2,1)S(1)}, u32[]{:S(2)}, u32[]{:S(2)}) collective-permute-start(bf16[128,8192]{1,0:T(8,128)(2,1)S(1)} %get-tuple-element.58), channel_id=1, source_target_pairs={{0,1},{1,0},{2,3},{3,2},{4,5},{5,4},{6,7},{7,6},{8,9},{9,8},{10,11... | collective-permute-start | bytes 6291464 | tf_op jit(solution)/shard_map/ppermute | solution.py:372
  212.3 1.3 copy-start.19
  212.3 6.4 %copy-start.1 = (bf16[2048,512]{1,0:T(8,128)(2,1)S(1)}, bf16[2048,512]{1,0:T(8,128)(2,1)}, u32[]{:S(2)}) copy-start(bf16[2048,512]{1,0:T(8,128)(2,1)} %copy-done) | copy-start | bytes 6291460
  212.3 6.4 %copy-start.4 = (bf16[2048,512]{1,0:T(8,128)(2,1)S(1)}, bf16[2048,512]{1,0:T(8,128)(2,1)}, u32[]{:S(2)}) copy-start(bf16[2048,512]{1,0:T(8,128)(2,1)} %copy-done.3) | copy-start | bytes 6291460
  213.6 15.2 %collective-permute-start.18 = (bf16[32,8192]{1,0:T(8,128)(2,1)S(1)}, bf16[32,8192]{1,0:T(8,128)(2,1)S(1)}, u32[]{:S(2)}, u32[]{:S(2)}) collective-permute-start(bf16[32,8192]{1,0:T(8,128)(2,1)S(1)} %get-tuple-element.65), channel_id=1, source_target_pairs={{0,2},{1,3},{2,4},{3,5},{4,6},{5,7},{6,0},{7,1},{8,10},{9,11},{10,... | collective-permute-start | bytes 1572872 | tf_op jit(solution)/shard_map/ppermute | solution.py:466
  215.1 14.9 %collective-permute-start.20 = (bf16[32,8192]{1,0:T(8,128)(2,1)S(1)}, bf16[32,8192]{1,0:T(8,128)(2,1)}, u32[]{:S(2)}, u32[]{:S(2)}) collective-permute-start(bf16[32,8192]{1,0:T(8,128)(2,1)S(1)} %get-tuple-element.66), channel_id=1, source_target_pairs={{0,6},{1,7},{2,0},{3,1},{4,2},{5,3},{6,4},{7,5},{8,14},{9,15},{10,... | collective-permute-start | bytes 1572872 | tf_op jit(solution)/shard_map/ppermute | solution.py:466
  216.8 24.3 %collective-permute-start.19 = (bf16[32,8192]{1,0:T(8,128)(2,1)S(1)}, bf16[32,8192]{1,0:T(8,128)(2,1)}, u32[]{:S(2)}, u32[]{:S(2)}) collective-permute-start(bf16[32,8192]{1,0:T(8,128)(2,1)S(1)} %get-tuple-element.67), channel_id=1, source_target_pairs={{0,4},{1,5},{2,6},{3,7},{4,0},{5,1},{6,2},{7,3},{8,12},{9,13},{10,... | collective-permute-start | bytes 1572872 | tf_op jit(solution)/shard_map/ppermute | solution.py:466
  220.9 30.7 %all-to-all-start.4 = ((bf16[8,256,256]{2,1,0:T(8,128)(2,1)}), bf16[8,256,256]{2,1,0:T(8,128)(2,1)S(1)}, u32[]{:S(2)}, u32[]{:S(2)}) async-start(bf16[8,256,256]{2,1,0:T(8,128)(2,1)} %weight_terms.1), calls=%async_computation.4 | async-start | bytes 2097152 | tf_op jit(solution)/shard_map/all_to_all | solution.py:453

commit v5 on v4

--- a/solution.py
+++ b/solution.py
@@ -41,24 +41,40 @@
     return pl.BlockSpec(memory_space=pltpu.HBM)
 
 
-def weight_blocks(table_ref, kw_ref, vw_refs, zones):
-    for ref, offset in zip(vw_refs, zones):
-        z = lax.rem(table_ref[PLACE, 1] + offset, NZ)
-        block = ref.shape[0] // NY
-        for i in range(NY):
-            y = lax.rem(table_ref[PLACE, 0] + i, NY)
-            here = pl.ds(pl.multiple_of((y * NZ + z) * block, block), block)
-            v = ref[i * block : (i + 1) * block, :]
-            yield here, jnp.concatenate([kw_ref[here, :], v], axis=1)
-
-
-def project_kernel(table_ref, f_ref, kw_ref, *refs, zones):
-    vw_refs, (gain_ref, send_ref, raw_ref, kv) = refs[: len(zones)], refs[len(zones) :]
+def weight_blocks(table_ref, w_refs, zones):
+    spots = {}
+    for n, blocks in enumerate(zones):
+        for i, at in enumerate(blocks):
+            size = w_refs[n].shape[0] // len(blocks)
+            spots.setdefault(at, []).append((w_refs[n], slice(i * size, (i + 1) * size)))
+    found = []
+    for (y_off, z_off), spot in spots.items():
+        y = lax.rem(table_ref[PLACE, 0] + y_off, NY)
+        z = lax.rem(table_ref[PLACE, 1] + z_off, NZ)
+        size = spot[0][1].stop - spot[0][1].start
+        found.append((pl.ds(pl.multiple_of((y * NZ + z) * size, size), size), spot))
+    return found
+
+
+def side_by_side(spot):
+    return jnp.concatenate([ref[rows, :] for ref, rows in spot], axis=1)
+
+
+def project_kernel(table_ref, f_ref, *refs, zones):
+    w_refs, (gain_ref, send_ref, raw_ref, kv, held, sems) = refs[: len(zones)], refs[len(zones) :]
     head_dim = gain_ref.shape[1]
     tokens = send_ref.shape[1]
+    blocks = weight_blocks(table_ref, w_refs, zones)
+    copies = [
+        pltpu.make_async_copy(f_ref.at[:, cols], held.at[i], sems.at[i])
+        for i, (cols, _) in enumerate(blocks)
+    ]
+    for copy in copies:
+        copy.start()
     total = jnp.zeros((f_ref.shape[0], 2 * head_dim), F32)
-    for cols, w in weight_blocks(table_ref, kw_ref, vw_refs, zones):
-        total = total + jnp.dot(f_ref[:, cols], w, preferred_element_type=F32)
+    for i, (_, spot) in enumerate(blocks):
+        copies[i].wait()
+        total = total + jnp.dot(held[i], side_by_side(spot), preferred_element_type=F32)
     raw = total[:, :head_dim]
     raw_ref[...] = raw
     scale = lax.rsqrt(jnp.mean(raw * raw, axis=-1, keepdims=True) + EPS)
@@ -75,16 +91,21 @@
     lax.fori_loop(0, send_ref.shape[0], put, 0, unroll=4)
 
 
-def project(table, rows, k_full, v_pieces, zones, gain, dp, images, tokens):
+def project(table, rows, pieces, zones, gain, dp, images, tokens):
     cols = 2 * gain.shape[1]
+    depth = rows.shape[1] // dp
     return pl.pallas_call(
         functools.partial(project_kernel, zones=zones),
         grid_spec=pltpu.PrefetchScalarGridSpec(
             num_scalar_prefetch=1,
             grid=(),
-            in_specs=[in_vmem()] * (3 + len(v_pieces)),
+            in_specs=[in_hbm()] + [in_vmem()] * (1 + len(pieces)),
             out_specs=[in_vmem()] * 2,
-            scratch_shapes=[pltpu.VMEM((images, tokens, cols), BF16)],
+            scratch_shapes=[
+                pltpu.VMEM((images, tokens, cols), BF16),
+                pltpu.VMEM((dp, rows.shape[0], depth), BF16),
+                pltpu.SemaphoreType.DMA((dp,)),
+            ],
         ),
         out_shape=[
             pltpu.HBM((dp, tokens, cols), BF16),
@@ -93,7 +114,7 @@
         compiler_params=limit(14),
         cost_estimate=cost(2 * rows.size * cols, 10),
         name="project",
-    )(table, *hold(rows), k_full, *v_pieces, gain)
+    )(table, rows, *pieces, gain)
 
 
 def load_heads(ref, start, rows, head_dim):
@@ -318,8 +339,8 @@
     )(own_cols, other_cols, *lines)
 
 
-def feature_kernel(table_ref, grad_ref, kw_ref, *refs, zones, targets):
-    vw_refs, (own_ref, other_ref, lhs) = refs[: len(zones)], refs[len(zones) :]
+def feature_kernel(table_ref, grad_ref, *refs, zones, targets):
+    w_refs, (own_ref, other_ref, lhs) = refs[: len(zones)], refs[len(zones) :]
     half = own_ref.shape[0]
     chips = targets // 2
     tokens = grad_ref.shape[0] // 2
@@ -332,20 +353,20 @@
                 at = pl.multiple_of(i * tokens + target * share, share)
                 to = ((core * chips + chip) * 2 + i) * share
                 lhs[to : to + share, :] = grad_ref[pl.ds(at, share), :]
-    for cols, w in weight_blocks(table_ref, kw_ref, vw_refs, zones):
-        part = dot_dims(lhs[...], w, 1, 1).astype(BF16)
+    for cols, spot in weight_blocks(table_ref, w_refs, zones):
+        part = dot_dims(lhs[...], side_by_side(spot), 1, 1).astype(BF16)
         own_ref[:, cols] = part[:half]
         other_ref[:, cols] = part[half:]
 
 
-def feature_terms(table, grads, k_full, v_pieces, zones, width, targets):
+def feature_terms(table, grads, pieces, zones, width, targets):
     half = jax.ShapeDtypeStruct((grads.shape[0] // 2, width), BF16)
     return pl.pallas_call(
         functools.partial(feature_kernel, zones=zones, targets=targets),
         grid_spec=pltpu.PrefetchScalarGridSpec(
             num_scalar_prefetch=1,
             grid=(),
-            in_specs=[in_vmem()] * (2 + len(v_pieces)),
+            in_specs=[in_vmem()] * (1 + len(pieces)),
             out_specs=[in_vmem()] * 2,
             scratch_shapes=[pltpu.VMEM(grads.shape, BF16)],
         ),
@@ -353,7 +374,7 @@
         compiler_params=limit(13),
         cost_estimate=cost(4 * half.size * grads.shape[1], 8),
         name="feature_terms",
-    )(table, grads, k_full, *v_pieces)
+    )(table, grads, *pieces)
 
 
 def shift_y(x, by):
@@ -366,6 +387,18 @@
 def shift_z(x, by):
     pairs = [(y * NZ + z, y * NZ + (z + by) % NZ) for y in range(NY) for z in range(NZ)]
     return lax.ppermute(x, "dp", pairs)
+
+
+def ring_z(x, blocks):
+    pieces, zones = [x], [blocks]
+    below = above = x
+    for hop in range(1, NZ // 2):
+        below, above = shift_z(below, 1), shift_z(above, -1)
+        pieces += [below, above]
+        zones += [[(y, off) for y, _ in blocks] for off in (NZ - hop, hop)]
+    pieces += [shift_z(below, 1)]
+    zones += [[(y, NZ // 2) for y, _ in blocks]]
+    return pieces, zones
 
 
 def swap_cores(x, count):
@@ -400,28 +433,21 @@
     place = jnp.pad(place, (0, pos.shape[0] - place.shape[0]))
     table = jnp.stack([pos, my_slots // images, my_tiles * (tokens // TILES), first, place])
 
-    k_line = lax.all_to_all(
-        jnp.broadcast_to(k_weight, (NZ,) + k_weight.shape),
-        "dp", 0, 0, tiled=True, axis_index_groups=Z_GROUPS,
-    )
     v_line = jnp.concatenate([shift_y(v_weight, (NY - i) % NY) for i in range(NY)])
-    below, above = shift_z(v_line, 1), shift_z(v_line, -1)
-    k_line, below, above, table = lax.optimization_barrier((k_line, below, above, table))
-    k_full = lax.all_to_all(
-        jnp.broadcast_to(k_line, (NY,) + k_line.shape),
-        "dp", 0, 0, tiled=True, axis_index_groups=Y_GROUPS,
-    ).reshape(width, head_dim)
-    v_pieces, zones = [v_line], [0]
-    for hop in range(1, NZ // 2):
-        if hop > 1:
-            below, above = shift_z(below, 1), shift_z(above, -1)
-        v_pieces += [below, above]
-        zones += [NZ - hop, hop]
-    v_pieces += [shift_z(below, 1)]
-    zones += [NZ // 2]
+    k_ring, k_zones = ring_z(k_weight, [(0, 0)])
+    v_ring, v_zones = ring_z(v_line, [(i, 0) for i in range(NY)])
+    k_line = jnp.concatenate(k_ring)
+    half = k_line.shape[0] // 2
+    after, before = shift_y(k_line, -1), shift_y(k_line, 1)
+    pieces = [k_line, after, before, shift_y(after[:half], -1), shift_y(before[half:], 1)]
+    offsets = [z for ((_, z),) in k_zones]
+    k_zones = [[(y, z) for z in offsets] for y in (0, 1, NY - 1)]
+    far = [(NY // 2, z) for z in offsets]
+    k_zones += [far[: NZ // 2], far[NZ // 2 :]]
+    pieces, zones = pieces + v_ring, k_zones + v_zones
 
     send, raw = project(
-        table, rows, k_full, v_pieces, zones, gain, dp_count, images, tokens
+        table, rows, pieces, zones, gain, dp_count, images, tokens
     )
     kv = lax.all_to_all(send, "dp", 0, 0, tiled=True)
 
@@ -450,10 +476,10 @@
 
     lines = [shift_y(by_core, s) for s in range(NY)]
     shares = weight_terms(own_cols, other_cols, lines)
+    shares, grads = lax.optimization_barrier((shares, grads))
     shares = lax.all_to_all(shares, "dp", 0, 0, tiled=True, axis_index_groups=Z_GROUPS)
 
-    grads, _ = lax.optimization_barrier((grads, lines))
-    own, other = feature_terms(table, grads, k_full, v_pieces, zones, width, tensor_count)
+    own, other = feature_terms(table, grads, pieces, zones, width, tensor_count)
     other = swap_cores(other, tensor_count)
     share = own.shape[0] * 2 // tensor_count
     pairs = [
@@ -469,7 +495,6 @@
             [(t, (t + 2 * s) % tensor_count) for t in range(tensor_count)],
         ).astype(F32)
     grad_features = grad_features.astype(BF16).reshape(images, tokens // tensor_count, width)
-    shares, grad_features = lax.optimization_barrier((shares, grad_features))
     weight_grads = jnp.sum(shares.astype(F32), axis=0)
     return (
         attended,

time: 256 us -> 236 us (0.922)
  waiting for transfers between devices: 145 us -> 114 us
  starting transfers between devices: 56.5 us -> 63 us
  Pallas kernels: 29.9 us -> 33.3 us
    ppermute x3, waiting for transfers between devices: 16.3 us -> 1.79 us  [local(): lax.ppermute(pairs[s].astype(BF16), 'tensor', [(t, (t + 2 * s) % tensor_c...]
    ppermute x7 -> x14, starting transfers between devices: 6.82 us -> 19.4 us  [shift_z(): return lax.ppermute(x, 'dp', pairs)]
    all_to_all x2 -> x0, starting transfers between devices: 12.3 us -> none  [the longest x1 8.57 us: local(): lax.all_to_all(jnp.broadcast_to(k_weight, (NZ,) + k_weight.shape), 'dp',...]
    all_to_all x1, waiting for transfers between devices: 7.79 us -> 20 us  [local(): lax.all_to_all(shares, 'dp', 0, 0, tiled=True, axis_index_groups=Z_GROUPS)]
    ppermute x7 -> x14, waiting for transfers between devices: 29.5 us -> 18.4 us  [shift_z(): return lax.ppermute(x, 'dp', pairs)]
    all_to_all x1, waiting for transfers between devices: 39.1 us -> 29.1 us  [local(): parts = lax.all_to_all(parts, 'dp', 0, 0, tiled=True)]
    all_to_all x1, waiting for transfers between devices: 41.4 us -> 33.3 us  [local(): kv = lax.all_to_all(send, 'dp', 0, 0, tiled=True)]
    ppermute x9 -> x13, starting transfers between devices: 13.3 us -> 19.9 us  [shift_y(): return lax.ppermute(x, 'dp', pairs)]
  transfers between devices with their start and end apart: 26 -> 35, of which waited for: 16 -> 17; matrix products, arithmetic and copies ran while one was open for 4% -> 5% of each run, Pallas kernels for 8% -> 7%
where the time goes in v5:
time: 236 us; the launch traced here: 234 us
  waiting for transfers between devices  114 us (48%)
  starting transfers between devices  63 us (27%)
  Pallas kernels  33.3 us (14%)
  local copies, waits for them, and re-layouts  15.8 us (7%)
  other arithmetic  6.68 us (3%)
    all_to_all x1, waiting for transfers between devices, local(): kv = lax.all_to_all(send, 'dp', 0, 0, tiled=True)  33.3 us
    all_to_all x1, waiting for transfers between devices, local(): parts = lax.all_to_all(parts, 'dp', 0, 0, tiled=True)  29.1 us
    all_to_all x1, waiting for transfers between devices, local(): lax.all_to_all(shares, 'dp', 0, 0, tiled=True, axis_index_groups=Z_GROUPS)  20 us
    ppermute x13, starting transfers between devices, shift_y(): return lax.ppermute(x, 'dp', pairs)  19.9 us
    ppermute x14, starting transfers between devices, shift_z(): return lax.ppermute(x, 'dp', pairs)  19.4 us
    ppermute x14, waiting for transfers between devices, shift_z(): return lax.ppermute(x, 'dp', pairs)  18.4 us
    ppermute x13, waiting for transfers between devices, shift_y(): return lax.ppermute(x, 'dp', pairs)  11.7 us
    unnamed x60, local copies, waits for them, and re-layouts  10.7 us
  transfers between devices with their start and end apart: 35, of which 17 were waited for; matrix products, arithmetic and copies ran while one was open for 5% of the time, Pallas kernels for 7%

profile of v5, /device:TPU:32, one launch (start us, length us, event | category | flops | bytes accessed | tf_op | source)
XLA Modules:
  0.0 234.3 jit_solution(524508514705856003)
XLA Ops:
  0.6 2.0 collective-permute-start
  2.7 3.2 %collective-permute-start.12 = (bf16[256,128]{1,0:T(8,128)(2,1)}, bf16[256,128]{1,0:T(8,128)(2,1)S(1)}, u32[]{:S(2)}, u32[]{:S(2)}) collective-permute-start(bf16[256,128]{1,0:T(8,128)(2,1)} %param.12), channel_id=1, source_target_pairs={{0,128},{8,136},{16,144},{24,152},{32,160},{40,168},{48,176},{56,1... | collective-permute-start | bytes 196616 | tf_op jit(solution)/shard_map/ppermute | solution.py:384
  5.9 1.1 collective-permute-start.11
  10.6 2.1 collective-permute-done.13
  12.7 4.1 %collective-permute-start.15 = (bf16[1024,128]{1,0:T(8,128)(2,1)S(1)}, bf16[1024,128]{1,0:T(8,128)(2,1)S(1)}, u32[]{:S(2)}, u32[]{:S(2)}) collective-permute-start(bf16[1024,128]{1,0:T(8,128)(2,1)S(1)} %constant_dynamic-update-slice_fusion.8.refs_5_), channel_id=1, source_target_pairs={{0,56},{8,0},{16,8},{24,16},{32,24},{40,32},{48,40},{56,48},{64,12... | collective-permute-start | bytes 786440 | tf_op jit(solution)/shard_map/ppermute | solution.py:389
  17.8 1.1 collective-permute-start.3
  19.0 5.0 %collective-permute-done.2 = bf16[256,128]{1,0:T(8,128)(2,1)S(1)} collective-permute-done((bf16[256,128]{1,0:T(8,128)(2,1)S(1)}, bf16[256,128]{1,0:T(8,128)(2,1)S(1)}, u32[]{:S(2)}, u32[]{:S(2)}) %collective-permute-start.2) | collective-permute-done | bytes 65568 | tf_op jit(solution)/shard_map/ppermute | solution.py:389
  24.7 2.3 collective-permute-start.5
  27.1 2.9 %collective-permute-done.4 = bf16[256,128]{1,0:T(8,128)(2,1)S(1)} collective-permute-done((bf16[256,128]{1,0:T(8,128)(2,1)S(1)}, bf16[256,128]{1,0:T(8,128)(2,1)S(1)}, u32[]{:S(2)}, u32[]{:S(2)}) %collective-permute-start.4) | collective-permute-done | bytes 65568 | tf_op jit(solution)/shard_map/ppermute | solution.py:389
  30.0 2.0 collective-permute-start.16
  32.1 3.3 %collective-permute-done.6 = bf16[256,128]{1,0:T(8,128)(2,1)S(1)} collective-permute-done((bf16[256,128]{1,0:T(8,128)(2,1)S(1)}, bf16[256,128]{1,0:T(8,128)(2,1)S(1)}, u32[]{:S(2)}, u32[]{:S(2)}) %collective-permute-start.6) | collective-permute-done | bytes 65568 | tf_op jit(solution)/shard_map/ppermute | solution.py:389
  35.5 3.2 %collective-permute-start.7 = (bf16[2048,128]{1,0:T(8,128)(2,1)S(1)}, bf16[2048,128]{1,0:T(8,128)(2,1)S(1)}, u32[]{:S(2)}, u32[]{:S(2)}) collective-permute-start(bf16[2048,128]{1,0:T(8,128)(2,1)S(1)} %constant_dynamic-update-slice_fusion.refs_0_), channel_id=1, source_target_pairs={{0,192},{8,200},{16,208},{24,216},{32,224},{40,232},{48,240},{56,2... | collective-permute-start | bytes 1572872 | tf_op jit(solution)/shard_map/ppermute | solution.py:384
  38.8 3.5 %collective-permute-start.17 = (bf16[1024,128]{1,0:T(8,128)(2,1)S(1)}, bf16[1024,128]{1,0:T(8,128)(2,1)S(1)}, u32[]{:S(2)}, u32[]{:S(2)}) collective-permute-start(bf16[1024,128]{1,0:T(8,128)(2,1)S(1)} %collective-permute-done.15.refs_7_), channel_id=1, source_target_pairs={{0,56},{8,0},{16,8},{24,16},{32,24},{40,32},{48,40},{56,48},{64,12... | collective-permute-start | bytes 786440 | tf_op jit(solution)/shard_map/ppermute | solution.py:389
  42.5 4.4 %collective-permute-done.17.refs_9_ = bf16[1024,128]{1,0:T(8,128)(2,1)S(1)} collective-permute-done((bf16[1024,128]{1,0:T(8,128)(2,1)S(1)}, bf16[1024,128]{1,0:T(8,128)(2,1)S(1)}, u32[]{:S(2)}, u32[]{:S(2)}) %collective-permute-start.17) | collective-permute-done | bytes 262176 | tf_op jit(solution)/shard_map/ppermute | solution.py:389
  46.9 2.5 %collective-permute-start.19 = (bf16[1024,128]{1,0:T(8,128)(2,1)S(1)}, bf16[1024,128]{1,0:T(8,128)(2,1)S(1)}, u32[]{:S(2)}, u32[]{:S(2)}) collective-permute-start(bf16[1024,128]{1,0:T(8,128)(2,1)S(1)} %collective-permute-done.17.refs_9_), channel_id=1, source_target_pairs={{0,56},{8,0},{16,8},{24,16},{32,24},{40,32},{48,40},{56,48},{64,12... | collective-permute-start | bytes 786440 | tf_op jit(solution)/shard_map/ppermute | solution.py:389
  50.8 3.2 %collective-permute-start.9 = (bf16[1024,128]{1,0:T(8,128)(2,1)}, bf16[1024,128]{1,0:T(8,128)(2,1)}, u32[]{:S(2)}, u32[]{:S(2)}) collective-permute-start(bf16[1024,128]{1,0:T(8,128)(2,1)} %slice.58), channel_id=1, source_target_pairs={{0,192},{8,200},{16,208},{24,216},{32,224},{40,232},{48,240},{56,2... | collective-permute-start | bytes 786440 | tf_op jit(solution)/shard_map/ppermute | solution.py:384
  54.4 3.7 %collective-permute-done.10.refs_4_ = bf16[1024,128]{1,0:T(8,128)(2,1)} collective-permute-done((bf16[1024,128]{1,0:T(8,128)(2,1)}, bf16[1024,128]{1,0:T(8,128)(2,1)}, u32[]{:S(2)}, u32[]{:S(2)}) %collective-permute-start.10) | collective-permute-done | bytes 262176 | tf_op jit(solution)/shard_map/ppermute | solution.py:384
  58.3 2.7 %collective-permute-done.20.refs_12_ = bf16[1024,128]{1,0:T(8,128)(2,1)} collective-permute-done((bf16[1024,128]{1,0:T(8,128)(2,1)S(1)}, bf16[1024,128]{1,0:T(8,128)(2,1)}, u32[]{:S(2)}, u32[]{:S(2)}) %collective-permute-start.20) | collective-permute-done | bytes 262176 | tf_op jit(solution)/shard_map/ppermute | solution.py:389
  61.0 2.2 copy-done
  63.2 7.8 %project.1 = (bf16[32,128,256]{2,1,0:T(8,128)(2,1)}, f32[256,128]{1,0:T(8,128)}) custom-call(s32[5,32]{1,0:T(8,128)S(1)} %stack.41.table_ref, bf16[256,8192]{1,0:T(8,128)(2,1)S(1)} %bitcast.22, bf16[2048,128]{1,0:T(8,128)(2,1)S(1)} %constant_dynamic-update-slice_fusion.refs_0_, bf16[2048,128]{1,0:T(8,128)(2,1)S(1)} %collective-permute-done.7.refs_1_, ...), custom_call_target="tpu_custom_call" | custom-call | flops 1073741824 | bytes 10485760 | tf_op jit(solution)/shard_map/project/pallas_call | solution.py:97
  71.0 8.3 %all-to-all-start = ((bf16[32,128,256]{2,1,0:T(8,128)(2,1)}), bf16[32,128,256]{2,1,0:T(8,128)(2,1)}, u32[]{:S(2)}, u32[]{:S(2)}) async-start(bf16[32,128,256]{2,1,0:T(8,128)(2,1)} %get-tuple-element.28), calls=%async_computation | async-start | bytes 4194304 | tf_op jit(solution)/shard_map/all_to_all | solution.py:452
  79.5 2.7 %dynamic-slice_bitcast_fusion = (bf16[128,2048]{1,0:T(8,128)(2,1)}, bf16[128,2048]{1,0:T(8,128)(2,1)}, bf16[128,2048]{1,0:T(8,128)(2,1)S(1)}, bf16[128,2048]{1,0:T(8,128)(2,1)}) fusion(bf16[2,128,8192]{2,1,0:T(8,128)(2,1)} %param.10, s32[]{:T(128)S(6)} %select_n.86, s32[]{:T(128)S(6)} %select_n.94, s32[]{:T(128)S(6)} %select_n.92, s32[]{:T(128)S(6)} %select_n.90, ...), kind=kLoop, calls=%fused_computation.5 | loop fusion | bytes 4194324 | tf_op jit(solution)/shard_map/squeeze | solution.py:458
  82.2 2.7 %collective-permute-start.23 = (bf16[128,2048]{1,0:T(8,128)(2,1)}, bf16[128,2048]{1,0:T(8,128)(2,1)S(1)}, u32[]{:S(2)}, u32[]{:S(2)}) collective-permute-start(bf16[128,2048]{1,0:T(8,128)(2,1)} %get-tuple-element.58), channel_id=1, source_target_pairs={{0,192},{8,200},{16,208},{24,216},{32,224},{40,232},{48,240},{56,2... | collective-permute-start | bytes 1572872 | tf_op jit(solution)/shard_map/ppermute | solution.py:384
  86.6 33.3 %all-to-all-done.kv_ref = bf16[32,128,256]{2,1,0:T(8,128)(2,1)} async-done(((bf16[32,128,256]{2,1,0:T(8,128)(2,1)}), bf16[32,128,256]{2,1,0:T(8,128)(2,1)}, u32[]{:S(2)}, u32[]{:S(2)}) %all-to-all-start) | async-done | bytes 2097184 | tf_op jit(solution)/shard_map/all_to_all | solution.py:452
  119.9 9.0 %attend.1 = (bf16[32,128,256]{2,1,0:T(8,128)(2,1)}, bf16[32,128,128]{2,1,0:T(8,128)(2,1)}, bf16[32,128,128]{2,1,0:T(8,128)(2,1)}) custom-call(s32[5,32]{1,0:T(8,128)S(1)} %stack.41.table_ref, bf16[512,1024]{1,0:T(8,128)(2,1)} %q_ref.1, bf16[512,1024]{1,0:T(8,128)(2,1)} %ct_ref.1, bf16[32,128,256]{2,1,0:T(8,128)(2,1)} %all-to-all-done.kv_ref), custom_call_target="tpu_custom_call" | custom-call | flops 536870912 | bytes 8388608 | tf_op jit(solution)/shard_map/attend/pallas_call | solution.py:195
  130.0 5.8 %all-to-all-start.1 = ((bf16[32,128,256]{2,1,0:T(8,128)(2,1)}), bf16[32,128,256]{2,1,0:T(8,128)(2,1)}, u32[]{:S(2)}, u32[]{:S(2)}) async-start(bf16[32,128,256]{2,1,0:T(8,128)(2,1)} %get-tuple-element.32), calls=%async_computation.1 | async-start | bytes 4194304 | tf_op jit(solution)/shard_map/all_to_all | solution.py:468
  136.9 1.0 copy-done.19
  137.9 1.0 copy-done.21
  139.0 1.0 copy-done.23
  140.7 6.2 %apply.1 = (bf16[512,1024]{1,0:T(8,128)(2,1)}, bf16[512,1024]{1,0:T(8,128)(2,1)}) custom-call(s32[5,32]{1,0:T(8,128)S(1)} %stack.41.table_ref, bf16[32,128,256]{2,1,0:T(8,128)(2,1)} %all-to-all-done.kv_ref, bf16[32,128,128]{2,1,0:T(8,128)(2,1)} %get-tuple-element.37.probs_ref, bf16[32,128,128]{2,1,0:T(8,128)(2,1)} %get-tuple-element.38.ds_ref), custom_call_target="tpu_custom_call" | custom-call | flops 268435456 | bytes 6291456 | tf_op jit(solution)/shard_map/apply/pallas_call | solution.py:234
  146.9 1.4 copy-done.3
  148.2 29.1 %all-to-all-done.1.part_ref = bf16[32,128,256]{2,1,0:T(8,128)(2,1)} async-done(((bf16[32,128,256]{2,1,0:T(8,128)(2,1)}), bf16[32,128,256]{2,1,0:T(8,128)(2,1)}, u32[]{:S(2)}, u32[]{:S(2)}) %all-to-all-start.1) | async-done | bytes 2097184 | tf_op jit(solution)/shard_map/all_to_all | solution.py:468
  177.3 3.0 %owner_grads.1 = (bf16[256,256]{1,0:T(8,128)(2,1)S(1)}, bf16[256,256]{1,0:T(8,128)(2,1)S(1)}) custom-call(s32[5,32]{1,0:T(8,128)S(1)} %stack.41.table_ref, bf16[32,128,256]{2,1,0:T(8,128)(2,1)} %all-to-all-done.1.part_ref, f32[256,128]{1,0:T(8,128)} %get-tuple-element.30.raw_ref, f32[1,128]{1,0:T(1,128)S(1)} %bitcast.24), custom_call_target="tpu_custom_call" | custom-call | bytes 3145728 | tf_op jit(solution)/shard_map/owner_grads/pallas_call | solution.py:280
  180.5 1.6 collective-permute-start.27
  182.0 1.7 collective-permute-start.26
  184.2 1.5 collective-permute-done.27.refs_3_
  185.7 2.8 %collective-permute-done.26.refs_2_ = bf16[256,256]{1,0:T(8,128)(2,1)S(1)} collective-permute-done((bf16[256,256]{1,0:T(8,128)(2,1)S(1)}, bf16[256,256]{1,0:T(8,128)(2,1)S(1)}, u32[]{:S(2)}, u32[]{:S(2)}) %collective-permute-start.26) | collective-permute-done | bytes 131104 | tf_op jit(solution)/shard_map/ppermute | solution.py:384
  188.5 1.4 collective-permute-done.25.refs_1_
  189.9 2.3 weight_terms.1
  192.2 4.5 %feature_terms.1 = (bf16[128,8192]{1,0:T(8,128)(2,1)S(1)}, bf16[128,8192]{1,0:T(8,128)(2,1)}) custom-call(s32[5,32]{1,0:T(8,128)S(1)} %stack.41.table_ref, bf16[256,256]{1,0:T(8,128)(2,1)S(1)} %get-tuple-element.47.grad_ref, bf16[2048,128]{1,0:T(8,128)(2,1)S(1)} %copy-done.2, bf16[2048,128]{1,0:T(8,128)(2,1)S(1)} %collective-permute-done.7.refs_1_, ...), custom_call_target="tpu_custom_call" | custom-call | flops 1073741824 | bytes 8388608 | tf_op jit(solution)/shard_map/feature_terms/pallas_call | solution.py:364
  196.7 4.3 %all-to-all-start.2 = ((bf16[8,256,256]{2,1,0:T(8,128)(2,1)}), bf16[8,256,256]{2,1,0:T(8,128)(2,1)S(1)}, u32[]{:S(2)}, u32[]{:S(2)}) async-start(bf16[8,256,256]{2,1,0:T(8,128)(2,1)} %weight_terms.1), calls=%async_computation.2 | async-start | bytes 2097152 | tf_op jit(solution)/shard_map/all_to_all | solution.py:480
  201.2 2.7 %add_convert_fusion.3 = (bf16[32,8192]{1,0:T(8,128)(2,1)}, bf16[32,8192]{1,0:T(8,128)(2,1)}, bf16[32,8192]{1,0:T(8,128)(2,1)}) fusion(bf16[128,8192]{1,0:T(8,128)(2,1)} %collective-permute-done.28, bf16[128,8192]{1,0:T(8,128)(2,1)S(1)} %get-tuple-element.48), kind=kLoop, calls=%fused_computation.4 | loop fusion | flops 3145728 | bytes 4718592 | tf_op jit(solution)/shard_map/convert_element_type | solution.py:493
  203.9 1.5 collective-permute-start.29
  205.4 1.7 collective-permute-start.31
  207.1 1.8 collective-permute-start.30
  209.0 20.0 %all-to-all-done.2 = bf16[8,256,256]{2,1,0:T(8,128)(2,1)S(1)} async-done(((bf16[8,256,256]{2,1,0:T(8,128)(2,1)}), bf16[8,256,256]{2,1,0:T(8,128)(2,1)S(1)}, u32[]{:S(2)}, u32[]{:S(2)}) %all-to-all-start.2) | async-done | bytes 1048608 | tf_op jit(solution)/shard_map/all_to_all | solution.py:480
  229.9 1.7 collective-permute-done.30
  231.6 2.6 %add_convert_fusion = bf16[32,8192]{1,0:T(8,128)(2,1)} fusion(bf16[32,8192]{1,0:T(8,128)(2,1)} %collective-permute-done.31, bf16[32,8192]{1,0:T(8,128)(2,1)} %collective-permute-done.30, bf16[32,8192]{1,0:T(8,128)(2,1)} %collective-permute-done.29, bf16[128,8192]{1,0:T(8,128)(2,1)} %collective-permute-done.28, bf16[128,8192]{1,0:T(8,128)(2,1)S(1)} %get-tuple-element.48), kind=kLoop, calls=%fused_computation.1 | loop fusion | flops 2621440 | bytes 3145728 | tf_op jit(solution)/shard_map/convert_element_type | solution.py:497
  (109 shorter events, 14.0 us)
Async XLA Ops:
  0.6 60.3 %copy-start.24 = (f32[128]{0:T(128)S(1)}, f32[128]{0:T(128)}, u32[]{:S(2)}) copy-start(f32[128]{0:T(128)} %param.13) | copy-start | bytes 1540
  0.6 16.2 %collective-permute-start = (bf16[256,128]{1,0:T(8,128)(2,1)}, bf16[256,128]{1,0:T(8,128)(2,1)S(1)}, u32[]{:S(2)}, u32[]{:S(2)}) collective-permute-start(bf16[256,128]{1,0:T(8,128)(2,1)} %param.11), channel_id=1, source_target_pairs={{0,8},{8,16},{16,24},{24,32},{32,40},{40,48},{48,56},{56,0},{64,72... | collective-permute-start | bytes 196616 | tf_op jit(solution)/shard_map/ppermute | solution.py:389
  2.6 15.2 %collective-permute-start.1 = (bf16[256,128]{1,0:T(8,128)(2,1)}, bf16[256,128]{1,0:T(8,128)(2,1)S(1)}, u32[]{:S(2)}, u32[]{:S(2)}) collective-permute-start(bf16[256,128]{1,0:T(8,128)(2,1)} %param.11), channel_id=1, source_target_pairs={{0,56},{8,0},{16,8},{24,16},{32,24},{40,32},{48,40},{56,48},{64,12... | collective-permute-start | bytes 196616 | tf_op jit(solution)/shard_map/ppermute | solution.py:389
  2.7 7.9 %collective-permute-start.12 = (bf16[256,128]{1,0:T(8,128)(2,1)}, bf16[256,128]{1,0:T(8,128)(2,1)S(1)}, u32[]{:S(2)}, u32[]{:S(2)}) collective-permute-start(bf16[256,128]{1,0:T(8,128)(2,1)} %param.12), channel_id=1, source_target_pairs={{0,128},{8,136},{16,144},{24,152},{32,160},{40,168},{48,176},{56,1... | collective-permute-start | bytes 196616 | tf_op jit(solution)/shard_map/ppermute | solution.py:384
  5.9 4.6 %collective-permute-start.11 = (bf16[256,128]{1,0:T(8,128)(2,1)}, bf16[256,128]{1,0:T(8,128)(2,1)S(1)}, u32[]{:S(2)}, u32[]{:S(2)}) collective-permute-start(bf16[256,128]{1,0:T(8,128)(2,1)} %param.12), channel_id=1, source_target_pairs={{0,192},{8,200},{16,208},{24,216},{32,224},{40,232},{48,240},{56,2... | collective-permute-start | bytes 196616 | tf_op jit(solution)/shard_map/ppermute | solution.py:384
  7.0 5.7 %collective-permute-start.13 = (bf16[256,128]{1,0:T(8,128)(2,1)}, bf16[256,128]{1,0:T(8,128)(2,1)S(1)}, u32[]{:S(2)}, u32[]{:S(2)}) collective-permute-start(bf16[256,128]{1,0:T(8,128)(2,1)} %param.12), channel_id=1, source_target_pairs={{0,64},{8,72},{16,80},{24,88},{32,96},{40,104},{48,112},{56,120},{... | collective-permute-start | bytes 196616 | tf_op jit(solution)/shard_map/ppermute | solution.py:384
  12.7 26.1 %collective-permute-start.15 = (bf16[1024,128]{1,0:T(8,128)(2,1)S(1)}, bf16[1024,128]{1,0:T(8,128)(2,1)S(1)}, u32[]{:S(2)}, u32[]{:S(2)}) collective-permute-start(bf16[1024,128]{1,0:T(8,128)(2,1)S(1)} %constant_dynamic-update-slice_fusion.8.refs_5_), channel_id=1, source_target_pairs={{0,56},{8,0},{16,8},{24,16},{32,24},{40,32},{48,40},{56,48},{64,12... | collective-permute-start | bytes 786440 | tf_op jit(solution)/shard_map/ppermute | solution.py:389
  16.8 13.2 %collective-permute-start.14 = (bf16[1024,128]{1,0:T(8,128)(2,1)S(1)}, bf16[1024,128]{1,0:T(8,128)(2,1)S(1)}, u32[]{:S(2)}, u32[]{:S(2)}) collective-permute-start(bf16[1024,128]{1,0:T(8,128)(2,1)S(1)} %constant_dynamic-update-slice_fusion.8.refs_5_), channel_id=1, source_target_pairs={{0,8},{8,16},{16,24},{24,32},{32,40},{40,48},{48,56},{56,0},{64,72... | collective-permute-start | bytes 786440 | tf_op jit(solution)/shard_map/ppermute | solution.py:389
  16.8 7.2 %collective-permute-start.2 = (bf16[256,128]{1,0:T(8,128)(2,1)S(1)}, bf16[256,128]{1,0:T(8,128)(2,1)S(1)}, u32[]{:S(2)}, u32[]{:S(2)}) collective-permute-start(bf16[256,128]{1,0:T(8,128)(2,1)S(1)} %collective-permute-done), channel_id=1, source_target_pairs={{0,8},{8,16},{16,24},{24,32},{32,40},{40,48},{48,56},{56,0},{64,72... | collective-permute-start | bytes 196616 | tf_op jit(solution)/shard_map/ppermute | solution.py:389
  17.8 6.9 %collective-permute-start.3 = (bf16[256,128]{1,0:T(8,128)(2,1)S(1)}, bf16[256,128]{1,0:T(8,128)(2,1)S(1)}, u32[]{:S(2)}, u32[]{:S(2)}) collective-permute-start(bf16[256,128]{1,0:T(8,128)(2,1)S(1)} %collective-permute-done.1), channel_id=1, source_target_pairs={{0,56},{8,0},{16,8},{24,16},{32,24},{40,32},{48,40},{56,48},{64,12... | collective-permute-start | bytes 196616 | tf_op jit(solution)/shard_map/ppermute | solution.py:389
  24.0 6.0 %collective-permute-start.4 = (bf16[256,128]{1,0:T(8,128)(2,1)S(1)}, bf16[256,128]{1,0:T(8,128)(2,1)S(1)}, u32[]{:S(2)}, u32[]{:S(2)}) collective-permute-start(bf16[256,128]{1,0:T(8,128)(2,1)S(1)} %collective-permute-done.2), channel_id=1, source_target_pairs={{0,8},{8,16},{16,24},{24,32},{32,40},{40,48},{48,56},{56,0},{64,72... | collective-permute-start | bytes 196616 | tf_op jit(solution)/shard_map/ppermute | solution.py:389
  24.7 5.3 %collective-permute-start.5 = (bf16[256,128]{1,0:T(8,128)(2,1)S(1)}, bf16[256,128]{1,0:T(8,128)(2,1)S(1)}, u32[]{:S(2)}, u32[]{:S(2)}) collective-permute-start(bf16[256,128]{1,0:T(8,128)(2,1)S(1)} %collective-permute-done.3), channel_id=1, source_target_pairs={{0,56},{8,0},{16,8},{24,16},{32,24},{40,32},{48,40},{56,48},{64,12... | collective-permute-start | bytes 196616 | tf_op jit(solution)/shard_map/ppermute | solution.py:389
  30.0 5.4 %collective-permute-start.6 = (bf16[256,128]{1,0:T(8,128)(2,1)S(1)}, bf16[256,128]{1,0:T(8,128)(2,1)S(1)}, u32[]{:S(2)}, u32[]{:S(2)}) collective-permute-start(bf16[256,128]{1,0:T(8,128)(2,1)S(1)} %collective-permute-done.4), channel_id=1, source_target_pairs={{0,8},{8,16},{16,24},{24,32},{32,40},{40,48},{48,56},{56,0},{64,72... | collective-permute-start | bytes 196616 | tf_op jit(solution)/shard_map/ppermute | solution.py:389
  30.0 41.0 %copy-start.8 = (bf16[1024,128]{1,0:T(8,128)(2,1)}, bf16[1024,128]{1,0:T(8,128)(2,1)S(1)}, u32[]{:S(2)}) copy-start(bf16[1024,128]{1,0:T(8,128)(2,1)S(1)} %collective-permute-done.14.refs_6_) | copy-start | bytes 786436
  30.0 12.3 %collective-permute-start.16 = (bf16[1024,128]{1,0:T(8,128)(2,1)S(1)}, bf16[1024,128]{1,0:T(8,128)(2,1)S(1)}, u32[]{:S(2)}, u32[]{:S(2)}) collective-permute-start(bf16[1024,128]{1,0:T(8,128)(2,1)S(1)} %collective-permute-done.14.refs_6_), channel_id=1, source_target_pairs={{0,8},{8,16},{16,24},{24,32},{32,40},{40,48},{48,56},{56,0},{64,72... | collective-permute-start | bytes 786440 | tf_op jit(solution)/shard_map/ppermute | solution.py:389
  35.4 35.6 %copy-start.1 = (bf16[2048,128]{1,0:T(8,128)(2,1)}, bf16[2048,128]{1,0:T(8,128)(2,1)S(1)}, u32[]{:S(2)}) copy-start(bf16[2048,128]{1,0:T(8,128)(2,1)S(1)} %constant_dynamic-update-slice_fusion.refs_0_) | copy-start | bytes 1572868
  35.4 14.0 %collective-permute-start.8 = (bf16[2048,128]{1,0:T(8,128)(2,1)S(1)}, bf16[2048,128]{1,0:T(8,128)(2,1)S(1)}, u32[]{:S(2)}, u32[]{:S(2)}) collective-permute-start(bf16[2048,128]{1,0:T(8,128)(2,1)S(1)} %constant_dynamic-update-slice_fusion.refs_0_), channel_id=1, source_target_pairs={{0,64},{8,72},{16,80},{24,88},{32,96},{40,104},{48,112},{56,120},{... | collective-permute-start | bytes 1572872 | tf_op jit(solution)/shard_map/ppermute | solution.py:384
  35.5 14.6 %collective-permute-start.7 = (bf16[2048,128]{1,0:T(8,128)(2,1)S(1)}, bf16[2048,128]{1,0:T(8,128)(2,1)S(1)}, u32[]{:S(2)}, u32[]{:S(2)}) collective-permute-start(bf16[2048,128]{1,0:T(8,128)(2,1)S(1)} %constant_dynamic-update-slice_fusion.refs_0_), channel_id=1, source_target_pairs={{0,192},{8,200},{16,208},{24,216},{32,224},{40,232},{48,240},{56,2... | collective-permute-start | bytes 1572872 | tf_op jit(solution)/shard_map/ppermute | solution.py:384
  38.8 32.2 %copy-start.6 = (bf16[1024,128]{1,0:T(8,128)(2,1)}, bf16[1024,128]{1,0:T(8,128)(2,1)S(1)}, u32[]{:S(2)}) copy-start(bf16[1024,128]{1,0:T(8,128)(2,1)S(1)} %collective-permute-done.15.refs_7_) | copy-start | bytes 786436
  38.8 8.1 %collective-permute-start.17 = (bf16[1024,128]{1,0:T(8,128)(2,1)S(1)}, bf16[1024,128]{1,0:T(8,128)(2,1)S(1)}, u32[]{:S(2)}, u32[]{:S(2)}) collective-permute-start(bf16[1024,128]{1,0:T(8,128)(2,1)S(1)} %collective-permute-done.15.refs_7_), channel_id=1, source_target_pairs={{0,56},{8,0},{16,8},{24,16},{32,24},{40,32},{48,40},{56,48},{64,12... | collective-permute-start | bytes 786440 | tf_op jit(solution)/shard_map/ppermute | solution.py:389
  42.3 28.7 %copy-start.10 = (bf16[1024,128]{1,0:T(8,128)(2,1)}, bf16[1024,128]{1,0:T(8,128)(2,1)S(1)}, u32[]{:S(2)}) copy-start(bf16[1024,128]{1,0:T(8,128)(2,1)S(1)} %collective-permute-done.16.refs_8_) | copy-start | bytes 786436
  42.3 11.8 %collective-permute-start.18 = (bf16[1024,128]{1,0:T(8,128)(2,1)S(1)}, bf16[1024,128]{1,0:T(8,128)(2,1)S(1)}, u32[]{:S(2)}, u32[]{:S(2)}) collective-permute-start(bf16[1024,128]{1,0:T(8,128)(2,1)S(1)} %collective-permute-done.16.refs_8_), channel_id=1, source_target_pairs={{0,8},{8,16},{16,24},{24,32},{32,40},{40,48},{48,56},{56,0},{64,72... | collective-permute-start | bytes 786440 | tf_op jit(solution)/shard_map/ppermute | solution.py:389
  46.9 24.1 %copy-start.12 = (bf16[1024,128]{1,0:T(8,128)(2,1)}, bf16[1024,128]{1,0:T(8,128)(2,1)S(1)}, u32[]{:S(2)}) copy-start(bf16[1024,128]{1,0:T(8,128)(2,1)S(1)} %collective-permute-done.17.refs_9_) | copy-start | bytes 786436
  46.9 7.4 %collective-permute-start.19 = (bf16[1024,128]{1,0:T(8,128)(2,1)S(1)}, bf16[1024,128]{1,0:T(8,128)(2,1)S(1)}, u32[]{:S(2)}, u32[]{:S(2)}) collective-permute-start(bf16[1024,128]{1,0:T(8,128)(2,1)S(1)} %collective-permute-done.17.refs_9_), channel_id=1, source_target_pairs={{0,56},{8,0},{16,8},{24,16},{32,24},{40,32},{48,40},{56,48},{64,12... | collective-permute-start | bytes 786440 | tf_op jit(solution)/shard_map/ppermute | solution.py:389
  50.1 7.9 %collective-permute-start.10 = (bf16[1024,128]{1,0:T(8,128)(2,1)}, bf16[1024,128]{1,0:T(8,128)(2,1)}, u32[]{:S(2)}, u32[]{:S(2)}) collective-permute-start(bf16[1024,128]{1,0:T(8,128)(2,1)} %slice.59), channel_id=1, source_target_pairs={{0,64},{8,72},{16,80},{24,88},{32,96},{40,104},{48,112},{56,120},{... | collective-permute-start | bytes 786440 | tf_op jit(solution)/shard_map/ppermute | solution.py:384
  50.8 7.4 %collective-permute-start.9 = (bf16[1024,128]{1,0:T(8,128)(2,1)}, bf16[1024,128]{1,0:T(8,128)(2,1)}, u32[]{:S(2)}, u32[]{:S(2)}) collective-permute-start(bf16[1024,128]{1,0:T(8,128)(2,1)} %slice.58), channel_id=1, source_target_pairs={{0,192},{8,200},{16,208},{24,216},{32,224},{40,232},{48,240},{56,2... | collective-permute-start | bytes 786440 | tf_op jit(solution)/shard_map/ppermute | solution.py:384
  54.1 17.0 %copy-start.14 = (bf16[1024,128]{1,0:T(8,128)(2,1)}, bf16[1024,128]{1,0:T(8,128)(2,1)S(1)}, u32[]{:S(2)}) copy-start(bf16[1024,128]{1,0:T(8,128)(2,1)S(1)} %collective-permute-done.18.refs_10_) | copy-start | bytes 786436
  54.1 6.9 %collective-permute-start.20 = (bf16[1024,128]{1,0:T(8,128)(2,1)S(1)}, bf16[1024,128]{1,0:T(8,128)(2,1)}, u32[]{:S(2)}, u32[]{:S(2)}) collective-permute-start(bf16[1024,128]{1,0:T(8,128)(2,1)S(1)} %collective-permute-done.18.refs_10_), channel_id=1, source_target_pairs={{0,8},{8,16},{16,24},{24,32},{32,40},{40,48},{48,56},{56,0},{64,72... | collective-permute-start | bytes 786440 | tf_op jit(solution)/shard_map/ppermute | solution.py:389
  54.3 16.7 %copy-start.16 = (bf16[1024,128]{1,0:T(8,128)(2,1)}, bf16[1024,128]{1,0:T(8,128)(2,1)S(1)}, u32[]{:S(2)}) copy-start(bf16[1024,128]{1,0:T(8,128)(2,1)S(1)} %collective-permute-done.19.refs_11_) | copy-start | bytes 786436
  71.0 48.8 %all-to-all-start = ((bf16[32,128,256]{2,1,0:T(8,128)(2,1)}), bf16[32,128,256]{2,1,0:T(8,128)(2,1)}, u32[]{:S(2)}, u32[]{:S(2)}) async-start(bf16[32,128,256]{2,1,0:T(8,128)(2,1)} %get-tuple-element.28), calls=%async_computation | async-start | bytes 4194304 | tf_op jit(solution)/shard_map/all_to_all | solution.py:452
  82.2 46.6 %collective-permute-start.23 = (bf16[128,2048]{1,0:T(8,128)(2,1)}, bf16[128,2048]{1,0:T(8,128)(2,1)S(1)}, u32[]{:S(2)}, u32[]{:S(2)}) collective-permute-start(bf16[128,2048]{1,0:T(8,128)(2,1)} %get-tuple-element.58), channel_id=1, source_target_pairs={{0,192},{8,200},{16,208},{24,216},{32,224},{40,232},{48,240},{56,2... | collective-permute-start | bytes 1572872 | tf_op jit(solution)/shard_map/ppermute | solution.py:384
  84.9 43.9 %collective-permute-start.22 = (bf16[128,2048]{1,0:T(8,128)(2,1)}, bf16[128,2048]{1,0:T(8,128)(2,1)S(1)}, u32[]{:S(2)}, u32[]{:S(2)}) collective-permute-start(bf16[128,2048]{1,0:T(8,128)(2,1)} %get-tuple-element.59), channel_id=1, source_target_pairs={{0,128},{8,136},{16,144},{24,152},{32,160},{40,168},{48,176},{56,1... | collective-permute-start | bytes 1572872 | tf_op jit(solution)/shard_map/ppermute | solution.py:384
  85.7 43.1 %collective-permute-start.21 = (bf16[128,2048]{1,0:T(8,128)(2,1)S(1)}, bf16[128,2048]{1,0:T(8,128)(2,1)S(1)}, u32[]{:S(2)}, u32[]{:S(2)}) collective-permute-start(bf16[128,2048]{1,0:T(8,128)(2,1)S(1)} %get-tuple-element.60), channel_id=1, source_target_pairs={{0,64},{8,72},{16,80},{24,88},{32,96},{40,104},{48,112},{56,120},{... | collective-permute-start | bytes 1572872 | tf_op jit(solution)/shard_map/ppermute | solution.py:384
  130.0 47.4 %all-to-all-start.1 = ((bf16[32,128,256]{2,1,0:T(8,128)(2,1)}), bf16[32,128,256]{2,1,0:T(8,128)(2,1)}, u32[]{:S(2)}, u32[]{:S(2)}) async-start(bf16[32,128,256]{2,1,0:T(8,128)(2,1)} %get-tuple-element.32), calls=%async_computation.1 | async-start | bytes 4194304 | tf_op jit(solution)/shard_map/all_to_all | solution.py:468
  140.6 6.3 %collective-permute-start.24 = (bf16[2048,512]{1,0:T(8,128)(2,1)S(1)}, bf16[2048,512]{1,0:T(8,128)(2,1)S(1)}, u32[]{:S(2)}, u32[]{:S(2)}) collective-permute-start(bf16[2048,512]{1,0:T(8,128)(2,1)S(1)} %transpose_pieces.1.own_ref), channel_id=1, source_target_pairs={{0,1},{1,0},{2,3},{3,2},{4,5},{5,4},{6,7},{7,6},{8,9},{9,8},{10,11... | collective-permute-start | bytes 6291464 | tf_op jit(solution)/shard_map/ppermute | solution.py:405
  177.3 12.6 %copy-start.4 = (bf16[2048,512]{1,0:T(8,128)(2,1)S(1)}, bf16[2048,512]{1,0:T(8,128)(2,1)}, u32[]{:S(2)}) copy-start(bf16[2048,512]{1,0:T(8,128)(2,1)} %copy-done.3) | copy-start | bytes 6291460
  180.4 11.8 %copy-start.2 = (bf16[2048,128]{1,0:T(8,128)(2,1)S(1)}, bf16[2048,128]{1,0:T(8,128)(2,1)}, u32[]{:S(2)}) copy-start(bf16[2048,128]{1,0:T(8,128)(2,1)} %copy-done.1) | copy-start | bytes 1572868
  180.4 11.8 %copy-start.7 = (bf16[1024,128]{1,0:T(8,128)(2,1)S(1)}, bf16[1024,128]{1,0:T(8,128)(2,1)}, u32[]{:S(2)}) copy-start(bf16[1024,128]{1,0:T(8,128)(2,1)} %copy-done.6) | copy-start | bytes 786436
  180.4 11.8 %copy-start.9 = (bf16[1024,128]{1,0:T(8,128)(2,1)S(1)}, bf16[1024,128]{1,0:T(8,128)(2,1)}, u32[]{:S(2)}) copy-start(bf16[1024,128]{1,0:T(8,128)(2,1)} %copy-done.8) | copy-start | bytes 786436
  180.4 11.8 %copy-start.11 = (bf16[1024,128]{1,0:T(8,128)(2,1)S(1)}, bf16[1024,128]{1,0:T(8,128)(2,1)}, u32[]{:S(2)}) copy-start(bf16[1024,128]{1,0:T(8,128)(2,1)} %copy-done.10) | copy-start | bytes 786436
  180.5 5.3 %collective-permute-start.27 = (bf16[256,256]{1,0:T(8,128)(2,1)S(1)}, bf16[256,256]{1,0:T(8,128)(2,1)S(1)}, u32[]{:S(2)}, u32[]{:S(2)}) collective-permute-start(bf16[256,256]{1,0:T(8,128)(2,1)S(1)} %get-tuple-element.45.refs_0_), channel_id=1, source_target_pairs={{0,192},{8,200},{16,208},{24,216},{32,224},{40,232},{48,240},{56,2... | collective-permute-start | bytes 393224 | tf_op jit(solution)/shard_map/ppermute | solution.py:384
  182.0 6.5 %collective-permute-start.26 = (bf16[256,256]{1,0:T(8,128)(2,1)S(1)}, bf16[256,256]{1,0:T(8,128)(2,1)S(1)}, u32[]{:S(2)}, u32[]{:S(2)}) collective-permute-start(bf16[256,256]{1,0:T(8,128)(2,1)S(1)} %get-tuple-element.45.refs_0_), channel_id=1, source_target_pairs={{0,128},{8,136},{16,144},{24,152},{32,160},{40,168},{48,176},{56,1... | collective-permute-start | bytes 393224 | tf_op jit(solution)/shard_map/ppermute | solution.py:384
  183.7 6.2 %collective-permute-start.25 = (bf16[256,256]{1,0:T(8,128)(2,1)S(1)}, bf16[256,256]{1,0:T(8,128)(2,1)S(1)}, u32[]{:S(2)}, u32[]{:S(2)}) collective-permute-start(bf16[256,256]{1,0:T(8,128)(2,1)S(1)} %get-tuple-element.45.refs_0_), channel_id=1, source_target_pairs={{0,64},{8,72},{16,80},{24,88},{32,96},{40,104},{48,112},{56,120},{... | collective-permute-start | bytes 393224 | tf_op jit(solution)/shard_map/ppermute | solution.py:384
  196.7 4.5 %collective-permute-start.28 = (bf16[128,8192]{1,0:T(8,128)(2,1)}, bf16[128,8192]{1,0:T(8,128)(2,1)}, u32[]{:S(2)}, u32[]{:S(2)}) collective-permute-start(bf16[128,8192]{1,0:T(8,128)(2,1)} %get-tuple-element.49), channel_id=1, source_target_pairs={{0,1},{1,0},{2,3},{3,2},{4,5},{5,4},{6,7},{7,6},{8,9},{9,8},{10,11... | collective-permute-start | bytes 6291464 | tf_op jit(solution)/shard_map/ppermute | solution.py:405
  196.7 32.3 %all-to-all-start.2 = ((bf16[8,256,256]{2,1,0:T(8,128)(2,1)}), bf16[8,256,256]{2,1,0:T(8,128)(2,1)S(1)}, u32[]{:S(2)}, u32[]{:S(2)}) async-start(bf16[8,256,256]{2,1,0:T(8,128)(2,1)} %weight_terms.1), calls=%async_computation.2 | async-start | bytes 2097152 | tf_op jit(solution)/shard_map/all_to_all | solution.py:480
  203.9 25.9 %collective-permute-start.29 = (bf16[32,8192]{1,0:T(8,128)(2,1)}, bf16[32,8192]{1,0:T(8,128)(2,1)}, u32[]{:S(2)}, u32[]{:S(2)}) collective-permute-start(bf16[32,8192]{1,0:T(8,128)(2,1)} %get-tuple-element.55), channel_id=1, source_target_pairs={{0,2},{1,3},{2,4},{3,5},{4,6},{5,7},{6,0},{7,1},{8,10},{9,11},{10,... | collective-permute-start | bytes 1572872 | tf_op jit(solution)/shard_map/ppermute | solution.py:492
  205.4 24.5 %collective-permute-start.31 = (bf16[32,8192]{1,0:T(8,128)(2,1)}, bf16[32,8192]{1,0:T(8,128)(2,1)}, u32[]{:S(2)}, u32[]{:S(2)}) collective-permute-start(bf16[32,8192]{1,0:T(8,128)(2,1)} %get-tuple-element.56), channel_id=1, source_target_pairs={{0,6},{1,7},{2,0},{3,1},{4,2},{5,3},{6,4},{7,5},{8,14},{9,15},{10,... | collective-permute-start | bytes 1572872 | tf_op jit(solution)/shard_map/ppermute | solution.py:492
  207.1 24.5 %collective-permute-start.30 = (bf16[32,8192]{1,0:T(8,128)(2,1)}, bf16[32,8192]{1,0:T(8,128)(2,1)}, u32[]{:S(2)}, u32[]{:S(2)}) collective-permute-start(bf16[32,8192]{1,0:T(8,128)(2,1)} %get-tuple-element.57), channel_id=1, source_target_pairs={{0,4},{1,5},{2,6},{3,7},{4,0},{5,1},{6,2},{7,3},{8,12},{9,13},{10,... | collective-permute-start | bytes 1572872 | tf_op jit(solution)/shard_map/ppermute | solution.py:492
  (12 other events, 45.9 us)

commit v6 on v5

--- a/solution.py
+++ b/solution.py
@@ -61,20 +61,12 @@
 
 
 def project_kernel(table_ref, f_ref, *refs, zones):
-    w_refs, (gain_ref, send_ref, raw_ref, kv, held, sems) = refs[: len(zones)], refs[len(zones) :]
+    w_refs, (gain_ref, send_ref, raw_ref, kv) = refs[: len(zones)], refs[len(zones) :]
     head_dim = gain_ref.shape[1]
     tokens = send_ref.shape[1]
-    blocks = weight_blocks(table_ref, w_refs, zones)
-    copies = [
-        pltpu.make_async_copy(f_ref.at[:, cols], held.at[i], sems.at[i])
-        for i, (cols, _) in enumerate(blocks)
-    ]
-    for copy in copies:
-        copy.start()
     total = jnp.zeros((f_ref.shape[0], 2 * head_dim), F32)
-    for i, (_, spot) in enumerate(blocks):
-        copies[i].wait()
-        total = total + jnp.dot(held[i], side_by_side(spot), preferred_element_type=F32)
+    for cols, spot in weight_blocks(table_ref, w_refs, zones):
+        total = total + jnp.dot(f_ref[:, cols], side_by_side(spot), preferred_element_type=F32)
     raw = total[:, :head_dim]
     raw_ref[...] = raw
     scale = lax.rsqrt(jnp.mean(raw * raw, axis=-1, keepdims=True) + EPS)
@@ -93,19 +85,14 @@
 
 def project(table, rows, pieces, zones, gain, dp, images, tokens):
     cols = 2 * gain.shape[1]
-    depth = rows.shape[1] // dp
     return pl.pallas_call(
         functools.partial(project_kernel, zones=zones),
         grid_spec=pltpu.PrefetchScalarGridSpec(
             num_scalar_prefetch=1,
             grid=(),
-            in_specs=[in_hbm()] + [in_vmem()] * (1 + len(pieces)),
+            in_specs=[in_vmem()] * (2 + len(pieces)),
             out_specs=[in_vmem()] * 2,
-            scratch_shapes=[
-                pltpu.VMEM((images, tokens, cols), BF16),
-                pltpu.VMEM((dp, rows.shape[0], depth), BF16),
-                pltpu.SemaphoreType.DMA((dp,)),
-            ],
+            scratch_shapes=[pltpu.VMEM((images, tokens, cols), BF16)],
         ),
         out_shape=[
             pltpu.HBM((dp, tokens, cols), BF16),
@@ -114,7 +101,7 @@
         compiler_params=limit(14),
         cost_estimate=cost(2 * rows.size * cols, 10),
         name="project",
-    )(table, rows, *pieces, gain)
+    )(table, *hold(rows), *pieces, gain)
 
 
 def load_heads(ref, start, rows, head_dim):
@@ -339,42 +326,83 @@
     )(own_cols, other_cols, *lines)
 
 
-def feature_kernel(table_ref, grad_ref, *refs, zones, targets):
-    w_refs, (own_ref, other_ref, lhs) = refs[: len(zones)], refs[len(zones) :]
-    half = own_ref.shape[0]
-    chips = targets // 2
-    tokens = grad_ref.shape[0] // 2
-    share = tokens // targets
-    for core in range(2):
-        for chip in range(chips):
-            x = lax.rem(table_ref[PLACE, 2] + chip, chips)
-            target = x * 2 + lax.rem(table_ref[PLACE, 3] + core, 2)
-            for i in range(2):
-                at = pl.multiple_of(i * tokens + target * share, share)
-                to = ((core * chips + chip) * 2 + i) * share
-                lhs[to : to + share, :] = grad_ref[pl.ds(at, share), :]
-    for cols, spot in weight_blocks(table_ref, w_refs, zones):
-        part = dot_dims(lhs[...], side_by_side(spot), 1, 1).astype(BF16)
-        own_ref[:, cols] = part[:half]
-        other_ref[:, cols] = part[half:]
-
-
-def feature_terms(table, grads, pieces, zones, width, targets):
-    half = jax.ShapeDtypeStruct((grads.shape[0] // 2, width), BF16)
-    return pl.pallas_call(
-        functools.partial(feature_kernel, zones=zones, targets=targets),
+def assemble_kernel(table_ref, *refs, zones):
+    w_refs, out_ref = refs[:-1], refs[-1]
+    for rows, spot in weight_blocks(table_ref, w_refs, zones):
+        out_ref[rows, :] = side_by_side(spot)
+
+
+def assemble(table, pieces, zones, width, cols):
+    return pl.pallas_call(
+        functools.partial(assemble_kernel, zones=zones),
         grid_spec=pltpu.PrefetchScalarGridSpec(
             num_scalar_prefetch=1,
             grid=(),
-            in_specs=[in_vmem()] * (1 + len(pieces)),
-            out_specs=[in_vmem()] * 2,
-            scratch_shapes=[pltpu.VMEM(grads.shape, BF16)],
+            in_specs=[in_vmem()] * len(pieces),
+            out_specs=in_vmem(),
         ),
-        out_shape=[half, half],
-        compiler_params=limit(13),
-        cost_estimate=cost(4 * half.size * grads.shape[1], 8),
+        out_shape=pltpu.HBM((width, cols), BF16),
+        compiler_params=limit(10),
+        cost_estimate=cost(0, 8),
+        name="assemble",
+    )(table, *pieces)
+
+
+def feature_kernel(table_ref, own_ref, other_ref, w_own_ref, w_other_ref, *refs, targets):
+    out_refs, (lhs, held, sems) = refs[:-3], refs[-3:]
+    chips = len(out_refs)
+    tokens = own_ref.shape[0] // 2
+    share = tokens // targets
+    steps, block = held.shape[1:3]
+    copies = []
+    for step in range(steps):
+        for core, w_ref in enumerate((w_own_ref, w_other_ref)):
+            here = pl.ds(step * block, block)
+            copies.append(
+                pltpu.make_async_copy(w_ref.at[here, :], held.at[core, step], sems.at[core, step])
+            )
+    for copy in copies:
+        copy.start()
+    for core, ref in enumerate((own_ref, other_ref)):
+        for chip in range(chips):
+            target = lax.rem(table_ref[PLACE, 2] + chip, chips) * 2 + table_ref[PLACE, 3]
+            for i in range(2):
+                at = pl.multiple_of(i * tokens + target * share, share)
+                to = (chip * 2 + i) * share
+                lhs[core, to : to + share, :] = ref[pl.ds(at, share), :]
+    for step in range(steps):
+        copies[2 * step].wait()
+        part = dot_dims(lhs[0], held[0, step], 1, 1)
+        copies[2 * step + 1].wait()
+        part = (part + dot_dims(lhs[1], held[1, step], 1, 1)).astype(BF16)
+        for chip, ref in enumerate(out_refs):
+            ref[:, step * block : (step + 1) * block] = part[
+                chip * 2 * share : (chip + 1) * 2 * share
+            ]
+
+
+def feature_terms(table, own, other, w_own, w_other, targets):
+    width, cols = w_own.shape
+    chips, steps = targets // 2, 8
+    rows = own.shape[0] // targets
+    return pl.pallas_call(
+        functools.partial(feature_kernel, targets=targets),
+        grid_spec=pltpu.PrefetchScalarGridSpec(
+            num_scalar_prefetch=1,
+            grid=(),
+            in_specs=[in_vmem()] * 2 + [in_hbm()] * 2,
+            out_specs=[in_vmem()] * chips,
+            scratch_shapes=[
+                pltpu.VMEM((2, own.shape[0] // 2, cols), BF16),
+                pltpu.VMEM((2, steps, width // steps, cols), BF16),
+                pltpu.SemaphoreType.DMA((2, steps)),
+            ],
+        ),
+        out_shape=[jax.ShapeDtypeStruct((rows, width), BF16)] * chips,
+        compiler_params=limit(14),
+        cost_estimate=cost(4 * own.size * width, 10),
         name="feature_terms",
-    )(table, grads, *pieces)
+    )(table, own, other, w_own, w_other)
 
 
 def shift_y(x, by):
@@ -451,7 +479,7 @@
     )
     kv = lax.all_to_all(send, "dp", 0, 0, tiled=True)
 
-    rows_later, _ = lax.optimization_barrier((features, raw))
+    rows_later, pieces_later, _ = lax.optimization_barrier((features, pieces, raw))
     span = width // NY
     col_pieces = [
         shift_y(
@@ -463,8 +491,11 @@
         for s in range(NY)
     ]
 
+    w_own = assemble(table, pieces_later, zones, width, 2 * head_dim)
+    w_other = swap_cores(w_own, tensor_count)
+
     parts, probs, d_scores = attend(table, queries, cotangent, kv)
-    parts, col_pieces = lax.optimization_barrier((parts, col_pieces))
+    parts, col_pieces, w_other = lax.optimization_barrier((parts, col_pieces, w_other))
     parts = lax.all_to_all(parts, "dp", 0, 0, tiled=True)
     own_cols = transpose_pieces(col_pieces)
     other_cols = swap_cores(own_cols, tensor_count)
@@ -476,24 +507,15 @@
 
     lines = [shift_y(by_core, s) for s in range(NY)]
     shares = weight_terms(own_cols, other_cols, lines)
-    shares, grads = lax.optimization_barrier((shares, grads))
+    other_grads = swap_cores(grads, tensor_count)
+    shares, grads, other_grads = lax.optimization_barrier((shares, grads, other_grads))
     shares = lax.all_to_all(shares, "dp", 0, 0, tiled=True, axis_index_groups=Z_GROUPS)
 
-    own, other = feature_terms(table, grads, pieces, zones, width, tensor_count)
-    other = swap_cores(other, tensor_count)
-    share = own.shape[0] * 2 // tensor_count
-    pairs = [
-        own[s * share : (s + 1) * share].astype(F32)
-        + other[s * share : (s + 1) * share].astype(F32)
-        for s in range(tensor_count // 2)
-    ]
-    grad_features = pairs[0]
+    terms = feature_terms(table, grads, other_grads, w_own, w_other, tensor_count)
+    grad_features = terms[0].astype(F32)
     for s in range(1, tensor_count // 2):
-        grad_features = grad_features + lax.ppermute(
-            pairs[s].astype(BF16),
-            "tensor",
-            [(t, (t + 2 * s) % tensor_count) for t in range(tensor_count)],
-        ).astype(F32)
+        pairs = [(t, (t + 2 * s) % tensor_count) for t in range(tensor_count)]
+        grad_features = grad_features + lax.ppermute(terms[s], "tensor", pairs).astype(F32)
     grad_features = grad_features.astype(BF16).reshape(images, tokens // tensor_count, width)
     weight_grads = jnp.sum(shares.astype(F32), axis=0)
     return (

time: 236 us -> 260 us (1.10)
  waiting for transfers between devices: 114 us -> 137 us
  local copies, waits for them, and re-layouts: 15.8 us -> 11.1 us
  starting transfers between devices: 63 us -> 67.2 us
  Pallas kernels: 33.3 us -> 36.8 us
  other arithmetic: 6.68 us -> 3.74 us
    ppermute x3, waiting for transfers between devices: 1.79 us -> 15.7 us  [local(): lax.ppermute(terms[s], 'tensor', pairs).astype(F32)]
    all_to_all x1, waiting for transfers between devices: 20 us -> 8.52 us  [local(): lax.all_to_all(shares, 'dp', 0, 0, tiled=True, axis_index_groups=Z_GROUPS)]
    all_to_all x1, waiting for transfers between devices: 29.1 us -> 38.9 us  [local(): parts = lax.all_to_all(parts, 'dp', 0, 0, tiled=True)]
    all_to_all x1, waiting for transfers between devices: 33.3 us -> 42.8 us  [local(): kv = lax.all_to_all(send, 'dp', 0, 0, tiled=True)]
    pallas_call x1 -> x2, Pallas kernels: 4.46 us -> 10.1 us  [the longest x1 5.89 us: feature_terms(): pl.pallas_call(functools.partial(feature_kernel, targets=targets), grid_s...]
    unnamed x60 -> x26, local copies, waits for them, and re-layouts: 10.7 us -> 6.23 us
    convert_element_type x1 -> x0, other arithmetic: 2.71 us -> none  [local(): pairs[s].astype(BF16)]
  transfers between devices with their start and end apart: 35 -> 36, of which waited for: 17 -> 16; matrix products, arithmetic and copies ran while one was open for 5% -> 4% of each run, Pallas kernels for 7% -> 7%
where the time goes in v6:
time: 260 us; the launch traced here: 257 us
  waiting for transfers between devices  137 us (53%)
  starting transfers between devices  67.2 us (26%)
  Pallas kernels  36.8 us (14%)
  local copies, waits for them, and re-layouts  11.1 us (4%)
  other arithmetic  3.74 us (1%)
    all_to_all x1, waiting for transfers between devices, local(): kv = lax.all_to_all(send, 'dp', 0, 0, tiled=True)  42.8 us
    all_to_all x1, waiting for transfers between devices, local(): parts = lax.all_to_all(parts, 'dp', 0, 0, tiled=True)  38.9 us
    ppermute x13, starting transfers between devices, shift_y(): return lax.ppermute(x, 'dp', pairs)  20.8 us
    ppermute x14, starting transfers between devices, shift_z(): return lax.ppermute(x, 'dp', pairs)  19.4 us
    ppermute x14, waiting for transfers between devices, shift_z(): return lax.ppermute(x, 'dp', pairs)  18.4 us
    ppermute x3, waiting for transfers between devices, local(): lax.ppermute(terms[s], 'tensor', pairs).astype(F32)  15.7 us
    ppermute x13, waiting for transfers between devices, shift_y(): return lax.ppermute(x, 'dp', pairs)  12.7 us
    pallas_call x1, Pallas kernels, attend(): pl.pallas_call(attend_kernel, grid_spec=pltpu.PrefetchScalarGridSpec(num_...  8.78 us
  transfers between devices with their start and end apart: 36, of which 16 were waited for; matrix products, arithmetic and copies ran while one was open for 4% of the time, Pallas kernels for 7%

profile of v6, /device:TPU:32, one launch (start us, length us, event | category | flops | bytes accessed | tf_op | source)
XLA Modules:
  0.0 256.9 jit_solution(7773494192793631308)
XLA Ops:
  0.6 2.0 collective-permute-start
  2.7 3.2 %collective-permute-start.12 = (bf16[256,128]{1,0:T(8,128)(2,1)}, bf16[256,128]{1,0:T(8,128)(2,1)S(1)}, u32[]{:S(2)}, u32[]{:S(2)}) collective-permute-start(bf16[256,128]{1,0:T(8,128)(2,1)} %param.12), channel_id=1, source_target_pairs={{0,128},{8,136},{16,144},{24,152},{32,160},{40,168},{48,176},{56,1... | collective-permute-start | bytes 196616 | tf_op jit(solution)/shard_map/ppermute | solution.py:412
  5.9 1.1 collective-permute-start.11
  10.6 2.1 collective-permute-done.13
  12.7 4.1 %collective-permute-start.15 = (bf16[1024,128]{1,0:T(8,128)(2,1)S(1)}, bf16[1024,128]{1,0:T(8,128)(2,1)S(1)}, u32[]{:S(2)}, u32[]{:S(2)}) collective-permute-start(bf16[1024,128]{1,0:T(8,128)(2,1)S(1)} %constant_dynamic-update-slice_fusion.8.refs_5_), channel_id=1, source_target_pairs={{0,56},{8,0},{16,8},{24,16},{32,24},{40,32},{48,40},{56,48},{64,12... | collective-permute-start | bytes 786440 | tf_op jit(solution)/shard_map/ppermute | solution.py:417
  16.8 1.0 collective-permute-start.2
  17.8 1.1 collective-permute-start.3
  19.0 5.0 %collective-permute-done.2 = bf16[256,128]{1,0:T(8,128)(2,1)S(1)} collective-permute-done((bf16[256,128]{1,0:T(8,128)(2,1)S(1)}, bf16[256,128]{1,0:T(8,128)(2,1)S(1)}, u32[]{:S(2)}, u32[]{:S(2)}) %collective-permute-start.2) | collective-permute-done | bytes 65568 | tf_op jit(solution)/shard_map/ppermute | solution.py:417
  24.7 2.3 collective-permute-start.5
  27.1 2.9 %collective-permute-done.4 = bf16[256,128]{1,0:T(8,128)(2,1)S(1)} collective-permute-done((bf16[256,128]{1,0:T(8,128)(2,1)S(1)}, bf16[256,128]{1,0:T(8,128)(2,1)S(1)}, u32[]{:S(2)}, u32[]{:S(2)}) %collective-permute-start.4) | collective-permute-done | bytes 65568 | tf_op jit(solution)/shard_map/ppermute | solution.py:417
  30.0 2.0 collective-permute-start.16
  32.0 3.3 %collective-permute-done.6 = bf16[256,128]{1,0:T(8,128)(2,1)S(1)} collective-permute-done((bf16[256,128]{1,0:T(8,128)(2,1)S(1)}, bf16[256,128]{1,0:T(8,128)(2,1)S(1)}, u32[]{:S(2)}, u32[]{:S(2)}) %collective-permute-start.6) | collective-permute-done | bytes 65568 | tf_op jit(solution)/shard_map/ppermute | solution.py:417
  35.5 3.2 %collective-permute-start.7 = (bf16[2048,128]{1,0:T(8,128)(2,1)S(1)}, bf16[2048,128]{1,0:T(8,128)(2,1)S(1)}, u32[]{:S(2)}, u32[]{:S(2)}) collective-permute-start(bf16[2048,128]{1,0:T(8,128)(2,1)S(1)} %constant_dynamic-update-slice_fusion.refs_0_), channel_id=1, source_target_pairs={{0,192},{8,200},{16,208},{24,216},{32,224},{40,232},{48,240},{56,2... | collective-permute-start | bytes 1572872 | tf_op jit(solution)/shard_map/ppermute | solution.py:412
  38.8 3.5 %collective-permute-start.17 = (bf16[1024,128]{1,0:T(8,128)(2,1)S(1)}, bf16[1024,128]{1,0:T(8,128)(2,1)S(1)}, u32[]{:S(2)}, u32[]{:S(2)}) collective-permute-start(bf16[1024,128]{1,0:T(8,128)(2,1)S(1)} %collective-permute-done.15.refs_7_), channel_id=1, source_target_pairs={{0,56},{8,0},{16,8},{24,16},{32,24},{40,32},{48,40},{56,48},{64,12... | collective-permute-start | bytes 786440 | tf_op jit(solution)/shard_map/ppermute | solution.py:417
  42.4 4.4 %collective-permute-done.17.refs_9_ = bf16[1024,128]{1,0:T(8,128)(2,1)S(1)} collective-permute-done((bf16[1024,128]{1,0:T(8,128)(2,1)S(1)}, bf16[1024,128]{1,0:T(8,128)(2,1)S(1)}, u32[]{:S(2)}, u32[]{:S(2)}) %collective-permute-start.17) | collective-permute-done | bytes 262176 | tf_op jit(solution)/shard_map/ppermute | solution.py:417
  46.9 2.5 collective-permute-start.19
  50.8 3.2 %collective-permute-start.9 = (bf16[1024,128]{1,0:T(8,128)(2,1)}, bf16[1024,128]{1,0:T(8,128)(2,1)}, u32[]{:S(2)}, u32[]{:S(2)}) collective-permute-start(bf16[1024,128]{1,0:T(8,128)(2,1)} %slice.26), channel_id=1, source_target_pairs={{0,192},{8,200},{16,208},{24,216},{32,224},{40,232},{48,240},{56,2... | collective-permute-start | bytes 786440 | tf_op jit(solution)/shard_map/ppermute | solution.py:412
  54.3 3.7 %collective-permute-done.10.refs_4_ = bf16[1024,128]{1,0:T(8,128)(2,1)} collective-permute-done((bf16[1024,128]{1,0:T(8,128)(2,1)}, bf16[1024,128]{1,0:T(8,128)(2,1)}, u32[]{:S(2)}, u32[]{:S(2)}) %collective-permute-start.10) | collective-permute-done | bytes 262176 | tf_op jit(solution)/shard_map/ppermute | solution.py:412
  58.3 2.7 %collective-permute-done.20.refs_12_ = bf16[1024,128]{1,0:T(8,128)(2,1)} collective-permute-done((bf16[1024,128]{1,0:T(8,128)(2,1)S(1)}, bf16[1024,128]{1,0:T(8,128)(2,1)}, u32[]{:S(2)}, u32[]{:S(2)}) %collective-permute-start.20) | collective-permute-done | bytes 262176 | tf_op jit(solution)/shard_map/ppermute | solution.py:417
  60.9 6.0 %project.1 = (bf16[32,128,256]{2,1,0:T(8,128)(2,1)}, f32[256,128]{1,0:T(8,128)}) custom-call(s32[5,32]{1,0:T(8,128)S(1)} %stack.41.table_ref, bf16[256,8192]{1,0:T(8,128)(2,1)} %bitcast.24, bf16[2048,128]{1,0:T(8,128)(2,1)S(1)} %constant_dynamic-update-slice_fusion.refs_0_, bf16[2048,128]{1,0:T(8,128)(2,1)S(1)} %collective-permute-done.7.refs_1_, ...), custom_call_target="tpu_custom_call" | custom-call | flops 1073741824 | bytes 10485760 | tf_op jit(solution)/shard_map/project/pallas_call | solution.py:88
  66.9 4.2 %assemble.1.w_own_ref = bf16[8192,256]{1,0:T(8,128)(2,1)} custom-call(s32[5,32]{1,0:T(8,128)S(1)} %stack.41.table_ref, bf16[2048,128]{1,0:T(8,128)(2,1)S(1)} %constant_dynamic-update-slice_fusion.refs_0_, bf16[2048,128]{1,0:T(8,128)(2,1)S(1)} %collective-permute-done.7.refs_1_, bf16[2048,128]{1,0:T(8,128)(2,1)S(1)} %collective-permute-done.8.refs_2_, ...), custom_call_target="tpu_custom_call" | custom-call | bytes 8388608 | tf_op jit(solution)/shard_map/assemble/pallas_call | solution.py:336
  71.1 8.3 %all-to-all-start = ((bf16[32,128,256]{2,1,0:T(8,128)(2,1)}), bf16[32,128,256]{2,1,0:T(8,128)(2,1)}, u32[]{:S(2)}, u32[]{:S(2)}) async-start(bf16[32,128,256]{2,1,0:T(8,128)(2,1)} %get-tuple-element.45), calls=%async_computation | async-start | bytes 4194304 | tf_op jit(solution)/shard_map/all_to_all | solution.py:480
  79.5 2.5 dynamic-slice_bitcast_fusion
  82.0 2.7 %collective-permute-start.23 = (bf16[128,2048]{1,0:T(8,128)(2,1)}, bf16[128,2048]{1,0:T(8,128)(2,1)S(1)}, u32[]{:S(2)}, u32[]{:S(2)}) collective-permute-start(bf16[128,2048]{1,0:T(8,128)(2,1)} %get-tuple-element.89), channel_id=1, source_target_pairs={{0,192},{8,200},{16,208},{24,216},{32,224},{40,232},{48,240},{56,2... | collective-permute-start | bytes 1572872 | tf_op jit(solution)/shard_map/ppermute | solution.py:412
  86.4 42.8 %all-to-all-done.kv_ref = bf16[32,128,256]{2,1,0:T(8,128)(2,1)} async-done(((bf16[32,128,256]{2,1,0:T(8,128)(2,1)}), bf16[32,128,256]{2,1,0:T(8,128)(2,1)}, u32[]{:S(2)}, u32[]{:S(2)}) %all-to-all-start) | async-done | bytes 2097184 | tf_op jit(solution)/shard_map/all_to_all | solution.py:480
  129.2 8.8 %attend.1 = (bf16[32,128,256]{2,1,0:T(8,128)(2,1)}, bf16[32,128,128]{2,1,0:T(8,128)(2,1)}, bf16[32,128,128]{2,1,0:T(8,128)(2,1)}) custom-call(s32[5,32]{1,0:T(8,128)S(1)} %stack.41.table_ref, bf16[512,1024]{1,0:T(8,128)(2,1)} %q_ref.1, bf16[512,1024]{1,0:T(8,128)(2,1)} %ct_ref.1, bf16[32,128,256]{2,1,0:T(8,128)(2,1)} %all-to-all-done.kv_ref), custom_call_target="tpu_custom_call" | custom-call | flops 536870912 | bytes 8388608 | tf_op jit(solution)/shard_map/attend/pallas_call | solution.py:182
  139.0 7.6 %all-to-all-start.1 = ((bf16[32,128,256]{2,1,0:T(8,128)(2,1)}), bf16[32,128,256]{2,1,0:T(8,128)(2,1)}, u32[]{:S(2)}, u32[]{:S(2)}) async-start(bf16[32,128,256]{2,1,0:T(8,128)(2,1)} %get-tuple-element.62), calls=%async_computation.1 | async-start | bytes 4194304 | tf_op jit(solution)/shard_map/all_to_all | solution.py:499
  146.6 1.0 copy-done.4
  147.7 1.0 copy-done.6
  149.4 6.2 %apply.1 = (bf16[512,1024]{1,0:T(8,128)(2,1)}, bf16[512,1024]{1,0:T(8,128)(2,1)}) custom-call(s32[5,32]{1,0:T(8,128)S(1)} %stack.41.table_ref, bf16[32,128,256]{2,1,0:T(8,128)(2,1)} %all-to-all-done.kv_ref, bf16[32,128,128]{2,1,0:T(8,128)(2,1)} %get-tuple-element.67.probs_ref, bf16[32,128,128]{2,1,0:T(8,128)(2,1)} %get-tuple-element.68.ds_ref), custom_call_target="tpu_custom_call" | custom-call | flops 268435456 | bytes 6291456 | tf_op jit(solution)/shard_map/apply/pallas_call | solution.py:221
  155.6 1.4 copy-done.1
  157.0 38.9 %all-to-all-done.1.part_ref = bf16[32,128,256]{2,1,0:T(8,128)(2,1)} async-done(((bf16[32,128,256]{2,1,0:T(8,128)(2,1)}), bf16[32,128,256]{2,1,0:T(8,128)(2,1)}, u32[]{:S(2)}, u32[]{:S(2)}) %all-to-all-start.1) | async-done | bytes 2097184 | tf_op jit(solution)/shard_map/all_to_all | solution.py:499
  195.9 3.0 %owner_grads.1 = (bf16[256,256]{1,0:T(8,128)(2,1)S(1)}, bf16[256,256]{1,0:T(8,128)(2,1)S(1)}) custom-call(s32[5,32]{1,0:T(8,128)S(1)} %stack.41.table_ref, bf16[32,128,256]{2,1,0:T(8,128)(2,1)} %all-to-all-done.1.part_ref, f32[256,128]{1,0:T(8,128)} %get-tuple-element.47.raw_ref, f32[1,128]{1,0:T(1,128)S(1)} %bitcast.23), custom_call_target="tpu_custom_call" | custom-call | bytes 3145728 | tf_op jit(solution)/shard_map/owner_grads/pallas_call | solution.py:267
  198.9 1.9 collective-permute-start.28
  200.8 2.1 collective-permute-start.27
  203.5 1.8 collective-permute-done.28.refs_3_
  205.3 3.4 %collective-permute-done.27.refs_2_ = bf16[256,256]{1,0:T(8,128)(2,1)S(1)} collective-permute-done((bf16[256,256]{1,0:T(8,128)(2,1)S(1)}, bf16[256,256]{1,0:T(8,128)(2,1)S(1)}, u32[]{:S(2)}, u32[]{:S(2)}) %collective-permute-start.27) | collective-permute-done | bytes 131104 | tf_op jit(solution)/shard_map/ppermute | solution.py:412
  208.7 1.5 collective-permute-done.26.refs_1_
  210.2 2.2 weight_terms.1
  212.5 5.9 %feature_terms.1 = (bf16[32,8192]{1,0:T(8,128)(2,1)S(1)}, bf16[32,8192]{1,0:T(8,128)(2,1)S(1)}, bf16[32,8192]{1,0:T(8,128)(2,1)S(1)}, bf16[32,8192]{1,0:T(8,128)(2,1)S(1)}) custom-call(s32[5,32]{1,0:T(8,128)S(1)} %stack.41.table_ref, bf16[256,256]{1,0:T(8,128)(2,1)S(1)} %get-tuple-element.77.own_ref, bf16[256,256]{1,0:T(8,128)(2,1)S(1)} %collective-permute-done.29.other_ref, ...), custom_call_target="tpu_custom_call" | custom-call | flops 2147483648 | bytes 10485760 | tf_op jit(solution)/shard_map/feature_terms/pallas_call | solution.py:388
  218.4 1.6 collective-permute-start.30
  219.9 2.7 %collective-permute-start.31 = (bf16[32,8192]{1,0:T(8,128)(2,1)S(1)}, bf16[32,8192]{1,0:T(8,128)(2,1)}, u32[]{:S(2)}, u32[]{:S(2)}) collective-permute-start(bf16[32,8192]{1,0:T(8,128)(2,1)S(1)} %get-tuple-element.82), channel_id=1, source_target_pairs={{0,4},{1,5},{2,6},{3,7},{4,0},{5,1},{6,2},{7,3},{8,12},{9,13},{10,... | collective-permute-start | bytes 1572872 | tf_op jit(solution)/shard_map/ppermute | solution.py:518
  222.7 1.4 collective-permute-start.32
  224.1 5.3 %all-to-all-start.2 = ((bf16[8,256,256]{2,1,0:T(8,128)(2,1)}), bf16[8,256,256]{2,1,0:T(8,128)(2,1)S(1)}, u32[]{:S(2)}, u32[]{:S(2)}) async-start(bf16[8,256,256]{2,1,0:T(8,128)(2,1)} %weight_terms.1), calls=%async_computation.2 | async-start | bytes 2097152 | tf_op jit(solution)/shard_map/all_to_all | solution.py:512
  229.4 4.2 %collective-permute-done.30 = bf16[32,8192]{1,0:T(8,128)(2,1)} collective-permute-done((bf16[32,8192]{1,0:T(8,128)(2,1)S(1)}, bf16[32,8192]{1,0:T(8,128)(2,1)}, u32[]{:S(2)}, u32[]{:S(2)}) %collective-permute-start.30) | collective-permute-done | bytes 524320 | tf_op jit(solution)/shard_map/ppermute | solution.py:518
  233.6 11.4 %collective-permute-done.31 = bf16[32,8192]{1,0:T(8,128)(2,1)} collective-permute-done((bf16[32,8192]{1,0:T(8,128)(2,1)S(1)}, bf16[32,8192]{1,0:T(8,128)(2,1)}, u32[]{:S(2)}, u32[]{:S(2)}) %collective-permute-start.31) | collective-permute-done | bytes 524320 | tf_op jit(solution)/shard_map/ppermute | solution.py:518
  245.1 2.4 add_convert_fusion
  247.5 8.5 %all-to-all-done.2 = bf16[8,256,256]{2,1,0:T(8,128)(2,1)S(1)} async-done(((bf16[8,256,256]{2,1,0:T(8,128)(2,1)}), bf16[8,256,256]{2,1,0:T(8,128)(2,1)S(1)}, u32[]{:S(2)}, u32[]{:S(2)}) %all-to-all-start.2) | async-done | bytes 1048608 | tf_op jit(solution)/shard_map/all_to_all | solution.py:512
  (77 shorter events, 11.6 us)
Async XLA Ops:
  0.6 60.3 %copy-start.7 = (f32[128]{0:T(128)S(1)}, f32[128]{0:T(128)}, u32[]{:S(2)}) copy-start(f32[128]{0:T(128)} %param.13) | copy-start | bytes 1540
  0.6 16.2 %collective-permute-start = (bf16[256,128]{1,0:T(8,128)(2,1)}, bf16[256,128]{1,0:T(8,128)(2,1)S(1)}, u32[]{:S(2)}, u32[]{:S(2)}) collective-permute-start(bf16[256,128]{1,0:T(8,128)(2,1)} %param.11), channel_id=1, source_target_pairs={{0,8},{8,16},{16,24},{24,32},{32,40},{40,48},{48,56},{56,0},{64,72... | collective-permute-start | bytes 196616 | tf_op jit(solution)/shard_map/ppermute | solution.py:417
  2.6 15.2 %collective-permute-start.1 = (bf16[256,128]{1,0:T(8,128)(2,1)}, bf16[256,128]{1,0:T(8,128)(2,1)S(1)}, u32[]{:S(2)}, u32[]{:S(2)}) collective-permute-start(bf16[256,128]{1,0:T(8,128)(2,1)} %param.11), channel_id=1, source_target_pairs={{0,56},{8,0},{16,8},{24,16},{32,24},{40,32},{48,40},{56,48},{64,12... | collective-permute-start | bytes 196616 | tf_op jit(solution)/shard_map/ppermute | solution.py:417
  2.7 7.9 %collective-permute-start.12 = (bf16[256,128]{1,0:T(8,128)(2,1)}, bf16[256,128]{1,0:T(8,128)(2,1)S(1)}, u32[]{:S(2)}, u32[]{:S(2)}) collective-permute-start(bf16[256,128]{1,0:T(8,128)(2,1)} %param.12), channel_id=1, source_target_pairs={{0,128},{8,136},{16,144},{24,152},{32,160},{40,168},{48,176},{56,1... | collective-permute-start | bytes 196616 | tf_op jit(solution)/shard_map/ppermute | solution.py:412
  5.9 4.6 %collective-permute-start.11 = (bf16[256,128]{1,0:T(8,128)(2,1)}, bf16[256,128]{1,0:T(8,128)(2,1)S(1)}, u32[]{:S(2)}, u32[]{:S(2)}) collective-permute-start(bf16[256,128]{1,0:T(8,128)(2,1)} %param.12), channel_id=1, source_target_pairs={{0,192},{8,200},{16,208},{24,216},{32,224},{40,232},{48,240},{56,2... | collective-permute-start | bytes 196616 | tf_op jit(solution)/shard_map/ppermute | solution.py:412
  7.0 5.7 %collective-permute-start.13 = (bf16[256,128]{1,0:T(8,128)(2,1)}, bf16[256,128]{1,0:T(8,128)(2,1)S(1)}, u32[]{:S(2)}, u32[]{:S(2)}) collective-permute-start(bf16[256,128]{1,0:T(8,128)(2,1)} %param.12), channel_id=1, source_target_pairs={{0,64},{8,72},{16,80},{24,88},{32,96},{40,104},{48,112},{56,120},{... | collective-permute-start | bytes 196616 | tf_op jit(solution)/shard_map/ppermute | solution.py:412
  12.7 26.1 %collective-permute-start.15 = (bf16[1024,128]{1,0:T(8,128)(2,1)S(1)}, bf16[1024,128]{1,0:T(8,128)(2,1)S(1)}, u32[]{:S(2)}, u32[]{:S(2)}) collective-permute-start(bf16[1024,128]{1,0:T(8,128)(2,1)S(1)} %constant_dynamic-update-slice_fusion.8.refs_5_), channel_id=1, source_target_pairs={{0,56},{8,0},{16,8},{24,16},{32,24},{40,32},{48,40},{56,48},{64,12... | collective-permute-start | bytes 786440 | tf_op jit(solution)/shard_map/ppermute | solution.py:417
  16.8 13.2 %collective-permute-start.14 = (bf16[1024,128]{1,0:T(8,128)(2,1)S(1)}, bf16[1024,128]{1,0:T(8,128)(2,1)S(1)}, u32[]{:S(2)}, u32[]{:S(2)}) collective-permute-start(bf16[1024,128]{1,0:T(8,128)(2,1)S(1)} %constant_dynamic-update-slice_fusion.8.refs_5_), channel_id=1, source_target_pairs={{0,8},{8,16},{16,24},{24,32},{32,40},{40,48},{48,56},{56,0},{64,72... | collective-permute-start | bytes 786440 | tf_op jit(solution)/shard_map/ppermute | solution.py:417
  16.8 7.2 %collective-permute-start.2 = (bf16[256,128]{1,0:T(8,128)(2,1)S(1)}, bf16[256,128]{1,0:T(8,128)(2,1)S(1)}, u32[]{:S(2)}, u32[]{:S(2)}) collective-permute-start(bf16[256,128]{1,0:T(8,128)(2,1)S(1)} %collective-permute-done), channel_id=1, source_target_pairs={{0,8},{8,16},{16,24},{24,32},{32,40},{40,48},{48,56},{56,0},{64,72... | collective-permute-start | bytes 196616 | tf_op jit(solution)/shard_map/ppermute | solution.py:417
  17.8 6.9 %collective-permute-start.3 = (bf16[256,128]{1,0:T(8,128)(2,1)S(1)}, bf16[256,128]{1,0:T(8,128)(2,1)S(1)}, u32[]{:S(2)}, u32[]{:S(2)}) collective-permute-start(bf16[256,128]{1,0:T(8,128)(2,1)S(1)} %collective-permute-done.1), channel_id=1, source_target_pairs={{0,56},{8,0},{16,8},{24,16},{32,24},{40,32},{48,40},{56,48},{64,12... | collective-permute-start | bytes 196616 | tf_op jit(solution)/shard_map/ppermute | solution.py:417
  24.0 6.0 %collective-permute-start.4 = (bf16[256,128]{1,0:T(8,128)(2,1)S(1)}, bf16[256,128]{1,0:T(8,128)(2,1)S(1)}, u32[]{:S(2)}, u32[]{:S(2)}) collective-permute-start(bf16[256,128]{1,0:T(8,128)(2,1)S(1)} %collective-permute-done.2), channel_id=1, source_target_pairs={{0,8},{8,16},{16,24},{24,32},{32,40},{40,48},{48,56},{56,0},{64,72... | collective-permute-start | bytes 196616 | tf_op jit(solution)/shard_map/ppermute | solution.py:417
  24.7 5.3 %collective-permute-start.5 = (bf16[256,128]{1,0:T(8,128)(2,1)S(1)}, bf16[256,128]{1,0:T(8,128)(2,1)S(1)}, u32[]{:S(2)}, u32[]{:S(2)}) collective-permute-start(bf16[256,128]{1,0:T(8,128)(2,1)S(1)} %collective-permute-done.3), channel_id=1, source_target_pairs={{0,56},{8,0},{16,8},{24,16},{32,24},{40,32},{48,40},{56,48},{64,12... | collective-permute-start | bytes 196616 | tf_op jit(solution)/shard_map/ppermute | solution.py:417
  30.0 5.4 %collective-permute-start.6 = (bf16[256,128]{1,0:T(8,128)(2,1)S(1)}, bf16[256,128]{1,0:T(8,128)(2,1)S(1)}, u32[]{:S(2)}, u32[]{:S(2)}) collective-permute-start(bf16[256,128]{1,0:T(8,128)(2,1)S(1)} %collective-permute-done.4), channel_id=1, source_target_pairs={{0,8},{8,16},{16,24},{24,32},{32,40},{40,48},{48,56},{56,0},{64,72... | collective-permute-start | bytes 196616 | tf_op jit(solution)/shard_map/ppermute | solution.py:417
  30.0 12.3 %collective-permute-start.16 = (bf16[1024,128]{1,0:T(8,128)(2,1)S(1)}, bf16[1024,128]{1,0:T(8,128)(2,1)S(1)}, u32[]{:S(2)}, u32[]{:S(2)}) collective-permute-start(bf16[1024,128]{1,0:T(8,128)(2,1)S(1)} %collective-permute-done.14.refs_6_), channel_id=1, source_target_pairs={{0,8},{8,16},{16,24},{24,32},{32,40},{40,48},{48,56},{56,0},{64,72... | collective-permute-start | bytes 786440 | tf_op jit(solution)/shard_map/ppermute | solution.py:417
  35.4 14.0 %collective-permute-start.8 = (bf16[2048,128]{1,0:T(8,128)(2,1)S(1)}, bf16[2048,128]{1,0:T(8,128)(2,1)S(1)}, u32[]{:S(2)}, u32[]{:S(2)}) collective-permute-start(bf16[2048,128]{1,0:T(8,128)(2,1)S(1)} %constant_dynamic-update-slice_fusion.refs_0_), channel_id=1, source_target_pairs={{0,64},{8,72},{16,80},{24,88},{32,96},{40,104},{48,112},{56,120},{... | collective-permute-start | bytes 1572872 | tf_op jit(solution)/shard_map/ppermute | solution.py:412
  35.5 14.6 %collective-permute-start.7 = (bf16[2048,128]{1,0:T(8,128)(2,1)S(1)}, bf16[2048,128]{1,0:T(8,128)(2,1)S(1)}, u32[]{:S(2)}, u32[]{:S(2)}) collective-permute-start(bf16[2048,128]{1,0:T(8,128)(2,1)S(1)} %constant_dynamic-update-slice_fusion.refs_0_), channel_id=1, source_target_pairs={{0,192},{8,200},{16,208},{24,216},{32,224},{40,232},{48,240},{56,2... | collective-permute-start | bytes 1572872 | tf_op jit(solution)/shard_map/ppermute | solution.py:412
  38.8 8.1 %collective-permute-start.17 = (bf16[1024,128]{1,0:T(8,128)(2,1)S(1)}, bf16[1024,128]{1,0:T(8,128)(2,1)S(1)}, u32[]{:S(2)}, u32[]{:S(2)}) collective-permute-start(bf16[1024,128]{1,0:T(8,128)(2,1)S(1)} %collective-permute-done.15.refs_7_), channel_id=1, source_target_pairs={{0,56},{8,0},{16,8},{24,16},{32,24},{40,32},{48,40},{56,48},{64,12... | collective-permute-start | bytes 786440 | tf_op jit(solution)/shard_map/ppermute | solution.py:417
  42.3 11.8 %collective-permute-start.18 = (bf16[1024,128]{1,0:T(8,128)(2,1)S(1)}, bf16[1024,128]{1,0:T(8,128)(2,1)S(1)}, u32[]{:S(2)}, u32[]{:S(2)}) collective-permute-start(bf16[1024,128]{1,0:T(8,128)(2,1)S(1)} %collective-permute-done.16.refs_8_), channel_id=1, source_target_pairs={{0,8},{8,16},{16,24},{24,32},{32,40},{40,48},{48,56},{56,0},{64,72... | collective-permute-start | bytes 786440 | tf_op jit(solution)/shard_map/ppermute | solution.py:417
  46.9 7.4 %collective-permute-start.19 = (bf16[1024,128]{1,0:T(8,128)(2,1)S(1)}, bf16[1024,128]{1,0:T(8,128)(2,1)S(1)}, u32[]{:S(2)}, u32[]{:S(2)}) collective-permute-start(bf16[1024,128]{1,0:T(8,128)(2,1)S(1)} %collective-permute-done.17.refs_9_), channel_id=1, source_target_pairs={{0,56},{8,0},{16,8},{24,16},{32,24},{40,32},{48,40},{56,48},{64,12... | collective-permute-start | bytes 786440 | tf_op jit(solution)/shard_map/ppermute | solution.py:417
  50.1 7.9 %collective-permute-start.10 = (bf16[1024,128]{1,0:T(8,128)(2,1)}, bf16[1024,128]{1,0:T(8,128)(2,1)}, u32[]{:S(2)}, u32[]{:S(2)}) collective-permute-start(bf16[1024,128]{1,0:T(8,128)(2,1)} %slice.27), channel_id=1, source_target_pairs={{0,64},{8,72},{16,80},{24,88},{32,96},{40,104},{48,112},{56,120},{... | collective-permute-start | bytes 786440 | tf_op jit(solution)/shard_map/ppermute | solution.py:412
  50.8 7.4 %collective-permute-start.9 = (bf16[1024,128]{1,0:T(8,128)(2,1)}, bf16[1024,128]{1,0:T(8,128)(2,1)}, u32[]{:S(2)}, u32[]{:S(2)}) collective-permute-start(bf16[1024,128]{1,0:T(8,128)(2,1)} %slice.26), channel_id=1, source_target_pairs={{0,192},{8,200},{16,208},{24,216},{32,224},{40,232},{48,240},{56,2... | collective-permute-start | bytes 786440 | tf_op jit(solution)/shard_map/ppermute | solution.py:412
  54.0 6.9 %collective-permute-start.20 = (bf16[1024,128]{1,0:T(8,128)(2,1)S(1)}, bf16[1024,128]{1,0:T(8,128)(2,1)}, u32[]{:S(2)}, u32[]{:S(2)}) collective-permute-start(bf16[1024,128]{1,0:T(8,128)(2,1)S(1)} %collective-permute-done.18.refs_10_), channel_id=1, source_target_pairs={{0,8},{8,16},{16,24},{24,32},{32,40},{40,48},{48,56},{56,0},{64,72... | collective-permute-start | bytes 786440 | tf_op jit(solution)/shard_map/ppermute | solution.py:417
  71.1 67.0 %collective-permute-start.24 = (bf16[8192,256]{1,0:T(8,128)(2,1)}, bf16[8192,256]{1,0:T(8,128)(2,1)}, u32[]{:S(2)}, u32[]{:S(2)}) collective-permute-start(bf16[8192,256]{1,0:T(8,128)(2,1)} %assemble.1.w_own_ref), channel_id=1, source_target_pairs={{0,1},{1,0},{2,3},{3,2},{4,5},{5,4},{6,7},{7,6},{8,9},{9,8},{10,11... | collective-permute-start | bytes 12582920 | tf_op jit(solution)/shard_map/ppermute | solution.py:433
  71.1 58.1 %all-to-all-start = ((bf16[32,128,256]{2,1,0:T(8,128)(2,1)}), bf16[32,128,256]{2,1,0:T(8,128)(2,1)}, u32[]{:S(2)}, u32[]{:S(2)}) async-start(bf16[32,128,256]{2,1,0:T(8,128)(2,1)} %get-tuple-element.45), calls=%async_computation | async-start | bytes 4194304 | tf_op jit(solution)/shard_map/all_to_all | solution.py:480
  82.0 56.0 %collective-permute-start.23 = (bf16[128,2048]{1,0:T(8,128)(2,1)}, bf16[128,2048]{1,0:T(8,128)(2,1)S(1)}, u32[]{:S(2)}, u32[]{:S(2)}) collective-permute-start(bf16[128,2048]{1,0:T(8,128)(2,1)} %get-tuple-element.89), channel_id=1, source_target_pairs={{0,192},{8,200},{16,208},{24,216},{32,224},{40,232},{48,240},{56,2... | collective-permute-start | bytes 1572872 | tf_op jit(solution)/shard_map/ppermute | solution.py:412
  84.7 53.3 %collective-permute-start.22 = (bf16[128,2048]{1,0:T(8,128)(2,1)S(1)}, bf16[128,2048]{1,0:T(8,128)(2,1)S(1)}, u32[]{:S(2)}, u32[]{:S(2)}) collective-permute-start(bf16[128,2048]{1,0:T(8,128)(2,1)S(1)} %get-tuple-element.90), channel_id=1, source_target_pairs={{0,128},{8,136},{16,144},{24,152},{32,160},{40,168},{48,176},{56,1... | collective-permute-start | bytes 1572872 | tf_op jit(solution)/shard_map/ppermute | solution.py:412
  85.5 52.5 %collective-permute-start.21 = (bf16[128,2048]{1,0:T(8,128)(2,1)S(1)}, bf16[128,2048]{1,0:T(8,128)(2,1)S(1)}, u32[]{:S(2)}, u32[]{:S(2)}) collective-permute-start(bf16[128,2048]{1,0:T(8,128)(2,1)S(1)} %get-tuple-element.91), channel_id=1, source_target_pairs={{0,64},{8,72},{16,80},{24,88},{32,96},{40,104},{48,112},{56,120},{... | collective-permute-start | bytes 1572872 | tf_op jit(solution)/shard_map/ppermute | solution.py:412
  138.0 0.8 copy-start.3
  138.0 0.9 copy-start.5
  139.0 56.9 %all-to-all-start.1 = ((bf16[32,128,256]{2,1,0:T(8,128)(2,1)}), bf16[32,128,256]{2,1,0:T(8,128)(2,1)}, u32[]{:S(2)}, u32[]{:S(2)}) async-start(bf16[32,128,256]{2,1,0:T(8,128)(2,1)} %get-tuple-element.62), calls=%async_computation.1 | async-start | bytes 4194304 | tf_op jit(solution)/shard_map/all_to_all | solution.py:499
  146.6 1.0 copy-start.4
  147.7 1.0 copy-start.6
  149.3 6.3 %collective-permute-start.25 = (bf16[2048,512]{1,0:T(8,128)(2,1)S(1)}, bf16[2048,512]{1,0:T(8,128)(2,1)S(1)}, u32[]{:S(2)}, u32[]{:S(2)}) collective-permute-start(bf16[2048,512]{1,0:T(8,128)(2,1)S(1)} %transpose_pieces.1.own_ref), channel_id=1, source_target_pairs={{0,1},{1,0},{2,3},{3,2},{4,5},{5,4},{6,7},{7,6},{8,9},{9,8},{10,11... | collective-permute-start | bytes 6291464 | tf_op jit(solution)/shard_map/ppermute | solution.py:433
  155.6 1.4 copy-start.1
  195.9 14.3 %copy-start.2 = (bf16[2048,512]{1,0:T(8,128)(2,1)S(1)}, bf16[2048,512]{1,0:T(8,128)(2,1)}, u32[]{:S(2)}) copy-start(bf16[2048,512]{1,0:T(8,128)(2,1)} %copy-done.1) | copy-start | bytes 6291460
  198.9 6.4 %collective-permute-start.28 = (bf16[256,256]{1,0:T(8,128)(2,1)S(1)}, bf16[256,256]{1,0:T(8,128)(2,1)S(1)}, u32[]{:S(2)}, u32[]{:S(2)}) collective-permute-start(bf16[256,256]{1,0:T(8,128)(2,1)S(1)} %get-tuple-element.75.refs_0_), channel_id=1, source_target_pairs={{0,192},{8,200},{16,208},{24,216},{32,224},{40,232},{48,240},{56,2... | collective-permute-start | bytes 393224 | tf_op jit(solution)/shard_map/ppermute | solution.py:412
  200.8 7.9 %collective-permute-start.27 = (bf16[256,256]{1,0:T(8,128)(2,1)S(1)}, bf16[256,256]{1,0:T(8,128)(2,1)S(1)}, u32[]{:S(2)}, u32[]{:S(2)}) collective-permute-start(bf16[256,256]{1,0:T(8,128)(2,1)S(1)} %get-tuple-element.75.refs_0_), channel_id=1, source_target_pairs={{0,128},{8,136},{16,144},{24,152},{32,160},{40,168},{48,176},{56,1... | collective-permute-start | bytes 393224 | tf_op jit(solution)/shard_map/ppermute | solution.py:412
  202.9 7.3 %collective-permute-start.26 = (bf16[256,256]{1,0:T(8,128)(2,1)S(1)}, bf16[256,256]{1,0:T(8,128)(2,1)S(1)}, u32[]{:S(2)}, u32[]{:S(2)}) collective-permute-start(bf16[256,256]{1,0:T(8,128)(2,1)S(1)} %get-tuple-element.75.refs_0_), channel_id=1, source_target_pairs={{0,64},{8,72},{16,80},{24,88},{32,96},{40,104},{48,112},{56,120},{... | collective-permute-start | bytes 393224 | tf_op jit(solution)/shard_map/ppermute | solution.py:412
  203.5 9.0 %copy-start = (bf16[8192,256]{1,0:T(8,128)(2,1)S(1)}, bf16[8192,256]{1,0:T(8,128)(2,1)}, u32[]{:S(2)}) copy-start(bf16[8192,256]{1,0:T(8,128)(2,1)} %assemble.1.w_own_ref) | copy-start | bytes 12582916
  203.5 9.0 %collective-permute-start.29 = (bf16[256,256]{1,0:T(8,128)(2,1)S(1)}, bf16[256,256]{1,0:T(8,128)(2,1)S(1)}, u32[]{:S(2)}, u32[]{:S(2)}) collective-permute-start(bf16[256,256]{1,0:T(8,128)(2,1)S(1)} %get-tuple-element.77.own_ref), channel_id=1, source_target_pairs={{0,1},{1,0},{2,3},{3,2},{4,5},{5,4},{6,7},{7,6},{8,9},{9,8},{10,11... | collective-permute-start | bytes 393224 | tf_op jit(solution)/shard_map/ppermute | solution.py:433
  218.4 15.3 %collective-permute-start.30 = (bf16[32,8192]{1,0:T(8,128)(2,1)S(1)}, bf16[32,8192]{1,0:T(8,128)(2,1)}, u32[]{:S(2)}, u32[]{:S(2)}) collective-permute-start(bf16[32,8192]{1,0:T(8,128)(2,1)S(1)} %get-tuple-element.81), channel_id=1, source_target_pairs={{0,2},{1,3},{2,4},{3,5},{4,6},{5,7},{6,0},{7,1},{8,10},{9,11},{10,... | collective-permute-start | bytes 1572872 | tf_op jit(solution)/shard_map/ppermute | solution.py:518
  219.9 25.1 %collective-permute-start.31 = (bf16[32,8192]{1,0:T(8,128)(2,1)S(1)}, bf16[32,8192]{1,0:T(8,128)(2,1)}, u32[]{:S(2)}, u32[]{:S(2)}) collective-permute-start(bf16[32,8192]{1,0:T(8,128)(2,1)S(1)} %get-tuple-element.82), channel_id=1, source_target_pairs={{0,4},{1,5},{2,6},{3,7},{4,0},{5,1},{6,2},{7,3},{8,12},{9,13},{10,... | collective-permute-start | bytes 1572872 | tf_op jit(solution)/shard_map/ppermute | solution.py:518
  222.7 22.4 %collective-permute-start.32 = (bf16[32,8192]{1,0:T(8,128)(2,1)S(1)}, bf16[32,8192]{1,0:T(8,128)(2,1)}, u32[]{:S(2)}, u32[]{:S(2)}) collective-permute-start(bf16[32,8192]{1,0:T(8,128)(2,1)S(1)} %get-tuple-element.83), channel_id=1, source_target_pairs={{0,6},{1,7},{2,0},{3,1},{4,2},{5,3},{6,4},{7,5},{8,14},{9,15},{10,... | collective-permute-start | bytes 1572872 | tf_op jit(solution)/shard_map/ppermute | solution.py:518
  224.1 31.9 %all-to-all-start.2 = ((bf16[8,256,256]{2,1,0:T(8,128)(2,1)}), bf16[8,256,256]{2,1,0:T(8,128)(2,1)S(1)}, u32[]{:S(2)}, u32[]{:S(2)}) async-start(bf16[8,256,256]{2,1,0:T(8,128)(2,1)} %weight_terms.1), calls=%async_computation.2 | async-start | bytes 2097152 | tf_op jit(solution)/shard_map/all_to_all | solution.py:512

commit v7 on v6

--- a/solution.py
+++ b/solution.py
@@ -327,62 +327,72 @@
 
 
 def assemble_kernel(table_ref, *refs, zones):
-    w_refs, out_ref = refs[:-1], refs[-1]
-    for rows, spot in weight_blocks(table_ref, w_refs, zones):
-        out_ref[rows, :] = side_by_side(spot)
-
-
-def assemble(table, pieces, zones, width, cols):
+    w_refs, out_refs = refs[:-2], refs[-2:]
+    for here, spot in weight_blocks(table_ref, w_refs, zones):
+        for out_ref, (ref, rows) in zip(out_refs, spot):
+            out_ref[here, :] = ref[rows, :]
+
+
+def assemble(table, pieces, zones, width, head_dim):
     return pl.pallas_call(
         functools.partial(assemble_kernel, zones=zones),
         grid_spec=pltpu.PrefetchScalarGridSpec(
             num_scalar_prefetch=1,
             grid=(),
             in_specs=[in_vmem()] * len(pieces),
-            out_specs=in_vmem(),
+            out_specs=[in_vmem()] * 2,
         ),
-        out_shape=pltpu.HBM((width, cols), BF16),
+        out_shape=[pltpu.HBM((width, head_dim), BF16)] * 2,
         compiler_params=limit(10),
-        cost_estimate=cost(0, 8),
+        cost_estimate=cost(0, 1),
         name="assemble",
     )(table, *pieces)
 
 
-def feature_kernel(table_ref, own_ref, other_ref, w_own_ref, w_other_ref, *refs, targets):
-    out_refs, (lhs, held, sems) = refs[:-3], refs[-3:]
+def feature_kernel(table_ref, own_ref, other_ref, *refs, targets):
+    w_refs, out_refs, (lhs, held, sems) = refs[:4], refs[4:-3], refs[-3:]
     chips = len(out_refs)
-    tokens = own_ref.shape[0] // 2
+    tokens, head_dim = own_ref.shape[0] // 2, own_ref.shape[1] // 2
     share = tokens // targets
     steps, block = held.shape[1:3]
-    copies = []
+    copies = [
+        [
+            pltpu.make_async_copy(
+                w_ref.at[pl.ds(step * block, block), :], held.at[n, step], sems.at[n, step]
+            )
+            for n, w_ref in enumerate(w_refs)
+        ]
+        for step in range(steps)
+    ]
     for step in range(steps):
-        for core, w_ref in enumerate((w_own_ref, w_other_ref)):
-            here = pl.ds(step * block, block)
-            copies.append(
-                pltpu.make_async_copy(w_ref.at[here, :], held.at[core, step], sems.at[core, step])
-            )
-    for copy in copies:
-        copy.start()
+        for copy in copies[step]:
+            copy.start()
     for core, ref in enumerate((own_ref, other_ref)):
         for chip in range(chips):
             target = lax.rem(table_ref[PLACE, 2] + chip, chips) * 2 + table_ref[PLACE, 3]
             for i in range(2):
                 at = pl.multiple_of(i * tokens + target * share, share)
                 to = (chip * 2 + i) * share
-                lhs[core, to : to + share, :] = ref[pl.ds(at, share), :]
+                for n in range(2):
+                    lhs[core, n, to : to + share, :] = ref[
+                        pl.ds(at, share), n * head_dim : (n + 1) * head_dim
+                    ]
     for step in range(steps):
-        copies[2 * step].wait()
-        part = dot_dims(lhs[0], held[0, step], 1, 1)
-        copies[2 * step + 1].wait()
-        part = (part + dot_dims(lhs[1], held[1, step], 1, 1)).astype(BF16)
+        part = 0.0
+        for core in range(2):
+            for n in range(2):
+                copies[step][2 * core + n].wait()
+            left = jnp.concatenate([lhs[core, 0], lhs[core, 1]], axis=1)
+            right = jnp.concatenate([held[2 * core, step], held[2 * core + 1, step]], axis=1)
+            part = part + dot_dims(left, right, 1, 1)
         for chip, ref in enumerate(out_refs):
             ref[:, step * block : (step + 1) * block] = part[
                 chip * 2 * share : (chip + 1) * 2 * share
-            ]
-
-
-def feature_terms(table, own, other, w_own, w_other, targets):
-    width, cols = w_own.shape
+            ].astype(BF16)
+
+
+def feature_terms(table, own, other, weights, targets):
+    width, head_dim = weights[0].shape
     chips, steps = targets // 2, 8
     rows = own.shape[0] // targets
     return pl.pallas_call(
@@ -390,19 +400,19 @@
         grid_spec=pltpu.PrefetchScalarGridSpec(
             num_scalar_prefetch=1,
             grid=(),
-            in_specs=[in_vmem()] * 2 + [in_hbm()] * 2,
+            in_specs=[in_vmem()] * 2 + [in_hbm()] * 4,
             out_specs=[in_vmem()] * chips,
             scratch_shapes=[
-                pltpu.VMEM((2, own.shape[0] // 2, cols), BF16),
-                pltpu.VMEM((2, steps, width // steps, cols), BF16),
-                pltpu.SemaphoreType.DMA((2, steps)),
+                pltpu.VMEM((2, 2, own.shape[0] // 2, head_dim), BF16),
+                pltpu.VMEM((4, steps, width // steps, head_dim), BF16),
+                pltpu.SemaphoreType.DMA((4, steps)),
             ],
         ),
         out_shape=[jax.ShapeDtypeStruct((rows, width), BF16)] * chips,
         compiler_params=limit(14),
         cost_estimate=cost(4 * own.size * width, 10),
         name="feature_terms",
-    )(table, own, other, w_own, w_other)
+    )(table, own, other, *weights)
 
 
 def shift_y(x, by):
@@ -479,7 +489,7 @@
     )
     kv = lax.all_to_all(send, "dp", 0, 0, tiled=True)
 
-    rows_later, pieces_later, _ = lax.optimization_barrier((features, pieces, raw))
+    rows_later, _ = lax.optimization_barrier((features, raw))
     span = width // NY
     col_pieces = [
         shift_y(
@@ -491,17 +501,16 @@
         for s in range(NY)
     ]
 
-    w_own = assemble(table, pieces_later, zones, width, 2 * head_dim)
-    w_other = swap_cores(w_own, tensor_count)
-
     parts, probs, d_scores = attend(table, queries, cotangent, kv)
-    parts, col_pieces, w_other = lax.optimization_barrier((parts, col_pieces, w_other))
+    parts, col_pieces, pieces = lax.optimization_barrier((parts, col_pieces, pieces))
     parts = lax.all_to_all(parts, "dp", 0, 0, tiled=True)
     own_cols = transpose_pieces(col_pieces)
     other_cols = swap_cores(own_cols, tensor_count)
+    weights = list(assemble(table, pieces, zones, width, head_dim))
+    weights += [swap_cores(w, tensor_count) for w in weights]
     attended, grad_queries = apply(table, kv, probs, d_scores, queries.shape)
-    parts, other_cols, attended, grad_queries = lax.optimization_barrier(
-        (parts, other_cols, attended, grad_queries)
+    parts, other_cols, attended, grad_queries, weights = lax.optimization_barrier(
+        (parts, other_cols, attended, grad_queries, weights)
     )
     grads, by_core = owner_grads(table, parts, raw, gain, images)
 
@@ -511,12 +520,13 @@
     shares, grads, other_grads = lax.optimization_barrier((shares, grads, other_grads))
     shares = lax.all_to_all(shares, "dp", 0, 0, tiled=True, axis_index_groups=Z_GROUPS)
 
-    terms = feature_terms(table, grads, other_grads, w_own, w_other, tensor_count)
-    grad_features = terms[0].astype(F32)
+    terms = list(feature_terms(table, grads, other_grads, weights, tensor_count))
     for s in range(1, tensor_count // 2):
         pairs = [(t, (t + 2 * s) % tensor_count) for t in range(tensor_count)]
-        grad_features = grad_features + lax.ppermute(terms[s], "tensor", pairs).astype(F32)
-    grad_features = grad_features.astype(BF16).reshape(images, tokens // tensor_count, width)
+        terms[s] = lax.ppermute(terms[s], "tensor", pairs)
+    shares, terms = lax.optimization_barrier((shares, terms))
+    grad_features = sum(term.astype(F32) for term in terms).astype(BF16)
+    grad_features = grad_features.reshape(images, tokens // tensor_count, width)
     weight_grads = jnp.sum(shares.astype(F32), axis=0)
     return (
         attended,

time: 260 us -> 229 us (0.88)
  waiting for transfers between devices: 137 us -> 101 us
  local copies, waits for them, and re-layouts: 11.1 us -> 21.8 us
  starting transfers between devices: 67.2 us -> 64.2 us
    all_to_all x1, waiting for transfers between devices: 38.9 us -> 21.2 us  [local(): parts = lax.all_to_all(parts, 'dp', 0, 0, tiled=True)]
    unnamed x26 -> x70, local copies, waits for them, and re-layouts: 6.23 us -> 16.7 us
    all_to_all x1, waiting for transfers between devices: 42.8 us -> 33.3 us  [local(): kv = lax.all_to_all(send, 'dp', 0, 0, tiled=True)]
    all_to_all x1, waiting for transfers between devices: 8.52 us -> 0.01 us  [local(): lax.all_to_all(shares, 'dp', 0, 0, tiled=True, axis_index_groups=Z_GROUPS)]
  transfers between devices with their start and end apart: 36 -> 37, of which waited for: 16 -> 15; matrix products, arithmetic and copies ran while one was open for 4% -> 3% of each run, Pallas kernels for 7% -> 12%
where the time goes in v7:
time: 229 us; the launch traced here: 228 us
  waiting for transfers between devices  101 us (44%)
  starting transfers between devices  64.2 us (28%)
  Pallas kernels  36.4 us (16%)
  local copies, waits for them, and re-layouts  21.8 us (10%)
  other arithmetic  3.63 us (2%)
    all_to_all x1, waiting for transfers between devices, local(): kv = lax.all_to_all(send, 'dp', 0, 0, tiled=True)  33.3 us
    all_to_all x1, waiting for transfers between devices, local(): parts = lax.all_to_all(parts, 'dp', 0, 0, tiled=True)  21.2 us
    ppermute x13, starting transfers between devices, shift_y(): return lax.ppermute(x, 'dp', pairs)  20 us
    ppermute x14, starting transfers between devices, shift_z(): return lax.ppermute(x, 'dp', pairs)  19.4 us
    ppermute x14, waiting for transfers between devices, shift_z(): return lax.ppermute(x, 'dp', pairs)  18.4 us
    unnamed x70, local copies, waits for them, and re-layouts  16.7 us
    ppermute x3, waiting for transfers between devices, local(): terms[s] = lax.ppermute(terms[s], 'tensor', pairs)  16.2 us
    ppermute x13, waiting for transfers between devices, shift_y(): return lax.ppermute(x, 'dp', pairs)  11.9 us
  transfers between devices with their start and end apart: 37, of which 15 were waited for; matrix products, arithmetic and copies ran while one was open for 3% of the time, Pallas kernels for 12%

profile of v7, /device:TPU:32, one launch (start us, length us, event | category | flops | bytes accessed | tf_op | source)
XLA Modules:
  0.0 228.2 jit_solution(7984276297427220269)
XLA Ops:
  0.6 2.0 collective-permute-start
  2.7 3.2 %collective-permute-start.12 = (bf16[256,128]{1,0:T(8,128)(2,1)}, bf16[256,128]{1,0:T(8,128)(2,1)S(1)}, u32[]{:S(2)}, u32[]{:S(2)}) collective-permute-start(bf16[256,128]{1,0:T(8,128)(2,1)} %param.12), channel_id=1, source_target_pairs={{0,128},{8,136},{16,144},{24,152},{32,160},{40,168},{48,176},{56,1... | collective-permute-start | bytes 196616 | tf_op jit(solution)/shard_map/ppermute | solution.py:422
  10.6 2.1 collective-permute-done.13
  12.7 4.1 %collective-permute-start.15 = (bf16[1024,128]{1,0:T(8,128)(2,1)S(1)}, bf16[1024,128]{1,0:T(8,128)(2,1)S(1)}, u32[]{:S(2)}, u32[]{:S(2)}) collective-permute-start(bf16[1024,128]{1,0:T(8,128)(2,1)S(1)} %constant_dynamic-update-slice_fusion.8.refs_5_), channel_id=1, source_target_pairs={{0,56},{8,0},{16,8},{24,16},{32,24},{40,32},{48,40},{56,48},{64,12... | collective-permute-start | bytes 786440 | tf_op jit(solution)/shard_map/ppermute | solution.py:427
  17.8 1.1 collective-permute-start.3
  19.0 5.0 %collective-permute-done.2 = bf16[256,128]{1,0:T(8,128)(2,1)S(1)} collective-permute-done((bf16[256,128]{1,0:T(8,128)(2,1)S(1)}, bf16[256,128]{1,0:T(8,128)(2,1)S(1)}, u32[]{:S(2)}, u32[]{:S(2)}) %collective-permute-start.2) | collective-permute-done | bytes 65568 | tf_op jit(solution)/shard_map/ppermute | solution.py:427
  24.7 2.3 %collective-permute-start.5 = (bf16[256,128]{1,0:T(8,128)(2,1)S(1)}, bf16[256,128]{1,0:T(8,128)(2,1)S(1)}, u32[]{:S(2)}, u32[]{:S(2)}) collective-permute-start(bf16[256,128]{1,0:T(8,128)(2,1)S(1)} %collective-permute-done.3), channel_id=1, source_target_pairs={{0,56},{8,0},{16,8},{24,16},{32,24},{40,32},{48,40},{56,48},{64,12... | collective-permute-start | bytes 196616 | tf_op jit(solution)/shard_map/ppermute | solution.py:427
  27.1 2.9 %collective-permute-done.4 = bf16[256,128]{1,0:T(8,128)(2,1)S(1)} collective-permute-done((bf16[256,128]{1,0:T(8,128)(2,1)S(1)}, bf16[256,128]{1,0:T(8,128)(2,1)S(1)}, u32[]{:S(2)}, u32[]{:S(2)}) %collective-permute-start.4) | collective-permute-done | bytes 65568 | tf_op jit(solution)/shard_map/ppermute | solution.py:427
  30.0 2.0 collective-permute-start.16
  32.1 3.3 %collective-permute-done.6 = bf16[256,128]{1,0:T(8,128)(2,1)S(1)} collective-permute-done((bf16[256,128]{1,0:T(8,128)(2,1)S(1)}, bf16[256,128]{1,0:T(8,128)(2,1)S(1)}, u32[]{:S(2)}, u32[]{:S(2)}) %collective-permute-start.6) | collective-permute-done | bytes 65568 | tf_op jit(solution)/shard_map/ppermute | solution.py:427
  35.5 3.2 %collective-permute-start.7 = (bf16[2048,128]{1,0:T(8,128)(2,1)S(1)}, bf16[2048,128]{1,0:T(8,128)(2,1)S(1)}, u32[]{:S(2)}, u32[]{:S(2)}) collective-permute-start(bf16[2048,128]{1,0:T(8,128)(2,1)S(1)} %constant_dynamic-update-slice_fusion.refs_0_), channel_id=1, source_target_pairs={{0,192},{8,200},{16,208},{24,216},{32,224},{40,232},{48,240},{56,2... | collective-permute-start | bytes 1572872 | tf_op jit(solution)/shard_map/ppermute | solution.py:422
  38.8 3.5 %collective-permute-start.17 = (bf16[1024,128]{1,0:T(8,128)(2,1)S(1)}, bf16[1024,128]{1,0:T(8,128)(2,1)S(1)}, u32[]{:S(2)}, u32[]{:S(2)}) collective-permute-start(bf16[1024,128]{1,0:T(8,128)(2,1)S(1)} %collective-permute-done.15.refs_7_), channel_id=1, source_target_pairs={{0,56},{8,0},{16,8},{24,16},{32,24},{40,32},{48,40},{56,48},{64,12... | collective-permute-start | bytes 786440 | tf_op jit(solution)/shard_map/ppermute | solution.py:427
  42.5 4.4 %collective-permute-done.17.refs_9_ = bf16[1024,128]{1,0:T(8,128)(2,1)S(1)} collective-permute-done((bf16[1024,128]{1,0:T(8,128)(2,1)S(1)}, bf16[1024,128]{1,0:T(8,128)(2,1)S(1)}, u32[]{:S(2)}, u32[]{:S(2)}) %collective-permute-start.17) | collective-permute-done | bytes 262176 | tf_op jit(solution)/shard_map/ppermute | solution.py:427
  46.9 2.5 %collective-permute-start.19 = (bf16[1024,128]{1,0:T(8,128)(2,1)S(1)}, bf16[1024,128]{1,0:T(8,128)(2,1)S(1)}, u32[]{:S(2)}, u32[]{:S(2)}) collective-permute-start(bf16[1024,128]{1,0:T(8,128)(2,1)S(1)} %collective-permute-done.17.refs_9_), channel_id=1, source_target_pairs={{0,56},{8,0},{16,8},{24,16},{32,24},{40,32},{48,40},{56,48},{64,12... | collective-permute-start | bytes 786440 | tf_op jit(solution)/shard_map/ppermute | solution.py:427
  50.8 3.2 %collective-permute-start.9 = (bf16[1024,128]{1,0:T(8,128)(2,1)}, bf16[1024,128]{1,0:T(8,128)(2,1)}, u32[]{:S(2)}, u32[]{:S(2)}) collective-permute-start(bf16[1024,128]{1,0:T(8,128)(2,1)} %slice.26), channel_id=1, source_target_pairs={{0,192},{8,200},{16,208},{24,216},{32,224},{40,232},{48,240},{56,2... | collective-permute-start | bytes 786440 | tf_op jit(solution)/shard_map/ppermute | solution.py:422
  54.4 3.7 %collective-permute-done.10.refs_4_ = bf16[1024,128]{1,0:T(8,128)(2,1)} collective-permute-done((bf16[1024,128]{1,0:T(8,128)(2,1)}, bf16[1024,128]{1,0:T(8,128)(2,1)}, u32[]{:S(2)}, u32[]{:S(2)}) %collective-permute-start.10) | collective-permute-done | bytes 262176 | tf_op jit(solution)/shard_map/ppermute | solution.py:422
  58.3 2.7 %collective-permute-done.20.refs_12_ = bf16[1024,128]{1,0:T(8,128)(2,1)} collective-permute-done((bf16[1024,128]{1,0:T(8,128)(2,1)S(1)}, bf16[1024,128]{1,0:T(8,128)(2,1)}, u32[]{:S(2)}, u32[]{:S(2)}) %collective-permute-start.20) | collective-permute-done | bytes 262176 | tf_op jit(solution)/shard_map/ppermute | solution.py:427
  61.0 6.0 %project.1 = (bf16[32,128,256]{2,1,0:T(8,128)(2,1)}, f32[256,128]{1,0:T(8,128)}) custom-call(s32[5,32]{1,0:T(8,128)S(1)} %stack.41.table_ref, bf16[256,8192]{1,0:T(8,128)(2,1)} %bitcast.24, bf16[2048,128]{1,0:T(8,128)(2,1)S(1)} %constant_dynamic-update-slice_fusion.refs_0_, bf16[2048,128]{1,0:T(8,128)(2,1)S(1)} %collective-permute-done.7.refs_1_, ...), custom_call_target="tpu_custom_call" | custom-call | flops 1073741824 | bytes 10485760 | tf_op jit(solution)/shard_map/project/pallas_call | solution.py:88
  67.0 8.3 %all-to-all-start = ((bf16[32,128,256]{2,1,0:T(8,128)(2,1)}), bf16[32,128,256]{2,1,0:T(8,128)(2,1)}, u32[]{:S(2)}, u32[]{:S(2)}) async-start(bf16[32,128,256]{2,1,0:T(8,128)(2,1)} %get-tuple-element.55), calls=%async_computation | async-start | bytes 4194304 | tf_op jit(solution)/shard_map/all_to_all | solution.py:490
  75.4 2.7 %dynamic-slice_bitcast_fusion = (bf16[128,2048]{1,0:T(8,128)(2,1)}, bf16[128,2048]{1,0:T(8,128)(2,1)}, bf16[128,2048]{1,0:T(8,128)(2,1)S(1)}, bf16[128,2048]{1,0:T(8,128)(2,1)}) fusion(bf16[2,128,8192]{2,1,0:T(8,128)(2,1)} %param.10, s32[]{:T(128)S(6)} %select_n.86, s32[]{:T(128)S(6)} %select_n.94, s32[]{:T(128)S(6)} %select_n.92, s32[]{:T(128)S(6)} %select_n.90, ...), kind=kLoop, calls=%fused_computation.2 | loop fusion | bytes 4194324 | tf_op jit(solution)/shard_map/squeeze | solution.py:496
  78.1 2.7 %collective-permute-start.23 = (bf16[128,2048]{1,0:T(8,128)(2,1)}, bf16[128,2048]{1,0:T(8,128)(2,1)S(1)}, u32[]{:S(2)}, u32[]{:S(2)}) collective-permute-start(bf16[128,2048]{1,0:T(8,128)(2,1)} %get-tuple-element.109), channel_id=1, source_target_pairs={{0,192},{8,200},{16,208},{24,216},{32,224},{40,232},{48,240},{56,2... | collective-permute-start | bytes 1572872 | tf_op jit(solution)/shard_map/ppermute | solution.py:422
  82.5 33.3 %all-to-all-done.kv_ref = bf16[32,128,256]{2,1,0:T(8,128)(2,1)} async-done(((bf16[32,128,256]{2,1,0:T(8,128)(2,1)}), bf16[32,128,256]{2,1,0:T(8,128)(2,1)}, u32[]{:S(2)}, u32[]{:S(2)}) %all-to-all-start) | async-done | bytes 2097184 | tf_op jit(solution)/shard_map/all_to_all | solution.py:490
  115.8 8.8 %attend.1 = (bf16[32,128,256]{2,1,0:T(8,128)(2,1)}, bf16[32,128,128]{2,1,0:T(8,128)(2,1)}, bf16[32,128,128]{2,1,0:T(8,128)(2,1)}) custom-call(s32[5,32]{1,0:T(8,128)S(1)} %stack.41.table_ref, bf16[512,1024]{1,0:T(8,128)(2,1)} %q_ref.1, bf16[512,1024]{1,0:T(8,128)(2,1)} %ct_ref.1, bf16[32,128,256]{2,1,0:T(8,128)(2,1)} %all-to-all-done.kv_ref), custom_call_target="tpu_custom_call" | custom-call | flops 536870912 | bytes 8388608 | tf_op jit(solution)/shard_map/attend/pallas_call | solution.py:182
  125.7 5.8 %all-to-all-start.1 = ((bf16[32,128,256]{2,1,0:T(8,128)(2,1)}), bf16[32,128,256]{2,1,0:T(8,128)(2,1)}, u32[]{:S(2)}, u32[]{:S(2)}) async-start(bf16[32,128,256]{2,1,0:T(8,128)(2,1)} %get-tuple-element.59), calls=%async_computation.1 | async-start | bytes 4194304 | tf_op jit(solution)/shard_map/all_to_all | solution.py:506
  137.3 4.1 %assemble.1 = (bf16[8192,128]{1,0:T(8,128)(2,1)}, bf16[8192,128]{1,0:T(8,128)(2,1)}) custom-call(s32[5,32]{1,0:T(8,128)S(1)} %stack.41.table_ref, bf16[2048,128]{1,0:T(8,128)(2,1)S(1)} %copy-done.1, bf16[2048,128]{1,0:T(8,128)(2,1)S(1)} %collective-permute-done.7.refs_1_, bf16[2048,128]{1,0:T(8,128)(2,1)S(1)} %collective-permute-done.8.refs_2_, ...), custom_call_target="tpu_custom_call" | custom-call | bytes 1048576 | tf_op jit(solution)/shard_map/assemble/pallas_call | solution.py:337
  141.9 6.2 %apply.1 = (bf16[512,1024]{1,0:T(8,128)(2,1)}, bf16[512,1024]{1,0:T(8,128)(2,1)}) custom-call(s32[5,32]{1,0:T(8,128)S(1)} %stack.41.table_ref, bf16[32,128,256]{2,1,0:T(8,128)(2,1)} %all-to-all-done.kv_ref, bf16[32,128,128]{2,1,0:T(8,128)(2,1)} %get-tuple-element.64.probs_ref, bf16[32,128,128]{2,1,0:T(8,128)(2,1)} %get-tuple-element.65.ds_ref), custom_call_target="tpu_custom_call" | custom-call | flops 268435456 | bytes 6291456 | tf_op jit(solution)/shard_map/apply/pallas_call | solution.py:221
  148.1 1.3 copy-done.6
  149.4 1.3 copy-done.4
  150.7 1.4 copy-done.8
  152.1 21.2 %all-to-all-done.1.part_ref = bf16[32,128,256]{2,1,0:T(8,128)(2,1)} async-done(((bf16[32,128,256]{2,1,0:T(8,128)(2,1)}), bf16[32,128,256]{2,1,0:T(8,128)(2,1)}, u32[]{:S(2)}, u32[]{:S(2)}) %all-to-all-start.1) | async-done | bytes 2097184 | tf_op jit(solution)/shard_map/all_to_all | solution.py:506
  173.3 3.0 %owner_grads.1 = (bf16[256,256]{1,0:T(8,128)(2,1)S(1)}, bf16[256,256]{1,0:T(8,128)(2,1)S(1)}) custom-call(s32[5,32]{1,0:T(8,128)S(1)} %stack.41.table_ref, bf16[32,128,256]{2,1,0:T(8,128)(2,1)} %all-to-all-done.1.part_ref, f32[256,128]{1,0:T(8,128)} %get-tuple-element.57.raw_ref, f32[1,128]{1,0:T(1,128)S(1)} %bitcast.23), custom_call_target="tpu_custom_call" | custom-call | bytes 3145728 | tf_op jit(solution)/shard_map/owner_grads/pallas_call | solution.py:267
  176.3 1.6 collective-permute-start.29
  177.8 2.0 collective-permute-start.28
  180.1 1.4 collective-permute-done.29.refs_3_
  181.5 2.8 %collective-permute-done.28.refs_2_ = bf16[256,256]{1,0:T(8,128)(2,1)S(1)} collective-permute-done((bf16[256,256]{1,0:T(8,128)(2,1)S(1)}, bf16[256,256]{1,0:T(8,128)(2,1)S(1)}, u32[]{:S(2)}, u32[]{:S(2)}) %collective-permute-start.28) | collective-permute-done | bytes 131104 | tf_op jit(solution)/shard_map/ppermute | solution.py:422
  184.3 1.7 collective-permute-done.27.refs_1_
  186.0 2.2 weight_terms.1
  188.3 4.3 %all-to-all-start.2 = ((bf16[8,256,256]{2,1,0:T(8,128)(2,1)}), bf16[8,256,256]{2,1,0:T(8,128)(2,1)}, u32[]{:S(2)}, u32[]{:S(2)}) async-start(bf16[8,256,256]{2,1,0:T(8,128)(2,1)} %weight_terms.1), calls=%async_computation.2 | async-start | bytes 2097152 | tf_op jit(solution)/shard_map/all_to_all | solution.py:521
  192.6 1.6 copy-done.3
  194.2 1.6 copy-done.5
  195.8 1.6 copy-done.9
  197.4 5.6 %feature_terms.1 = (bf16[32,8192]{1,0:T(8,128)(2,1)S(1)}, bf16[32,8192]{1,0:T(8,128)(2,1)S(1)}, bf16[32,8192]{1,0:T(8,128)(2,1)S(1)}, bf16[32,8192]{1,0:T(8,128)(2,1)S(1)}) custom-call(s32[5,32]{1,0:T(8,128)S(1)} %stack.41.table_ref, bf16[256,256]{1,0:T(8,128)(2,1)S(1)} %get-tuple-element.90.own_ref, bf16[256,256]{1,0:T(8,128)(2,1)S(1)} %collective-permute-done.30.other_ref, ...), custom_call_target="tpu_custom_call" | custom-call | flops 2147483648 | bytes 10485760 | tf_op jit(solution)/shard_map/feature_terms/pallas_call | solution.py:398
  203.0 1.6 collective-permute-start.31
  204.6 2.6 %collective-permute-start.32 = (bf16[32,8192]{1,0:T(8,128)(2,1)S(1)}, bf16[32,8192]{1,0:T(8,128)(2,1)S(1)}, u32[]{:S(2)}, u32[]{:S(2)}) collective-permute-start(bf16[32,8192]{1,0:T(8,128)(2,1)S(1)} %get-tuple-element.98), channel_id=1, source_target_pairs={{0,4},{1,5},{2,6},{3,7},{4,0},{5,1},{6,2},{7,3},{8,12},{9,13},{10,... | collective-permute-start | bytes 1572872 | tf_op jit(solution)/shard_map/ppermute | solution.py:526
  207.2 1.5 collective-permute-start.33
  208.8 10.3 %collective-permute-done.31 = bf16[32,8192]{1,0:T(8,128)(2,1)S(1)} collective-permute-done((bf16[32,8192]{1,0:T(8,128)(2,1)S(1)}, bf16[32,8192]{1,0:T(8,128)(2,1)S(1)}, u32[]{:S(2)}, u32[]{:S(2)}) %collective-permute-start.31) | collective-permute-done | bytes 524320 | tf_op jit(solution)/shard_map/ppermute | solution.py:526
  219.1 5.9 %collective-permute-done.32 = bf16[32,8192]{1,0:T(8,128)(2,1)S(1)} collective-permute-done((bf16[32,8192]{1,0:T(8,128)(2,1)S(1)}, bf16[32,8192]{1,0:T(8,128)(2,1)S(1)}, u32[]{:S(2)}, u32[]{:S(2)}) %collective-permute-start.32) | collective-permute-done | bytes 524320 | tf_op jit(solution)/shard_map/ppermute | solution.py:526
  225.0 1.4 convert_reduce_fusion
  (123 shorter events, 19.9 us)
Async XLA Ops:
  0.6 60.3 %copy-start.29 = (f32[128]{0:T(128)S(1)}, f32[128]{0:T(128)}, u32[]{:S(2)}) copy-start(f32[128]{0:T(128)} %param.13) | copy-start | bytes 1540
  0.6 16.2 %collective-permute-start = (bf16[256,128]{1,0:T(8,128)(2,1)}, bf16[256,128]{1,0:T(8,128)(2,1)S(1)}, u32[]{:S(2)}, u32[]{:S(2)}) collective-permute-start(bf16[256,128]{1,0:T(8,128)(2,1)} %param.11), channel_id=1, source_target_pairs={{0,8},{8,16},{16,24},{24,32},{32,40},{40,48},{48,56},{56,0},{64,72... | collective-permute-start | bytes 196616 | tf_op jit(solution)/shard_map/ppermute | solution.py:427
  2.6 15.2 %collective-permute-start.1 = (bf16[256,128]{1,0:T(8,128)(2,1)}, bf16[256,128]{1,0:T(8,128)(2,1)S(1)}, u32[]{:S(2)}, u32[]{:S(2)}) collective-permute-start(bf16[256,128]{1,0:T(8,128)(2,1)} %param.11), channel_id=1, source_target_pairs={{0,56},{8,0},{16,8},{24,16},{32,24},{40,32},{48,40},{56,48},{64,12... | collective-permute-start | bytes 196616 | tf_op jit(solution)/shard_map/ppermute | solution.py:427
  2.7 7.9 %collective-permute-start.12 = (bf16[256,128]{1,0:T(8,128)(2,1)}, bf16[256,128]{1,0:T(8,128)(2,1)S(1)}, u32[]{:S(2)}, u32[]{:S(2)}) collective-permute-start(bf16[256,128]{1,0:T(8,128)(2,1)} %param.12), channel_id=1, source_target_pairs={{0,128},{8,136},{16,144},{24,152},{32,160},{40,168},{48,176},{56,1... | collective-permute-start | bytes 196616 | tf_op jit(solution)/shard_map/ppermute | solution.py:422
  5.9 4.6 %collective-permute-start.11 = (bf16[256,128]{1,0:T(8,128)(2,1)}, bf16[256,128]{1,0:T(8,128)(2,1)S(1)}, u32[]{:S(2)}, u32[]{:S(2)}) collective-permute-start(bf16[256,128]{1,0:T(8,128)(2,1)} %param.12), channel_id=1, source_target_pairs={{0,192},{8,200},{16,208},{24,216},{32,224},{40,232},{48,240},{56,2... | collective-permute-start | bytes 196616 | tf_op jit(solution)/shard_map/ppermute | solution.py:422
  7.0 5.7 %collective-permute-start.13 = (bf16[256,128]{1,0:T(8,128)(2,1)}, bf16[256,128]{1,0:T(8,128)(2,1)S(1)}, u32[]{:S(2)}, u32[]{:S(2)}) collective-permute-start(bf16[256,128]{1,0:T(8,128)(2,1)} %param.12), channel_id=1, source_target_pairs={{0,64},{8,72},{16,80},{24,88},{32,96},{40,104},{48,112},{56,120},{... | collective-permute-start | bytes 196616 | tf_op jit(solution)/shard_map/ppermute | solution.py:422
  12.7 26.1 %collective-permute-start.15 = (bf16[1024,128]{1,0:T(8,128)(2,1)S(1)}, bf16[1024,128]{1,0:T(8,128)(2,1)S(1)}, u32[]{:S(2)}, u32[]{:S(2)}) collective-permute-start(bf16[1024,128]{1,0:T(8,128)(2,1)S(1)} %constant_dynamic-update-slice_fusion.8.refs_5_), channel_id=1, source_target_pairs={{0,56},{8,0},{16,8},{24,16},{32,24},{40,32},{48,40},{56,48},{64,12... | collective-permute-start | bytes 786440 | tf_op jit(solution)/shard_map/ppermute | solution.py:427
  16.8 13.2 %collective-permute-start.14 = (bf16[1024,128]{1,0:T(8,128)(2,1)S(1)}, bf16[1024,128]{1,0:T(8,128)(2,1)S(1)}, u32[]{:S(2)}, u32[]{:S(2)}) collective-permute-start(bf16[1024,128]{1,0:T(8,128)(2,1)S(1)} %constant_dynamic-update-slice_fusion.8.refs_5_), channel_id=1, source_target_pairs={{0,8},{8,16},{16,24},{24,32},{32,40},{40,48},{48,56},{56,0},{64,72... | collective-permute-start | bytes 786440 | tf_op jit(solution)/shard_map/ppermute | solution.py:427
  16.8 7.2 %collective-permute-start.2 = (bf16[256,128]{1,0:T(8,128)(2,1)S(1)}, bf16[256,128]{1,0:T(8,128)(2,1)S(1)}, u32[]{:S(2)}, u32[]{:S(2)}) collective-permute-start(bf16[256,128]{1,0:T(8,128)(2,1)S(1)} %collective-permute-done), channel_id=1, source_target_pairs={{0,8},{8,16},{16,24},{24,32},{32,40},{40,48},{48,56},{56,0},{64,72... | collective-permute-start | bytes 196616 | tf_op jit(solution)/shard_map/ppermute | solution.py:427
  17.8 6.9 %collective-permute-start.3 = (bf16[256,128]{1,0:T(8,128)(2,1)S(1)}, bf16[256,128]{1,0:T(8,128)(2,1)S(1)}, u32[]{:S(2)}, u32[]{:S(2)}) collective-permute-start(bf16[256,128]{1,0:T(8,128)(2,1)S(1)} %collective-permute-done.1), channel_id=1, source_target_pairs={{0,56},{8,0},{16,8},{24,16},{32,24},{40,32},{48,40},{56,48},{64,12... | collective-permute-start | bytes 196616 | tf_op jit(solution)/shard_map/ppermute | solution.py:427
  24.0 6.0 %collective-permute-start.4 = (bf16[256,128]{1,0:T(8,128)(2,1)S(1)}, bf16[256,128]{1,0:T(8,128)(2,1)S(1)}, u32[]{:S(2)}, u32[]{:S(2)}) collective-permute-start(bf16[256,128]{1,0:T(8,128)(2,1)S(1)} %collective-permute-done.2), channel_id=1, source_target_pairs={{0,8},{8,16},{16,24},{24,32},{32,40},{40,48},{48,56},{56,0},{64,72... | collective-permute-start | bytes 196616 | tf_op jit(solution)/shard_map/ppermute | solution.py:427
  24.7 5.3 %collective-permute-start.5 = (bf16[256,128]{1,0:T(8,128)(2,1)S(1)}, bf16[256,128]{1,0:T(8,128)(2,1)S(1)}, u32[]{:S(2)}, u32[]{:S(2)}) collective-permute-start(bf16[256,128]{1,0:T(8,128)(2,1)S(1)} %collective-permute-done.3), channel_id=1, source_target_pairs={{0,56},{8,0},{16,8},{24,16},{32,24},{40,32},{48,40},{56,48},{64,12... | collective-permute-start | bytes 196616 | tf_op jit(solution)/shard_map/ppermute | solution.py:427
  30.0 5.4 %collective-permute-start.6 = (bf16[256,128]{1,0:T(8,128)(2,1)S(1)}, bf16[256,128]{1,0:T(8,128)(2,1)S(1)}, u32[]{:S(2)}, u32[]{:S(2)}) collective-permute-start(bf16[256,128]{1,0:T(8,128)(2,1)S(1)} %collective-permute-done.4), channel_id=1, source_target_pairs={{0,8},{8,16},{16,24},{24,32},{32,40},{40,48},{48,56},{56,0},{64,72... | collective-permute-start | bytes 196616 | tf_op jit(solution)/shard_map/ppermute | solution.py:427
  30.0 36.9 %copy-start.13 = (bf16[1024,128]{1,0:T(8,128)(2,1)}, bf16[1024,128]{1,0:T(8,128)(2,1)S(1)}, u32[]{:S(2)}) copy-start(bf16[1024,128]{1,0:T(8,128)(2,1)S(1)} %collective-permute-done.14.refs_6_) | copy-start | bytes 786436
  30.0 12.3 %collective-permute-start.16 = (bf16[1024,128]{1,0:T(8,128)(2,1)S(1)}, bf16[1024,128]{1,0:T(8,128)(2,1)S(1)}, u32[]{:S(2)}, u32[]{:S(2)}) collective-permute-start(bf16[1024,128]{1,0:T(8,128)(2,1)S(1)} %collective-permute-done.14.refs_6_), channel_id=1, source_target_pairs={{0,8},{8,16},{16,24},{24,32},{32,40},{40,48},{48,56},{56,0},{64,72... | collective-permute-start | bytes 786440 | tf_op jit(solution)/shard_map/ppermute | solution.py:427
  35.4 31.6 %copy-start = (bf16[2048,128]{1,0:T(8,128)(2,1)}, bf16[2048,128]{1,0:T(8,128)(2,1)S(1)}, u32[]{:S(2)}) copy-start(bf16[2048,128]{1,0:T(8,128)(2,1)S(1)} %constant_dynamic-update-slice_fusion.refs_0_) | copy-start | bytes 1572868
  35.4 14.0 %collective-permute-start.8 = (bf16[2048,128]{1,0:T(8,128)(2,1)S(1)}, bf16[2048,128]{1,0:T(8,128)(2,1)S(1)}, u32[]{:S(2)}, u32[]{:S(2)}) collective-permute-start(bf16[2048,128]{1,0:T(8,128)(2,1)S(1)} %constant_dynamic-update-slice_fusion.refs_0_), channel_id=1, source_target_pairs={{0,64},{8,72},{16,80},{24,88},{32,96},{40,104},{48,112},{56,120},{... | collective-permute-start | bytes 1572872 | tf_op jit(solution)/shard_map/ppermute | solution.py:422
  35.5 14.6 %collective-permute-start.7 = (bf16[2048,128]{1,0:T(8,128)(2,1)S(1)}, bf16[2048,128]{1,0:T(8,128)(2,1)S(1)}, u32[]{:S(2)}, u32[]{:S(2)}) collective-permute-start(bf16[2048,128]{1,0:T(8,128)(2,1)S(1)} %constant_dynamic-update-slice_fusion.refs_0_), channel_id=1, source_target_pairs={{0,192},{8,200},{16,208},{24,216},{32,224},{40,232},{48,240},{56,2... | collective-permute-start | bytes 1572872 | tf_op jit(solution)/shard_map/ppermute | solution.py:422
  38.8 28.1 %copy-start.11 = (bf16[1024,128]{1,0:T(8,128)(2,1)}, bf16[1024,128]{1,0:T(8,128)(2,1)S(1)}, u32[]{:S(2)}) copy-start(bf16[1024,128]{1,0:T(8,128)(2,1)S(1)} %collective-permute-done.15.refs_7_) | copy-start | bytes 786436
  38.8 8.1 %collective-permute-start.17 = (bf16[1024,128]{1,0:T(8,128)(2,1)S(1)}, bf16[1024,128]{1,0:T(8,128)(2,1)S(1)}, u32[]{:S(2)}, u32[]{:S(2)}) collective-permute-start(bf16[1024,128]{1,0:T(8,128)(2,1)S(1)} %collective-permute-done.15.refs_7_), channel_id=1, source_target_pairs={{0,56},{8,0},{16,8},{24,16},{32,24},{40,32},{48,40},{56,48},{64,12... | collective-permute-start | bytes 786440 | tf_op jit(solution)/shard_map/ppermute | solution.py:427
  42.3 24.6 %copy-start.15 = (bf16[1024,128]{1,0:T(8,128)(2,1)}, bf16[1024,128]{1,0:T(8,128)(2,1)S(1)}, u32[]{:S(2)}) copy-start(bf16[1024,128]{1,0:T(8,128)(2,1)S(1)} %collective-permute-done.16.refs_8_) | copy-start | bytes 786436
  42.3 11.8 %collective-permute-start.18 = (bf16[1024,128]{1,0:T(8,128)(2,1)S(1)}, bf16[1024,128]{1,0:T(8,128)(2,1)S(1)}, u32[]{:S(2)}, u32[]{:S(2)}) collective-permute-start(bf16[1024,128]{1,0:T(8,128)(2,1)S(1)} %collective-permute-done.16.refs_8_), channel_id=1, source_target_pairs={{0,8},{8,16},{16,24},{24,32},{32,40},{40,48},{48,56},{56,0},{64,72... | collective-permute-start | bytes 786440 | tf_op jit(solution)/shard_map/ppermute | solution.py:427
  46.9 20.0 %copy-start.17 = (bf16[1024,128]{1,0:T(8,128)(2,1)}, bf16[1024,128]{1,0:T(8,128)(2,1)S(1)}, u32[]{:S(2)}) copy-start(bf16[1024,128]{1,0:T(8,128)(2,1)S(1)} %collective-permute-done.17.refs_9_) | copy-start | bytes 786436
  46.9 7.4 %collective-permute-start.19 = (bf16[1024,128]{1,0:T(8,128)(2,1)S(1)}, bf16[1024,128]{1,0:T(8,128)(2,1)S(1)}, u32[]{:S(2)}, u32[]{:S(2)}) collective-permute-start(bf16[1024,128]{1,0:T(8,128)(2,1)S(1)} %collective-permute-done.17.refs_9_), channel_id=1, source_target_pairs={{0,56},{8,0},{16,8},{24,16},{32,24},{40,32},{48,40},{56,48},{64,12... | collective-permute-start | bytes 786440 | tf_op jit(solution)/shard_map/ppermute | solution.py:427
  50.1 7.9 %collective-permute-start.10 = (bf16[1024,128]{1,0:T(8,128)(2,1)}, bf16[1024,128]{1,0:T(8,128)(2,1)}, u32[]{:S(2)}, u32[]{:S(2)}) collective-permute-start(bf16[1024,128]{1,0:T(8,128)(2,1)} %slice.27), channel_id=1, source_target_pairs={{0,64},{8,72},{16,80},{24,88},{32,96},{40,104},{48,112},{56,120},{... | collective-permute-start | bytes 786440 | tf_op jit(solution)/shard_map/ppermute | solution.py:422
  50.8 7.4 %collective-permute-start.9 = (bf16[1024,128]{1,0:T(8,128)(2,1)}, bf16[1024,128]{1,0:T(8,128)(2,1)}, u32[]{:S(2)}, u32[]{:S(2)}) collective-permute-start(bf16[1024,128]{1,0:T(8,128)(2,1)} %slice.26), channel_id=1, source_target_pairs={{0,192},{8,200},{16,208},{24,216},{32,224},{40,232},{48,240},{56,2... | collective-permute-start | bytes 786440 | tf_op jit(solution)/shard_map/ppermute | solution.py:422
  54.1 12.9 %copy-start.19 = (bf16[1024,128]{1,0:T(8,128)(2,1)}, bf16[1024,128]{1,0:T(8,128)(2,1)S(1)}, u32[]{:S(2)}) copy-start(bf16[1024,128]{1,0:T(8,128)(2,1)S(1)} %collective-permute-done.18.refs_10_) | copy-start | bytes 786436
  54.1 6.9 %collective-permute-start.20 = (bf16[1024,128]{1,0:T(8,128)(2,1)S(1)}, bf16[1024,128]{1,0:T(8,128)(2,1)}, u32[]{:S(2)}, u32[]{:S(2)}) collective-permute-start(bf16[1024,128]{1,0:T(8,128)(2,1)S(1)} %collective-permute-done.18.refs_10_), channel_id=1, source_target_pairs={{0,8},{8,16},{16,24},{24,32},{32,40},{40,48},{48,56},{56,0},{64,72... | collective-permute-start | bytes 786440 | tf_op jit(solution)/shard_map/ppermute | solution.py:427
  54.3 12.6 %copy-start.21 = (bf16[1024,128]{1,0:T(8,128)(2,1)}, bf16[1024,128]{1,0:T(8,128)(2,1)S(1)}, u32[]{:S(2)}) copy-start(bf16[1024,128]{1,0:T(8,128)(2,1)S(1)} %collective-permute-done.19.refs_11_) | copy-start | bytes 786436
  67.0 48.8 %all-to-all-start = ((bf16[32,128,256]{2,1,0:T(8,128)(2,1)}), bf16[32,128,256]{2,1,0:T(8,128)(2,1)}, u32[]{:S(2)}, u32[]{:S(2)}) async-start(bf16[32,128,256]{2,1,0:T(8,128)(2,1)} %get-tuple-element.55), calls=%async_computation | async-start | bytes 4194304 | tf_op jit(solution)/shard_map/all_to_all | solution.py:490
  78.1 46.5 %collective-permute-start.23 = (bf16[128,2048]{1,0:T(8,128)(2,1)}, bf16[128,2048]{1,0:T(8,128)(2,1)S(1)}, u32[]{:S(2)}, u32[]{:S(2)}) collective-permute-start(bf16[128,2048]{1,0:T(8,128)(2,1)} %get-tuple-element.109), channel_id=1, source_target_pairs={{0,192},{8,200},{16,208},{24,216},{32,224},{40,232},{48,240},{56,2... | collective-permute-start | bytes 1572872 | tf_op jit(solution)/shard_map/ppermute | solution.py:422
  80.8 43.8 %collective-permute-start.22 = (bf16[128,2048]{1,0:T(8,128)(2,1)}, bf16[128,2048]{1,0:T(8,128)(2,1)S(1)}, u32[]{:S(2)}, u32[]{:S(2)}) collective-permute-start(bf16[128,2048]{1,0:T(8,128)(2,1)} %get-tuple-element.110), channel_id=1, source_target_pairs={{0,128},{8,136},{16,144},{24,152},{32,160},{40,168},{48,176},{56,1... | collective-permute-start | bytes 1572872 | tf_op jit(solution)/shard_map/ppermute | solution.py:422
  81.6 43.0 %collective-permute-start.21 = (bf16[128,2048]{1,0:T(8,128)(2,1)S(1)}, bf16[128,2048]{1,0:T(8,128)(2,1)S(1)}, u32[]{:S(2)}, u32[]{:S(2)}) collective-permute-start(bf16[128,2048]{1,0:T(8,128)(2,1)S(1)} %get-tuple-element.111), channel_id=1, source_target_pairs={{0,64},{8,72},{16,80},{24,88},{32,96},{40,104},{48,112},{56,120},{... | collective-permute-start | bytes 1572872 | tf_op jit(solution)/shard_map/ppermute | solution.py:422
  125.7 47.5 %all-to-all-start.1 = ((bf16[32,128,256]{2,1,0:T(8,128)(2,1)}), bf16[32,128,256]{2,1,0:T(8,128)(2,1)}, u32[]{:S(2)}, u32[]{:S(2)}) async-start(bf16[32,128,256]{2,1,0:T(8,128)(2,1)} %get-tuple-element.59), calls=%async_computation.1 | async-start | bytes 4194304 | tf_op jit(solution)/shard_map/all_to_all | solution.py:506
  136.4 11.6 %collective-permute-start.24 = (bf16[2048,512]{1,0:T(8,128)(2,1)S(1)}, bf16[2048,512]{1,0:T(8,128)(2,1)S(1)}, u32[]{:S(2)}, u32[]{:S(2)}) collective-permute-start(bf16[2048,512]{1,0:T(8,128)(2,1)S(1)} %transpose_pieces.1.own_ref), channel_id=1, source_target_pairs={{0,1},{1,0},{2,3},{3,2},{4,5},{5,4},{6,7},{7,6},{8,9},{9,8},{10,11... | collective-permute-start | bytes 6291464 | tf_op jit(solution)/shard_map/ppermute | solution.py:443
  141.4 8.0 %collective-permute-start.25 = (bf16[8192,128]{1,0:T(8,128)(2,1)}, bf16[8192,128]{1,0:T(8,128)(2,1)S(1)}, u32[]{:S(2)}, u32[]{:S(2)}) collective-permute-start(bf16[8192,128]{1,0:T(8,128)(2,1)} %get-tuple-element.92.refs_0_), channel_id=1, source_target_pairs={{0,1},{1,0},{2,3},{3,2},{4,5},{5,4},{6,7},{7,6},{8,9},{9,8},{10,11... | collective-permute-start | bytes 6291464 | tf_op jit(solution)/shard_map/ppermute | solution.py:443
  141.4 9.3 %collective-permute-start.26 = (bf16[8192,128]{1,0:T(8,128)(2,1)}, bf16[8192,128]{1,0:T(8,128)(2,1)S(1)}, u32[]{:S(2)}, u32[]{:S(2)}) collective-permute-start(bf16[8192,128]{1,0:T(8,128)(2,1)} %get-tuple-element.93.refs_1_), channel_id=1, source_target_pairs={{0,1},{1,0},{2,3},{3,2},{4,5},{5,4},{6,7},{7,6},{8,9},{9,8},{10,11... | collective-permute-start | bytes 6291464 | tf_op jit(solution)/shard_map/ppermute | solution.py:443
  173.3 12.8 %copy-start.7 = (bf16[2048,512]{1,0:T(8,128)(2,1)S(1)}, bf16[2048,512]{1,0:T(8,128)(2,1)}, u32[]{:S(2)}) copy-start(bf16[2048,512]{1,0:T(8,128)(2,1)} %copy-done.6) | copy-start | bytes 6291460
  176.3 5.3 %collective-permute-start.29 = (bf16[256,256]{1,0:T(8,128)(2,1)S(1)}, bf16[256,256]{1,0:T(8,128)(2,1)S(1)}, u32[]{:S(2)}, u32[]{:S(2)}) collective-permute-start(bf16[256,256]{1,0:T(8,128)(2,1)S(1)} %get-tuple-element.87.refs_0_), channel_id=1, source_target_pairs={{0,192},{8,200},{16,208},{24,216},{32,224},{40,232},{48,240},{56,2... | collective-permute-start | bytes 393224 | tf_op jit(solution)/shard_map/ppermute | solution.py:422
  177.8 6.5 %collective-permute-start.28 = (bf16[256,256]{1,0:T(8,128)(2,1)S(1)}, bf16[256,256]{1,0:T(8,128)(2,1)S(1)}, u32[]{:S(2)}, u32[]{:S(2)}) collective-permute-start(bf16[256,256]{1,0:T(8,128)(2,1)S(1)} %get-tuple-element.87.refs_0_), channel_id=1, source_target_pairs={{0,128},{8,136},{16,144},{24,152},{32,160},{40,168},{48,176},{56,1... | collective-permute-start | bytes 393224 | tf_op jit(solution)/shard_map/ppermute | solution.py:422
  179.9 6.2 %collective-permute-start.27 = (bf16[256,256]{1,0:T(8,128)(2,1)S(1)}, bf16[256,256]{1,0:T(8,128)(2,1)S(1)}, u32[]{:S(2)}, u32[]{:S(2)}) collective-permute-start(bf16[256,256]{1,0:T(8,128)(2,1)S(1)} %get-tuple-element.87.refs_0_), channel_id=1, source_target_pairs={{0,64},{8,72},{16,80},{24,88},{32,96},{40,104},{48,112},{56,120},{... | collective-permute-start | bytes 393224 | tf_op jit(solution)/shard_map/ppermute | solution.py:422
  180.1 8.2 %collective-permute-start.30 = (bf16[256,256]{1,0:T(8,128)(2,1)S(1)}, bf16[256,256]{1,0:T(8,128)(2,1)S(1)}, u32[]{:S(2)}, u32[]{:S(2)}) collective-permute-start(bf16[256,256]{1,0:T(8,128)(2,1)S(1)} %get-tuple-element.90.own_ref), channel_id=1, source_target_pairs={{0,1},{1,0},{2,3},{3,2},{4,5},{5,4},{6,7},{7,6},{8,9},{9,8},{10,11... | collective-permute-start | bytes 393224 | tf_op jit(solution)/shard_map/ppermute | solution.py:443
  188.3 4.3 %copy-start.2 = (bf16[8192,128]{1,0:T(8,128)(2,1)S(1)}, bf16[8192,128]{1,0:T(8,128)(2,1)}, u32[]{:S(2)}) copy-start(bf16[8192,128]{1,0:T(8,128)(2,1)} %get-tuple-element.92.refs_0_) | copy-start | bytes 6291460
  188.3 36.7 %all-to-all-start.2 = ((bf16[8,256,256]{2,1,0:T(8,128)(2,1)}), bf16[8,256,256]{2,1,0:T(8,128)(2,1)}, u32[]{:S(2)}, u32[]{:S(2)}) async-start(bf16[8,256,256]{2,1,0:T(8,128)(2,1)} %weight_terms.1), calls=%async_computation.2 | async-start | bytes 2097152 | tf_op jit(solution)/shard_map/all_to_all | solution.py:521
  192.6 1.6 copy-start.3
  203.0 16.1 %collective-permute-start.31 = (bf16[32,8192]{1,0:T(8,128)(2,1)S(1)}, bf16[32,8192]{1,0:T(8,128)(2,1)S(1)}, u32[]{:S(2)}, u32[]{:S(2)}) collective-permute-start(bf16[32,8192]{1,0:T(8,128)(2,1)S(1)} %get-tuple-element.97), channel_id=1, source_target_pairs={{0,2},{1,3},{2,4},{3,5},{4,6},{5,7},{6,0},{7,1},{8,10},{9,11},{10,... | collective-permute-start | bytes 1572872 | tf_op jit(solution)/shard_map/ppermute | solution.py:526
  204.6 20.4 %collective-permute-start.32 = (bf16[32,8192]{1,0:T(8,128)(2,1)S(1)}, bf16[32,8192]{1,0:T(8,128)(2,1)S(1)}, u32[]{:S(2)}, u32[]{:S(2)}) collective-permute-start(bf16[32,8192]{1,0:T(8,128)(2,1)S(1)} %get-tuple-element.98), channel_id=1, source_target_pairs={{0,4},{1,5},{2,6},{3,7},{4,0},{5,1},{6,2},{7,3},{8,12},{9,13},{10,... | collective-permute-start | bytes 1572872 | tf_op jit(solution)/shard_map/ppermute | solution.py:526
  207.2 17.7 %collective-permute-start.33 = (bf16[32,8192]{1,0:T(8,128)(2,1)S(1)}, bf16[32,8192]{1,0:T(8,128)(2,1)S(1)}, u32[]{:S(2)}, u32[]{:S(2)}) collective-permute-start(bf16[32,8192]{1,0:T(8,128)(2,1)S(1)} %get-tuple-element.99), channel_id=1, source_target_pairs={{0,6},{1,7},{2,0},{3,1},{4,2},{5,3},{6,4},{7,5},{8,14},{9,15},{10,... | collective-permute-start | bytes 1572872 | tf_op jit(solution)/shard_map/ppermute | solution.py:526
  (19 other events, 23.1 us)

commit v8 on v7

--- a/solution.py
+++ b/solution.py
@@ -35,10 +35,6 @@
 
 def in_vmem():
     return pl.BlockSpec(memory_space=pltpu.VMEM)
-
-
-def in_hbm():
-    return pl.BlockSpec(memory_space=pltpu.HBM)
 
 
 def weight_blocks(table_ref, w_refs, zones):
@@ -342,7 +338,7 @@
             in_specs=[in_vmem()] * len(pieces),
             out_specs=[in_vmem()] * 2,
         ),
-        out_shape=[pltpu.HBM((width, head_dim), BF16)] * 2,
+        out_shape=[jax.ShapeDtypeStruct((width, head_dim), BF16)] * 2,
         compiler_params=limit(10),
         cost_estimate=cost(0, 1),
         name="assemble",
@@ -350,23 +346,11 @@
 
 
 def feature_kernel(table_ref, own_ref, other_ref, *refs, targets):
-    w_refs, out_refs, (lhs, held, sems) = refs[:4], refs[4:-3], refs[-3:]
+    w_refs, out_refs, lhs = refs[:4], refs[4:-1], refs[-1]
     chips = len(out_refs)
     tokens, head_dim = own_ref.shape[0] // 2, own_ref.shape[1] // 2
     share = tokens // targets
-    steps, block = held.shape[1:3]
-    copies = [
-        [
-            pltpu.make_async_copy(
-                w_ref.at[pl.ds(step * block, block), :], held.at[n, step], sems.at[n, step]
-            )
-            for n, w_ref in enumerate(w_refs)
-        ]
-        for step in range(steps)
-    ]
-    for step in range(steps):
-        for copy in copies[step]:
-            copy.start()
+    block = w_refs[0].shape[0] // NZ
     for core, ref in enumerate((own_ref, other_ref)):
         for chip in range(chips):
             target = lax.rem(table_ref[PLACE, 2] + chip, chips) * 2 + table_ref[PLACE, 3]
@@ -377,36 +361,31 @@
                     lhs[core, n, to : to + share, :] = ref[
                         pl.ds(at, share), n * head_dim : (n + 1) * head_dim
                     ]
-    for step in range(steps):
+    for step in range(NZ):
+        here = slice(step * block, (step + 1) * block)
         part = 0.0
         for core in range(2):
-            for n in range(2):
-                copies[step][2 * core + n].wait()
             left = jnp.concatenate([lhs[core, 0], lhs[core, 1]], axis=1)
-            right = jnp.concatenate([held[2 * core, step], held[2 * core + 1, step]], axis=1)
+            right = jnp.concatenate(
+                [w_refs[2 * core][here, :], w_refs[2 * core + 1][here, :]], axis=1
+            )
             part = part + dot_dims(left, right, 1, 1)
         for chip, ref in enumerate(out_refs):
-            ref[:, step * block : (step + 1) * block] = part[
-                chip * 2 * share : (chip + 1) * 2 * share
-            ].astype(BF16)
+            ref[:, here] = part[chip * 2 * share : (chip + 1) * 2 * share].astype(BF16)
 
 
 def feature_terms(table, own, other, weights, targets):
     width, head_dim = weights[0].shape
-    chips, steps = targets // 2, 8
+    chips = targets // 2
     rows = own.shape[0] // targets
     return pl.pallas_call(
         functools.partial(feature_kernel, targets=targets),
         grid_spec=pltpu.PrefetchScalarGridSpec(
             num_scalar_prefetch=1,
             grid=(),
-            in_specs=[in_vmem()] * 2 + [in_hbm()] * 4,
+            in_specs=[in_vmem()] * 6,
             out_specs=[in_vmem()] * chips,
-            scratch_shapes=[
-                pltpu.VMEM((2, 2, own.shape[0] // 2, head_dim), BF16),
-                pltpu.VMEM((4, steps, width // steps, head_dim), BF16),
-                pltpu.SemaphoreType.DMA((4, steps)),
-            ],
+            scratch_shapes=[pltpu.VMEM((2, 2, own.shape[0] // 2, head_dim), BF16)],
         ),
         out_shape=[jax.ShapeDtypeStruct((rows, width), BF16)] * chips,
         compiler_params=limit(14),
@@ -423,6 +402,8 @@
 
 
 def shift_z(x, by):
+    if by == 0:
+        return x
     pairs = [(y * NZ + z, y * NZ + (z + by) % NZ) for y in range(NY) for z in range(NZ)]
     return lax.ppermute(x, "dp", pairs)
 
@@ -472,13 +453,12 @@
     table = jnp.stack([pos, my_slots // images, my_tiles * (tokens // TILES), first, place])
 
     v_line = jnp.concatenate([shift_y(v_weight, (NY - i) % NY) for i in range(NY)])
-    k_ring, k_zones = ring_z(k_weight, [(0, 0)])
+    k_line = jnp.concatenate([shift_z(k_weight, s) for s in range(NZ)])
     v_ring, v_zones = ring_z(v_line, [(i, 0) for i in range(NY)])
-    k_line = jnp.concatenate(k_ring)
     half = k_line.shape[0] // 2
     after, before = shift_y(k_line, -1), shift_y(k_line, 1)
     pieces = [k_line, after, before, shift_y(after[:half], -1), shift_y(before[half:], 1)]
-    offsets = [z for ((_, z),) in k_zones]
+    offsets = [(NZ - s) % NZ for s in range(NZ)]
     k_zones = [[(y, z) for z in offsets] for y in (0, 1, NY - 1)]
     far = [(NY // 2, z) for z in offsets]
     k_zones += [far[: NZ // 2], far[NZ // 2 :]]

time: 229 us -> 240 us (1.048)
  waiting for transfers between devices: 101 us -> 111 us
  starting transfers between devices: 64.2 us -> 69.7 us
  Pallas kernels: 36.4 us -> 32.3 us
    ppermute x14, starting transfers between devices: 19.4 us -> 25.7 us  [shift_z(): return lax.ppermute(x, 'dp', pairs)]
    ppermute x14, waiting for transfers between devices: 18.4 us -> 24.5 us  [shift_z(): return lax.ppermute(x, 'dp', pairs)]
    all_to_all x1, waiting for transfers between devices: 33.3 us -> 36.5 us  [local(): kv = lax.all_to_all(send, 'dp', 0, 0, tiled=True)]
    all_to_all x1, waiting for transfers between devices: 21.2 us -> 24.2 us  [local(): parts = lax.all_to_all(parts, 'dp', 0, 0, tiled=True)]
    ppermute x13, waiting for transfers between devices: 11.9 us -> 8.99 us  [shift_y(): return lax.ppermute(x, 'dp', pairs)]
    unnamed x70 -> x74, local copies, waits for them, and re-layouts: 16.7 us -> 16.7 us
  transfers between devices with their start and end apart: 37 -> 37, of which waited for: 15 -> 13; matrix products, arithmetic and copies ran while one was open for 3% -> 3% of each run, Pallas kernels for 12% -> 10%
where the time goes in v8:
time: 240 us; the launch traced here: 239 us
  waiting for transfers between devices  111 us (46%)
  starting transfers between devices  69.7 us (29%)
  Pallas kernels  32.3 us (13%)
  local copies, waits for them, and re-layouts  21.8 us (9%)
  other arithmetic  3.62 us (2%)
    all_to_all x1, waiting for transfers between devices, local(): kv = lax.all_to_all(send, 'dp', 0, 0, tiled=True)  36.5 us
    ppermute x14, starting transfers between devices, shift_z(): return lax.ppermute(x, 'dp', pairs)  25.7 us
    ppermute x14, waiting for transfers between devices, shift_z(): return lax.ppermute(x, 'dp', pairs)  24.5 us
    all_to_all x1, waiting for transfers between devices, local(): parts = lax.all_to_all(parts, 'dp', 0, 0, tiled=True)  24.2 us
    ppermute x13, starting transfers between devices, shift_y(): return lax.ppermute(x, 'dp', pairs)  20.3 us
    unnamed x74, local copies, waits for them, and re-layouts  16.7 us
    ppermute x3, waiting for transfers between devices, local(): terms[s] = lax.ppermute(terms[s], 'tensor', pairs)  16.3 us
    ppermute x13, waiting for transfers between devices, shift_y(): return lax.ppermute(x, 'dp', pairs)  8.99 us
  transfers between devices with their start and end apart: 37, of which 13 were waited for; matrix products, arithmetic and copies ran while one was open for 3% of the time, Pallas kernels for 10%

profile of v8, /device:TPU:32, one launch (start us, length us, event | category | flops | bytes accessed | tf_op | source)
XLA Modules:
  0.0 239.1 jit_solution(3464217866068840316)
XLA Ops:
  0.6 3.3 %collective-permute-start.12 = (bf16[256,128]{1,0:T(8,128)(2,1)}, bf16[256,128]{1,0:T(8,128)(2,1)S(1)}, u32[]{:S(2)}, u32[]{:S(2)}) collective-permute-start(bf16[256,128]{1,0:T(8,128)(2,1)} %param.12), channel_id=1, source_target_pairs={{0,128},{8,136},{16,144},{24,152},{32,160},{40,168},{48,176},{56,1... | collective-permute-start | bytes 196616 | tf_op jit(solution)/shard_map/ppermute | solution.py:401
  5.9 5.4 %collective-permute-start.5 = (bf16[256,128]{1,0:T(8,128)(2,1)}, bf16[256,128]{1,0:T(8,128)(2,1)S(1)}, u32[]{:S(2)}, u32[]{:S(2)}) collective-permute-start(bf16[256,128]{1,0:T(8,128)(2,1)} %param.11), channel_id=1, source_target_pairs={{0,48},{8,56},{16,0},{24,8},{32,16},{40,24},{48,32},{56,40},{64,11... | collective-permute-start | bytes 196616 | tf_op jit(solution)/shard_map/ppermute | solution.py:408
  11.4 1.9 collective-permute-start.4
  15.9 4.6 %collective-permute-start.2 = (bf16[256,128]{1,0:T(8,128)(2,1)}, bf16[256,128]{1,0:T(8,128)(2,1)S(1)}, u32[]{:S(2)}, u32[]{:S(2)}) collective-permute-start(bf16[256,128]{1,0:T(8,128)(2,1)} %param.11), channel_id=1, source_target_pairs={{0,24},{8,32},{16,40},{24,48},{32,56},{40,0},{48,8},{56,16},{64,88... | collective-permute-start | bytes 196616 | tf_op jit(solution)/shard_map/ppermute | solution.py:408
  20.5 2.0 collective-permute-start
  22.5 5.6 %collective-permute-done = bf16[256,128]{1,0:T(8,128)(2,1)S(1)} collective-permute-done((bf16[256,128]{1,0:T(8,128)(2,1)}, bf16[256,128]{1,0:T(8,128)(2,1)S(1)}, u32[]{:S(2)}, u32[]{:S(2)}) %collective-permute-start) | collective-permute-done | bytes 65568 | tf_op jit(solution)/shard_map/ppermute | solution.py:408
  28.5 7.0 %collective-permute-done.1 = bf16[256,128]{1,0:T(8,128)(2,1)S(1)} collective-permute-done((bf16[256,128]{1,0:T(8,128)(2,1)}, bf16[256,128]{1,0:T(8,128)(2,1)S(1)}, u32[]{:S(2)}, u32[]{:S(2)}) %collective-permute-start.1) | collective-permute-done | bytes 65568 | tf_op jit(solution)/shard_map/ppermute | solution.py:408
  35.9 2.1 collective-permute-start.14
  38.1 4.9 %collective-permute-done.14.refs_6_ = bf16[1024,128]{1,0:T(8,128)(2,1)S(1)} collective-permute-done((bf16[1024,128]{1,0:T(8,128)(2,1)S(1)}, bf16[1024,128]{1,0:T(8,128)(2,1)S(1)}, u32[]{:S(2)}, u32[]{:S(2)}) %collective-permute-start.14) | collective-permute-done | bytes 262176 | tf_op jit(solution)/shard_map/ppermute | solution.py:408
  43.0 2.8 %collective-permute-start.16 = (bf16[1024,128]{1,0:T(8,128)(2,1)S(1)}, bf16[1024,128]{1,0:T(8,128)(2,1)S(1)}, u32[]{:S(2)}, u32[]{:S(2)}) collective-permute-start(bf16[1024,128]{1,0:T(8,128)(2,1)S(1)} %collective-permute-done.14.refs_6_), channel_id=1, source_target_pairs={{0,8},{8,16},{16,24},{24,32},{32,40},{40,48},{48,56},{56,0},{64,72... | collective-permute-start | bytes 786440 | tf_op jit(solution)/shard_map/ppermute | solution.py:408
  46.6 2.6 %collective-permute-start.7 = (bf16[2048,128]{1,0:T(8,128)(2,1)S(1)}, bf16[2048,128]{1,0:T(8,128)(2,1)S(1)}, u32[]{:S(2)}, u32[]{:S(2)}) collective-permute-start(bf16[2048,128]{1,0:T(8,128)(2,1)S(1)} %constant_dynamic-update-slice_fusion.refs_0_), channel_id=1, source_target_pairs={{0,192},{8,200},{16,208},{24,216},{32,224},{40,232},{48,240},{56,2... | collective-permute-start | bytes 1572872 | tf_op jit(solution)/shard_map/ppermute | solution.py:401
  49.4 3.0 %collective-permute-done.16.refs_8_ = bf16[1024,128]{1,0:T(8,128)(2,1)S(1)} collective-permute-done((bf16[1024,128]{1,0:T(8,128)(2,1)S(1)}, bf16[1024,128]{1,0:T(8,128)(2,1)S(1)}, u32[]{:S(2)}, u32[]{:S(2)}) %collective-permute-start.16) | collective-permute-done | bytes 262176 | tf_op jit(solution)/shard_map/ppermute | solution.py:408
  52.3 2.5 %collective-permute-start.18 = (bf16[1024,128]{1,0:T(8,128)(2,1)S(1)}, bf16[1024,128]{1,0:T(8,128)(2,1)S(1)}, u32[]{:S(2)}, u32[]{:S(2)}) collective-permute-start(bf16[1024,128]{1,0:T(8,128)(2,1)S(1)} %collective-permute-done.16.refs_8_), channel_id=1, source_target_pairs={{0,8},{8,16},{16,24},{24,32},{32,40},{40,48},{48,56},{56,0},{64,72... | collective-permute-start | bytes 786440 | tf_op jit(solution)/shard_map/ppermute | solution.py:408
  55.0 3.2 %collective-permute-done.8.refs_2_ = bf16[2048,128]{1,0:T(8,128)(2,1)S(1)} collective-permute-done((bf16[2048,128]{1,0:T(8,128)(2,1)S(1)}, bf16[2048,128]{1,0:T(8,128)(2,1)S(1)}, u32[]{:S(2)}, u32[]{:S(2)}) %collective-permute-start.8) | collective-permute-done | bytes 524320 | tf_op jit(solution)/shard_map/ppermute | solution.py:401
  59.6 3.2 %collective-permute-start.9 = (bf16[1024,128]{1,0:T(8,128)(2,1)}, bf16[1024,128]{1,0:T(8,128)(2,1)}, u32[]{:S(2)}, u32[]{:S(2)}) collective-permute-start(bf16[1024,128]{1,0:T(8,128)(2,1)} %slice.26), channel_id=1, source_target_pairs={{0,192},{8,200},{16,208},{24,216},{32,224},{40,232},{48,240},{56,2... | collective-permute-start | bytes 786440 | tf_op jit(solution)/shard_map/ppermute | solution.py:401
  62.9 3.5 %collective-permute-start.20 = (bf16[1024,128]{1,0:T(8,128)(2,1)S(1)}, bf16[1024,128]{1,0:T(8,128)(2,1)}, u32[]{:S(2)}, u32[]{:S(2)}) collective-permute-start(bf16[1024,128]{1,0:T(8,128)(2,1)S(1)} %collective-permute-done.18.refs_10_), channel_id=1, source_target_pairs={{0,8},{8,16},{16,24},{24,32},{32,40},{40,48},{48,56},{56,0},{64,72... | collective-permute-start | bytes 786440 | tf_op jit(solution)/shard_map/ppermute | solution.py:408
  66.7 4.1 %collective-permute-done.19.refs_11_ = bf16[1024,128]{1,0:T(8,128)(2,1)} collective-permute-done((bf16[1024,128]{1,0:T(8,128)(2,1)S(1)}, bf16[1024,128]{1,0:T(8,128)(2,1)}, u32[]{:S(2)}, u32[]{:S(2)}) %collective-permute-start.19) | collective-permute-done | bytes 262176 | tf_op jit(solution)/shard_map/ppermute | solution.py:408
  70.8 6.0 %project.1 = (bf16[32,128,256]{2,1,0:T(8,128)(2,1)}, f32[256,128]{1,0:T(8,128)}) custom-call(s32[5,32]{1,0:T(8,128)S(1)} %stack.41.table_ref, bf16[256,8192]{1,0:T(8,128)(2,1)} %bitcast.24, bf16[2048,128]{1,0:T(8,128)(2,1)S(1)} %constant_dynamic-update-slice_fusion.refs_0_, bf16[2048,128]{1,0:T(8,128)(2,1)S(1)} %collective-permute-done.7.refs_1_, ...), custom_call_target="tpu_custom_call" | custom-call | flops 1073741824 | bytes 10485760 | tf_op jit(solution)/shard_map/project/pallas_call | solution.py:84
  76.8 7.1 %all-to-all-start = ((bf16[32,128,256]{2,1,0:T(8,128)(2,1)}), bf16[32,128,256]{2,1,0:T(8,128)(2,1)}, u32[]{:S(2)}, u32[]{:S(2)}) async-start(bf16[32,128,256]{2,1,0:T(8,128)(2,1)} %get-tuple-element.55), calls=%async_computation | async-start | bytes 4194304 | tf_op jit(solution)/shard_map/all_to_all | solution.py:470
  84.0 2.7 %dynamic-slice_bitcast_fusion = (bf16[128,2048]{1,0:T(8,128)(2,1)}, bf16[128,2048]{1,0:T(8,128)(2,1)}, bf16[128,2048]{1,0:T(8,128)(2,1)S(1)}, bf16[128,2048]{1,0:T(8,128)(2,1)}) fusion(bf16[2,128,8192]{2,1,0:T(8,128)(2,1)} %param.10, s32[]{:T(128)S(6)} %select_n.86, s32[]{:T(128)S(6)} %select_n.94, s32[]{:T(128)S(6)} %select_n.92, s32[]{:T(128)S(6)} %select_n.90, ...), kind=kLoop, calls=%fused_computation.2 | loop fusion | bytes 4194324 | tf_op jit(solution)/shard_map/squeeze | solution.py:476
  86.7 2.7 %collective-permute-start.23 = (bf16[128,2048]{1,0:T(8,128)(2,1)}, bf16[128,2048]{1,0:T(8,128)(2,1)S(1)}, u32[]{:S(2)}, u32[]{:S(2)}) collective-permute-start(bf16[128,2048]{1,0:T(8,128)(2,1)} %get-tuple-element.109), channel_id=1, source_target_pairs={{0,192},{8,200},{16,208},{24,216},{32,224},{40,232},{48,240},{56,2... | collective-permute-start | bytes 1572872 | tf_op jit(solution)/shard_map/ppermute | solution.py:401
  91.1 36.5 %all-to-all-done.kv_ref = bf16[32,128,256]{2,1,0:T(8,128)(2,1)} async-done(((bf16[32,128,256]{2,1,0:T(8,128)(2,1)}), bf16[32,128,256]{2,1,0:T(8,128)(2,1)}, u32[]{:S(2)}, u32[]{:S(2)}) %all-to-all-start) | async-done | bytes 2097184 | tf_op jit(solution)/shard_map/all_to_all | solution.py:470
  127.6 8.8 %attend.1 = (bf16[32,128,256]{2,1,0:T(8,128)(2,1)}, bf16[32,128,128]{2,1,0:T(8,128)(2,1)}, bf16[32,128,128]{2,1,0:T(8,128)(2,1)}) custom-call(s32[5,32]{1,0:T(8,128)S(1)} %stack.41.table_ref, bf16[512,1024]{1,0:T(8,128)(2,1)} %q_ref.1, bf16[512,1024]{1,0:T(8,128)(2,1)} %ct_ref.1, bf16[32,128,256]{2,1,0:T(8,128)(2,1)} %all-to-all-done.kv_ref), custom_call_target="tpu_custom_call" | custom-call | flops 536870912 | bytes 8388608 | tf_op jit(solution)/shard_map/attend/pallas_call | solution.py:178
  137.5 5.8 %all-to-all-start.1 = ((bf16[32,128,256]{2,1,0:T(8,128)(2,1)}), bf16[32,128,256]{2,1,0:T(8,128)(2,1)}, u32[]{:S(2)}, u32[]{:S(2)}) async-start(bf16[32,128,256]{2,1,0:T(8,128)(2,1)} %get-tuple-element.59), calls=%async_computation.1 | async-start | bytes 4194304 | tf_op jit(solution)/shard_map/all_to_all | solution.py:486
  149.0 2.0 assemble.1
  151.6 6.4 %apply.1 = (bf16[512,1024]{1,0:T(8,128)(2,1)}, bf16[512,1024]{1,0:T(8,128)(2,1)}) custom-call(s32[5,32]{1,0:T(8,128)S(1)} %stack.41.table_ref, bf16[32,128,256]{2,1,0:T(8,128)(2,1)} %all-to-all-done.kv_ref, bf16[32,128,128]{2,1,0:T(8,128)(2,1)} %get-tuple-element.64.probs_ref, bf16[32,128,128]{2,1,0:T(8,128)(2,1)} %get-tuple-element.65.ds_ref), custom_call_target="tpu_custom_call" | custom-call | flops 268435456 | bytes 6291456 | tf_op jit(solution)/shard_map/apply/pallas_call | solution.py:217
  158.0 1.3 copy-done.8
  159.3 1.3 copy-done.6
  160.6 1.4 copy-done.10
  162.1 24.2 %all-to-all-done.1.part_ref = bf16[32,128,256]{2,1,0:T(8,128)(2,1)} async-done(((bf16[32,128,256]{2,1,0:T(8,128)(2,1)}), bf16[32,128,256]{2,1,0:T(8,128)(2,1)}, u32[]{:S(2)}, u32[]{:S(2)}) %all-to-all-start.1) | async-done | bytes 2097184 | tf_op jit(solution)/shard_map/all_to_all | solution.py:486
  186.3 2.9 %owner_grads.1 = (bf16[256,256]{1,0:T(8,128)(2,1)S(1)}, bf16[256,256]{1,0:T(8,128)(2,1)S(1)}) custom-call(s32[5,32]{1,0:T(8,128)S(1)} %stack.41.table_ref, bf16[32,128,256]{2,1,0:T(8,128)(2,1)} %all-to-all-done.1.part_ref, f32[256,128]{1,0:T(8,128)} %get-tuple-element.57.raw_ref, f32[1,128]{1,0:T(1,128)S(1)} %bitcast.23), custom_call_target="tpu_custom_call" | custom-call | bytes 3145728 | tf_op jit(solution)/shard_map/owner_grads/pallas_call | solution.py:263
  189.3 1.7 collective-permute-start.29
  190.9 2.0 collective-permute-start.28
  193.3 1.2 collective-permute-done.29.refs_3_
  194.5 2.9 %collective-permute-done.28.refs_2_ = bf16[256,256]{1,0:T(8,128)(2,1)S(1)} collective-permute-done((bf16[256,256]{1,0:T(8,128)(2,1)S(1)}, bf16[256,256]{1,0:T(8,128)(2,1)S(1)}, u32[]{:S(2)}, u32[]{:S(2)}) %collective-permute-start.28) | collective-permute-done | bytes 131104 | tf_op jit(solution)/shard_map/ppermute | solution.py:401
  197.4 1.7 collective-permute-done.27.refs_1_
  199.1 2.2 weight_terms.1
  201.3 4.3 %all-to-all-start.2 = ((bf16[8,256,256]{2,1,0:T(8,128)(2,1)}), bf16[8,256,256]{2,1,0:T(8,128)(2,1)}, u32[]{:S(2)}, u32[]{:S(2)}) async-start(bf16[8,256,256]{2,1,0:T(8,128)(2,1)} %weight_terms.1), calls=%async_computation.2 | async-start | bytes 2097152 | tf_op jit(solution)/shard_map/all_to_all | solution.py:501
  205.7 1.6 copy-done.5
  207.3 1.6 copy-done.7
  208.9 1.6 copy-done.11
  210.4 3.4 %feature_terms.1 = (bf16[32,8192]{1,0:T(8,128)(2,1)S(1)}, bf16[32,8192]{1,0:T(8,128)(2,1)S(1)}, bf16[32,8192]{1,0:T(8,128)(2,1)S(1)}, bf16[32,8192]{1,0:T(8,128)(2,1)S(1)}) custom-call(s32[5,32]{1,0:T(8,128)S(1)} %stack.41.table_ref, bf16[256,256]{1,0:T(8,128)(2,1)S(1)} %get-tuple-element.90.own_ref, bf16[256,256]{1,0:T(8,128)(2,1)S(1)} %collective-permute-done.30.other_ref, ...), custom_call_target="tpu_custom_call" | custom-call | flops 2147483648 | bytes 10485760 | tf_op jit(solution)/shard_map/feature_terms/pallas_call | solution.py:381
  213.8 1.6 collective-permute-start.31
  215.4 2.7 %collective-permute-start.32 = (bf16[32,8192]{1,0:T(8,128)(2,1)S(1)}, bf16[32,8192]{1,0:T(8,128)(2,1)S(1)}, u32[]{:S(2)}, u32[]{:S(2)}) collective-permute-start(bf16[32,8192]{1,0:T(8,128)(2,1)S(1)} %get-tuple-element.98), channel_id=1, source_target_pairs={{0,4},{1,5},{2,6},{3,7},{4,0},{5,1},{6,2},{7,3},{8,12},{9,13},{10,... | collective-permute-start | bytes 1572872 | tf_op jit(solution)/shard_map/ppermute | solution.py:506
  218.1 1.5 collective-permute-start.33
  219.6 10.3 %collective-permute-done.31 = bf16[32,8192]{1,0:T(8,128)(2,1)S(1)} collective-permute-done((bf16[32,8192]{1,0:T(8,128)(2,1)S(1)}, bf16[32,8192]{1,0:T(8,128)(2,1)S(1)}, u32[]{:S(2)}, u32[]{:S(2)}) %collective-permute-start.31) | collective-permute-done | bytes 524320 | tf_op jit(solution)/shard_map/ppermute | solution.py:506
  229.9 6.0 %collective-permute-done.32 = bf16[32,8192]{1,0:T(8,128)(2,1)S(1)} collective-permute-done((bf16[32,8192]{1,0:T(8,128)(2,1)S(1)}, bf16[32,8192]{1,0:T(8,128)(2,1)S(1)}, u32[]{:S(2)}, u32[]{:S(2)}) %collective-permute-start.32) | collective-permute-done | bytes 524320 | tf_op jit(solution)/shard_map/ppermute | solution.py:506
  236.0 1.4 convert_reduce_fusion
  (127 shorter events, 19.5 us)
Async XLA Ops:
  0.6 70.2 %copy-start.31 = (f32[128]{0:T(128)S(1)}, f32[128]{0:T(128)}, u32[]{:S(2)}) copy-start(f32[128]{0:T(128)} %param.13) | copy-start | bytes 1540
  0.6 15.2 %collective-permute-start.12 = (bf16[256,128]{1,0:T(8,128)(2,1)}, bf16[256,128]{1,0:T(8,128)(2,1)S(1)}, u32[]{:S(2)}, u32[]{:S(2)}) collective-permute-start(bf16[256,128]{1,0:T(8,128)(2,1)} %param.12), channel_id=1, source_target_pairs={{0,128},{8,136},{16,144},{24,152},{32,160},{40,168},{48,176},{56,1... | collective-permute-start | bytes 196616 | tf_op jit(solution)/shard_map/ppermute | solution.py:401
  3.9 11.9 %collective-permute-start.11 = (bf16[256,128]{1,0:T(8,128)(2,1)}, bf16[256,128]{1,0:T(8,128)(2,1)S(1)}, u32[]{:S(2)}, u32[]{:S(2)}) collective-permute-start(bf16[256,128]{1,0:T(8,128)(2,1)} %param.12), channel_id=1, source_target_pairs={{0,192},{8,200},{16,208},{24,216},{32,224},{40,232},{48,240},{56,2... | collective-permute-start | bytes 196616 | tf_op jit(solution)/shard_map/ppermute | solution.py:401
  5.0 15.5 %collective-permute-start.13 = (bf16[256,128]{1,0:T(8,128)(2,1)}, bf16[256,128]{1,0:T(8,128)(2,1)S(1)}, u32[]{:S(2)}, u32[]{:S(2)}) collective-permute-start(bf16[256,128]{1,0:T(8,128)(2,1)} %param.12), channel_id=1, source_target_pairs={{0,64},{8,72},{16,80},{24,88},{32,96},{40,104},{48,112},{56,120},{... | collective-permute-start | bytes 196616 | tf_op jit(solution)/shard_map/ppermute | solution.py:401
  5.9 32.1 %collective-permute-start.5 = (bf16[256,128]{1,0:T(8,128)(2,1)}, bf16[256,128]{1,0:T(8,128)(2,1)S(1)}, u32[]{:S(2)}, u32[]{:S(2)}) collective-permute-start(bf16[256,128]{1,0:T(8,128)(2,1)} %param.11), channel_id=1, source_target_pairs={{0,48},{8,56},{16,0},{24,8},{32,16},{40,24},{48,32},{56,40},{64,11... | collective-permute-start | bytes 196616 | tf_op jit(solution)/shard_map/ppermute | solution.py:408
  11.4 26.7 %collective-permute-start.4 = (bf16[256,128]{1,0:T(8,128)(2,1)}, bf16[256,128]{1,0:T(8,128)(2,1)S(1)}, u32[]{:S(2)}, u32[]{:S(2)}) collective-permute-start(bf16[256,128]{1,0:T(8,128)(2,1)} %param.11), channel_id=1, source_target_pairs={{0,40},{8,48},{16,56},{24,0},{32,8},{40,16},{48,24},{56,32},{64,10... | collective-permute-start | bytes 196616 | tf_op jit(solution)/shard_map/ppermute | solution.py:408
  15.8 20.1 %collective-permute-start.3 = (bf16[256,128]{1,0:T(8,128)(2,1)}, bf16[256,128]{1,0:T(8,128)(2,1)S(1)}, u32[]{:S(2)}, u32[]{:S(2)}) collective-permute-start(bf16[256,128]{1,0:T(8,128)(2,1)} %param.11), channel_id=1, source_target_pairs={{0,32},{8,40},{16,48},{24,56},{32,0},{40,8},{48,16},{56,24},{64,96... | collective-permute-start | bytes 196616 | tf_op jit(solution)/shard_map/ppermute | solution.py:408
  15.9 19.9 %collective-permute-start.2 = (bf16[256,128]{1,0:T(8,128)(2,1)}, bf16[256,128]{1,0:T(8,128)(2,1)S(1)}, u32[]{:S(2)}, u32[]{:S(2)}) collective-permute-start(bf16[256,128]{1,0:T(8,128)(2,1)} %param.11), channel_id=1, source_target_pairs={{0,24},{8,32},{16,40},{24,48},{32,56},{40,0},{48,8},{56,16},{64,88... | collective-permute-start | bytes 196616 | tf_op jit(solution)/shard_map/ppermute | solution.py:408
  20.5 7.6 %collective-permute-start = (bf16[256,128]{1,0:T(8,128)(2,1)}, bf16[256,128]{1,0:T(8,128)(2,1)S(1)}, u32[]{:S(2)}, u32[]{:S(2)}) collective-permute-start(bf16[256,128]{1,0:T(8,128)(2,1)} %param.11), channel_id=1, source_target_pairs={{0,8},{8,16},{16,24},{24,32},{32,40},{40,48},{48,56},{56,0},{64,72... | collective-permute-start | bytes 196616 | tf_op jit(solution)/shard_map/ppermute | solution.py:408
  28.1 7.3 %collective-permute-start.1 = (bf16[256,128]{1,0:T(8,128)(2,1)}, bf16[256,128]{1,0:T(8,128)(2,1)S(1)}, u32[]{:S(2)}, u32[]{:S(2)}) collective-permute-start(bf16[256,128]{1,0:T(8,128)(2,1)} %param.11), channel_id=1, source_target_pairs={{0,16},{8,24},{16,32},{24,40},{32,48},{40,56},{48,0},{56,8},{64,80... | collective-permute-start | bytes 196616 | tf_op jit(solution)/shard_map/ppermute | solution.py:408
  35.4 10.4 %collective-permute-start.6 = (bf16[256,128]{1,0:T(8,128)(2,1)}, bf16[256,128]{1,0:T(8,128)(2,1)S(1)}, u32[]{:S(2)}, u32[]{:S(2)}) collective-permute-start(bf16[256,128]{1,0:T(8,128)(2,1)} %param.11), channel_id=1, source_target_pairs={{0,56},{8,0},{16,8},{24,16},{32,24},{40,32},{48,40},{56,48},{64,12... | collective-permute-start | bytes 196616 | tf_op jit(solution)/shard_map/ppermute | solution.py:408
  35.8 13.5 %collective-permute-start.15 = (bf16[1024,128]{1,0:T(8,128)(2,1)S(1)}, bf16[1024,128]{1,0:T(8,128)(2,1)S(1)}, u32[]{:S(2)}, u32[]{:S(2)}) collective-permute-start(bf16[1024,128]{1,0:T(8,128)(2,1)S(1)} %constant_dynamic-update-slice_fusion.8.refs_5_), channel_id=1, source_target_pairs={{0,56},{8,0},{16,8},{24,16},{32,24},{40,32},{48,40},{56,48},{64,12... | collective-permute-start | bytes 786440 | tf_op jit(solution)/shard_map/ppermute | solution.py:408
  35.9 7.1 %collective-permute-start.14 = (bf16[1024,128]{1,0:T(8,128)(2,1)S(1)}, bf16[1024,128]{1,0:T(8,128)(2,1)S(1)}, u32[]{:S(2)}, u32[]{:S(2)}) collective-permute-start(bf16[1024,128]{1,0:T(8,128)(2,1)S(1)} %constant_dynamic-update-slice_fusion.8.refs_5_), channel_id=1, source_target_pairs={{0,8},{8,16},{16,24},{24,32},{32,40},{40,48},{48,56},{56,0},{64,72... | collective-permute-start | bytes 786440 | tf_op jit(solution)/shard_map/ppermute | solution.py:408
  43.0 33.8 %copy-start.15 = (bf16[1024,128]{1,0:T(8,128)(2,1)}, bf16[1024,128]{1,0:T(8,128)(2,1)S(1)}, u32[]{:S(2)}) copy-start(bf16[1024,128]{1,0:T(8,128)(2,1)S(1)} %collective-permute-done.14.refs_6_) | copy-start | bytes 786436
  43.0 9.3 %collective-permute-start.16 = (bf16[1024,128]{1,0:T(8,128)(2,1)S(1)}, bf16[1024,128]{1,0:T(8,128)(2,1)S(1)}, u32[]{:S(2)}, u32[]{:S(2)}) collective-permute-start(bf16[1024,128]{1,0:T(8,128)(2,1)S(1)} %collective-permute-done.14.refs_6_), channel_id=1, source_target_pairs={{0,8},{8,16},{16,24},{24,32},{32,40},{40,48},{48,56},{56,0},{64,72... | collective-permute-start | bytes 786440 | tf_op jit(solution)/shard_map/ppermute | solution.py:408
  45.8 30.9 %copy-start = (bf16[2048,128]{1,0:T(8,128)(2,1)}, bf16[2048,128]{1,0:T(8,128)(2,1)S(1)}, u32[]{:S(2)}) copy-start(bf16[2048,128]{1,0:T(8,128)(2,1)S(1)} %constant_dynamic-update-slice_fusion.refs_0_) | copy-start | bytes 1572868
  45.9 12.3 %collective-permute-start.8 = (bf16[2048,128]{1,0:T(8,128)(2,1)S(1)}, bf16[2048,128]{1,0:T(8,128)(2,1)S(1)}, u32[]{:S(2)}, u32[]{:S(2)}) collective-permute-start(bf16[2048,128]{1,0:T(8,128)(2,1)S(1)} %constant_dynamic-update-slice_fusion.refs_0_), channel_id=1, source_target_pairs={{0,64},{8,72},{16,80},{24,88},{32,96},{40,104},{48,112},{56,120},{... | collective-permute-start | bytes 1572872 | tf_op jit(solution)/shard_map/ppermute | solution.py:401
  46.6 12.3 %collective-permute-start.7 = (bf16[2048,128]{1,0:T(8,128)(2,1)S(1)}, bf16[2048,128]{1,0:T(8,128)(2,1)S(1)}, u32[]{:S(2)}, u32[]{:S(2)}) collective-permute-start(bf16[2048,128]{1,0:T(8,128)(2,1)S(1)} %constant_dynamic-update-slice_fusion.refs_0_), channel_id=1, source_target_pairs={{0,192},{8,200},{16,208},{24,216},{32,224},{40,232},{48,240},{56,2... | collective-permute-start | bytes 1572872 | tf_op jit(solution)/shard_map/ppermute | solution.py:401
  49.3 27.5 %copy-start.13 = (bf16[1024,128]{1,0:T(8,128)(2,1)}, bf16[1024,128]{1,0:T(8,128)(2,1)S(1)}, u32[]{:S(2)}) copy-start(bf16[1024,128]{1,0:T(8,128)(2,1)S(1)} %collective-permute-done.15.refs_7_) | copy-start | bytes 786436
  49.3 13.6 %collective-permute-start.17 = (bf16[1024,128]{1,0:T(8,128)(2,1)S(1)}, bf16[1024,128]{1,0:T(8,128)(2,1)S(1)}, u32[]{:S(2)}, u32[]{:S(2)}) collective-permute-start(bf16[1024,128]{1,0:T(8,128)(2,1)S(1)} %collective-permute-done.15.refs_7_), channel_id=1, source_target_pairs={{0,56},{8,0},{16,8},{24,16},{32,24},{40,32},{48,40},{56,48},{64,12... | collective-permute-start | bytes 786440 | tf_op jit(solution)/shard_map/ppermute | solution.py:408
  52.3 24.5 %copy-start.17 = (bf16[1024,128]{1,0:T(8,128)(2,1)}, bf16[1024,128]{1,0:T(8,128)(2,1)S(1)}, u32[]{:S(2)}) copy-start(bf16[1024,128]{1,0:T(8,128)(2,1)S(1)} %collective-permute-done.16.refs_8_) | copy-start | bytes 786436
  52.3 10.5 %collective-permute-start.18 = (bf16[1024,128]{1,0:T(8,128)(2,1)S(1)}, bf16[1024,128]{1,0:T(8,128)(2,1)S(1)}, u32[]{:S(2)}, u32[]{:S(2)}) collective-permute-start(bf16[1024,128]{1,0:T(8,128)(2,1)S(1)} %collective-permute-done.16.refs_8_), channel_id=1, source_target_pairs={{0,8},{8,16},{16,24},{24,32},{32,40},{40,48},{48,56},{56,0},{64,72... | collective-permute-start | bytes 786440 | tf_op jit(solution)/shard_map/ppermute | solution.py:408
  58.9 11.9 %collective-permute-start.10 = (bf16[1024,128]{1,0:T(8,128)(2,1)}, bf16[1024,128]{1,0:T(8,128)(2,1)S(1)}, u32[]{:S(2)}, u32[]{:S(2)}) collective-permute-start(bf16[1024,128]{1,0:T(8,128)(2,1)} %slice.27), channel_id=1, source_target_pairs={{0,64},{8,72},{16,80},{24,88},{32,96},{40,104},{48,112},{56,120},{... | collective-permute-start | bytes 786440 | tf_op jit(solution)/shard_map/ppermute | solution.py:401
  59.6 11.2 %collective-permute-start.9 = (bf16[1024,128]{1,0:T(8,128)(2,1)}, bf16[1024,128]{1,0:T(8,128)(2,1)}, u32[]{:S(2)}, u32[]{:S(2)}) collective-permute-start(bf16[1024,128]{1,0:T(8,128)(2,1)} %slice.26), channel_id=1, source_target_pairs={{0,192},{8,200},{16,208},{24,216},{32,224},{40,232},{48,240},{56,2... | collective-permute-start | bytes 786440 | tf_op jit(solution)/shard_map/ppermute | solution.py:401
  62.9 13.9 %copy-start.19 = (bf16[1024,128]{1,0:T(8,128)(2,1)}, bf16[1024,128]{1,0:T(8,128)(2,1)S(1)}, u32[]{:S(2)}) copy-start(bf16[1024,128]{1,0:T(8,128)(2,1)S(1)} %collective-permute-done.17.refs_9_) | copy-start | bytes 786436
  62.9 7.9 %collective-permute-start.19 = (bf16[1024,128]{1,0:T(8,128)(2,1)S(1)}, bf16[1024,128]{1,0:T(8,128)(2,1)}, u32[]{:S(2)}, u32[]{:S(2)}) collective-permute-start(bf16[1024,128]{1,0:T(8,128)(2,1)S(1)} %collective-permute-done.17.refs_9_), channel_id=1, source_target_pairs={{0,56},{8,0},{16,8},{24,16},{32,24},{40,32},{48,40},{56,48},{64,12... | collective-permute-start | bytes 786440 | tf_op jit(solution)/shard_map/ppermute | solution.py:408
  62.9 13.9 %copy-start.21 = (bf16[1024,128]{1,0:T(8,128)(2,1)}, bf16[1024,128]{1,0:T(8,128)(2,1)S(1)}, u32[]{:S(2)}) copy-start(bf16[1024,128]{1,0:T(8,128)(2,1)S(1)} %collective-permute-done.18.refs_10_) | copy-start | bytes 786436
  62.9 7.9 %collective-permute-start.20 = (bf16[1024,128]{1,0:T(8,128)(2,1)S(1)}, bf16[1024,128]{1,0:T(8,128)(2,1)}, u32[]{:S(2)}, u32[]{:S(2)}) collective-permute-start(bf16[1024,128]{1,0:T(8,128)(2,1)S(1)} %collective-permute-done.18.refs_10_), channel_id=1, source_target_pairs={{0,8},{8,16},{16,24},{24,32},{32,40},{40,48},{48,56},{56,0},{64,72... | collective-permute-start | bytes 786440 | tf_op jit(solution)/shard_map/ppermute | solution.py:408
  70.8 6.0 %copy-start.23 = (bf16[1024,128]{1,0:T(8,128)(2,1)}, bf16[1024,128]{1,0:T(8,128)(2,1)S(1)}, u32[]{:S(2)}) copy-start(bf16[1024,128]{1,0:T(8,128)(2,1)S(1)} %collective-permute-done.10.refs_4_) | copy-start | bytes 786436
  76.8 50.7 %all-to-all-start = ((bf16[32,128,256]{2,1,0:T(8,128)(2,1)}), bf16[32,128,256]{2,1,0:T(8,128)(2,1)}, u32[]{:S(2)}, u32[]{:S(2)}) async-start(bf16[32,128,256]{2,1,0:T(8,128)(2,1)} %get-tuple-element.55), calls=%async_computation | async-start | bytes 4194304 | tf_op jit(solution)/shard_map/all_to_all | solution.py:470
  86.7 49.7 %collective-permute-start.23 = (bf16[128,2048]{1,0:T(8,128)(2,1)}, bf16[128,2048]{1,0:T(8,128)(2,1)S(1)}, u32[]{:S(2)}, u32[]{:S(2)}) collective-permute-start(bf16[128,2048]{1,0:T(8,128)(2,1)} %get-tuple-element.109), channel_id=1, source_target_pairs={{0,192},{8,200},{16,208},{24,216},{32,224},{40,232},{48,240},{56,2... | collective-permute-start | bytes 1572872 | tf_op jit(solution)/shard_map/ppermute | solution.py:401
  89.4 46.9 %collective-permute-start.22 = (bf16[128,2048]{1,0:T(8,128)(2,1)}, bf16[128,2048]{1,0:T(8,128)(2,1)S(1)}, u32[]{:S(2)}, u32[]{:S(2)}) collective-permute-start(bf16[128,2048]{1,0:T(8,128)(2,1)} %get-tuple-element.110), channel_id=1, source_target_pairs={{0,128},{8,136},{16,144},{24,152},{32,160},{40,168},{48,176},{56,1... | collective-permute-start | bytes 1572872 | tf_op jit(solution)/shard_map/ppermute | solution.py:401
  90.2 46.1 %collective-permute-start.21 = (bf16[128,2048]{1,0:T(8,128)(2,1)S(1)}, bf16[128,2048]{1,0:T(8,128)(2,1)S(1)}, u32[]{:S(2)}, u32[]{:S(2)}) collective-permute-start(bf16[128,2048]{1,0:T(8,128)(2,1)S(1)} %get-tuple-element.111), channel_id=1, source_target_pairs={{0,64},{8,72},{16,80},{24,88},{32,96},{40,104},{48,112},{56,120},{... | collective-permute-start | bytes 1572872 | tf_op jit(solution)/shard_map/ppermute | solution.py:401
  137.5 48.8 %all-to-all-start.1 = ((bf16[32,128,256]{2,1,0:T(8,128)(2,1)}), bf16[32,128,256]{2,1,0:T(8,128)(2,1)}, u32[]{:S(2)}, u32[]{:S(2)}) async-start(bf16[32,128,256]{2,1,0:T(8,128)(2,1)} %get-tuple-element.59), calls=%async_computation.1 | async-start | bytes 4194304 | tf_op jit(solution)/shard_map/all_to_all | solution.py:486
  148.1 9.9 %collective-permute-start.24 = (bf16[2048,512]{1,0:T(8,128)(2,1)S(1)}, bf16[2048,512]{1,0:T(8,128)(2,1)S(1)}, u32[]{:S(2)}, u32[]{:S(2)}) collective-permute-start(bf16[2048,512]{1,0:T(8,128)(2,1)S(1)} %transpose_pieces.1.own_ref), channel_id=1, source_target_pairs={{0,1},{1,0},{2,3},{3,2},{4,5},{5,4},{6,7},{7,6},{8,9},{9,8},{10,11... | collective-permute-start | bytes 6291464 | tf_op jit(solution)/shard_map/ppermute | solution.py:424
  151.0 7.0 %copy-start.2 = (bf16[8192,128]{1,0:T(8,128)(2,1)}, bf16[8192,128]{1,0:T(8,128)(2,1)S(1)}, u32[]{:S(2)}) copy-start(bf16[8192,128]{1,0:T(8,128)(2,1)S(1)} %get-tuple-element.92.refs_0_) | copy-start | bytes 6291460
  151.0 7.0 %copy-start.4 = (bf16[8192,128]{1,0:T(8,128)(2,1)}, bf16[8192,128]{1,0:T(8,128)(2,1)S(1)}, u32[]{:S(2)}) copy-start(bf16[8192,128]{1,0:T(8,128)(2,1)S(1)} %get-tuple-element.93.refs_1_) | copy-start | bytes 6291460
  151.0 8.3 %collective-permute-start.25 = (bf16[8192,128]{1,0:T(8,128)(2,1)S(1)}, bf16[8192,128]{1,0:T(8,128)(2,1)S(1)}, u32[]{:S(2)}, u32[]{:S(2)}) collective-permute-start(bf16[8192,128]{1,0:T(8,128)(2,1)S(1)} %get-tuple-element.92.refs_0_), channel_id=1, source_target_pairs={{0,1},{1,0},{2,3},{3,2},{4,5},{5,4},{6,7},{7,6},{8,9},{9,8},{10,11... | collective-permute-start | bytes 6291464 | tf_op jit(solution)/shard_map/ppermute | solution.py:424
  151.1 9.5 %collective-permute-start.26 = (bf16[8192,128]{1,0:T(8,128)(2,1)S(1)}, bf16[8192,128]{1,0:T(8,128)(2,1)S(1)}, u32[]{:S(2)}, u32[]{:S(2)}) collective-permute-start(bf16[8192,128]{1,0:T(8,128)(2,1)S(1)} %get-tuple-element.93.refs_1_), channel_id=1, source_target_pairs={{0,1},{1,0},{2,3},{3,2},{4,5},{5,4},{6,7},{7,6},{8,9},{9,8},{10,11... | collective-permute-start | bytes 6291464 | tf_op jit(solution)/shard_map/ppermute | solution.py:424
  186.3 12.8 %copy-start.9 = (bf16[2048,512]{1,0:T(8,128)(2,1)S(1)}, bf16[2048,512]{1,0:T(8,128)(2,1)}, u32[]{:S(2)}) copy-start(bf16[2048,512]{1,0:T(8,128)(2,1)} %copy-done.8) | copy-start | bytes 6291460
  189.3 5.3 %collective-permute-start.29 = (bf16[256,256]{1,0:T(8,128)(2,1)S(1)}, bf16[256,256]{1,0:T(8,128)(2,1)S(1)}, u32[]{:S(2)}, u32[]{:S(2)}) collective-permute-start(bf16[256,256]{1,0:T(8,128)(2,1)S(1)} %get-tuple-element.87.refs_0_), channel_id=1, source_target_pairs={{0,192},{8,200},{16,208},{24,216},{32,224},{40,232},{48,240},{56,2... | collective-permute-start | bytes 393224 | tf_op jit(solution)/shard_map/ppermute | solution.py:401
  190.9 6.5 %collective-permute-start.28 = (bf16[256,256]{1,0:T(8,128)(2,1)S(1)}, bf16[256,256]{1,0:T(8,128)(2,1)S(1)}, u32[]{:S(2)}, u32[]{:S(2)}) collective-permute-start(bf16[256,256]{1,0:T(8,128)(2,1)S(1)} %get-tuple-element.87.refs_0_), channel_id=1, source_target_pairs={{0,128},{8,136},{16,144},{24,152},{32,160},{40,168},{48,176},{56,1... | collective-permute-start | bytes 393224 | tf_op jit(solution)/shard_map/ppermute | solution.py:401
  192.9 6.2 %collective-permute-start.27 = (bf16[256,256]{1,0:T(8,128)(2,1)S(1)}, bf16[256,256]{1,0:T(8,128)(2,1)S(1)}, u32[]{:S(2)}, u32[]{:S(2)}) collective-permute-start(bf16[256,256]{1,0:T(8,128)(2,1)S(1)} %get-tuple-element.87.refs_0_), channel_id=1, source_target_pairs={{0,64},{8,72},{16,80},{24,88},{32,96},{40,104},{48,112},{56,120},{... | collective-permute-start | bytes 393224 | tf_op jit(solution)/shard_map/ppermute | solution.py:401
  193.3 8.0 %collective-permute-start.30 = (bf16[256,256]{1,0:T(8,128)(2,1)S(1)}, bf16[256,256]{1,0:T(8,128)(2,1)S(1)}, u32[]{:S(2)}, u32[]{:S(2)}) collective-permute-start(bf16[256,256]{1,0:T(8,128)(2,1)S(1)} %get-tuple-element.90.own_ref), channel_id=1, source_target_pairs={{0,1},{1,0},{2,3},{3,2},{4,5},{5,4},{6,7},{7,6},{8,9},{9,8},{10,11... | collective-permute-start | bytes 393224 | tf_op jit(solution)/shard_map/ppermute | solution.py:424
  201.3 34.7 %all-to-all-start.2 = ((bf16[8,256,256]{2,1,0:T(8,128)(2,1)}), bf16[8,256,256]{2,1,0:T(8,128)(2,1)}, u32[]{:S(2)}, u32[]{:S(2)}) async-start(bf16[8,256,256]{2,1,0:T(8,128)(2,1)} %weight_terms.1), calls=%async_computation.2 | async-start | bytes 2097152 | tf_op jit(solution)/shard_map/all_to_all | solution.py:501
  213.8 16.1 %collective-permute-start.31 = (bf16[32,8192]{1,0:T(8,128)(2,1)S(1)}, bf16[32,8192]{1,0:T(8,128)(2,1)S(1)}, u32[]{:S(2)}, u32[]{:S(2)}) collective-permute-start(bf16[32,8192]{1,0:T(8,128)(2,1)S(1)} %get-tuple-element.97), channel_id=1, source_target_pairs={{0,2},{1,3},{2,4},{3,5},{4,6},{5,7},{6,0},{7,1},{8,10},{9,11},{10,... | collective-permute-start | bytes 1572872 | tf_op jit(solution)/shard_map/ppermute | solution.py:506
  215.4 20.5 %collective-permute-start.32 = (bf16[32,8192]{1,0:T(8,128)(2,1)S(1)}, bf16[32,8192]{1,0:T(8,128)(2,1)S(1)}, u32[]{:S(2)}, u32[]{:S(2)}) collective-permute-start(bf16[32,8192]{1,0:T(8,128)(2,1)S(1)} %get-tuple-element.98), channel_id=1, source_target_pairs={{0,4},{1,5},{2,6},{3,7},{4,0},{5,1},{6,2},{7,3},{8,12},{9,13},{10,... | collective-permute-start | bytes 1572872 | tf_op jit(solution)/shard_map/ppermute | solution.py:506
  218.1 17.8 %collective-permute-start.33 = (bf16[32,8192]{1,0:T(8,128)(2,1)S(1)}, bf16[32,8192]{1,0:T(8,128)(2,1)S(1)}, u32[]{:S(2)}, u32[]{:S(2)}) collective-permute-start(bf16[32,8192]{1,0:T(8,128)(2,1)S(1)} %get-tuple-element.99), channel_id=1, source_target_pairs={{0,6},{1,7},{2,0},{3,1},{4,2},{5,3},{6,4},{7,5},{8,14},{9,15},{10,... | collective-permute-start | bytes 1572872 | tf_op jit(solution)/shard_map/ppermute | solution.py:506
  (21 other events, 29.1 us)

commit v9 on v7

--- a/solution.py
+++ b/solution.py
@@ -297,7 +297,7 @@
         compiler_params=limit(7),
         cost_estimate=cost(0, 4),
         name="transpose_pieces",
-    )(*pieces)
+    )(*hold(*pieces))
 
 
 def weight_kernel(own_ref, other_ref, *refs):
@@ -412,7 +412,7 @@
         compiler_params=limit(14),
         cost_estimate=cost(4 * own.size * width, 10),
         name="feature_terms",
-    )(table, own, other, *weights)
+    )(table, own, other, *hold(*weights))
 
 
 def shift_y(x, by):
@@ -425,18 +425,6 @@
 def shift_z(x, by):
     pairs = [(y * NZ + z, y * NZ + (z + by) % NZ) for y in range(NY) for z in range(NZ)]
     return lax.ppermute(x, "dp", pairs)
-
-
-def ring_z(x, blocks):
-    pieces, zones = [x], [blocks]
-    below = above = x
-    for hop in range(1, NZ // 2):
-        below, above = shift_z(below, 1), shift_z(above, -1)
-        pieces += [below, above]
-        zones += [[(y, off) for y, _ in blocks] for off in (NZ - hop, hop)]
-    pieces += [shift_z(below, 1)]
-    zones += [[(y, NZ // 2) for y, _ in blocks]]
-    return pieces, zones
 
 
 def swap_cores(x, count):
@@ -472,13 +460,24 @@
     table = jnp.stack([pos, my_slots // images, my_tiles * (tokens // TILES), first, place])
 
     v_line = jnp.concatenate([shift_y(v_weight, (NY - i) % NY) for i in range(NY)])
-    k_ring, k_zones = ring_z(k_weight, [(0, 0)])
-    v_ring, v_zones = ring_z(v_line, [(i, 0) for i in range(NY)])
+    k_ring, v_ring = [k_weight], [v_line]
+    for hop in range(1, NZ // 2):
+        k_ring += [shift_z(k_ring[max(-2, -len(k_ring))], 1), shift_z(k_ring[-1], -1)]
+        if hop == 1:
+            v_ring += [shift_z(v_line, 1), shift_z(v_line, -1)]
+    k_ring[-2], k_ring[-1], v_ring[-2], v_ring[-1] = lax.optimization_barrier(
+        (k_ring[-2], k_ring[-1], v_ring[-2], v_ring[-1])
+    )
+    for hop in range(2, NZ // 2):
+        v_ring += [shift_z(v_ring[-2], 1), shift_z(v_ring[-1], -1)]
+    k_ring += [shift_z(k_ring[-2], 1)]
+    v_ring += [shift_z(v_ring[-2], 1)]
+    offsets = [0] + [z for hop in range(1, NZ // 2) for z in (NZ - hop, hop)] + [NZ // 2]
+    v_zones = [[(y, z) for y in range(NY)] for z in offsets]
     k_line = jnp.concatenate(k_ring)
     half = k_line.shape[0] // 2
     after, before = shift_y(k_line, -1), shift_y(k_line, 1)
     pieces = [k_line, after, before, shift_y(after[:half], -1), shift_y(before[half:], 1)]
-    offsets = [z for ((_, z),) in k_zones]
     k_zones = [[(y, z) for z in offsets] for y in (0, 1, NY - 1)]
     far = [(NY // 2, z) for z in offsets]
     k_zones += [far[: NZ // 2], far[NZ // 2 :]]

time: 229 us -> 225 us (0.983)
  local copies, waits for them, and re-layouts: 21.8 us -> 11.1 us
  starting transfers between devices: 64.2 us -> 70.8 us
  Pallas kernels: 36.4 us -> 38.7 us
    unnamed x70 -> x54, local copies, waits for them, and re-layouts: 16.7 us -> 5.84 us
    ppermute x14, starting transfers between devices: 19.4 us -> 25 us  [shift_z(): return lax.ppermute(x, 'dp', pairs)]
    all_to_all x1, waiting for transfers between devices: 21.2 us -> 26.5 us  [local(): parts = lax.all_to_all(parts, 'dp', 0, 0, tiled=True)]
    ppermute x14, waiting for transfers between devices: 18.4 us -> 14.2 us  [shift_z(): return lax.ppermute(x, 'dp', pairs)]
  transfers between devices with their start and end apart: 37 -> 37, of which waited for: 15 -> 16; matrix products, arithmetic and copies ran while one was open for 3% -> 3% of each run, Pallas kernels for 12% -> 13%
where the time goes in v9:
time: 225 us; the launch traced here: 224 us
  waiting for transfers between devices  99.4 us (44%)
  starting transfers between devices  70.8 us (31%)
  Pallas kernels  38.7 us (17%)
  local copies, waits for them, and re-layouts  11.1 us (5%)
  other arithmetic  3.46 us (2%)
    all_to_all x1, waiting for transfers between devices, local(): kv = lax.all_to_all(send, 'dp', 0, 0, tiled=True)  32.5 us
    all_to_all x1, waiting for transfers between devices, local(): parts = lax.all_to_all(parts, 'dp', 0, 0, tiled=True)  26.5 us
    ppermute x14, starting transfers between devices, shift_z(): return lax.ppermute(x, 'dp', pairs)  25 us
    ppermute x13, starting transfers between devices, shift_y(): return lax.ppermute(x, 'dp', pairs)  19.9 us
    ppermute x3, waiting for transfers between devices, local(): terms[s] = lax.ppermute(terms[s], 'tensor', pairs)  15.7 us
    ppermute x14, waiting for transfers between devices, shift_z(): return lax.ppermute(x, 'dp', pairs)  14.2 us
    ppermute x13, waiting for transfers between devices, shift_y(): return lax.ppermute(x, 'dp', pairs)  10.5 us
    all_to_all x1, starting transfers between devices, local(): kv = lax.all_to_all(send, 'dp', 0, 0, tiled=True)  9.54 us
  transfers between devices with their start and end apart: 37, of which 16 were waited for; matrix products, arithmetic and copies ran while one was open for 3% of the time, Pallas kernels for 13%

profile of v9, /device:TPU:32, one launch (start us, length us, event | category | flops | bytes accessed | tf_op | source)
XLA Modules:
  0.0 224.5 jit_solution(154025426714378782)
XLA Ops:
  0.6 2.0 collective-permute-start
  2.7 3.2 %collective-permute-start.7 = (bf16[256,128]{1,0:T(8,128)(2,1)}, bf16[256,128]{1,0:T(8,128)(2,1)S(1)}, u32[]{:S(2)}, u32[]{:S(2)}) collective-permute-start(bf16[256,128]{1,0:T(8,128)(2,1)} %param.12), channel_id=1, source_target_pairs={{0,128},{8,136},{16,144},{24,152},{32,160},{40,168},{48,176},{56,1... | collective-permute-start | bytes 196616 | tf_op jit(solution)/shard_map/ppermute | solution.py:422
  10.6 2.1 collective-permute-done.8
  12.7 4.1 %collective-permute-start.10 = (bf16[1024,128]{1,0:T(8,128)(2,1)S(1)}, bf16[1024,128]{1,0:T(8,128)(2,1)S(1)}, u32[]{:S(2)}, u32[]{:S(2)}) collective-permute-start(bf16[1024,128]{1,0:T(8,128)(2,1)S(1)} %constant_dynamic-update-slice_fusion.refs_5_), channel_id=1, source_target_pairs={{0,56},{8,0},{16,8},{24,16},{32,24},{40,32},{48,40},{56,48},{64,12... | collective-permute-start | bytes 786440 | tf_op jit(solution)/shard_map/ppermute | solution.py:427
  17.8 1.1 collective-permute-start.3
  19.0 5.0 %collective-permute-done.2 = bf16[256,128]{1,0:T(8,128)(2,1)S(1)} collective-permute-done((bf16[256,128]{1,0:T(8,128)(2,1)S(1)}, bf16[256,128]{1,0:T(8,128)(2,1)S(1)}, u32[]{:S(2)}, u32[]{:S(2)}) %collective-permute-start.2) | collective-permute-done | bytes 65568 | tf_op jit(solution)/shard_map/ppermute | solution.py:427
  24.7 2.3 %collective-permute-start.5 = (bf16[256,128]{1,0:T(8,128)(2,1)S(1)}, bf16[256,128]{1,0:T(8,128)(2,1)S(1)}, u32[]{:S(2)}, u32[]{:S(2)}) collective-permute-start(bf16[256,128]{1,0:T(8,128)(2,1)S(1)} %collective-permute-done.3), channel_id=1, source_target_pairs={{0,56},{8,0},{16,8},{24,16},{32,24},{40,32},{48,40},{56,48},{64,12... | collective-permute-start | bytes 196616 | tf_op jit(solution)/shard_map/ppermute | solution.py:427
  27.1 2.9 %collective-permute-done.4 = bf16[256,128]{1,0:T(8,128)(2,1)S(1)} collective-permute-done((bf16[256,128]{1,0:T(8,128)(2,1)S(1)}, bf16[256,128]{1,0:T(8,128)(2,1)S(1)}, u32[]{:S(2)}, u32[]{:S(2)}) %collective-permute-start.4) | collective-permute-done | bytes 65568 | tf_op jit(solution)/shard_map/ppermute | solution.py:427
  30.0 1.8 collective-permute-start.11
  31.8 3.2 %collective-permute-start.16 = (bf16[1024,128]{1,0:T(8,128)(2,1)S(1)}, bf16[1024,128]{1,0:T(8,128)(2,1)S(1)}, u32[]{:S(2)}, u32[]{:S(2)}) collective-permute-start(bf16[1024,128]{1,0:T(8,128)(2,1)S(1)} %collective-permute-done.9.refs_6_), channel_id=1, source_target_pairs={{0,8},{8,16},{16,24},{24,32},{32,40},{40,48},{48,56},{56,0},{64,72... | collective-permute-start | bytes 786440 | tf_op jit(solution)/shard_map/ppermute | solution.py:427
  35.8 3.1 %collective-permute-start.12 = (bf16[2048,128]{1,0:T(8,128)(2,1)S(1)}, bf16[2048,128]{1,0:T(8,128)(2,1)S(1)}, u32[]{:S(2)}, u32[]{:S(2)}) collective-permute-start(bf16[2048,128]{1,0:T(8,128)(2,1)S(1)} %constant_dynamic-update-slice_fusion.4.refs_0_), channel_id=1, source_target_pairs={{0,192},{8,200},{16,208},{24,216},{32,224},{40,232},{48,240},{56,2... | collective-permute-start | bytes 1572872 | tf_op jit(solution)/shard_map/ppermute | solution.py:422
  39.0 3.5 %collective-permute-start.17 = (bf16[1024,128]{1,0:T(8,128)(2,1)S(1)}, bf16[1024,128]{1,0:T(8,128)(2,1)S(1)}, u32[]{:S(2)}, u32[]{:S(2)}) collective-permute-start(bf16[1024,128]{1,0:T(8,128)(2,1)S(1)} %collective-permute-done.10.refs_7_), channel_id=1, source_target_pairs={{0,56},{8,0},{16,8},{24,16},{32,24},{40,32},{48,40},{56,48},{64,12... | collective-permute-start | bytes 786440 | tf_op jit(solution)/shard_map/ppermute | solution.py:427
  42.5 1.5 collective-permute-start.18
  44.1 2.9 %collective-permute-done.17.refs_9_ = bf16[1024,128]{1,0:T(8,128)(2,1)S(1)} collective-permute-done((bf16[1024,128]{1,0:T(8,128)(2,1)S(1)}, bf16[1024,128]{1,0:T(8,128)(2,1)S(1)}, u32[]{:S(2)}, u32[]{:S(2)}) %collective-permute-start.17) | collective-permute-done | bytes 262176 | tf_op jit(solution)/shard_map/ppermute | solution.py:427
  47.0 2.5 %collective-permute-start.19 = (bf16[1024,128]{1,0:T(8,128)(2,1)S(1)}, bf16[1024,128]{1,0:T(8,128)(2,1)S(1)}, u32[]{:S(2)}, u32[]{:S(2)}) collective-permute-start(bf16[1024,128]{1,0:T(8,128)(2,1)S(1)} %collective-permute-done.17.refs_9_), channel_id=1, source_target_pairs={{0,56},{8,0},{16,8},{24,16},{32,24},{40,32},{48,40},{56,48},{64,12... | collective-permute-start | bytes 786440 | tf_op jit(solution)/shard_map/ppermute | solution.py:427
  49.5 1.5 collective-permute-done.18.refs_10_
  51.0 1.1 collective-permute-start.20
  54.4 2.4 %collective-permute-start.14 = (bf16[1024,128]{1,0:T(8,128)(2,1)}, bf16[1024,128]{1,0:T(8,128)(2,1)}, u32[]{:S(2)}, u32[]{:S(2)}) collective-permute-start(bf16[1024,128]{1,0:T(8,128)(2,1)} %slice.26), channel_id=1, source_target_pairs={{0,192},{8,200},{16,208},{24,216},{32,224},{40,232},{48,240},{56,2... | collective-permute-start | bytes 786440 | tf_op jit(solution)/shard_map/ppermute | solution.py:422
  57.1 1.3 collective-permute-done.20.refs_12_
  58.4 2.3 %collective-permute-done.15.refs_4_ = bf16[1024,128]{1,0:T(8,128)(2,1)} collective-permute-done((bf16[1024,128]{1,0:T(8,128)(2,1)}, bf16[1024,128]{1,0:T(8,128)(2,1)}, u32[]{:S(2)}, u32[]{:S(2)}) %collective-permute-start.15) | collective-permute-done | bytes 262176 | tf_op jit(solution)/shard_map/ppermute | solution.py:422
  61.1 6.0 %project.1 = (bf16[32,128,256]{2,1,0:T(8,128)(2,1)}, f32[256,128]{1,0:T(8,128)}) custom-call(s32[5,32]{1,0:T(8,128)S(1)} %stack.41.table_ref, bf16[256,8192]{1,0:T(8,128)(2,1)} %bitcast.24, bf16[2048,128]{1,0:T(8,128)(2,1)S(1)} %constant_dynamic-update-slice_fusion.4.refs_0_, bf16[2048,128]{1,0:T(8,128)(2,1)S(1)} %collective-permute-done.12.refs_1_, ...), custom_call_target="tpu_custom_call" | custom-call | flops 1073741824 | bytes 10485760 | tf_op jit(solution)/shard_map/project/pallas_call | solution.py:88
  67.1 9.5 %all-to-all-start = ((bf16[32,128,256]{2,1,0:T(8,128)(2,1)}), bf16[32,128,256]{2,1,0:T(8,128)(2,1)S(1)}, u32[]{:S(2)}, u32[]{:S(2)}) async-start(bf16[32,128,256]{2,1,0:T(8,128)(2,1)} %get-tuple-element.63), calls=%async_computation | async-start | bytes 4194304 | tf_op jit(solution)/shard_map/all_to_all | solution.py:489
  76.8 2.9 %dynamic-slice_bitcast_fusion = (bf16[128,2048]{1,0:T(8,128)(2,1)}, bf16[128,2048]{1,0:T(8,128)(2,1)}, bf16[128,2048]{1,0:T(8,128)(2,1)}, bf16[128,2048]{1,0:T(8,128)(2,1)}) fusion(bf16[2,128,8192]{2,1,0:T(8,128)(2,1)} %param.10, s32[]{:T(128)S(6)} %select_n.86, s32[]{:T(128)S(6)} %select_n.94, s32[]{:T(128)S(6)} %select_n.92, s32[]{:T(128)S(6)} %select_n.90, ...), kind=kLoop, calls=%fused_computation.2 | loop fusion | bytes 4194324 | tf_op jit(solution)/shard_map/squeeze | solution.py:495
  79.7 2.7 %collective-permute-start.23 = (bf16[128,2048]{1,0:T(8,128)(2,1)}, bf16[128,2048]{1,0:T(8,128)(2,1)}, u32[]{:S(2)}, u32[]{:S(2)}) collective-permute-start(bf16[128,2048]{1,0:T(8,128)(2,1)} %get-tuple-element.117), channel_id=1, source_target_pairs={{0,192},{8,200},{16,208},{24,216},{32,224},{40,232},{48,240},{56,2... | collective-permute-start | bytes 1572872 | tf_op jit(solution)/shard_map/ppermute | solution.py:422
  84.1 32.5 %all-to-all-done.kv_ref = bf16[32,128,256]{2,1,0:T(8,128)(2,1)S(1)} async-done(((bf16[32,128,256]{2,1,0:T(8,128)(2,1)}), bf16[32,128,256]{2,1,0:T(8,128)(2,1)S(1)}, u32[]{:S(2)}, u32[]{:S(2)}) %all-to-all-start) | async-done | bytes 2097184 | tf_op jit(solution)/shard_map/all_to_all | solution.py:489
  116.5 1.4 copy-done.17
  117.9 8.8 %attend.1 = (bf16[32,128,256]{2,1,0:T(8,128)(2,1)}, bf16[32,128,128]{2,1,0:T(8,128)(2,1)}, bf16[32,128,128]{2,1,0:T(8,128)(2,1)}) custom-call(s32[5,32]{1,0:T(8,128)S(1)} %stack.41.table_ref, bf16[512,1024]{1,0:T(8,128)(2,1)} %q_ref.1, bf16[512,1024]{1,0:T(8,128)(2,1)} %ct_ref.1, bf16[32,128,256]{2,1,0:T(8,128)(2,1)} %copy-done.17), custom_call_target="tpu_custom_call" | custom-call | flops 536870912 | bytes 8388608 | tf_op jit(solution)/shard_map/attend/pallas_call | solution.py:182
  126.7 5.9 %all-to-all-start.1 = ((bf16[32,128,256]{2,1,0:T(8,128)(2,1)}), bf16[32,128,256]{2,1,0:T(8,128)(2,1)}, u32[]{:S(2)}, u32[]{:S(2)}) async-start(bf16[32,128,256]{2,1,0:T(8,128)(2,1)} %get-tuple-element.67), calls=%async_computation.1 | async-start | bytes 4194304 | tf_op jit(solution)/shard_map/all_to_all | solution.py:505
  132.7 2.2 transpose_pieces.1.own_ref
  135.1 4.1 %assemble.1 = (bf16[8192,128]{1,0:T(8,128)(2,1)}, bf16[8192,128]{1,0:T(8,128)(2,1)}) custom-call(s32[5,32]{1,0:T(8,128)S(1)} %stack.41.table_ref, bf16[2048,128]{1,0:T(8,128)(2,1)S(1)} %copy-done.1, bf16[2048,128]{1,0:T(8,128)(2,1)S(1)} %collective-permute-done.12.refs_1_, bf16[2048,128]{1,0:T(8,128)(2,1)S(1)} %collective-permute-done.13.refs_2_, ...), custom_call_target="tpu_custom_call" | custom-call | bytes 1048576 | tf_op jit(solution)/shard_map/assemble/pallas_call | solution.py:337
  139.7 6.2 %apply.1 = (bf16[512,1024]{1,0:T(8,128)(2,1)}, bf16[512,1024]{1,0:T(8,128)(2,1)}) custom-call(s32[5,32]{1,0:T(8,128)S(1)} %stack.41.table_ref, bf16[32,128,256]{2,1,0:T(8,128)(2,1)} %copy-done.17, bf16[32,128,128]{2,1,0:T(8,128)(2,1)} %get-tuple-element.72.probs_ref, bf16[32,128,128]{2,1,0:T(8,128)(2,1)} %get-tuple-element.73.ds_ref), custom_call_target="tpu_custom_call" | custom-call | flops 268435456 | bytes 6291456 | tf_op jit(solution)/shard_map/apply/pallas_call | solution.py:221
  145.9 1.4 copy-done.2
  147.2 26.5 %all-to-all-done.1.part_ref = bf16[32,128,256]{2,1,0:T(8,128)(2,1)} async-done(((bf16[32,128,256]{2,1,0:T(8,128)(2,1)}), bf16[32,128,256]{2,1,0:T(8,128)(2,1)}, u32[]{:S(2)}, u32[]{:S(2)}) %all-to-all-start.1) | async-done | bytes 2097184 | tf_op jit(solution)/shard_map/all_to_all | solution.py:505
  173.7 3.0 %owner_grads.1 = (bf16[256,256]{1,0:T(8,128)(2,1)S(1)}, bf16[256,256]{1,0:T(8,128)(2,1)S(1)}) custom-call(s32[5,32]{1,0:T(8,128)S(1)} %stack.41.table_ref, bf16[32,128,256]{2,1,0:T(8,128)(2,1)} %all-to-all-done.1.part_ref, f32[256,128]{1,0:T(8,128)} %get-tuple-element.65.raw_ref, f32[1,128]{1,0:T(1,128)S(1)} %bitcast.23), custom_call_target="tpu_custom_call" | custom-call | bytes 3145728 | tf_op jit(solution)/shard_map/owner_grads/pallas_call | solution.py:267
  176.7 1.6 collective-permute-start.29
  178.4 1.7 collective-permute-start.28
  180.4 1.6 collective-permute-done.29.refs_3_
  182.0 2.8 %collective-permute-done.28.refs_2_ = bf16[256,256]{1,0:T(8,128)(2,1)S(1)} collective-permute-done((bf16[256,256]{1,0:T(8,128)(2,1)S(1)}, bf16[256,256]{1,0:T(8,128)(2,1)S(1)}, u32[]{:S(2)}, u32[]{:S(2)}) %collective-permute-start.28) | collective-permute-done | bytes 131104 | tf_op jit(solution)/shard_map/ppermute | solution.py:422
  184.8 1.4 collective-permute-done.27.refs_1_
  186.2 2.3 %weight_terms.1 = bf16[8,256,256]{2,1,0:T(8,128)(2,1)} custom-call(bf16[2048,512]{1,0:T(8,128)(2,1)S(1)} %transpose_pieces.1.own_ref, bf16[2048,512]{1,0:T(8,128)(2,1)S(1)} %copy-done.3, bf16[256,256]{1,0:T(8,128)(2,1)S(1)} %get-tuple-element.95.refs_0_, bf16[256,256]{1,0:T(8,128)(2,1)S(1)} %collective-permute-done.27.refs_1_, ...), custom_call_target="tpu_custom_call" | custom-call | flops 1073741824 | bytes 6291456 | tf_op jit(solution)/shard_map/weight_terms/pallas_call | solution.py:318
  188.5 4.2 %all-to-all-start.2 = ((bf16[8,256,256]{2,1,0:T(8,128)(2,1)}), bf16[8,256,256]{2,1,0:T(8,128)(2,1)S(1)}, u32[]{:S(2)}, u32[]{:S(2)}) async-start(bf16[8,256,256]{2,1,0:T(8,128)(2,1)} %weight_terms.1), calls=%async_computation.2 | async-start | bytes 2097152 | tf_op jit(solution)/shard_map/all_to_all | solution.py:520
  192.7 6.1 %feature_terms.1 = (bf16[32,8192]{1,0:T(8,128)(2,1)S(1)}, bf16[32,8192]{1,0:T(8,128)(2,1)S(1)}, bf16[32,8192]{1,0:T(8,128)(2,1)S(1)}, bf16[32,8192]{1,0:T(8,128)(2,1)S(1)}) custom-call(s32[5,32]{1,0:T(8,128)S(1)} %stack.41.table_ref, bf16[256,256]{1,0:T(8,128)(2,1)S(1)} %get-tuple-element.98.own_ref, bf16[256,256]{1,0:T(8,128)(2,1)S(1)} %collective-permute-done.30.other_ref, ...), custom_call_target="tpu_custom_call" | custom-call | flops 2147483648 | bytes 10485760 | tf_op jit(solution)/shard_map/feature_terms/pallas_call | solution.py:398
  198.9 1.5 collective-permute-start.31
  200.4 2.7 %collective-permute-start.32 = (bf16[32,8192]{1,0:T(8,128)(2,1)S(1)}, bf16[32,8192]{1,0:T(8,128)(2,1)S(1)}, u32[]{:S(2)}, u32[]{:S(2)}) collective-permute-start(bf16[32,8192]{1,0:T(8,128)(2,1)S(1)} %get-tuple-element.106), channel_id=1, source_target_pairs={{0,4},{1,5},{2,6},{3,7},{4,0},{5,1},{6,2},{7,3},{8,12},{9,13},{10,... | collective-permute-start | bytes 1572872 | tf_op jit(solution)/shard_map/ppermute | solution.py:525
  203.1 1.4 collective-permute-start.33
  204.6 10.1 %collective-permute-done.31 = bf16[32,8192]{1,0:T(8,128)(2,1)S(1)} collective-permute-done((bf16[32,8192]{1,0:T(8,128)(2,1)S(1)}, bf16[32,8192]{1,0:T(8,128)(2,1)S(1)}, u32[]{:S(2)}, u32[]{:S(2)}) %collective-permute-start.31) | collective-permute-done | bytes 524320 | tf_op jit(solution)/shard_map/ppermute | solution.py:525
  214.6 5.6 %collective-permute-done.32 = bf16[32,8192]{1,0:T(8,128)(2,1)S(1)} collective-permute-done((bf16[32,8192]{1,0:T(8,128)(2,1)S(1)}, bf16[32,8192]{1,0:T(8,128)(2,1)S(1)}, u32[]{:S(2)}, u32[]{:S(2)}) %collective-permute-start.32) | collective-permute-done | bytes 524320 | tf_op jit(solution)/shard_map/ppermute | solution.py:525
  222.4 2.1 add_convert_fusion
  (107 shorter events, 15.2 us)
Async XLA Ops:
  0.6 60.5 %copy-start.16 = (f32[128]{0:T(128)S(1)}, f32[128]{0:T(128)}, u32[]{:S(2)}) copy-start(f32[128]{0:T(128)} %param.13) | copy-start | bytes 1540
  0.6 16.2 %collective-permute-start = (bf16[256,128]{1,0:T(8,128)(2,1)}, bf16[256,128]{1,0:T(8,128)(2,1)S(1)}, u32[]{:S(2)}, u32[]{:S(2)}) collective-permute-start(bf16[256,128]{1,0:T(8,128)(2,1)} %param.11), channel_id=1, source_target_pairs={{0,8},{8,16},{16,24},{24,32},{32,40},{40,48},{48,56},{56,0},{64,72... | collective-permute-start | bytes 196616 | tf_op jit(solution)/shard_map/ppermute | solution.py:427
  2.6 15.2 %collective-permute-start.1 = (bf16[256,128]{1,0:T(8,128)(2,1)}, bf16[256,128]{1,0:T(8,128)(2,1)S(1)}, u32[]{:S(2)}, u32[]{:S(2)}) collective-permute-start(bf16[256,128]{1,0:T(8,128)(2,1)} %param.11), channel_id=1, source_target_pairs={{0,56},{8,0},{16,8},{24,16},{32,24},{40,32},{48,40},{56,48},{64,12... | collective-permute-start | bytes 196616 | tf_op jit(solution)/shard_map/ppermute | solution.py:427
  2.7 7.9 %collective-permute-start.7 = (bf16[256,128]{1,0:T(8,128)(2,1)}, bf16[256,128]{1,0:T(8,128)(2,1)S(1)}, u32[]{:S(2)}, u32[]{:S(2)}) collective-permute-start(bf16[256,128]{1,0:T(8,128)(2,1)} %param.12), channel_id=1, source_target_pairs={{0,128},{8,136},{16,144},{24,152},{32,160},{40,168},{48,176},{56,1... | collective-permute-start | bytes 196616 | tf_op jit(solution)/shard_map/ppermute | solution.py:422
  5.9 4.6 %collective-permute-start.6 = (bf16[256,128]{1,0:T(8,128)(2,1)}, bf16[256,128]{1,0:T(8,128)(2,1)S(1)}, u32[]{:S(2)}, u32[]{:S(2)}) collective-permute-start(bf16[256,128]{1,0:T(8,128)(2,1)} %param.12), channel_id=1, source_target_pairs={{0,192},{8,200},{16,208},{24,216},{32,224},{40,232},{48,240},{56,2... | collective-permute-start | bytes 196616 | tf_op jit(solution)/shard_map/ppermute | solution.py:422
  7.0 5.7 %collective-permute-start.8 = (bf16[256,128]{1,0:T(8,128)(2,1)}, bf16[256,128]{1,0:T(8,128)(2,1)S(1)}, u32[]{:S(2)}, u32[]{:S(2)}) collective-permute-start(bf16[256,128]{1,0:T(8,128)(2,1)} %param.12), channel_id=1, source_target_pairs={{0,64},{8,72},{16,80},{24,88},{32,96},{40,104},{48,112},{56,120},{... | collective-permute-start | bytes 196616 | tf_op jit(solution)/shard_map/ppermute | solution.py:422
  12.7 17.3 %collective-permute-start.10 = (bf16[1024,128]{1,0:T(8,128)(2,1)S(1)}, bf16[1024,128]{1,0:T(8,128)(2,1)S(1)}, u32[]{:S(2)}, u32[]{:S(2)}) collective-permute-start(bf16[1024,128]{1,0:T(8,128)(2,1)S(1)} %constant_dynamic-update-slice_fusion.refs_5_), channel_id=1, source_target_pairs={{0,56},{8,0},{16,8},{24,16},{32,24},{40,32},{48,40},{56,48},{64,12... | collective-permute-start | bytes 786440 | tf_op jit(solution)/shard_map/ppermute | solution.py:427
  16.8 13.2 %collective-permute-start.9 = (bf16[1024,128]{1,0:T(8,128)(2,1)S(1)}, bf16[1024,128]{1,0:T(8,128)(2,1)S(1)}, u32[]{:S(2)}, u32[]{:S(2)}) collective-permute-start(bf16[1024,128]{1,0:T(8,128)(2,1)S(1)} %constant_dynamic-update-slice_fusion.refs_5_), channel_id=1, source_target_pairs={{0,8},{8,16},{16,24},{24,32},{32,40},{40,48},{48,56},{56,0},{64,72... | collective-permute-start | bytes 786440 | tf_op jit(solution)/shard_map/ppermute | solution.py:427
  16.8 7.2 %collective-permute-start.2 = (bf16[256,128]{1,0:T(8,128)(2,1)S(1)}, bf16[256,128]{1,0:T(8,128)(2,1)S(1)}, u32[]{:S(2)}, u32[]{:S(2)}) collective-permute-start(bf16[256,128]{1,0:T(8,128)(2,1)S(1)} %collective-permute-done), channel_id=1, source_target_pairs={{0,8},{8,16},{16,24},{24,32},{32,40},{40,48},{48,56},{56,0},{64,72... | collective-permute-start | bytes 196616 | tf_op jit(solution)/shard_map/ppermute | solution.py:427
  17.8 6.9 %collective-permute-start.3 = (bf16[256,128]{1,0:T(8,128)(2,1)S(1)}, bf16[256,128]{1,0:T(8,128)(2,1)S(1)}, u32[]{:S(2)}, u32[]{:S(2)}) collective-permute-start(bf16[256,128]{1,0:T(8,128)(2,1)S(1)} %collective-permute-done.1), channel_id=1, source_target_pairs={{0,56},{8,0},{16,8},{24,16},{32,24},{40,32},{48,40},{56,48},{64,12... | collective-permute-start | bytes 196616 | tf_op jit(solution)/shard_map/ppermute | solution.py:427
  24.0 6.0 %collective-permute-start.4 = (bf16[256,128]{1,0:T(8,128)(2,1)S(1)}, bf16[256,128]{1,0:T(8,128)(2,1)S(1)}, u32[]{:S(2)}, u32[]{:S(2)}) collective-permute-start(bf16[256,128]{1,0:T(8,128)(2,1)S(1)} %collective-permute-done.2), channel_id=1, source_target_pairs={{0,8},{8,16},{16,24},{24,32},{32,40},{40,48},{48,56},{56,0},{64,72... | collective-permute-start | bytes 196616 | tf_op jit(solution)/shard_map/ppermute | solution.py:427
  24.7 5.3 %collective-permute-start.5 = (bf16[256,128]{1,0:T(8,128)(2,1)S(1)}, bf16[256,128]{1,0:T(8,128)(2,1)S(1)}, u32[]{:S(2)}, u32[]{:S(2)}) collective-permute-start(bf16[256,128]{1,0:T(8,128)(2,1)S(1)} %collective-permute-done.3), channel_id=1, source_target_pairs={{0,56},{8,0},{16,8},{24,16},{32,24},{40,32},{48,40},{56,48},{64,12... | collective-permute-start | bytes 196616 | tf_op jit(solution)/shard_map/ppermute | solution.py:427
  30.0 37.1 %copy-start.4 = (bf16[1024,128]{1,0:T(8,128)(2,1)}, bf16[1024,128]{1,0:T(8,128)(2,1)S(1)}, u32[]{:S(2)}) copy-start(bf16[1024,128]{1,0:T(8,128)(2,1)S(1)} %collective-permute-done.10.refs_7_) | copy-start | bytes 786436
  30.0 37.1 %copy-start.6 = (bf16[1024,128]{1,0:T(8,128)(2,1)}, bf16[1024,128]{1,0:T(8,128)(2,1)S(1)}, u32[]{:S(2)}) copy-start(bf16[1024,128]{1,0:T(8,128)(2,1)S(1)} %collective-permute-done.9.refs_6_) | copy-start | bytes 786436
  30.0 5.6 %collective-permute-start.11 = (bf16[256,128]{1,0:T(8,128)(2,1)S(1)}, bf16[256,128]{1,0:T(8,128)(2,1)S(1)}, u32[]{:S(2)}, u32[]{:S(2)}) collective-permute-start(bf16[256,128]{1,0:T(8,128)(2,1)S(1)} %collective-permute-done.4), channel_id=1, source_target_pairs={{0,8},{8,16},{16,24},{24,32},{32,40},{40,48},{48,56},{56,0},{64,72... | collective-permute-start | bytes 196616 | tf_op jit(solution)/shard_map/ppermute | solution.py:427
  31.8 10.7 %collective-permute-start.16 = (bf16[1024,128]{1,0:T(8,128)(2,1)S(1)}, bf16[1024,128]{1,0:T(8,128)(2,1)S(1)}, u32[]{:S(2)}, u32[]{:S(2)}) collective-permute-start(bf16[1024,128]{1,0:T(8,128)(2,1)S(1)} %collective-permute-done.9.refs_6_), channel_id=1, source_target_pairs={{0,8},{8,16},{16,24},{24,32},{32,40},{40,48},{48,56},{56,0},{64,72... | collective-permute-start | bytes 786440 | tf_op jit(solution)/shard_map/ppermute | solution.py:427
  35.6 31.5 %copy-start = (bf16[2048,128]{1,0:T(8,128)(2,1)}, bf16[2048,128]{1,0:T(8,128)(2,1)S(1)}, u32[]{:S(2)}) copy-start(bf16[2048,128]{1,0:T(8,128)(2,1)S(1)} %constant_dynamic-update-slice_fusion.4.refs_0_) | copy-start | bytes 1572868
  35.6 16.5 %collective-permute-start.13 = (bf16[2048,128]{1,0:T(8,128)(2,1)S(1)}, bf16[2048,128]{1,0:T(8,128)(2,1)S(1)}, u32[]{:S(2)}, u32[]{:S(2)}) collective-permute-start(bf16[2048,128]{1,0:T(8,128)(2,1)S(1)} %constant_dynamic-update-slice_fusion.4.refs_0_), channel_id=1, source_target_pairs={{0,64},{8,72},{16,80},{24,88},{32,96},{40,104},{48,112},{56,120},{... | collective-permute-start | bytes 1572872 | tf_op jit(solution)/shard_map/ppermute | solution.py:422
  35.8 17.9 %collective-permute-start.12 = (bf16[2048,128]{1,0:T(8,128)(2,1)S(1)}, bf16[2048,128]{1,0:T(8,128)(2,1)S(1)}, u32[]{:S(2)}, u32[]{:S(2)}) collective-permute-start(bf16[2048,128]{1,0:T(8,128)(2,1)S(1)} %constant_dynamic-update-slice_fusion.4.refs_0_), channel_id=1, source_target_pairs={{0,192},{8,200},{16,208},{24,216},{32,224},{40,232},{48,240},{56,2... | collective-permute-start | bytes 1572872 | tf_op jit(solution)/shard_map/ppermute | solution.py:422
  39.0 8.0 %collective-permute-start.17 = (bf16[1024,128]{1,0:T(8,128)(2,1)S(1)}, bf16[1024,128]{1,0:T(8,128)(2,1)S(1)}, u32[]{:S(2)}, u32[]{:S(2)}) collective-permute-start(bf16[1024,128]{1,0:T(8,128)(2,1)S(1)} %collective-permute-done.10.refs_7_), channel_id=1, source_target_pairs={{0,56},{8,0},{16,8},{24,16},{32,24},{40,32},{48,40},{56,48},{64,12... | collective-permute-start | bytes 786440 | tf_op jit(solution)/shard_map/ppermute | solution.py:427
  42.5 24.6 %copy-start.8 = (bf16[1024,128]{1,0:T(8,128)(2,1)}, bf16[1024,128]{1,0:T(8,128)(2,1)S(1)}, u32[]{:S(2)}) copy-start(bf16[1024,128]{1,0:T(8,128)(2,1)S(1)} %collective-permute-done.16.refs_8_) | copy-start | bytes 786436
  42.5 8.5 %collective-permute-start.18 = (bf16[1024,128]{1,0:T(8,128)(2,1)S(1)}, bf16[1024,128]{1,0:T(8,128)(2,1)S(1)}, u32[]{:S(2)}, u32[]{:S(2)}) collective-permute-start(bf16[1024,128]{1,0:T(8,128)(2,1)S(1)} %collective-permute-done.16.refs_8_), channel_id=1, source_target_pairs={{0,8},{8,16},{16,24},{24,32},{32,40},{40,48},{48,56},{56,0},{64,72... | collective-permute-start | bytes 786440 | tf_op jit(solution)/shard_map/ppermute | solution.py:427
  47.0 20.1 %copy-start.10 = (bf16[1024,128]{1,0:T(8,128)(2,1)}, bf16[1024,128]{1,0:T(8,128)(2,1)S(1)}, u32[]{:S(2)}) copy-start(bf16[1024,128]{1,0:T(8,128)(2,1)S(1)} %collective-permute-done.17.refs_9_) | copy-start | bytes 786436
  47.0 10.0 %collective-permute-start.19 = (bf16[1024,128]{1,0:T(8,128)(2,1)S(1)}, bf16[1024,128]{1,0:T(8,128)(2,1)S(1)}, u32[]{:S(2)}, u32[]{:S(2)}) collective-permute-start(bf16[1024,128]{1,0:T(8,128)(2,1)S(1)} %collective-permute-done.17.refs_9_), channel_id=1, source_target_pairs={{0,56},{8,0},{16,8},{24,16},{32,24},{40,32},{48,40},{56,48},{64,12... | collective-permute-start | bytes 786440 | tf_op jit(solution)/shard_map/ppermute | solution.py:427
  51.0 16.1 %copy-start.12 = (bf16[1024,128]{1,0:T(8,128)(2,1)}, bf16[1024,128]{1,0:T(8,128)(2,1)S(1)}, u32[]{:S(2)}) copy-start(bf16[1024,128]{1,0:T(8,128)(2,1)S(1)} %collective-permute-done.18.refs_10_) | copy-start | bytes 786436
  51.0 7.4 %collective-permute-start.20 = (bf16[1024,128]{1,0:T(8,128)(2,1)S(1)}, bf16[1024,128]{1,0:T(8,128)(2,1)}, u32[]{:S(2)}, u32[]{:S(2)}) collective-permute-start(bf16[1024,128]{1,0:T(8,128)(2,1)S(1)} %collective-permute-done.18.refs_10_), channel_id=1, source_target_pairs={{0,8},{8,16},{16,24},{24,32},{32,40},{40,48},{48,56},{56,0},{64,72... | collective-permute-start | bytes 786440 | tf_op jit(solution)/shard_map/ppermute | solution.py:427
  52.8 7.9 %collective-permute-start.15 = (bf16[1024,128]{1,0:T(8,128)(2,1)}, bf16[1024,128]{1,0:T(8,128)(2,1)}, u32[]{:S(2)}, u32[]{:S(2)}) collective-permute-start(bf16[1024,128]{1,0:T(8,128)(2,1)} %slice.27), channel_id=1, source_target_pairs={{0,64},{8,72},{16,80},{24,88},{32,96},{40,104},{48,112},{56,120},{... | collective-permute-start | bytes 786440 | tf_op jit(solution)/shard_map/ppermute | solution.py:422
  54.4 6.7 %collective-permute-start.14 = (bf16[1024,128]{1,0:T(8,128)(2,1)}, bf16[1024,128]{1,0:T(8,128)(2,1)}, u32[]{:S(2)}, u32[]{:S(2)}) collective-permute-start(bf16[1024,128]{1,0:T(8,128)(2,1)} %slice.26), channel_id=1, source_target_pairs={{0,192},{8,200},{16,208},{24,216},{32,224},{40,232},{48,240},{56,2... | collective-permute-start | bytes 786440 | tf_op jit(solution)/shard_map/ppermute | solution.py:422
  57.0 10.1 %copy-start.14 = (bf16[1024,128]{1,0:T(8,128)(2,1)}, bf16[1024,128]{1,0:T(8,128)(2,1)S(1)}, u32[]{:S(2)}) copy-start(bf16[1024,128]{1,0:T(8,128)(2,1)S(1)} %collective-permute-done.19.refs_11_) | copy-start | bytes 786436
  67.1 49.4 %all-to-all-start = ((bf16[32,128,256]{2,1,0:T(8,128)(2,1)}), bf16[32,128,256]{2,1,0:T(8,128)(2,1)S(1)}, u32[]{:S(2)}, u32[]{:S(2)}) async-start(bf16[32,128,256]{2,1,0:T(8,128)(2,1)} %get-tuple-element.63), calls=%async_computation | async-start | bytes 4194304 | tf_op jit(solution)/shard_map/all_to_all | solution.py:489
  79.7 47.0 %collective-permute-start.23 = (bf16[128,2048]{1,0:T(8,128)(2,1)}, bf16[128,2048]{1,0:T(8,128)(2,1)}, u32[]{:S(2)}, u32[]{:S(2)}) collective-permute-start(bf16[128,2048]{1,0:T(8,128)(2,1)} %get-tuple-element.117), channel_id=1, source_target_pairs={{0,192},{8,200},{16,208},{24,216},{32,224},{40,232},{48,240},{56,2... | collective-permute-start | bytes 1572872 | tf_op jit(solution)/shard_map/ppermute | solution.py:422
  82.4 44.3 %collective-permute-start.22 = (bf16[128,2048]{1,0:T(8,128)(2,1)}, bf16[128,2048]{1,0:T(8,128)(2,1)}, u32[]{:S(2)}, u32[]{:S(2)}) collective-permute-start(bf16[128,2048]{1,0:T(8,128)(2,1)} %get-tuple-element.118), channel_id=1, source_target_pairs={{0,128},{8,136},{16,144},{24,152},{32,160},{40,168},{48,176},{56,1... | collective-permute-start | bytes 1572872 | tf_op jit(solution)/shard_map/ppermute | solution.py:422
  83.2 43.5 %collective-permute-start.21 = (bf16[128,2048]{1,0:T(8,128)(2,1)}, bf16[128,2048]{1,0:T(8,128)(2,1)}, u32[]{:S(2)}, u32[]{:S(2)}) collective-permute-start(bf16[128,2048]{1,0:T(8,128)(2,1)} %get-tuple-element.119), channel_id=1, source_target_pairs={{0,64},{8,72},{16,80},{24,88},{32,96},{40,104},{48,112},{56,120},{... | collective-permute-start | bytes 1572872 | tf_op jit(solution)/shard_map/ppermute | solution.py:422
  126.7 47.0 %all-to-all-start.1 = ((bf16[32,128,256]{2,1,0:T(8,128)(2,1)}), bf16[32,128,256]{2,1,0:T(8,128)(2,1)}, u32[]{:S(2)}, u32[]{:S(2)}) async-start(bf16[32,128,256]{2,1,0:T(8,128)(2,1)} %get-tuple-element.67), calls=%async_computation.1 | async-start | bytes 4194304 | tf_op jit(solution)/shard_map/all_to_all | solution.py:505
  132.6 2.4 %copy-start.1 = (bf16[2048,128]{1,0:T(8,128)(2,1)S(1)}, bf16[2048,128]{1,0:T(8,128)(2,1)}, u32[]{:S(2)}) copy-start(bf16[2048,128]{1,0:T(8,128)(2,1)} %copy-done) | copy-start | bytes 1572868
  134.9 11.0 %collective-permute-start.24 = (bf16[2048,512]{1,0:T(8,128)(2,1)S(1)}, bf16[2048,512]{1,0:T(8,128)(2,1)S(1)}, u32[]{:S(2)}, u32[]{:S(2)}) collective-permute-start(bf16[2048,512]{1,0:T(8,128)(2,1)S(1)} %transpose_pieces.1.own_ref), channel_id=1, source_target_pairs={{0,1},{1,0},{2,3},{3,2},{4,5},{5,4},{6,7},{7,6},{8,9},{9,8},{10,11... | collective-permute-start | bytes 6291464 | tf_op jit(solution)/shard_map/ppermute | solution.py:431
  139.2 8.0 %collective-permute-start.25 = (bf16[8192,128]{1,0:T(8,128)(2,1)}, bf16[8192,128]{1,0:T(8,128)(2,1)}, u32[]{:S(2)}, u32[]{:S(2)}) collective-permute-start(bf16[8192,128]{1,0:T(8,128)(2,1)} %get-tuple-element.100.refs_0_), channel_id=1, source_target_pairs={{0,1},{1,0},{2,3},{3,2},{4,5},{5,4},{6,7},{7,6},{8,9},{9,8},{10,11... | collective-permute-start | bytes 6291464 | tf_op jit(solution)/shard_map/ppermute | solution.py:431
  139.7 7.6 %collective-permute-start.26 = (bf16[8192,128]{1,0:T(8,128)(2,1)}, bf16[8192,128]{1,0:T(8,128)(2,1)}, u32[]{:S(2)}, u32[]{:S(2)}) collective-permute-start(bf16[8192,128]{1,0:T(8,128)(2,1)} %get-tuple-element.101.refs_1_), channel_id=1, source_target_pairs={{0,1},{1,0},{2,3},{3,2},{4,5},{5,4},{6,7},{7,6},{8,9},{9,8},{10,11... | collective-permute-start | bytes 6291464 | tf_op jit(solution)/shard_map/ppermute | solution.py:431
  173.7 12.5 %copy-start.3 = (bf16[2048,512]{1,0:T(8,128)(2,1)S(1)}, bf16[2048,512]{1,0:T(8,128)(2,1)}, u32[]{:S(2)}) copy-start(bf16[2048,512]{1,0:T(8,128)(2,1)} %copy-done.2) | copy-start | bytes 6291460
  176.7 5.3 %collective-permute-start.29 = (bf16[256,256]{1,0:T(8,128)(2,1)S(1)}, bf16[256,256]{1,0:T(8,128)(2,1)S(1)}, u32[]{:S(2)}, u32[]{:S(2)}) collective-permute-start(bf16[256,256]{1,0:T(8,128)(2,1)S(1)} %get-tuple-element.95.refs_0_), channel_id=1, source_target_pairs={{0,192},{8,200},{16,208},{24,216},{32,224},{40,232},{48,240},{56,2... | collective-permute-start | bytes 393224 | tf_op jit(solution)/shard_map/ppermute | solution.py:422
  178.4 6.5 %collective-permute-start.28 = (bf16[256,256]{1,0:T(8,128)(2,1)S(1)}, bf16[256,256]{1,0:T(8,128)(2,1)S(1)}, u32[]{:S(2)}, u32[]{:S(2)}) collective-permute-start(bf16[256,256]{1,0:T(8,128)(2,1)S(1)} %get-tuple-element.95.refs_0_), channel_id=1, source_target_pairs={{0,128},{8,136},{16,144},{24,152},{32,160},{40,168},{48,176},{56,1... | collective-permute-start | bytes 393224 | tf_op jit(solution)/shard_map/ppermute | solution.py:422
  180.1 6.2 %collective-permute-start.27 = (bf16[256,256]{1,0:T(8,128)(2,1)S(1)}, bf16[256,256]{1,0:T(8,128)(2,1)S(1)}, u32[]{:S(2)}, u32[]{:S(2)}) collective-permute-start(bf16[256,256]{1,0:T(8,128)(2,1)S(1)} %get-tuple-element.95.refs_0_), channel_id=1, source_target_pairs={{0,64},{8,72},{16,80},{24,88},{32,96},{40,104},{48,112},{56,120},{... | collective-permute-start | bytes 393224 | tf_op jit(solution)/shard_map/ppermute | solution.py:422
  180.4 8.1 %collective-permute-start.30 = (bf16[256,256]{1,0:T(8,128)(2,1)S(1)}, bf16[256,256]{1,0:T(8,128)(2,1)S(1)}, u32[]{:S(2)}, u32[]{:S(2)}) collective-permute-start(bf16[256,256]{1,0:T(8,128)(2,1)S(1)} %get-tuple-element.98.own_ref), channel_id=1, source_target_pairs={{0,1},{1,0},{2,3},{3,2},{4,5},{5,4},{6,7},{7,6},{8,9},{9,8},{10,11... | collective-permute-start | bytes 393224 | tf_op jit(solution)/shard_map/ppermute | solution.py:431
  188.5 32.6 %all-to-all-start.2 = ((bf16[8,256,256]{2,1,0:T(8,128)(2,1)}), bf16[8,256,256]{2,1,0:T(8,128)(2,1)S(1)}, u32[]{:S(2)}, u32[]{:S(2)}) async-start(bf16[8,256,256]{2,1,0:T(8,128)(2,1)} %weight_terms.1), calls=%async_computation.2 | async-start | bytes 2097152 | tf_op jit(solution)/shard_map/all_to_all | solution.py:520
  198.9 15.8 %collective-permute-start.31 = (bf16[32,8192]{1,0:T(8,128)(2,1)S(1)}, bf16[32,8192]{1,0:T(8,128)(2,1)S(1)}, u32[]{:S(2)}, u32[]{:S(2)}) collective-permute-start(bf16[32,8192]{1,0:T(8,128)(2,1)S(1)} %get-tuple-element.105), channel_id=1, source_target_pairs={{0,2},{1,3},{2,4},{3,5},{4,6},{5,7},{6,0},{7,1},{8,10},{9,11},{10,... | collective-permute-start | bytes 1572872 | tf_op jit(solution)/shard_map/ppermute | solution.py:525
  200.4 19.9 %collective-permute-start.32 = (bf16[32,8192]{1,0:T(8,128)(2,1)S(1)}, bf16[32,8192]{1,0:T(8,128)(2,1)S(1)}, u32[]{:S(2)}, u32[]{:S(2)}) collective-permute-start(bf16[32,8192]{1,0:T(8,128)(2,1)S(1)} %get-tuple-element.106), channel_id=1, source_target_pairs={{0,4},{1,5},{2,6},{3,7},{4,0},{5,1},{6,2},{7,3},{8,12},{9,13},{10,... | collective-permute-start | bytes 1572872 | tf_op jit(solution)/shard_map/ppermute | solution.py:525
  203.1 17.9 %collective-permute-start.33 = (bf16[32,8192]{1,0:T(8,128)(2,1)S(1)}, bf16[32,8192]{1,0:T(8,128)(2,1)}, u32[]{:S(2)}, u32[]{:S(2)}) collective-permute-start(bf16[32,8192]{1,0:T(8,128)(2,1)S(1)} %get-tuple-element.107), channel_id=1, source_target_pairs={{0,6},{1,7},{2,0},{3,1},{4,2},{5,3},{6,4},{7,5},{8,14},{9,15},{10,... | collective-permute-start | bytes 1572872 | tf_op jit(solution)/shard_map/ppermute | solution.py:525
  214.6 5.6 %copy-start.18 = (bf16[32,8192]{1,0:T(8,128)(2,1)}, bf16[32,8192]{1,0:T(8,128)(2,1)S(1)}, u32[]{:S(2)}) copy-start(bf16[32,8192]{1,0:T(8,128)(2,1)S(1)} %collective-permute-done.31) | copy-start | bytes 1572868
  (11 other events, 20.4 us)

commit v10 on v9

--- a/solution.py
+++ b/solution.py
@@ -31,6 +31,10 @@
 
 def cost(flops, mib):
     return pl.CostEstimate(flops=flops, bytes_accessed=mib * MIB, transcendentals=0)
+
+
+def in_hbm():
+    return pl.BlockSpec(memory_space=pltpu.HBM)
 
 
 def in_vmem():
@@ -52,7 +56,7 @@
         y = lax.rem(table_ref[PLACE, 0] + y_off, NY)
         z = lax.rem(table_ref[PLACE, 1] + z_off, NZ)
         size = spot[0][1].stop - spot[0][1].start
-        found.append((pl.ds(pl.multiple_of((y * NZ + z) * size, size), size), spot))
+        found.append((pl.ds(pl.multiple_of((y * NZ + z) * size, size), size), spot, y_off, z))
     return found
 
 
@@ -61,12 +65,30 @@
 
 
 def project_kernel(table_ref, f_ref, *refs, zones):
-    w_refs, (gain_ref, send_ref, raw_ref, kv) = refs[: len(zones)], refs[len(zones) :]
+    w_refs, refs = refs[: len(zones)], refs[len(zones) :]
+    gain_ref, send_ref, raw_ref, kv, held, sems = refs
     head_dim = gain_ref.shape[1]
     tokens = send_ref.shape[1]
+    span = held.shape[2]
+    copies = []
+    for y_off in range(NY):
+        y = lax.rem(table_ref[PLACE, 0] + y_off, NY)
+        here = pl.ds(pl.multiple_of(y * span, span), span)
+        copies.append(
+            pltpu.make_async_copy(f_ref.at[:, here], held.at[y_off], sems.at[y_off])
+        )
+    for copy in copies:
+        copy.start()
     total = jnp.zeros((f_ref.shape[0], 2 * head_dim), F32)
-    for cols, spot in weight_blocks(table_ref, w_refs, zones):
-        total = total + jnp.dot(f_ref[:, cols], side_by_side(spot), preferred_element_type=F32)
+    blocks = weight_blocks(table_ref, w_refs, zones)
+    for y_off in range(NY):
+        copies[y_off].wait()
+        for cols, spot, y_at, z in blocks:
+            if y_at == y_off:
+                here = pl.ds(pl.multiple_of(z * cols.size, cols.size), cols.size)
+                total = total + jnp.dot(
+                    held[y_off, :, here], side_by_side(spot), preferred_element_type=F32
+                )
     raw = total[:, :head_dim]
     raw_ref[...] = raw
     scale = lax.rsqrt(jnp.mean(raw * raw, axis=-1, keepdims=True) + EPS)
@@ -90,9 +112,13 @@
         grid_spec=pltpu.PrefetchScalarGridSpec(
             num_scalar_prefetch=1,
             grid=(),
-            in_specs=[in_vmem()] * (2 + len(pieces)),
+            in_specs=[in_hbm()] + [in_vmem()] * (1 + len(pieces)),
             out_specs=[in_vmem()] * 2,
-            scratch_shapes=[pltpu.VMEM((images, tokens, cols), BF16)],
+            scratch_shapes=[
+                pltpu.VMEM((images, tokens, cols), BF16),
+                pltpu.VMEM((NY, rows.shape[0], rows.shape[1] // NY), BF16),
+                pltpu.SemaphoreType.DMA((NY,)),
+            ],
         ),
         out_shape=[
             pltpu.HBM((dp, tokens, cols), BF16),
@@ -119,8 +145,28 @@
         ]
 
 
-def attend_kernel(table_ref, q_ref, ct_ref, kv_ref, part_ref, probs_ref, ds_ref, acc):
+def attend_kernel(table_ref, q_hbm, ct_hbm, kv_ref, part_ref, probs_hbm, ds_hbm, *scratch):
+    q_ref, ct_ref, probs_ref, ds_ref, acc, in_sems, out_sems = scratch
     blocks = table_ref.shape[1]
+    steps = blocks // GROUP
+    text = q_ref.shape[0] // steps
+
+    def moves(step, pairs, size, sems):
+        here = pl.ds(pl.multiple_of(step * size, size), size)
+        return [
+            pltpu.make_async_copy(a.at[here], b.at[here], sems.at[n, step])
+            for n, (a, b) in enumerate(pairs)
+        ]
+
+    def fetch(step):
+        return moves(step, ((q_hbm, q_ref), (ct_hbm, ct_ref)), text, in_sems)
+
+    def stash(step):
+        return moves(step, ((probs_ref, probs_hbm), (ds_ref, ds_hbm)), GROUP, out_sems)
+
+    for step in range(steps):
+        for copy in fetch(step):
+            copy.start()
     rows = q_ref.shape[0] // blocks
     head_dim = kv_ref.shape[2] // 2
     tokens = kv_ref.shape[1]
@@ -129,6 +175,8 @@
     acc[...] = jnp.zeros_like(acc)
 
     def some_blocks(step, carry):
+        for copy in fetch(step):
+            copy.wait()
         at = [step * GROUP + i for i in range(GROUP)]
         owners = [table_ref[OWNER, b] for b in at]
         starts = [pl.multiple_of(b * rows, rows) for b in at]
@@ -166,9 +214,14 @@
             ds_ref[b] = d_scores[i]
         acc[:, :head_dim] = key_run
         acc[:, head_dim:] = value_run
+        for copy in stash(step):
+            copy.start()
         return carry
 
-    lax.fori_loop(0, blocks // GROUP, some_blocks, 0)
+    lax.fori_loop(0, steps, some_blocks, 0)
+    for step in range(steps):
+        for copy in stash(step):
+            copy.wait()
 
 
 def hold(*arrays):
@@ -184,15 +237,18 @@
         grid_spec=pltpu.PrefetchScalarGridSpec(
             num_scalar_prefetch=1,
             grid=(),
-            in_specs=[in_vmem()] * 3,
-            out_specs=[in_vmem()] * 3,
-            scratch_shapes=[pltpu.VMEM(kv.shape[1:], F32)],
+            in_specs=[in_hbm()] * 2 + [in_vmem()],
+            out_specs=[in_vmem()] + [in_hbm()] * 2,
+            scratch_shapes=[pltpu.VMEM(queries.shape, BF16)] * 2
+            + [pltpu.VMEM(stash.shape, BF16)] * 2
+            + [pltpu.VMEM(kv.shape[1:], F32)]
+            + [pltpu.SemaphoreType.DMA((2, blocks // GROUP))] * 2,
         ),
         out_shape=[pltpu.HBM(kv.shape, BF16), stash, stash],
         compiler_params=limit(13),
         cost_estimate=cost(8 * queries.size * tokens, 8),
         name="attend",
-    )(table, *hold(queries, cotangent, kv))
+    )(table, *hold(queries, cotangent), kv)
 
 
 def apply_kernel(table_ref, kv_ref, probs_ref, ds_ref, out_ref, gq_ref):
@@ -328,7 +384,7 @@
 
 def assemble_kernel(table_ref, *refs, zones):
     w_refs, out_refs = refs[:-2], refs[-2:]
-    for here, spot in weight_blocks(table_ref, w_refs, zones):
+    for here, spot, _, _ in weight_blocks(table_ref, w_refs, zones):
         for out_ref, (ref, rows) in zip(out_refs, spot):
             out_ref[here, :] = ref[rows, :]
 

time: 225 us -> 226 us (level)
  waiting for transfers between devices: 99.4 us -> 102 us
where the time goes in v10:
time: 226 us
  waiting for transfers between devices  102 us (45%)
  starting transfers between devices  70.7 us (31%)
  Pallas kernels  39 us (17%)
  local copies, waits for them, and re-layouts  9.73 us (4%)
  other arithmetic  3.46 us (2%)
    all_to_all x1, waiting for transfers between devices, local(): kv = lax.all_to_all(send, 'dp', 0, 0, tiled=True)  32.5 us
    all_to_all x1, waiting for transfers between devices, local(): parts = lax.all_to_all(parts, 'dp', 0, 0, tiled=True)  28.4 us
    ppermute x14, starting transfers between devices, shift_z(): return lax.ppermute(x, 'dp', pairs)  25 us
    ppermute x13, starting transfers between devices, shift_y(): return lax.ppermute(x, 'dp', pairs)  20.1 us
    ppermute x3, waiting for transfers between devices, local(): terms[s] = lax.ppermute(terms[s], 'tensor', pairs)  16.1 us
    ppermute x14, waiting for transfers between devices, shift_z(): return lax.ppermute(x, 'dp', pairs)  14.2 us
    ppermute x13, waiting for transfers between devices, shift_y(): return lax.ppermute(x, 'dp', pairs)  10.5 us
    all_to_all x1, starting transfers between devices, local(): kv = lax.all_to_all(send, 'dp', 0, 0, tiled=True)  9.56 us
  transfers between devices with their start and end apart: 37, of which 16 were waited for; matrix products, arithmetic and copies ran while one was open for 3% of the time, Pallas kernels for 13%

profile of v10, /device:TPU:32, one launch (start us, length us, event | category | flops | bytes accessed | tf_op | source)
XLA Modules:
  0.0 225.6 jit_solution(1546500053019325235)
XLA Ops:
  0.6 2.0 collective-permute-start
  2.7 3.2 %collective-permute-start.7 = (bf16[256,128]{1,0:T(8,128)(2,1)}, bf16[256,128]{1,0:T(8,128)(2,1)S(1)}, u32[]{:S(2)}, u32[]{:S(2)}) collective-permute-start(bf16[256,128]{1,0:T(8,128)(2,1)} %param.12), channel_id=1, source_target_pairs={{0,128},{8,136},{16,144},{24,152},{32,160},{40,168},{48,176},{56,1... | collective-permute-start | bytes 196616 | tf_op jit(solution)/shard_map/ppermute | solution.py:478
  5.9 1.1 collective-permute-start.6
  10.6 2.1 collective-permute-done.8
  12.7 4.1 %collective-permute-start.10 = (bf16[1024,128]{1,0:T(8,128)(2,1)S(1)}, bf16[1024,128]{1,0:T(8,128)(2,1)S(1)}, u32[]{:S(2)}, u32[]{:S(2)}) collective-permute-start(bf16[1024,128]{1,0:T(8,128)(2,1)S(1)} %constant_dynamic-update-slice_fusion.refs_5_), channel_id=1, source_target_pairs={{0,56},{8,0},{16,8},{24,16},{32,24},{40,32},{48,40},{56,48},{64,12... | collective-permute-start | bytes 786440 | tf_op jit(solution)/shard_map/ppermute | solution.py:483
  17.8 1.1 collective-permute-start.3
  19.0 5.0 %collective-permute-done.2 = bf16[256,128]{1,0:T(8,128)(2,1)S(1)} collective-permute-done((bf16[256,128]{1,0:T(8,128)(2,1)S(1)}, bf16[256,128]{1,0:T(8,128)(2,1)S(1)}, u32[]{:S(2)}, u32[]{:S(2)}) %collective-permute-start.2) | collective-permute-done | bytes 65568 | tf_op jit(solution)/shard_map/ppermute | solution.py:483
  24.7 2.3 %collective-permute-start.5 = (bf16[256,128]{1,0:T(8,128)(2,1)S(1)}, bf16[256,128]{1,0:T(8,128)(2,1)S(1)}, u32[]{:S(2)}, u32[]{:S(2)}) collective-permute-start(bf16[256,128]{1,0:T(8,128)(2,1)S(1)} %collective-permute-done.3), channel_id=1, source_target_pairs={{0,56},{8,0},{16,8},{24,16},{32,24},{40,32},{48,40},{56,48},{64,12... | collective-permute-start | bytes 196616 | tf_op jit(solution)/shard_map/ppermute | solution.py:483
  27.1 2.9 %collective-permute-done.4 = bf16[256,128]{1,0:T(8,128)(2,1)S(1)} collective-permute-done((bf16[256,128]{1,0:T(8,128)(2,1)S(1)}, bf16[256,128]{1,0:T(8,128)(2,1)S(1)}, u32[]{:S(2)}, u32[]{:S(2)}) %collective-permute-start.4) | collective-permute-done | bytes 65568 | tf_op jit(solution)/shard_map/ppermute | solution.py:483
  30.0 1.8 collective-permute-start.11
  31.8 3.2 %collective-permute-start.16 = (bf16[1024,128]{1,0:T(8,128)(2,1)S(1)}, bf16[1024,128]{1,0:T(8,128)(2,1)S(1)}, u32[]{:S(2)}, u32[]{:S(2)}) collective-permute-start(bf16[1024,128]{1,0:T(8,128)(2,1)S(1)} %collective-permute-done.9.refs_6_), channel_id=1, source_target_pairs={{0,8},{8,16},{16,24},{24,32},{32,40},{40,48},{48,56},{56,0},{64,72... | collective-permute-start | bytes 786440 | tf_op jit(solution)/shard_map/ppermute | solution.py:483
  35.8 3.1 %collective-permute-start.12 = (bf16[2048,128]{1,0:T(8,128)(2,1)S(1)}, bf16[2048,128]{1,0:T(8,128)(2,1)S(1)}, u32[]{:S(2)}, u32[]{:S(2)}) collective-permute-start(bf16[2048,128]{1,0:T(8,128)(2,1)S(1)} %constant_dynamic-update-slice_fusion.4.refs_0_), channel_id=1, source_target_pairs={{0,192},{8,200},{16,208},{24,216},{32,224},{40,232},{48,240},{56,2... | collective-permute-start | bytes 1572872 | tf_op jit(solution)/shard_map/ppermute | solution.py:478
  39.0 3.5 %collective-permute-start.17 = (bf16[1024,128]{1,0:T(8,128)(2,1)S(1)}, bf16[1024,128]{1,0:T(8,128)(2,1)S(1)}, u32[]{:S(2)}, u32[]{:S(2)}) collective-permute-start(bf16[1024,128]{1,0:T(8,128)(2,1)S(1)} %collective-permute-done.10.refs_7_), channel_id=1, source_target_pairs={{0,56},{8,0},{16,8},{24,16},{32,24},{40,32},{48,40},{56,48},{64,12... | collective-permute-start | bytes 786440 | tf_op jit(solution)/shard_map/ppermute | solution.py:483
  42.5 1.5 collective-permute-start.18
  44.1 2.9 %collective-permute-done.17.refs_9_ = bf16[1024,128]{1,0:T(8,128)(2,1)S(1)} collective-permute-done((bf16[1024,128]{1,0:T(8,128)(2,1)S(1)}, bf16[1024,128]{1,0:T(8,128)(2,1)S(1)}, u32[]{:S(2)}, u32[]{:S(2)}) %collective-permute-start.17) | collective-permute-done | bytes 262176 | tf_op jit(solution)/shard_map/ppermute | solution.py:483
  47.0 2.5 %collective-permute-start.19 = (bf16[1024,128]{1,0:T(8,128)(2,1)S(1)}, bf16[1024,128]{1,0:T(8,128)(2,1)S(1)}, u32[]{:S(2)}, u32[]{:S(2)}) collective-permute-start(bf16[1024,128]{1,0:T(8,128)(2,1)S(1)} %collective-permute-done.17.refs_9_), channel_id=1, source_target_pairs={{0,56},{8,0},{16,8},{24,16},{32,24},{40,32},{48,40},{56,48},{64,12... | collective-permute-start | bytes 786440 | tf_op jit(solution)/shard_map/ppermute | solution.py:483
  49.5 1.5 collective-permute-done.18.refs_10_
  51.0 1.1 collective-permute-start.20
  54.4 2.4 %collective-permute-start.14 = (bf16[1024,128]{1,0:T(8,128)(2,1)}, bf16[1024,128]{1,0:T(8,128)(2,1)}, u32[]{:S(2)}, u32[]{:S(2)}) collective-permute-start(bf16[1024,128]{1,0:T(8,128)(2,1)} %slice.26), channel_id=1, source_target_pairs={{0,192},{8,200},{16,208},{24,216},{32,224},{40,232},{48,240},{56,2... | collective-permute-start | bytes 786440 | tf_op jit(solution)/shard_map/ppermute | solution.py:478
  57.1 1.3 collective-permute-done.20.refs_12_
  58.4 2.3 %collective-permute-done.15.refs_4_ = bf16[1024,128]{1,0:T(8,128)(2,1)} collective-permute-done((bf16[1024,128]{1,0:T(8,128)(2,1)}, bf16[1024,128]{1,0:T(8,128)(2,1)}, u32[]{:S(2)}, u32[]{:S(2)}) %collective-permute-start.15) | collective-permute-done | bytes 262176 | tf_op jit(solution)/shard_map/ppermute | solution.py:478
  61.1 7.1 %project.1 = (bf16[32,128,256]{2,1,0:T(8,128)(2,1)}, f32[256,128]{1,0:T(8,128)}) custom-call(s32[5,32]{1,0:T(8,128)S(1)} %stack.41.table_ref, bf16[256,8192]{1,0:T(8,128)(2,1)} %bitcast.24, bf16[2048,128]{1,0:T(8,128)(2,1)S(1)} %constant_dynamic-update-slice_fusion.4.refs_0_, bf16[2048,128]{1,0:T(8,128)(2,1)S(1)} %collective-permute-done.12.refs_1_, ...), custom_call_target="tpu_custom_call" | custom-call | flops 1073741824 | bytes 10485760 | tf_op jit(solution)/shard_map/project/pallas_call | solution.py:110
  68.3 9.6 %all-to-all-start = ((bf16[32,128,256]{2,1,0:T(8,128)(2,1)}), bf16[32,128,256]{2,1,0:T(8,128)(2,1)S(1)}, u32[]{:S(2)}, u32[]{:S(2)}) async-start(bf16[32,128,256]{2,1,0:T(8,128)(2,1)} %get-tuple-element.63), calls=%async_computation | async-start | bytes 4194304 | tf_op jit(solution)/shard_map/all_to_all | solution.py:545
  77.9 2.9 %dynamic-slice_bitcast_fusion = (bf16[128,2048]{1,0:T(8,128)(2,1)}, bf16[128,2048]{1,0:T(8,128)(2,1)}, bf16[128,2048]{1,0:T(8,128)(2,1)}, bf16[128,2048]{1,0:T(8,128)(2,1)}) fusion(bf16[2,128,8192]{2,1,0:T(8,128)(2,1)} %param.10, s32[]{:T(128)S(6)} %select_n.86, s32[]{:T(128)S(6)} %select_n.94, s32[]{:T(128)S(6)} %select_n.92, s32[]{:T(128)S(6)} %select_n.90, ...), kind=kLoop, calls=%fused_computation.2 | loop fusion | bytes 4194324 | tf_op jit(solution)/shard_map/squeeze | solution.py:551
  80.9 2.7 %collective-permute-start.23 = (bf16[128,2048]{1,0:T(8,128)(2,1)}, bf16[128,2048]{1,0:T(8,128)(2,1)}, u32[]{:S(2)}, u32[]{:S(2)}) collective-permute-start(bf16[128,2048]{1,0:T(8,128)(2,1)} %get-tuple-element.117), channel_id=1, source_target_pairs={{0,192},{8,200},{16,208},{24,216},{32,224},{40,232},{48,240},{56,2... | collective-permute-start | bytes 1572872 | tf_op jit(solution)/shard_map/ppermute | solution.py:478
  85.2 32.5 %all-to-all-done.kv_ref = bf16[32,128,256]{2,1,0:T(8,128)(2,1)S(1)} async-done(((bf16[32,128,256]{2,1,0:T(8,128)(2,1)}), bf16[32,128,256]{2,1,0:T(8,128)(2,1)S(1)}, u32[]{:S(2)}, u32[]{:S(2)}) %all-to-all-start) | async-done | bytes 2097184 | tf_op jit(solution)/shard_map/all_to_all | solution.py:545
  117.7 7.9 %attend.1 = (bf16[32,128,256]{2,1,0:T(8,128)(2,1)}, bf16[32,128,128]{2,1,0:T(8,128)(2,1)}, bf16[32,128,128]{2,1,0:T(8,128)(2,1)}) custom-call(s32[5,32]{1,0:T(8,128)S(1)} %stack.41.table_ref, bf16[512,1024]{1,0:T(8,128)(2,1)} %q_hbm.1, bf16[512,1024]{1,0:T(8,128)(2,1)} %ct_hbm.1, bf16[32,128,256]{2,1,0:T(8,128)(2,1)S(1)} %all-to-all-done.kv_ref), custom_call_target="tpu_custom_call" | custom-call | flops 536870912 | bytes 8388608 | tf_op jit(solution)/shard_map/attend/pallas_call | solution.py:235
  125.7 5.9 %all-to-all-start.1 = ((bf16[32,128,256]{2,1,0:T(8,128)(2,1)}), bf16[32,128,256]{2,1,0:T(8,128)(2,1)}, u32[]{:S(2)}, u32[]{:S(2)}) async-start(bf16[32,128,256]{2,1,0:T(8,128)(2,1)} %get-tuple-element.67), calls=%async_computation.1 | async-start | bytes 4194304 | tf_op jit(solution)/shard_map/all_to_all | solution.py:561
  131.6 2.2 transpose_pieces.1.own_ref
  134.1 4.1 %assemble.1 = (bf16[8192,128]{1,0:T(8,128)(2,1)}, bf16[8192,128]{1,0:T(8,128)(2,1)}) custom-call(s32[5,32]{1,0:T(8,128)S(1)} %stack.41.table_ref, bf16[2048,128]{1,0:T(8,128)(2,1)S(1)} %copy-done.2, bf16[2048,128]{1,0:T(8,128)(2,1)S(1)} %collective-permute-done.12.refs_1_, bf16[2048,128]{1,0:T(8,128)(2,1)S(1)} %collective-permute-done.13.refs_2_, ...), custom_call_target="tpu_custom_call" | custom-call | bytes 1048576 | tf_op jit(solution)/shard_map/assemble/pallas_call | solution.py:393
  138.7 6.2 %apply.1 = (bf16[512,1024]{1,0:T(8,128)(2,1)}, bf16[512,1024]{1,0:T(8,128)(2,1)}) custom-call(s32[5,32]{1,0:T(8,128)S(1)} %stack.41.table_ref, bf16[32,128,256]{2,1,0:T(8,128)(2,1)} %copy-done, bf16[32,128,128]{2,1,0:T(8,128)(2,1)} %get-tuple-element.72.probs_ref, bf16[32,128,128]{2,1,0:T(8,128)(2,1)} %get-tuple-element.73.ds_ref), custom_call_target="tpu_custom_call" | custom-call | flops 268435456 | bytes 6291456 | tf_op jit(solution)/shard_map/apply/pallas_call | solution.py:277
  144.8 1.4 copy-done.3
  146.2 28.4 %all-to-all-done.1.part_ref = bf16[32,128,256]{2,1,0:T(8,128)(2,1)} async-done(((bf16[32,128,256]{2,1,0:T(8,128)(2,1)}), bf16[32,128,256]{2,1,0:T(8,128)(2,1)}, u32[]{:S(2)}, u32[]{:S(2)}) %all-to-all-start.1) | async-done | bytes 2097184 | tf_op jit(solution)/shard_map/all_to_all | solution.py:561
  174.6 3.0 %owner_grads.1 = (bf16[256,256]{1,0:T(8,128)(2,1)S(1)}, bf16[256,256]{1,0:T(8,128)(2,1)S(1)}) custom-call(s32[5,32]{1,0:T(8,128)S(1)} %stack.41.table_ref, bf16[32,128,256]{2,1,0:T(8,128)(2,1)} %all-to-all-done.1.part_ref, f32[256,128]{1,0:T(8,128)} %get-tuple-element.65.raw_ref, f32[1,128]{1,0:T(1,128)S(1)} %bitcast.23), custom_call_target="tpu_custom_call" | custom-call | bytes 3145728 | tf_op jit(solution)/shard_map/owner_grads/pallas_call | solution.py:323
  177.6 1.6 collective-permute-start.29
  179.2 1.9 collective-permute-start.28
  181.6 1.1 collective-permute-done.29.refs_3_
  182.7 3.0 %collective-permute-done.28.refs_2_ = bf16[256,256]{1,0:T(8,128)(2,1)S(1)} collective-permute-done((bf16[256,256]{1,0:T(8,128)(2,1)S(1)}, bf16[256,256]{1,0:T(8,128)(2,1)S(1)}, u32[]{:S(2)}, u32[]{:S(2)}) %collective-permute-start.28) | collective-permute-done | bytes 131104 | tf_op jit(solution)/shard_map/ppermute | solution.py:478
  185.7 1.6 collective-permute-done.27.refs_1_
  187.3 2.3 %weight_terms.1 = bf16[8,256,256]{2,1,0:T(8,128)(2,1)} custom-call(bf16[2048,512]{1,0:T(8,128)(2,1)S(1)} %transpose_pieces.1.own_ref, bf16[2048,512]{1,0:T(8,128)(2,1)S(1)} %copy-done.4, bf16[256,256]{1,0:T(8,128)(2,1)S(1)} %get-tuple-element.95.refs_0_, bf16[256,256]{1,0:T(8,128)(2,1)S(1)} %collective-permute-done.27.refs_1_, ...), custom_call_target="tpu_custom_call" | custom-call | flops 1073741824 | bytes 6291456 | tf_op jit(solution)/shard_map/weight_terms/pallas_call | solution.py:374
  189.6 3.8 %all-to-all-start.2 = ((bf16[8,256,256]{2,1,0:T(8,128)(2,1)}), bf16[8,256,256]{2,1,0:T(8,128)(2,1)S(1)}, u32[]{:S(2)}, u32[]{:S(2)}) async-start(bf16[8,256,256]{2,1,0:T(8,128)(2,1)} %weight_terms.1), calls=%async_computation.2 | async-start | bytes 2097152 | tf_op jit(solution)/shard_map/all_to_all | solution.py:576
  193.4 6.2 %feature_terms.1 = (bf16[32,8192]{1,0:T(8,128)(2,1)S(1)}, bf16[32,8192]{1,0:T(8,128)(2,1)S(1)}, bf16[32,8192]{1,0:T(8,128)(2,1)S(1)}, bf16[32,8192]{1,0:T(8,128)(2,1)S(1)}) custom-call(s32[5,32]{1,0:T(8,128)S(1)} %stack.41.table_ref, bf16[256,256]{1,0:T(8,128)(2,1)S(1)} %get-tuple-element.98.own_ref, bf16[256,256]{1,0:T(8,128)(2,1)S(1)} %collective-permute-done.30.other_ref, ...), custom_call_target="tpu_custom_call" | custom-call | flops 2147483648 | bytes 10485760 | tf_op jit(solution)/shard_map/feature_terms/pallas_call | solution.py:454
  199.6 1.6 collective-permute-start.31
  201.2 2.7 %collective-permute-start.32 = (bf16[32,8192]{1,0:T(8,128)(2,1)S(1)}, bf16[32,8192]{1,0:T(8,128)(2,1)S(1)}, u32[]{:S(2)}, u32[]{:S(2)}) collective-permute-start(bf16[32,8192]{1,0:T(8,128)(2,1)S(1)} %get-tuple-element.106), channel_id=1, source_target_pairs={{0,4},{1,5},{2,6},{3,7},{4,0},{5,1},{6,2},{7,3},{8,12},{9,13},{10,... | collective-permute-start | bytes 1572872 | tf_op jit(solution)/shard_map/ppermute | solution.py:581
  203.9 1.4 collective-permute-start.33
  205.3 10.4 %collective-permute-done.31 = bf16[32,8192]{1,0:T(8,128)(2,1)S(1)} collective-permute-done((bf16[32,8192]{1,0:T(8,128)(2,1)S(1)}, bf16[32,8192]{1,0:T(8,128)(2,1)S(1)}, u32[]{:S(2)}, u32[]{:S(2)}) %collective-permute-start.31) | collective-permute-done | bytes 524320 | tf_op jit(solution)/shard_map/ppermute | solution.py:581
  215.7 5.7 %collective-permute-done.32 = bf16[32,8192]{1,0:T(8,128)(2,1)S(1)} collective-permute-done((bf16[32,8192]{1,0:T(8,128)(2,1)S(1)}, bf16[32,8192]{1,0:T(8,128)(2,1)S(1)}, u32[]{:S(2)}, u32[]{:S(2)}) %collective-permute-start.32) | collective-permute-done | bytes 524320 | tf_op jit(solution)/shard_map/ppermute | solution.py:581
  223.5 2.1 add_convert_fusion
  (107 shorter events, 14.2 us)
Async XLA Ops:
  0.6 60.5 %copy-start.17 = (f32[128]{0:T(128)S(1)}, f32[128]{0:T(128)}, u32[]{:S(2)}) copy-start(f32[128]{0:T(128)} %param.13) | copy-start | bytes 1540
  0.6 16.2 %collective-permute-start = (bf16[256,128]{1,0:T(8,128)(2,1)}, bf16[256,128]{1,0:T(8,128)(2,1)S(1)}, u32[]{:S(2)}, u32[]{:S(2)}) collective-permute-start(bf16[256,128]{1,0:T(8,128)(2,1)} %param.11), channel_id=1, source_target_pairs={{0,8},{8,16},{16,24},{24,32},{32,40},{40,48},{48,56},{56,0},{64,72... | collective-permute-start | bytes 196616 | tf_op jit(solution)/shard_map/ppermute | solution.py:483
  2.6 15.2 %collective-permute-start.1 = (bf16[256,128]{1,0:T(8,128)(2,1)}, bf16[256,128]{1,0:T(8,128)(2,1)S(1)}, u32[]{:S(2)}, u32[]{:S(2)}) collective-permute-start(bf16[256,128]{1,0:T(8,128)(2,1)} %param.11), channel_id=1, source_target_pairs={{0,56},{8,0},{16,8},{24,16},{32,24},{40,32},{48,40},{56,48},{64,12... | collective-permute-start | bytes 196616 | tf_op jit(solution)/shard_map/ppermute | solution.py:483
  2.7 7.9 %collective-permute-start.7 = (bf16[256,128]{1,0:T(8,128)(2,1)}, bf16[256,128]{1,0:T(8,128)(2,1)S(1)}, u32[]{:S(2)}, u32[]{:S(2)}) collective-permute-start(bf16[256,128]{1,0:T(8,128)(2,1)} %param.12), channel_id=1, source_target_pairs={{0,128},{8,136},{16,144},{24,152},{32,160},{40,168},{48,176},{56,1... | collective-permute-start | bytes 196616 | tf_op jit(solution)/shard_map/ppermute | solution.py:478
  5.9 4.6 %collective-permute-start.6 = (bf16[256,128]{1,0:T(8,128)(2,1)}, bf16[256,128]{1,0:T(8,128)(2,1)S(1)}, u32[]{:S(2)}, u32[]{:S(2)}) collective-permute-start(bf16[256,128]{1,0:T(8,128)(2,1)} %param.12), channel_id=1, source_target_pairs={{0,192},{8,200},{16,208},{24,216},{32,224},{40,232},{48,240},{56,2... | collective-permute-start | bytes 196616 | tf_op jit(solution)/shard_map/ppermute | solution.py:478
  7.0 5.7 %collective-permute-start.8 = (bf16[256,128]{1,0:T(8,128)(2,1)}, bf16[256,128]{1,0:T(8,128)(2,1)S(1)}, u32[]{:S(2)}, u32[]{:S(2)}) collective-permute-start(bf16[256,128]{1,0:T(8,128)(2,1)} %param.12), channel_id=1, source_target_pairs={{0,64},{8,72},{16,80},{24,88},{32,96},{40,104},{48,112},{56,120},{... | collective-permute-start | bytes 196616 | tf_op jit(solution)/shard_map/ppermute | solution.py:478
  12.7 17.3 %collective-permute-start.10 = (bf16[1024,128]{1,0:T(8,128)(2,1)S(1)}, bf16[1024,128]{1,0:T(8,128)(2,1)S(1)}, u32[]{:S(2)}, u32[]{:S(2)}) collective-permute-start(bf16[1024,128]{1,0:T(8,128)(2,1)S(1)} %constant_dynamic-update-slice_fusion.refs_5_), channel_id=1, source_target_pairs={{0,56},{8,0},{16,8},{24,16},{32,24},{40,32},{48,40},{56,48},{64,12... | collective-permute-start | bytes 786440 | tf_op jit(solution)/shard_map/ppermute | solution.py:483
  16.8 13.2 %collective-permute-start.9 = (bf16[1024,128]{1,0:T(8,128)(2,1)S(1)}, bf16[1024,128]{1,0:T(8,128)(2,1)S(1)}, u32[]{:S(2)}, u32[]{:S(2)}) collective-permute-start(bf16[1024,128]{1,0:T(8,128)(2,1)S(1)} %constant_dynamic-update-slice_fusion.refs_5_), channel_id=1, source_target_pairs={{0,8},{8,16},{16,24},{24,32},{32,40},{40,48},{48,56},{56,0},{64,72... | collective-permute-start | bytes 786440 | tf_op jit(solution)/shard_map/ppermute | solution.py:483
  16.8 7.2 %collective-permute-start.2 = (bf16[256,128]{1,0:T(8,128)(2,1)S(1)}, bf16[256,128]{1,0:T(8,128)(2,1)S(1)}, u32[]{:S(2)}, u32[]{:S(2)}) collective-permute-start(bf16[256,128]{1,0:T(8,128)(2,1)S(1)} %collective-permute-done), channel_id=1, source_target_pairs={{0,8},{8,16},{16,24},{24,32},{32,40},{40,48},{48,56},{56,0},{64,72... | collective-permute-start | bytes 196616 | tf_op jit(solution)/shard_map/ppermute | solution.py:483
  17.8 6.9 %collective-permute-start.3 = (bf16[256,128]{1,0:T(8,128)(2,1)S(1)}, bf16[256,128]{1,0:T(8,128)(2,1)S(1)}, u32[]{:S(2)}, u32[]{:S(2)}) collective-permute-start(bf16[256,128]{1,0:T(8,128)(2,1)S(1)} %collective-permute-done.1), channel_id=1, source_target_pairs={{0,56},{8,0},{16,8},{24,16},{32,24},{40,32},{48,40},{56,48},{64,12... | collective-permute-start | bytes 196616 | tf_op jit(solution)/shard_map/ppermute | solution.py:483
  24.0 6.0 %collective-permute-start.4 = (bf16[256,128]{1,0:T(8,128)(2,1)S(1)}, bf16[256,128]{1,0:T(8,128)(2,1)S(1)}, u32[]{:S(2)}, u32[]{:S(2)}) collective-permute-start(bf16[256,128]{1,0:T(8,128)(2,1)S(1)} %collective-permute-done.2), channel_id=1, source_target_pairs={{0,8},{8,16},{16,24},{24,32},{32,40},{40,48},{48,56},{56,0},{64,72... | collective-permute-start | bytes 196616 | tf_op jit(solution)/shard_map/ppermute | solution.py:483
  24.7 5.3 %collective-permute-start.5 = (bf16[256,128]{1,0:T(8,128)(2,1)S(1)}, bf16[256,128]{1,0:T(8,128)(2,1)S(1)}, u32[]{:S(2)}, u32[]{:S(2)}) collective-permute-start(bf16[256,128]{1,0:T(8,128)(2,1)S(1)} %collective-permute-done.3), channel_id=1, source_target_pairs={{0,56},{8,0},{16,8},{24,16},{32,24},{40,32},{48,40},{56,48},{64,12... | collective-permute-start | bytes 196616 | tf_op jit(solution)/shard_map/ppermute | solution.py:483
  30.0 38.2 %copy-start.5 = (bf16[1024,128]{1,0:T(8,128)(2,1)}, bf16[1024,128]{1,0:T(8,128)(2,1)S(1)}, u32[]{:S(2)}) copy-start(bf16[1024,128]{1,0:T(8,128)(2,1)S(1)} %collective-permute-done.10.refs_7_) | copy-start | bytes 786436
  30.0 38.2 %copy-start.7 = (bf16[1024,128]{1,0:T(8,128)(2,1)}, bf16[1024,128]{1,0:T(8,128)(2,1)S(1)}, u32[]{:S(2)}) copy-start(bf16[1024,128]{1,0:T(8,128)(2,1)S(1)} %collective-permute-done.9.refs_6_) | copy-start | bytes 786436
  30.0 5.6 %collective-permute-start.11 = (bf16[256,128]{1,0:T(8,128)(2,1)S(1)}, bf16[256,128]{1,0:T(8,128)(2,1)S(1)}, u32[]{:S(2)}, u32[]{:S(2)}) collective-permute-start(bf16[256,128]{1,0:T(8,128)(2,1)S(1)} %collective-permute-done.4), channel_id=1, source_target_pairs={{0,8},{8,16},{16,24},{24,32},{32,40},{40,48},{48,56},{56,0},{64,72... | collective-permute-start | bytes 196616 | tf_op jit(solution)/shard_map/ppermute | solution.py:483
  31.8 10.7 %collective-permute-start.16 = (bf16[1024,128]{1,0:T(8,128)(2,1)S(1)}, bf16[1024,128]{1,0:T(8,128)(2,1)S(1)}, u32[]{:S(2)}, u32[]{:S(2)}) collective-permute-start(bf16[1024,128]{1,0:T(8,128)(2,1)S(1)} %collective-permute-done.9.refs_6_), channel_id=1, source_target_pairs={{0,8},{8,16},{16,24},{24,32},{32,40},{40,48},{48,56},{56,0},{64,72... | collective-permute-start | bytes 786440 | tf_op jit(solution)/shard_map/ppermute | solution.py:483
  35.6 32.7 %copy-start.1 = (bf16[2048,128]{1,0:T(8,128)(2,1)}, bf16[2048,128]{1,0:T(8,128)(2,1)S(1)}, u32[]{:S(2)}) copy-start(bf16[2048,128]{1,0:T(8,128)(2,1)S(1)} %constant_dynamic-update-slice_fusion.4.refs_0_) | copy-start | bytes 1572868
  35.6 16.5 %collective-permute-start.13 = (bf16[2048,128]{1,0:T(8,128)(2,1)S(1)}, bf16[2048,128]{1,0:T(8,128)(2,1)S(1)}, u32[]{:S(2)}, u32[]{:S(2)}) collective-permute-start(bf16[2048,128]{1,0:T(8,128)(2,1)S(1)} %constant_dynamic-update-slice_fusion.4.refs_0_), channel_id=1, source_target_pairs={{0,64},{8,72},{16,80},{24,88},{32,96},{40,104},{48,112},{56,120},{... | collective-permute-start | bytes 1572872 | tf_op jit(solution)/shard_map/ppermute | solution.py:478
  35.8 17.9 %collective-permute-start.12 = (bf16[2048,128]{1,0:T(8,128)(2,1)S(1)}, bf16[2048,128]{1,0:T(8,128)(2,1)S(1)}, u32[]{:S(2)}, u32[]{:S(2)}) collective-permute-start(bf16[2048,128]{1,0:T(8,128)(2,1)S(1)} %constant_dynamic-update-slice_fusion.4.refs_0_), channel_id=1, source_target_pairs={{0,192},{8,200},{16,208},{24,216},{32,224},{40,232},{48,240},{56,2... | collective-permute-start | bytes 1572872 | tf_op jit(solution)/shard_map/ppermute | solution.py:478
  39.0 8.0 %collective-permute-start.17 = (bf16[1024,128]{1,0:T(8,128)(2,1)S(1)}, bf16[1024,128]{1,0:T(8,128)(2,1)S(1)}, u32[]{:S(2)}, u32[]{:S(2)}) collective-permute-start(bf16[1024,128]{1,0:T(8,128)(2,1)S(1)} %collective-permute-done.10.refs_7_), channel_id=1, source_target_pairs={{0,56},{8,0},{16,8},{24,16},{32,24},{40,32},{48,40},{56,48},{64,12... | collective-permute-start | bytes 786440 | tf_op jit(solution)/shard_map/ppermute | solution.py:483
  42.5 25.8 %copy-start.9 = (bf16[1024,128]{1,0:T(8,128)(2,1)}, bf16[1024,128]{1,0:T(8,128)(2,1)S(1)}, u32[]{:S(2)}) copy-start(bf16[1024,128]{1,0:T(8,128)(2,1)S(1)} %collective-permute-done.16.refs_8_) | copy-start | bytes 786436
  42.5 8.5 %collective-permute-start.18 = (bf16[1024,128]{1,0:T(8,128)(2,1)S(1)}, bf16[1024,128]{1,0:T(8,128)(2,1)S(1)}, u32[]{:S(2)}, u32[]{:S(2)}) collective-permute-start(bf16[1024,128]{1,0:T(8,128)(2,1)S(1)} %collective-permute-done.16.refs_8_), channel_id=1, source_target_pairs={{0,8},{8,16},{16,24},{24,32},{32,40},{40,48},{48,56},{56,0},{64,72... | collective-permute-start | bytes 786440 | tf_op jit(solution)/shard_map/ppermute | solution.py:483
  47.0 21.2 %copy-start.11 = (bf16[1024,128]{1,0:T(8,128)(2,1)}, bf16[1024,128]{1,0:T(8,128)(2,1)S(1)}, u32[]{:S(2)}) copy-start(bf16[1024,128]{1,0:T(8,128)(2,1)S(1)} %collective-permute-done.17.refs_9_) | copy-start | bytes 786436
  47.0 10.0 %collective-permute-start.19 = (bf16[1024,128]{1,0:T(8,128)(2,1)S(1)}, bf16[1024,128]{1,0:T(8,128)(2,1)S(1)}, u32[]{:S(2)}, u32[]{:S(2)}) collective-permute-start(bf16[1024,128]{1,0:T(8,128)(2,1)S(1)} %collective-permute-done.17.refs_9_), channel_id=1, source_target_pairs={{0,56},{8,0},{16,8},{24,16},{32,24},{40,32},{48,40},{56,48},{64,12... | collective-permute-start | bytes 786440 | tf_op jit(solution)/shard_map/ppermute | solution.py:483
  51.0 17.3 %copy-start.13 = (bf16[1024,128]{1,0:T(8,128)(2,1)}, bf16[1024,128]{1,0:T(8,128)(2,1)S(1)}, u32[]{:S(2)}) copy-start(bf16[1024,128]{1,0:T(8,128)(2,1)S(1)} %collective-permute-done.18.refs_10_) | copy-start | bytes 786436
  51.0 7.4 %collective-permute-start.20 = (bf16[1024,128]{1,0:T(8,128)(2,1)S(1)}, bf16[1024,128]{1,0:T(8,128)(2,1)}, u32[]{:S(2)}, u32[]{:S(2)}) collective-permute-start(bf16[1024,128]{1,0:T(8,128)(2,1)S(1)} %collective-permute-done.18.refs_10_), channel_id=1, source_target_pairs={{0,8},{8,16},{16,24},{24,32},{32,40},{40,48},{48,56},{56,0},{64,72... | collective-permute-start | bytes 786440 | tf_op jit(solution)/shard_map/ppermute | solution.py:483
  52.8 7.9 %collective-permute-start.15 = (bf16[1024,128]{1,0:T(8,128)(2,1)}, bf16[1024,128]{1,0:T(8,128)(2,1)}, u32[]{:S(2)}, u32[]{:S(2)}) collective-permute-start(bf16[1024,128]{1,0:T(8,128)(2,1)} %slice.27), channel_id=1, source_target_pairs={{0,64},{8,72},{16,80},{24,88},{32,96},{40,104},{48,112},{56,120},{... | collective-permute-start | bytes 786440 | tf_op jit(solution)/shard_map/ppermute | solution.py:478
  54.4 6.7 %collective-permute-start.14 = (bf16[1024,128]{1,0:T(8,128)(2,1)}, bf16[1024,128]{1,0:T(8,128)(2,1)}, u32[]{:S(2)}, u32[]{:S(2)}) collective-permute-start(bf16[1024,128]{1,0:T(8,128)(2,1)} %slice.26), channel_id=1, source_target_pairs={{0,192},{8,200},{16,208},{24,216},{32,224},{40,232},{48,240},{56,2... | collective-permute-start | bytes 786440 | tf_op jit(solution)/shard_map/ppermute | solution.py:478
  57.0 11.2 %copy-start.15 = (bf16[1024,128]{1,0:T(8,128)(2,1)}, bf16[1024,128]{1,0:T(8,128)(2,1)S(1)}, u32[]{:S(2)}) copy-start(bf16[1024,128]{1,0:T(8,128)(2,1)S(1)} %collective-permute-done.19.refs_11_) | copy-start | bytes 786436
  68.3 49.4 %all-to-all-start = ((bf16[32,128,256]{2,1,0:T(8,128)(2,1)}), bf16[32,128,256]{2,1,0:T(8,128)(2,1)S(1)}, u32[]{:S(2)}, u32[]{:S(2)}) async-start(bf16[32,128,256]{2,1,0:T(8,128)(2,1)} %get-tuple-element.63), calls=%async_computation | async-start | bytes 4194304 | tf_op jit(solution)/shard_map/all_to_all | solution.py:545
  80.9 44.8 %collective-permute-start.23 = (bf16[128,2048]{1,0:T(8,128)(2,1)}, bf16[128,2048]{1,0:T(8,128)(2,1)}, u32[]{:S(2)}, u32[]{:S(2)}) collective-permute-start(bf16[128,2048]{1,0:T(8,128)(2,1)} %get-tuple-element.117), channel_id=1, source_target_pairs={{0,192},{8,200},{16,208},{24,216},{32,224},{40,232},{48,240},{56,2... | collective-permute-start | bytes 1572872 | tf_op jit(solution)/shard_map/ppermute | solution.py:478
  83.6 42.1 %collective-permute-start.22 = (bf16[128,2048]{1,0:T(8,128)(2,1)}, bf16[128,2048]{1,0:T(8,128)(2,1)}, u32[]{:S(2)}, u32[]{:S(2)}) collective-permute-start(bf16[128,2048]{1,0:T(8,128)(2,1)} %get-tuple-element.118), channel_id=1, source_target_pairs={{0,128},{8,136},{16,144},{24,152},{32,160},{40,168},{48,176},{56,1... | collective-permute-start | bytes 1572872 | tf_op jit(solution)/shard_map/ppermute | solution.py:478
  84.4 41.3 %collective-permute-start.21 = (bf16[128,2048]{1,0:T(8,128)(2,1)}, bf16[128,2048]{1,0:T(8,128)(2,1)}, u32[]{:S(2)}, u32[]{:S(2)}) collective-permute-start(bf16[128,2048]{1,0:T(8,128)(2,1)} %get-tuple-element.119), channel_id=1, source_target_pairs={{0,64},{8,72},{16,80},{24,88},{32,96},{40,104},{48,112},{56,120},{... | collective-permute-start | bytes 1572872 | tf_op jit(solution)/shard_map/ppermute | solution.py:478
  117.7 7.9 %copy-start = (bf16[32,128,256]{2,1,0:T(8,128)(2,1)}, bf16[32,128,256]{2,1,0:T(8,128)(2,1)S(1)}, u32[]{:S(2)}) copy-start(bf16[32,128,256]{2,1,0:T(8,128)(2,1)S(1)} %all-to-all-done.kv_ref) | copy-start | bytes 6291460
  125.7 48.9 %all-to-all-start.1 = ((bf16[32,128,256]{2,1,0:T(8,128)(2,1)}), bf16[32,128,256]{2,1,0:T(8,128)(2,1)}, u32[]{:S(2)}, u32[]{:S(2)}) async-start(bf16[32,128,256]{2,1,0:T(8,128)(2,1)} %get-tuple-element.67), calls=%async_computation.1 | async-start | bytes 4194304 | tf_op jit(solution)/shard_map/all_to_all | solution.py:561
  133.9 11.0 %collective-permute-start.24 = (bf16[2048,512]{1,0:T(8,128)(2,1)S(1)}, bf16[2048,512]{1,0:T(8,128)(2,1)S(1)}, u32[]{:S(2)}, u32[]{:S(2)}) collective-permute-start(bf16[2048,512]{1,0:T(8,128)(2,1)S(1)} %transpose_pieces.1.own_ref), channel_id=1, source_target_pairs={{0,1},{1,0},{2,3},{3,2},{4,5},{5,4},{6,7},{7,6},{8,9},{9,8},{10,11... | collective-permute-start | bytes 6291464 | tf_op jit(solution)/shard_map/ppermute | solution.py:487
  138.2 8.0 %collective-permute-start.25 = (bf16[8192,128]{1,0:T(8,128)(2,1)}, bf16[8192,128]{1,0:T(8,128)(2,1)}, u32[]{:S(2)}, u32[]{:S(2)}) collective-permute-start(bf16[8192,128]{1,0:T(8,128)(2,1)} %get-tuple-element.100.refs_0_), channel_id=1, source_target_pairs={{0,1},{1,0},{2,3},{3,2},{4,5},{5,4},{6,7},{7,6},{8,9},{9,8},{10,11... | collective-permute-start | bytes 6291464 | tf_op jit(solution)/shard_map/ppermute | solution.py:487
  138.6 7.6 %collective-permute-start.26 = (bf16[8192,128]{1,0:T(8,128)(2,1)}, bf16[8192,128]{1,0:T(8,128)(2,1)}, u32[]{:S(2)}, u32[]{:S(2)}) collective-permute-start(bf16[8192,128]{1,0:T(8,128)(2,1)} %get-tuple-element.101.refs_1_), channel_id=1, source_target_pairs={{0,1},{1,0},{2,3},{3,2},{4,5},{5,4},{6,7},{7,6},{8,9},{9,8},{10,11... | collective-permute-start | bytes 6291464 | tf_op jit(solution)/shard_map/ppermute | solution.py:487
  174.6 12.7 %copy-start.4 = (bf16[2048,512]{1,0:T(8,128)(2,1)S(1)}, bf16[2048,512]{1,0:T(8,128)(2,1)}, u32[]{:S(2)}) copy-start(bf16[2048,512]{1,0:T(8,128)(2,1)} %copy-done.3) | copy-start | bytes 6291460
  177.6 5.0 %collective-permute-start.29 = (bf16[256,256]{1,0:T(8,128)(2,1)S(1)}, bf16[256,256]{1,0:T(8,128)(2,1)S(1)}, u32[]{:S(2)}, u32[]{:S(2)}) collective-permute-start(bf16[256,256]{1,0:T(8,128)(2,1)S(1)} %get-tuple-element.95.refs_0_), channel_id=1, source_target_pairs={{0,192},{8,200},{16,208},{24,216},{32,224},{40,232},{48,240},{56,2... | collective-permute-start | bytes 393224 | tf_op jit(solution)/shard_map/ppermute | solution.py:478
  179.2 6.5 %collective-permute-start.28 = (bf16[256,256]{1,0:T(8,128)(2,1)S(1)}, bf16[256,256]{1,0:T(8,128)(2,1)S(1)}, u32[]{:S(2)}, u32[]{:S(2)}) collective-permute-start(bf16[256,256]{1,0:T(8,128)(2,1)S(1)} %get-tuple-element.95.refs_0_), channel_id=1, source_target_pairs={{0,128},{8,136},{16,144},{24,152},{32,160},{40,168},{48,176},{56,1... | collective-permute-start | bytes 393224 | tf_op jit(solution)/shard_map/ppermute | solution.py:478
  181.1 6.2 %collective-permute-start.27 = (bf16[256,256]{1,0:T(8,128)(2,1)S(1)}, bf16[256,256]{1,0:T(8,128)(2,1)S(1)}, u32[]{:S(2)}, u32[]{:S(2)}) collective-permute-start(bf16[256,256]{1,0:T(8,128)(2,1)S(1)} %get-tuple-element.95.refs_0_), channel_id=1, source_target_pairs={{0,64},{8,72},{16,80},{24,88},{32,96},{40,104},{48,112},{56,120},{... | collective-permute-start | bytes 393224 | tf_op jit(solution)/shard_map/ppermute | solution.py:478
  181.6 8.0 %collective-permute-start.30 = (bf16[256,256]{1,0:T(8,128)(2,1)S(1)}, bf16[256,256]{1,0:T(8,128)(2,1)S(1)}, u32[]{:S(2)}, u32[]{:S(2)}) collective-permute-start(bf16[256,256]{1,0:T(8,128)(2,1)S(1)} %get-tuple-element.98.own_ref), channel_id=1, source_target_pairs={{0,1},{1,0},{2,3},{3,2},{4,5},{5,4},{6,7},{7,6},{8,9},{9,8},{10,11... | collective-permute-start | bytes 393224 | tf_op jit(solution)/shard_map/ppermute | solution.py:487
  189.6 32.6 %all-to-all-start.2 = ((bf16[8,256,256]{2,1,0:T(8,128)(2,1)}), bf16[8,256,256]{2,1,0:T(8,128)(2,1)S(1)}, u32[]{:S(2)}, u32[]{:S(2)}) async-start(bf16[8,256,256]{2,1,0:T(8,128)(2,1)} %weight_terms.1), calls=%async_computation.2 | async-start | bytes 2097152 | tf_op jit(solution)/shard_map/all_to_all | solution.py:576
  199.6 16.1 %collective-permute-start.31 = (bf16[32,8192]{1,0:T(8,128)(2,1)S(1)}, bf16[32,8192]{1,0:T(8,128)(2,1)S(1)}, u32[]{:S(2)}, u32[]{:S(2)}) collective-permute-start(bf16[32,8192]{1,0:T(8,128)(2,1)S(1)} %get-tuple-element.105), channel_id=1, source_target_pairs={{0,2},{1,3},{2,4},{3,5},{4,6},{5,7},{6,0},{7,1},{8,10},{9,11},{10,... | collective-permute-start | bytes 1572872 | tf_op jit(solution)/shard_map/ppermute | solution.py:581
  201.2 20.3 %collective-permute-start.32 = (bf16[32,8192]{1,0:T(8,128)(2,1)S(1)}, bf16[32,8192]{1,0:T(8,128)(2,1)S(1)}, u32[]{:S(2)}, u32[]{:S(2)}) collective-permute-start(bf16[32,8192]{1,0:T(8,128)(2,1)S(1)} %get-tuple-element.106), channel_id=1, source_target_pairs={{0,4},{1,5},{2,6},{3,7},{4,0},{5,1},{6,2},{7,3},{8,12},{9,13},{10,... | collective-permute-start | bytes 1572872 | tf_op jit(solution)/shard_map/ppermute | solution.py:581
  203.9 18.3 %collective-permute-start.33 = (bf16[32,8192]{1,0:T(8,128)(2,1)S(1)}, bf16[32,8192]{1,0:T(8,128)(2,1)}, u32[]{:S(2)}, u32[]{:S(2)}) collective-permute-start(bf16[32,8192]{1,0:T(8,128)(2,1)S(1)} %get-tuple-element.107), channel_id=1, source_target_pairs={{0,6},{1,7},{2,0},{3,1},{4,2},{5,3},{6,4},{7,5},{8,14},{9,15},{10,... | collective-permute-start | bytes 1572872 | tf_op jit(solution)/shard_map/ppermute | solution.py:581
  215.7 5.7 %copy-start.18 = (bf16[32,8192]{1,0:T(8,128)(2,1)}, bf16[32,8192]{1,0:T(8,128)(2,1)S(1)}, u32[]{:S(2)}) copy-start(bf16[32,8192]{1,0:T(8,128)(2,1)S(1)} %collective-permute-done.31) | copy-start | bytes 1572868
  (11 other events, 21.5 us)

commit v11 on v10

--- a/solution.py
+++ b/solution.py
@@ -65,30 +65,12 @@
 
 
 def project_kernel(table_ref, f_ref, *refs, zones):
-    w_refs, refs = refs[: len(zones)], refs[len(zones) :]
-    gain_ref, send_ref, raw_ref, kv, held, sems = refs
+    w_refs, (gain_ref, send_ref, raw_ref, kv) = refs[: len(zones)], refs[len(zones) :]
     head_dim = gain_ref.shape[1]
     tokens = send_ref.shape[1]
-    span = held.shape[2]
-    copies = []
-    for y_off in range(NY):
-        y = lax.rem(table_ref[PLACE, 0] + y_off, NY)
-        here = pl.ds(pl.multiple_of(y * span, span), span)
-        copies.append(
-            pltpu.make_async_copy(f_ref.at[:, here], held.at[y_off], sems.at[y_off])
-        )
-    for copy in copies:
-        copy.start()
     total = jnp.zeros((f_ref.shape[0], 2 * head_dim), F32)
-    blocks = weight_blocks(table_ref, w_refs, zones)
-    for y_off in range(NY):
-        copies[y_off].wait()
-        for cols, spot, y_at, z in blocks:
-            if y_at == y_off:
-                here = pl.ds(pl.multiple_of(z * cols.size, cols.size), cols.size)
-                total = total + jnp.dot(
-                    held[y_off, :, here], side_by_side(spot), preferred_element_type=F32
-                )
+    for cols, spot, _, _ in weight_blocks(table_ref, w_refs, zones):
+        total = total + jnp.dot(f_ref[:, cols], side_by_side(spot), preferred_element_type=F32)
     raw = total[:, :head_dim]
     raw_ref[...] = raw
     scale = lax.rsqrt(jnp.mean(raw * raw, axis=-1, keepdims=True) + EPS)
@@ -112,13 +94,9 @@
         grid_spec=pltpu.PrefetchScalarGridSpec(
             num_scalar_prefetch=1,
             grid=(),
-            in_specs=[in_hbm()] + [in_vmem()] * (1 + len(pieces)),
+            in_specs=[in_vmem()] * (2 + len(pieces)),
             out_specs=[in_vmem()] * 2,
-            scratch_shapes=[
-                pltpu.VMEM((images, tokens, cols), BF16),
-                pltpu.VMEM((NY, rows.shape[0], rows.shape[1] // NY), BF16),
-                pltpu.SemaphoreType.DMA((NY,)),
-            ],
+            scratch_shapes=[pltpu.VMEM((images, tokens, cols), BF16)],
         ),
         out_shape=[
             pltpu.HBM((dp, tokens, cols), BF16),
@@ -530,14 +508,14 @@
     v_ring += [shift_z(v_ring[-2], 1)]
     offsets = [0] + [z for hop in range(1, NZ // 2) for z in (NZ - hop, hop)] + [NZ // 2]
     v_zones = [[(y, z) for y in range(NY)] for z in offsets]
-    k_line = jnp.concatenate(k_ring)
-    half = k_line.shape[0] // 2
-    after, before = shift_y(k_line, -1), shift_y(k_line, 1)
-    pieces = [k_line, after, before, shift_y(after[:half], -1), shift_y(before[half:], 1)]
-    k_zones = [[(y, z) for z in offsets] for y in (0, 1, NY - 1)]
-    far = [(NY // 2, z) for z in offsets]
-    k_zones += [far[: NZ // 2], far[NZ // 2 :]]
-    pieces, zones = pieces + v_ring, k_zones + v_zones
+    k_pieces, k_zones = [], []
+    for part in (slice(0, NZ // 2), slice(NZ // 2, NZ)):
+        k_line = jnp.concatenate(k_ring[part])
+        after, before = shift_y(k_line, -1), shift_y(k_line, 1)
+        far = shift_y(before, 1) if part.start else shift_y(after, -1)
+        k_pieces += [k_line, after, before, far]
+        k_zones += [[(y, z) for z in offsets[part]] for y in (0, 1, NY - 1, NY // 2)]
+    pieces, zones = k_pieces + v_ring, k_zones + v_zones
 
     send, raw = project(
         table, rows, pieces, zones, gain, dp_count, images, tokens

time: 226 us -> 225 us (level)
  waiting for transfers between devices: 102 us -> 113 us
  starting transfers between devices: 70.7 us -> 62 us
    ppermute x14, starting transfers between devices: 25 us -> 16.1 us  [shift_z(): return lax.ppermute(x, 'dp', pairs)]
    ppermute x14, waiting for transfers between devices: 14.2 us -> 22.5 us  [shift_z(): return lax.ppermute(x, 'dp', pairs)]
    all_to_all x1, waiting for transfers between devices: 32.5 us -> 34.9 us  [local(): kv = lax.all_to_all(send, 'dp', 0, 0, tiled=True)]
    ppermute x13 -> x15, starting transfers between devices: 20.1 us -> 21.6 us  [shift_y(): return lax.ppermute(x, 'dp', pairs)]
    ppermute x13 -> x15, waiting for transfers between devices: 10.5 us -> 10.8 us  [shift_y(): return lax.ppermute(x, 'dp', pairs)]
  transfers between devices with their start and end apart: 37 -> 39, of which waited for: 16 -> 17; matrix products, arithmetic and copies ran while one was open for 3% -> 3% of each run, Pallas kernels for 13% -> 13%
where the time goes in v11:
time: 225 us
  waiting for transfers between devices  113 us (50%)
  starting transfers between devices  62 us (28%)
  Pallas kernels  37.8 us (17%)
  local copies, waits for them, and re-layouts  7.68 us (3%)
  other arithmetic  3.44 us (2%)
    all_to_all x1, waiting for transfers between devices, local(): kv = lax.all_to_all(send, 'dp', 0, 0, tiled=True)  34.9 us
    all_to_all x1, waiting for transfers between devices, local(): parts = lax.all_to_all(parts, 'dp', 0, 0, tiled=True)  28.2 us
    ppermute x14, waiting for transfers between devices, shift_z(): return lax.ppermute(x, 'dp', pairs)  22.5 us
    ppermute x15, starting transfers between devices, shift_y(): return lax.ppermute(x, 'dp', pairs)  21.6 us
    ppermute x3, waiting for transfers between devices, local(): terms[s] = lax.ppermute(terms[s], 'tensor', pairs)  16.2 us
    ppermute x14, starting transfers between devices, shift_z(): return lax.ppermute(x, 'dp', pairs)  16.1 us
    ppermute x15, waiting for transfers between devices, shift_y(): return lax.ppermute(x, 'dp', pairs)  10.8 us
    all_to_all x1, starting transfers between devices, local(): kv = lax.all_to_all(send, 'dp', 0, 0, tiled=True)  7.99 us
  transfers between devices with their start and end apart: 39, of which 17 were waited for; matrix products, arithmetic and copies ran while one was open for 3% of the time, Pallas kernels for 13%

profile of v11, /device:TPU:32, one launch (start us, length us, event | category | flops | bytes accessed | tf_op | source)
XLA Modules:
  0.0 224.7 jit_solution(13604812584639384960)
XLA Ops:
  0.6 2.0 collective-permute-start
  2.7 3.2 %collective-permute-start.10 = (bf16[256,128]{1,0:T(8,128)(2,1)}, bf16[256,128]{1,0:T(8,128)(2,1)S(1)}, u32[]{:S(2)}, u32[]{:S(2)}) collective-permute-start(bf16[256,128]{1,0:T(8,128)(2,1)} %param.12), channel_id=1, source_target_pairs={{0,128},{8,136},{16,144},{24,152},{32,160},{40,168},{48,176},{56,1... | collective-permute-start | bytes 196616 | tf_op jit(solution)/shard_map/ppermute | solution.py:456
  5.9 1.1 collective-permute-start.9
  7.0 1.0 collective-permute-start.11
  10.7 2.0 collective-permute-done.11
  12.7 4.1 %collective-permute-start.13 = (bf16[1024,128]{1,0:T(8,128)(2,1)S(1)}, bf16[1024,128]{1,0:T(8,128)(2,1)S(1)}, u32[]{:S(2)}, u32[]{:S(2)}) collective-permute-start(bf16[1024,128]{1,0:T(8,128)(2,1)S(1)} %constant_dynamic-update-slice_fusion.4.refs_8_), channel_id=1, source_target_pairs={{0,56},{8,0},{16,8},{24,16},{32,24},{40,32},{48,40},{56,48},{64,12... | collective-permute-start | bytes 786440 | tf_op jit(solution)/shard_map/ppermute | solution.py:461
  16.8 1.0 collective-permute-start.2
  17.8 1.1 collective-permute-start.6
  18.9 5.0 %collective-permute-done.2 = bf16[256,128]{1,0:T(8,128)(2,1)S(1)} collective-permute-done((bf16[256,128]{1,0:T(8,128)(2,1)S(1)}, bf16[256,128]{1,0:T(8,128)(2,1)S(1)}, u32[]{:S(2)}, u32[]{:S(2)}) %collective-permute-start.2) | collective-permute-done | bytes 65568 | tf_op jit(solution)/shard_map/ppermute | solution.py:461
  25.0 2.4 %collective-permute-start.8 = (bf16[256,128]{1,0:T(8,128)(2,1)S(1)}, bf16[256,128]{1,0:T(8,128)(2,1)S(1)}, u32[]{:S(2)}, u32[]{:S(2)}) collective-permute-start(bf16[256,128]{1,0:T(8,128)(2,1)S(1)} %collective-permute-done.6), channel_id=1, source_target_pairs={{0,56},{8,0},{16,8},{24,16},{32,24},{40,32},{48,40},{56,48},{64,12... | collective-permute-start | bytes 196616 | tf_op jit(solution)/shard_map/ppermute | solution.py:461
  27.5 2.2 collective-permute-done.7
  29.7 3.4 %collective-permute-start.3 = (bf16[1024,128]{1,0:T(8,128)(2,1)S(1)}, bf16[1024,128]{1,0:T(8,128)(2,1)S(1)}, u32[]{:S(2)}, u32[]{:S(2)}) collective-permute-start(bf16[1024,128]{1,0:T(8,128)(2,1)S(1)} %constant_dynamic-update-slice_fusion.refs_0_), channel_id=1, source_target_pairs={{0,192},{8,200},{16,208},{24,216},{32,224},{40,232},{48,240},{56,2... | collective-permute-start | bytes 786440 | tf_op jit(solution)/shard_map/ppermute | solution.py:456
  33.2 2.4 %collective-permute-start.18 = (bf16[1024,128]{1,0:T(8,128)(2,1)S(1)}, bf16[1024,128]{1,0:T(8,128)(2,1)S(1)}, u32[]{:S(2)}, u32[]{:S(2)}) collective-permute-start(bf16[1024,128]{1,0:T(8,128)(2,1)S(1)} %collective-permute-done.12.refs_9_), channel_id=1, source_target_pairs={{0,8},{8,16},{16,24},{24,32},{32,40},{40,48},{48,56},{56,0},{64,72... | collective-permute-start | bytes 786440 | tf_op jit(solution)/shard_map/ppermute | solution.py:461
  35.6 1.4 collective-permute-start.19
  37.0 2.4 %collective-permute-done.14 = bf16[256,128]{1,0:T(8,128)(2,1)S(1)} collective-permute-done((bf16[256,128]{1,0:T(8,128)(2,1)S(1)}, bf16[256,128]{1,0:T(8,128)(2,1)S(1)}, u32[]{:S(2)}, u32[]{:S(2)}) %collective-permute-start.14) | collective-permute-done | bytes 65568 | tf_op jit(solution)/shard_map/ppermute | solution.py:461
  39.5 5.0 %collective-permute-done.18.refs_11_ = bf16[1024,128]{1,0:T(8,128)(2,1)S(1)} collective-permute-done((bf16[1024,128]{1,0:T(8,128)(2,1)S(1)}, bf16[1024,128]{1,0:T(8,128)(2,1)S(1)}, u32[]{:S(2)}, u32[]{:S(2)}) %collective-permute-start.18) | collective-permute-done | bytes 262176 | tf_op jit(solution)/shard_map/ppermute | solution.py:461
  44.9 1.9 collective-permute-start.5
  47.0 1.0 collective-permute-start.21
  48.6 1.3 collective-permute-start.17
  50.0 3.4 %collective-permute-done.20.refs_13_ = bf16[1024,128]{1,0:T(8,128)(2,1)S(1)} collective-permute-done((bf16[1024,128]{1,0:T(8,128)(2,1)S(1)}, bf16[1024,128]{1,0:T(8,128)(2,1)S(1)}, u32[]{:S(2)}, u32[]{:S(2)}) %collective-permute-start.20) | collective-permute-done | bytes 262176 | tf_op jit(solution)/shard_map/ppermute | solution.py:461
  54.1 2.2 collective-permute-done.17.refs_7_
  56.3 4.4 %collective-permute-done.22.refs_15_ = bf16[1024,128]{1,0:T(8,128)(2,1)} collective-permute-done((bf16[1024,128]{1,0:T(8,128)(2,1)S(1)}, bf16[1024,128]{1,0:T(8,128)(2,1)}, u32[]{:S(2)}, u32[]{:S(2)}) %collective-permute-start.22) | collective-permute-done | bytes 262176 | tf_op jit(solution)/shard_map/ppermute | solution.py:461
  61.4 6.0 %project.1 = (bf16[32,128,256]{2,1,0:T(8,128)(2,1)}, f32[256,128]{1,0:T(8,128)}) custom-call(s32[5,32]{1,0:T(8,128)S(1)} %stack.41.table_ref, bf16[256,8192]{1,0:T(8,128)(2,1)} %bitcast.24, bf16[1024,128]{1,0:T(8,128)(2,1)S(1)} %constant_dynamic-update-slice_fusion.refs_0_, bf16[1024,128]{1,0:T(8,128)(2,1)S(1)} %collective-permute-done.3.refs_1_, ...), custom_call_target="tpu_custom_call" | custom-call | flops 1073741824 | bytes 10485760 | tf_op jit(solution)/shard_map/project/pallas_call | solution.py:92
  67.5 8.0 %all-to-all-start = ((bf16[32,128,256]{2,1,0:T(8,128)(2,1)}), bf16[32,128,256]{2,1,0:T(8,128)(2,1)S(1)}, u32[]{:S(2)}, u32[]{:S(2)}) async-start(bf16[32,128,256]{2,1,0:T(8,128)(2,1)} %get-tuple-element.66), calls=%async_computation | async-start | bytes 4194304 | tf_op jit(solution)/shard_map/all_to_all | solution.py:523
  75.6 2.9 %dynamic-slice_bitcast_fusion = (bf16[128,2048]{1,0:T(8,128)(2,1)}, bf16[128,2048]{1,0:T(8,128)(2,1)}, bf16[128,2048]{1,0:T(8,128)(2,1)}, bf16[128,2048]{1,0:T(8,128)(2,1)}) fusion(bf16[2,128,8192]{2,1,0:T(8,128)(2,1)} %param.10, s32[]{:T(128)S(6)} %select_n.86, s32[]{:T(128)S(6)} %select_n.94, s32[]{:T(128)S(6)} %select_n.92, s32[]{:T(128)S(6)} %select_n.90, ...), kind=kLoop, calls=%fused_computation.2 | loop fusion | bytes 4194324 | tf_op jit(solution)/shard_map/squeeze | solution.py:529
  78.5 2.7 %collective-permute-start.25 = (bf16[128,2048]{1,0:T(8,128)(2,1)}, bf16[128,2048]{1,0:T(8,128)(2,1)}, u32[]{:S(2)}, u32[]{:S(2)}) collective-permute-start(bf16[128,2048]{1,0:T(8,128)(2,1)} %get-tuple-element.123), channel_id=1, source_target_pairs={{0,192},{8,200},{16,208},{24,216},{32,224},{40,232},{48,240},{56,2... | collective-permute-start | bytes 1572872 | tf_op jit(solution)/shard_map/ppermute | solution.py:456
  82.9 34.9 %all-to-all-done.kv_ref = bf16[32,128,256]{2,1,0:T(8,128)(2,1)S(1)} async-done(((bf16[32,128,256]{2,1,0:T(8,128)(2,1)}), bf16[32,128,256]{2,1,0:T(8,128)(2,1)S(1)}, u32[]{:S(2)}, u32[]{:S(2)}) %all-to-all-start) | async-done | bytes 2097184 | tf_op jit(solution)/shard_map/all_to_all | solution.py:523
  117.8 7.9 %attend.1 = (bf16[32,128,256]{2,1,0:T(8,128)(2,1)}, bf16[32,128,128]{2,1,0:T(8,128)(2,1)}, bf16[32,128,128]{2,1,0:T(8,128)(2,1)}) custom-call(s32[5,32]{1,0:T(8,128)S(1)} %stack.41.table_ref, bf16[512,1024]{1,0:T(8,128)(2,1)} %q_hbm.1, bf16[512,1024]{1,0:T(8,128)(2,1)} %ct_hbm.1, bf16[32,128,256]{2,1,0:T(8,128)(2,1)S(1)} %all-to-all-done.kv_ref), custom_call_target="tpu_custom_call" | custom-call | flops 536870912 | bytes 8388608 | tf_op jit(solution)/shard_map/attend/pallas_call | solution.py:213
  125.8 5.8 %all-to-all-start.1 = ((bf16[32,128,256]{2,1,0:T(8,128)(2,1)}), bf16[32,128,256]{2,1,0:T(8,128)(2,1)}, u32[]{:S(2)}, u32[]{:S(2)}) async-start(bf16[32,128,256]{2,1,0:T(8,128)(2,1)} %get-tuple-element.70), calls=%async_computation.1 | async-start | bytes 4194304 | tf_op jit(solution)/shard_map/all_to_all | solution.py:539
  131.6 2.2 transpose_pieces.1.own_ref
  134.3 4.1 %assemble.1 = (bf16[8192,128]{1,0:T(8,128)(2,1)}, bf16[8192,128]{1,0:T(8,128)(2,1)}) custom-call(s32[5,32]{1,0:T(8,128)S(1)} %stack.41.table_ref, bf16[1024,128]{1,0:T(8,128)(2,1)S(1)} %constant_dynamic-update-slice_fusion.refs_0_, bf16[1024,128]{1,0:T(8,128)(2,1)S(1)} %copy-done.6, bf16[1024,128]{1,0:T(8,128)(2,1)S(1)} %copy-done.4, ...), custom_call_target="tpu_custom_call" | custom-call | bytes 1048576 | tf_op jit(solution)/shard_map/assemble/pallas_call | solution.py:371
  138.9 6.2 %apply.1 = (bf16[512,1024]{1,0:T(8,128)(2,1)}, bf16[512,1024]{1,0:T(8,128)(2,1)}) custom-call(s32[5,32]{1,0:T(8,128)S(1)} %stack.41.table_ref, bf16[32,128,256]{2,1,0:T(8,128)(2,1)} %copy-done, bf16[32,128,128]{2,1,0:T(8,128)(2,1)} %get-tuple-element.75.probs_ref, bf16[32,128,128]{2,1,0:T(8,128)(2,1)} %get-tuple-element.76.ds_ref), custom_call_target="tpu_custom_call" | custom-call | flops 268435456 | bytes 6291456 | tf_op jit(solution)/shard_map/apply/pallas_call | solution.py:255
  145.0 1.4 copy-done.1
  146.4 28.2 %all-to-all-done.1.part_ref = bf16[32,128,256]{2,1,0:T(8,128)(2,1)} async-done(((bf16[32,128,256]{2,1,0:T(8,128)(2,1)}), bf16[32,128,256]{2,1,0:T(8,128)(2,1)}, u32[]{:S(2)}, u32[]{:S(2)}) %all-to-all-start.1) | async-done | bytes 2097184 | tf_op jit(solution)/shard_map/all_to_all | solution.py:539
  174.6 3.0 %owner_grads.1 = (bf16[256,256]{1,0:T(8,128)(2,1)S(1)}, bf16[256,256]{1,0:T(8,128)(2,1)S(1)}) custom-call(s32[5,32]{1,0:T(8,128)S(1)} %stack.41.table_ref, bf16[32,128,256]{2,1,0:T(8,128)(2,1)} %all-to-all-done.1.part_ref, f32[256,128]{1,0:T(8,128)} %get-tuple-element.68.raw_ref, f32[1,128]{1,0:T(1,128)S(1)} %bitcast.23), custom_call_target="tpu_custom_call" | custom-call | bytes 3145728 | tf_op jit(solution)/shard_map/owner_grads/pallas_call | solution.py:301
  177.6 1.8 collective-permute-start.31
  179.4 1.7 collective-permute-start.30
  182.7 3.2 %collective-permute-done.30.refs_2_ = bf16[256,256]{1,0:T(8,128)(2,1)S(1)} collective-permute-done((bf16[256,256]{1,0:T(8,128)(2,1)S(1)}, bf16[256,256]{1,0:T(8,128)(2,1)S(1)}, u32[]{:S(2)}, u32[]{:S(2)}) %collective-permute-start.30) | collective-permute-done | bytes 131104 | tf_op jit(solution)/shard_map/ppermute | solution.py:456
  185.9 1.4 collective-permute-done.29.refs_1_
  187.3 2.3 %weight_terms.1 = bf16[8,256,256]{2,1,0:T(8,128)(2,1)} custom-call(bf16[2048,512]{1,0:T(8,128)(2,1)S(1)} %transpose_pieces.1.own_ref, bf16[2048,512]{1,0:T(8,128)(2,1)S(1)} %copy-done.2, bf16[256,256]{1,0:T(8,128)(2,1)S(1)} %get-tuple-element.101.refs_0_, bf16[256,256]{1,0:T(8,128)(2,1)S(1)} %collective-permute-done.29.refs_1_, ...), custom_call_target="tpu_custom_call" | custom-call | flops 1073741824 | bytes 6291456 | tf_op jit(solution)/shard_map/weight_terms/pallas_call | solution.py:352
  189.6 4.0 %all-to-all-start.2 = ((bf16[8,256,256]{2,1,0:T(8,128)(2,1)}), bf16[8,256,256]{2,1,0:T(8,128)(2,1)S(1)}, u32[]{:S(2)}, u32[]{:S(2)}) async-start(bf16[8,256,256]{2,1,0:T(8,128)(2,1)} %weight_terms.1), calls=%async_computation.2 | async-start | bytes 2097152 | tf_op jit(solution)/shard_map/all_to_all | solution.py:554
  193.6 6.1 %feature_terms.1 = (bf16[32,8192]{1,0:T(8,128)(2,1)S(1)}, bf16[32,8192]{1,0:T(8,128)(2,1)S(1)}, bf16[32,8192]{1,0:T(8,128)(2,1)S(1)}, bf16[32,8192]{1,0:T(8,128)(2,1)S(1)}) custom-call(s32[5,32]{1,0:T(8,128)S(1)} %stack.41.table_ref, bf16[256,256]{1,0:T(8,128)(2,1)S(1)} %get-tuple-element.104.own_ref, ...), custom_call_target="tpu_custom_call" | custom-call | flops 2147483648 | bytes 10485760 | tf_op jit(solution)/shard_map/feature_terms/pallas_call | solution.py:432
  199.8 1.6 collective-permute-start.33
  201.3 2.7 %collective-permute-start.34 = (bf16[32,8192]{1,0:T(8,128)(2,1)S(1)}, bf16[32,8192]{1,0:T(8,128)(2,1)S(1)}, u32[]{:S(2)}, u32[]{:S(2)}) collective-permute-start(bf16[32,8192]{1,0:T(8,128)(2,1)S(1)} %get-tuple-element.112), channel_id=1, source_target_pairs={{0,4},{1,5},{2,6},{3,7},{4,0},{5,1},{6,2},{7,3},{8,12},{9,13},{10,... | collective-permute-start | bytes 1572872 | tf_op jit(solution)/shard_map/ppermute | solution.py:559
  204.1 1.4 collective-permute-start.35
  205.5 10.3 %collective-permute-done.33 = bf16[32,8192]{1,0:T(8,128)(2,1)S(1)} collective-permute-done((bf16[32,8192]{1,0:T(8,128)(2,1)S(1)}, bf16[32,8192]{1,0:T(8,128)(2,1)S(1)}, u32[]{:S(2)}, u32[]{:S(2)}) %collective-permute-start.33) | collective-permute-done | bytes 524320 | tf_op jit(solution)/shard_map/ppermute | solution.py:559
  215.9 5.8 %collective-permute-done.34 = bf16[32,8192]{1,0:T(8,128)(2,1)S(1)} collective-permute-done((bf16[32,8192]{1,0:T(8,128)(2,1)S(1)}, bf16[32,8192]{1,0:T(8,128)(2,1)S(1)}, u32[]{:S(2)}, u32[]{:S(2)}) %collective-permute-start.34) | collective-permute-done | bytes 524320 | tf_op jit(solution)/shard_map/ppermute | solution.py:559
  222.6 2.1 add_convert_fusion
  (107 shorter events, 11.8 us)
Async XLA Ops:
  0.6 16.2 %collective-permute-start = (bf16[256,128]{1,0:T(8,128)(2,1)}, bf16[256,128]{1,0:T(8,128)(2,1)S(1)}, u32[]{:S(2)}, u32[]{:S(2)}) collective-permute-start(bf16[256,128]{1,0:T(8,128)(2,1)} %param.11), channel_id=1, source_target_pairs={{0,8},{8,16},{16,24},{24,32},{32,40},{40,48},{48,56},{56,0},{64,72... | collective-permute-start | bytes 196616 | tf_op jit(solution)/shard_map/ppermute | solution.py:461
  2.6 15.2 %collective-permute-start.1 = (bf16[256,128]{1,0:T(8,128)(2,1)}, bf16[256,128]{1,0:T(8,128)(2,1)S(1)}, u32[]{:S(2)}, u32[]{:S(2)}) collective-permute-start(bf16[256,128]{1,0:T(8,128)(2,1)} %param.11), channel_id=1, source_target_pairs={{0,56},{8,0},{16,8},{24,16},{32,24},{40,32},{48,40},{56,48},{64,12... | collective-permute-start | bytes 196616 | tf_op jit(solution)/shard_map/ppermute | solution.py:461
  2.7 7.9 %collective-permute-start.10 = (bf16[256,128]{1,0:T(8,128)(2,1)}, bf16[256,128]{1,0:T(8,128)(2,1)S(1)}, u32[]{:S(2)}, u32[]{:S(2)}) collective-permute-start(bf16[256,128]{1,0:T(8,128)(2,1)} %param.12), channel_id=1, source_target_pairs={{0,128},{8,136},{16,144},{24,152},{32,160},{40,168},{48,176},{56,1... | collective-permute-start | bytes 196616 | tf_op jit(solution)/shard_map/ppermute | solution.py:456
  5.9 4.7 %collective-permute-start.9 = (bf16[256,128]{1,0:T(8,128)(2,1)}, bf16[256,128]{1,0:T(8,128)(2,1)S(1)}, u32[]{:S(2)}, u32[]{:S(2)}) collective-permute-start(bf16[256,128]{1,0:T(8,128)(2,1)} %param.12), channel_id=1, source_target_pairs={{0,192},{8,200},{16,208},{24,216},{32,224},{40,232},{48,240},{56,2... | collective-permute-start | bytes 196616 | tf_op jit(solution)/shard_map/ppermute | solution.py:456
  7.0 5.7 %collective-permute-start.11 = (bf16[256,128]{1,0:T(8,128)(2,1)}, bf16[256,128]{1,0:T(8,128)(2,1)S(1)}, u32[]{:S(2)}, u32[]{:S(2)}) collective-permute-start(bf16[256,128]{1,0:T(8,128)(2,1)} %param.12), channel_id=1, source_target_pairs={{0,64},{8,72},{16,80},{24,88},{32,96},{40,104},{48,112},{56,120},{... | collective-permute-start | bytes 196616 | tf_op jit(solution)/shard_map/ppermute | solution.py:456
  12.7 20.4 %collective-permute-start.13 = (bf16[1024,128]{1,0:T(8,128)(2,1)S(1)}, bf16[1024,128]{1,0:T(8,128)(2,1)S(1)}, u32[]{:S(2)}, u32[]{:S(2)}) collective-permute-start(bf16[1024,128]{1,0:T(8,128)(2,1)S(1)} %constant_dynamic-update-slice_fusion.4.refs_8_), channel_id=1, source_target_pairs={{0,56},{8,0},{16,8},{24,16},{32,24},{40,32},{48,40},{56,48},{64,12... | collective-permute-start | bytes 786440 | tf_op jit(solution)/shard_map/ppermute | solution.py:461
  16.8 16.3 %collective-permute-start.12 = (bf16[1024,128]{1,0:T(8,128)(2,1)S(1)}, bf16[1024,128]{1,0:T(8,128)(2,1)S(1)}, u32[]{:S(2)}, u32[]{:S(2)}) collective-permute-start(bf16[1024,128]{1,0:T(8,128)(2,1)S(1)} %constant_dynamic-update-slice_fusion.4.refs_8_), channel_id=1, source_target_pairs={{0,8},{8,16},{16,24},{24,32},{32,40},{40,48},{48,56},{56,0},{64,72... | collective-permute-start | bytes 786440 | tf_op jit(solution)/shard_map/ppermute | solution.py:461
  16.8 7.2 %collective-permute-start.2 = (bf16[256,128]{1,0:T(8,128)(2,1)S(1)}, bf16[256,128]{1,0:T(8,128)(2,1)S(1)}, u32[]{:S(2)}, u32[]{:S(2)}) collective-permute-start(bf16[256,128]{1,0:T(8,128)(2,1)S(1)} %collective-permute-done), channel_id=1, source_target_pairs={{0,8},{8,16},{16,24},{24,32},{32,40},{40,48},{48,56},{56,0},{64,72... | collective-permute-start | bytes 196616 | tf_op jit(solution)/shard_map/ppermute | solution.py:461
  17.8 7.2 %collective-permute-start.6 = (bf16[256,128]{1,0:T(8,128)(2,1)S(1)}, bf16[256,128]{1,0:T(8,128)(2,1)S(1)}, u32[]{:S(2)}, u32[]{:S(2)}) collective-permute-start(bf16[256,128]{1,0:T(8,128)(2,1)S(1)} %collective-permute-done.1), channel_id=1, source_target_pairs={{0,56},{8,0},{16,8},{24,16},{32,24},{40,32},{48,40},{56,48},{64,12... | collective-permute-start | bytes 196616 | tf_op jit(solution)/shard_map/ppermute | solution.py:461
  24.0 22.8 %collective-permute-start.4 = (bf16[1024,128]{1,0:T(8,128)(2,1)S(1)}, bf16[1024,128]{1,0:T(8,128)(2,1)S(1)}, u32[]{:S(2)}, u32[]{:S(2)}) collective-permute-start(bf16[1024,128]{1,0:T(8,128)(2,1)S(1)} %constant_dynamic-update-slice_fusion.refs_0_), channel_id=1, source_target_pairs={{0,64},{8,72},{16,80},{24,88},{32,96},{40,104},{48,112},{56,120},{... | collective-permute-start | bytes 786440 | tf_op jit(solution)/shard_map/ppermute | solution.py:456
  24.7 5.0 %collective-permute-start.7 = (bf16[256,128]{1,0:T(8,128)(2,1)S(1)}, bf16[256,128]{1,0:T(8,128)(2,1)S(1)}, u32[]{:S(2)}, u32[]{:S(2)}) collective-permute-start(bf16[256,128]{1,0:T(8,128)(2,1)S(1)} %collective-permute-done.2), channel_id=1, source_target_pairs={{0,8},{8,16},{16,24},{24,32},{32,40},{40,48},{48,56},{56,0},{64,72... | collective-permute-start | bytes 196616 | tf_op jit(solution)/shard_map/ppermute | solution.py:461
  25.0 8.1 %collective-permute-start.8 = (bf16[256,128]{1,0:T(8,128)(2,1)S(1)}, bf16[256,128]{1,0:T(8,128)(2,1)S(1)}, u32[]{:S(2)}, u32[]{:S(2)}) collective-permute-start(bf16[256,128]{1,0:T(8,128)(2,1)S(1)} %collective-permute-done.6), channel_id=1, source_target_pairs={{0,56},{8,0},{16,8},{24,16},{32,24},{40,32},{48,40},{56,48},{64,12... | collective-permute-start | bytes 196616 | tf_op jit(solution)/shard_map/ppermute | solution.py:461
  29.7 15.2 %collective-permute-start.3 = (bf16[1024,128]{1,0:T(8,128)(2,1)S(1)}, bf16[1024,128]{1,0:T(8,128)(2,1)S(1)}, u32[]{:S(2)}, u32[]{:S(2)}) collective-permute-start(bf16[1024,128]{1,0:T(8,128)(2,1)S(1)} %constant_dynamic-update-slice_fusion.refs_0_), channel_id=1, source_target_pairs={{0,192},{8,200},{16,208},{24,216},{32,224},{40,232},{48,240},{56,2... | collective-permute-start | bytes 786440 | tf_op jit(solution)/shard_map/ppermute | solution.py:456
  33.1 6.3 %collective-permute-start.14 = (bf16[256,128]{1,0:T(8,128)(2,1)S(1)}, bf16[256,128]{1,0:T(8,128)(2,1)S(1)}, u32[]{:S(2)}, u32[]{:S(2)}) collective-permute-start(bf16[256,128]{1,0:T(8,128)(2,1)S(1)} %collective-permute-done.7), channel_id=1, source_target_pairs={{0,8},{8,16},{16,24},{24,32},{32,40},{40,48},{48,56},{56,0},{64,72... | collective-permute-start | bytes 196616 | tf_op jit(solution)/shard_map/ppermute | solution.py:461
  33.2 11.3 %collective-permute-start.18 = (bf16[1024,128]{1,0:T(8,128)(2,1)S(1)}, bf16[1024,128]{1,0:T(8,128)(2,1)S(1)}, u32[]{:S(2)}, u32[]{:S(2)}) collective-permute-start(bf16[1024,128]{1,0:T(8,128)(2,1)S(1)} %collective-permute-done.12.refs_9_), channel_id=1, source_target_pairs={{0,8},{8,16},{16,24},{24,32},{32,40},{40,48},{48,56},{56,0},{64,72... | collective-permute-start | bytes 786440 | tf_op jit(solution)/shard_map/ppermute | solution.py:461
  35.6 11.4 %collective-permute-start.19 = (bf16[1024,128]{1,0:T(8,128)(2,1)S(1)}, bf16[1024,128]{1,0:T(8,128)(2,1)S(1)}, u32[]{:S(2)}, u32[]{:S(2)}) collective-permute-start(bf16[1024,128]{1,0:T(8,128)(2,1)S(1)} %collective-permute-done.13.refs_10_), channel_id=1, source_target_pairs={{0,56},{8,0},{16,8},{24,16},{32,24},{40,32},{48,40},{56,48},{64,12... | collective-permute-start | bytes 786440 | tf_op jit(solution)/shard_map/ppermute | solution.py:461
  39.4 9.2 %collective-permute-start.16 = (bf16[1024,128]{1,0:T(8,128)(2,1)S(1)}, bf16[1024,128]{1,0:T(8,128)(2,1)S(1)}, u32[]{:S(2)}, u32[]{:S(2)}) collective-permute-start(bf16[1024,128]{1,0:T(8,128)(2,1)S(1)} %constant_dynamic-update-slice_fusion.8.refs_4_), channel_id=1, source_target_pairs={{0,64},{8,72},{16,80},{24,88},{32,96},{40,104},{48,112},{56,120},{... | collective-permute-start | bytes 786440 | tf_op jit(solution)/shard_map/ppermute | solution.py:456
  44.5 22.9 %copy-start.7 = (bf16[1024,128]{1,0:T(8,128)(2,1)}, bf16[1024,128]{1,0:T(8,128)(2,1)S(1)}, u32[]{:S(2)}) copy-start(bf16[1024,128]{1,0:T(8,128)(2,1)S(1)} %collective-permute-done.18.refs_11_) | copy-start | bytes 786436
  44.5 8.9 %collective-permute-start.20 = (bf16[1024,128]{1,0:T(8,128)(2,1)S(1)}, bf16[1024,128]{1,0:T(8,128)(2,1)S(1)}, u32[]{:S(2)}, u32[]{:S(2)}) collective-permute-start(bf16[1024,128]{1,0:T(8,128)(2,1)S(1)} %collective-permute-done.18.refs_11_), channel_id=1, source_target_pairs={{0,8},{8,16},{16,24},{24,32},{32,40},{40,48},{48,56},{56,0},{64,72... | collective-permute-start | bytes 786440 | tf_op jit(solution)/shard_map/ppermute | solution.py:461
  44.9 22.5 %copy-start.5 = (bf16[1024,128]{1,0:T(8,128)(2,1)}, bf16[1024,128]{1,0:T(8,128)(2,1)S(1)}, u32[]{:S(2)}) copy-start(bf16[1024,128]{1,0:T(8,128)(2,1)S(1)} %collective-permute-done.3.refs_1_) | copy-start | bytes 786436
  44.9 9.2 %collective-permute-start.5 = (bf16[1024,128]{1,0:T(8,128)(2,1)S(1)}, bf16[1024,128]{1,0:T(8,128)(2,1)S(1)}, u32[]{:S(2)}, u32[]{:S(2)}) collective-permute-start(bf16[1024,128]{1,0:T(8,128)(2,1)S(1)} %collective-permute-done.3.refs_1_), channel_id=1, source_target_pairs={{0,192},{8,200},{16,208},{24,216},{32,224},{40,232},{48,240},{56,2... | collective-permute-start | bytes 786440 | tf_op jit(solution)/shard_map/ppermute | solution.py:456
  46.8 20.6 %copy-start.3 = (bf16[1024,128]{1,0:T(8,128)(2,1)}, bf16[1024,128]{1,0:T(8,128)(2,1)S(1)}, u32[]{:S(2)}) copy-start(bf16[1024,128]{1,0:T(8,128)(2,1)S(1)} %collective-permute-done.4.refs_2_) | copy-start | bytes 786436
  46.8 7.3 %collective-permute-start.15 = (bf16[1024,128]{1,0:T(8,128)(2,1)S(1)}, bf16[1024,128]{1,0:T(8,128)(2,1)S(1)}, u32[]{:S(2)}, u32[]{:S(2)}) collective-permute-start(bf16[1024,128]{1,0:T(8,128)(2,1)S(1)} %constant_dynamic-update-slice_fusion.8.refs_4_), channel_id=1, source_target_pairs={{0,192},{8,200},{16,208},{24,216},{32,224},{40,232},{48,240},{56,2... | collective-permute-start | bytes 786440 | tf_op jit(solution)/shard_map/ppermute | solution.py:456
  47.0 20.4 %copy-start.9 = (bf16[1024,128]{1,0:T(8,128)(2,1)}, bf16[1024,128]{1,0:T(8,128)(2,1)S(1)}, u32[]{:S(2)}) copy-start(bf16[1024,128]{1,0:T(8,128)(2,1)S(1)} %collective-permute-done.19.refs_12_) | copy-start | bytes 786436
  47.0 7.1 %collective-permute-start.21 = (bf16[1024,128]{1,0:T(8,128)(2,1)S(1)}, bf16[1024,128]{1,0:T(8,128)(2,1)}, u32[]{:S(2)}, u32[]{:S(2)}) collective-permute-start(bf16[1024,128]{1,0:T(8,128)(2,1)S(1)} %collective-permute-done.19.refs_12_), channel_id=1, source_target_pairs={{0,56},{8,0},{16,8},{24,16},{32,24},{40,32},{48,40},{56,48},{64,12... | collective-permute-start | bytes 786440 | tf_op jit(solution)/shard_map/ppermute | solution.py:461
  48.6 18.8 %copy-start.11 = (bf16[1024,128]{1,0:T(8,128)(2,1)}, bf16[1024,128]{1,0:T(8,128)(2,1)S(1)}, u32[]{:S(2)}) copy-start(bf16[1024,128]{1,0:T(8,128)(2,1)S(1)} %collective-permute-done.16.refs_6_) | copy-start | bytes 786436
  48.6 7.7 %collective-permute-start.17 = (bf16[1024,128]{1,0:T(8,128)(2,1)S(1)}, bf16[1024,128]{1,0:T(8,128)(2,1)}, u32[]{:S(2)}, u32[]{:S(2)}) collective-permute-start(bf16[1024,128]{1,0:T(8,128)(2,1)S(1)} %collective-permute-done.16.refs_6_), channel_id=1, source_target_pairs={{0,64},{8,72},{16,80},{24,88},{32,96},{40,104},{48,112},{56,120},{... | collective-permute-start | bytes 786440 | tf_op jit(solution)/shard_map/ppermute | solution.py:456
  53.4 14.1 %copy-start.13 = (bf16[1024,128]{1,0:T(8,128)(2,1)}, bf16[1024,128]{1,0:T(8,128)(2,1)S(1)}, u32[]{:S(2)}) copy-start(bf16[1024,128]{1,0:T(8,128)(2,1)S(1)} %collective-permute-done.20.refs_13_) | copy-start | bytes 786436
  53.4 7.4 %collective-permute-start.22 = (bf16[1024,128]{1,0:T(8,128)(2,1)S(1)}, bf16[1024,128]{1,0:T(8,128)(2,1)}, u32[]{:S(2)}, u32[]{:S(2)}) collective-permute-start(bf16[1024,128]{1,0:T(8,128)(2,1)S(1)} %collective-permute-done.20.refs_13_), channel_id=1, source_target_pairs={{0,8},{8,16},{16,24},{24,32},{32,40},{40,48},{48,56},{56,0},{64,72... | collective-permute-start | bytes 786440 | tf_op jit(solution)/shard_map/ppermute | solution.py:461
  54.1 13.3 %copy-start.17 = (bf16[1024,128]{1,0:T(8,128)(2,1)}, bf16[1024,128]{1,0:T(8,128)(2,1)S(1)}, u32[]{:S(2)}) copy-start(bf16[1024,128]{1,0:T(8,128)(2,1)S(1)} %collective-permute-done.15.refs_5_) | copy-start | bytes 786436
  54.1 13.3 %copy-start.15 = (bf16[1024,128]{1,0:T(8,128)(2,1)}, bf16[1024,128]{1,0:T(8,128)(2,1)S(1)}, u32[]{:S(2)}) copy-start(bf16[1024,128]{1,0:T(8,128)(2,1)S(1)} %collective-permute-done.5.refs_3_) | copy-start | bytes 786436
  67.5 50.3 %all-to-all-start = ((bf16[32,128,256]{2,1,0:T(8,128)(2,1)}), bf16[32,128,256]{2,1,0:T(8,128)(2,1)S(1)}, u32[]{:S(2)}, u32[]{:S(2)}) async-start(bf16[32,128,256]{2,1,0:T(8,128)(2,1)} %get-tuple-element.66), calls=%async_computation | async-start | bytes 4194304 | tf_op jit(solution)/shard_map/all_to_all | solution.py:523
  78.5 47.3 %collective-permute-start.25 = (bf16[128,2048]{1,0:T(8,128)(2,1)}, bf16[128,2048]{1,0:T(8,128)(2,1)}, u32[]{:S(2)}, u32[]{:S(2)}) collective-permute-start(bf16[128,2048]{1,0:T(8,128)(2,1)} %get-tuple-element.123), channel_id=1, source_target_pairs={{0,192},{8,200},{16,208},{24,216},{32,224},{40,232},{48,240},{56,2... | collective-permute-start | bytes 1572872 | tf_op jit(solution)/shard_map/ppermute | solution.py:456
  81.2 44.6 %collective-permute-start.24 = (bf16[128,2048]{1,0:T(8,128)(2,1)}, bf16[128,2048]{1,0:T(8,128)(2,1)}, u32[]{:S(2)}, u32[]{:S(2)}) collective-permute-start(bf16[128,2048]{1,0:T(8,128)(2,1)} %get-tuple-element.124), channel_id=1, source_target_pairs={{0,128},{8,136},{16,144},{24,152},{32,160},{40,168},{48,176},{56,1... | collective-permute-start | bytes 1572872 | tf_op jit(solution)/shard_map/ppermute | solution.py:456
  82.0 43.8 %collective-permute-start.23 = (bf16[128,2048]{1,0:T(8,128)(2,1)}, bf16[128,2048]{1,0:T(8,128)(2,1)}, u32[]{:S(2)}, u32[]{:S(2)}) collective-permute-start(bf16[128,2048]{1,0:T(8,128)(2,1)} %get-tuple-element.125), channel_id=1, source_target_pairs={{0,64},{8,72},{16,80},{24,88},{32,96},{40,104},{48,112},{56,120},{... | collective-permute-start | bytes 1572872 | tf_op jit(solution)/shard_map/ppermute | solution.py:456
  125.8 48.9 %all-to-all-start.1 = ((bf16[32,128,256]{2,1,0:T(8,128)(2,1)}), bf16[32,128,256]{2,1,0:T(8,128)(2,1)}, u32[]{:S(2)}, u32[]{:S(2)}) async-start(bf16[32,128,256]{2,1,0:T(8,128)(2,1)} %get-tuple-element.70), calls=%async_computation.1 | async-start | bytes 4194304 | tf_op jit(solution)/shard_map/all_to_all | solution.py:539
  133.9 11.2 %collective-permute-start.26 = (bf16[2048,512]{1,0:T(8,128)(2,1)S(1)}, bf16[2048,512]{1,0:T(8,128)(2,1)S(1)}, u32[]{:S(2)}, u32[]{:S(2)}) collective-permute-start(bf16[2048,512]{1,0:T(8,128)(2,1)S(1)} %transpose_pieces.1.own_ref), channel_id=1, source_target_pairs={{0,1},{1,0},{2,3},{3,2},{4,5},{5,4},{6,7},{7,6},{8,9},{9,8},{10,11... | collective-permute-start | bytes 6291464 | tf_op jit(solution)/shard_map/ppermute | solution.py:465
  138.3 8.0 %collective-permute-start.27 = (bf16[8192,128]{1,0:T(8,128)(2,1)}, bf16[8192,128]{1,0:T(8,128)(2,1)}, u32[]{:S(2)}, u32[]{:S(2)}) collective-permute-start(bf16[8192,128]{1,0:T(8,128)(2,1)} %get-tuple-element.106.refs_0_), channel_id=1, source_target_pairs={{0,1},{1,0},{2,3},{3,2},{4,5},{5,4},{6,7},{7,6},{8,9},{9,8},{10,11... | collective-permute-start | bytes 6291464 | tf_op jit(solution)/shard_map/ppermute | solution.py:465
  138.8 7.6 %collective-permute-start.28 = (bf16[8192,128]{1,0:T(8,128)(2,1)}, bf16[8192,128]{1,0:T(8,128)(2,1)}, u32[]{:S(2)}, u32[]{:S(2)}) collective-permute-start(bf16[8192,128]{1,0:T(8,128)(2,1)} %get-tuple-element.107.refs_1_), channel_id=1, source_target_pairs={{0,1},{1,0},{2,3},{3,2},{4,5},{5,4},{6,7},{7,6},{8,9},{9,8},{10,11... | collective-permute-start | bytes 6291464 | tf_op jit(solution)/shard_map/ppermute | solution.py:465
  138.9 35.8 %copy-start.20 = (f32[128]{0:T(128)S(1)}, f32[128]{0:T(128)}, u32[]{:S(2)}) copy-start(f32[128]{0:T(128)} %param.13) | copy-start | bytes 1540
  177.6 5.0 %collective-permute-start.31 = (bf16[256,256]{1,0:T(8,128)(2,1)S(1)}, bf16[256,256]{1,0:T(8,128)(2,1)S(1)}, u32[]{:S(2)}, u32[]{:S(2)}) collective-permute-start(bf16[256,256]{1,0:T(8,128)(2,1)S(1)} %get-tuple-element.101.refs_0_), channel_id=1, source_target_pairs={{0,192},{8,200},{16,208},{24,216},{32,224},{40,232},{48,240},{56,2... | collective-permute-start | bytes 393224 | tf_op jit(solution)/shard_map/ppermute | solution.py:456
  179.4 6.5 %collective-permute-start.30 = (bf16[256,256]{1,0:T(8,128)(2,1)S(1)}, bf16[256,256]{1,0:T(8,128)(2,1)S(1)}, u32[]{:S(2)}, u32[]{:S(2)}) collective-permute-start(bf16[256,256]{1,0:T(8,128)(2,1)S(1)} %get-tuple-element.101.refs_0_), channel_id=1, source_target_pairs={{0,128},{8,136},{16,144},{24,152},{32,160},{40,168},{48,176},{56,1... | collective-permute-start | bytes 393224 | tf_op jit(solution)/shard_map/ppermute | solution.py:456
  181.1 6.2 %collective-permute-start.29 = (bf16[256,256]{1,0:T(8,128)(2,1)S(1)}, bf16[256,256]{1,0:T(8,128)(2,1)S(1)}, u32[]{:S(2)}, u32[]{:S(2)}) collective-permute-start(bf16[256,256]{1,0:T(8,128)(2,1)S(1)} %get-tuple-element.101.refs_0_), channel_id=1, source_target_pairs={{0,64},{8,72},{16,80},{24,88},{32,96},{40,104},{48,112},{56,120},{... | collective-permute-start | bytes 393224 | tf_op jit(solution)/shard_map/ppermute | solution.py:456
  181.9 7.7 %collective-permute-start.32 = (bf16[256,256]{1,0:T(8,128)(2,1)S(1)}, bf16[256,256]{1,0:T(8,128)(2,1)S(1)}, u32[]{:S(2)}, u32[]{:S(2)}) collective-permute-start(bf16[256,256]{1,0:T(8,128)(2,1)S(1)} %get-tuple-element.104.own_ref), channel_id=1, source_target_pairs={{0,1},{1,0},{2,3},{3,2},{4,5},{5,4},{6,7},{7,6},{8,9},{9,8},{10,11... | collective-permute-start | bytes 393224 | tf_op jit(solution)/shard_map/ppermute | solution.py:465
  189.6 32.1 %all-to-all-start.2 = ((bf16[8,256,256]{2,1,0:T(8,128)(2,1)}), bf16[8,256,256]{2,1,0:T(8,128)(2,1)S(1)}, u32[]{:S(2)}, u32[]{:S(2)}) async-start(bf16[8,256,256]{2,1,0:T(8,128)(2,1)} %weight_terms.1), calls=%async_computation.2 | async-start | bytes 2097152 | tf_op jit(solution)/shard_map/all_to_all | solution.py:554
  199.8 16.1 %collective-permute-start.33 = (bf16[32,8192]{1,0:T(8,128)(2,1)S(1)}, bf16[32,8192]{1,0:T(8,128)(2,1)S(1)}, u32[]{:S(2)}, u32[]{:S(2)}) collective-permute-start(bf16[32,8192]{1,0:T(8,128)(2,1)S(1)} %get-tuple-element.111), channel_id=1, source_target_pairs={{0,2},{1,3},{2,4},{3,5},{4,6},{5,7},{6,0},{7,1},{8,10},{9,11},{10,... | collective-permute-start | bytes 1572872 | tf_op jit(solution)/shard_map/ppermute | solution.py:559
  201.3 20.4 %collective-permute-start.34 = (bf16[32,8192]{1,0:T(8,128)(2,1)S(1)}, bf16[32,8192]{1,0:T(8,128)(2,1)S(1)}, u32[]{:S(2)}, u32[]{:S(2)}) collective-permute-start(bf16[32,8192]{1,0:T(8,128)(2,1)S(1)} %get-tuple-element.112), channel_id=1, source_target_pairs={{0,4},{1,5},{2,6},{3,7},{4,0},{5,1},{6,2},{7,3},{8,12},{9,13},{10,... | collective-permute-start | bytes 1572872 | tf_op jit(solution)/shard_map/ppermute | solution.py:559
  204.1 17.6 %collective-permute-start.35 = (bf16[32,8192]{1,0:T(8,128)(2,1)S(1)}, bf16[32,8192]{1,0:T(8,128)(2,1)}, u32[]{:S(2)}, u32[]{:S(2)}) collective-permute-start(bf16[32,8192]{1,0:T(8,128)(2,1)S(1)} %get-tuple-element.113), channel_id=1, source_target_pairs={{0,6},{1,7},{2,0},{3,1},{4,2},{5,3},{6,4},{7,5},{8,14},{9,15},{10,... | collective-permute-start | bytes 1572872 | tf_op jit(solution)/shard_map/ppermute | solution.py:559
  (12 other events, 43.8 us)

commit v12 on v11

--- a/solution.py
+++ b/solution.py
@@ -499,9 +499,10 @@
         k_ring += [shift_z(k_ring[max(-2, -len(k_ring))], 1), shift_z(k_ring[-1], -1)]
         if hop == 1:
             v_ring += [shift_z(v_line, 1), shift_z(v_line, -1)]
-    k_ring[-2], k_ring[-1], v_ring[-2], v_ring[-1] = lax.optimization_barrier(
-        (k_ring[-2], k_ring[-1], v_ring[-2], v_ring[-1])
-    )
+        if hop == 2:
+            k_ring[-2], k_ring[-1], v_ring[-2], v_ring[-1] = lax.optimization_barrier(
+                (k_ring[-2], k_ring[-1], v_ring[-2], v_ring[-1])
+            )
     for hop in range(2, NZ // 2):
         v_ring += [shift_z(v_ring[-2], 1), shift_z(v_ring[-1], -1)]
     k_ring += [shift_z(k_ring[-2], 1)]
@@ -554,7 +555,7 @@
     shares = lax.all_to_all(shares, "dp", 0, 0, tiled=True, axis_index_groups=Z_GROUPS)
 
     terms = list(feature_terms(table, grads, other_grads, weights, tensor_count))
-    for s in range(1, tensor_count // 2):
+    for s in (2, 1, 3):
         pairs = [(t, (t + 2 * s) % tensor_count) for t in range(tensor_count)]
         terms[s] = lax.ppermute(terms[s], "tensor", pairs)
     shares, terms = lax.optimization_barrier((shares, terms))

time: 225 us -> 223 us (level)
  waiting for transfers between devices: 113 us -> 106 us
  starting transfers between devices: 62 us -> 66.3 us
    ppermute x14, waiting for transfers between devices: 22.5 us -> 13 us  [shift_z(): return lax.ppermute(x, 'dp', pairs)]
    ppermute x14, starting transfers between devices: 16.1 us -> 20.4 us  [shift_z(): return lax.ppermute(x, 'dp', pairs)]
    ppermute x15, waiting for transfers between devices: 10.8 us -> 14.4 us  [shift_y(): return lax.ppermute(x, 'dp', pairs)]
where the time goes in v12:
time: 223 us
  waiting for transfers between devices  106 us (48%)
  starting transfers between devices  66.3 us (30%)
  Pallas kernels  37.8 us (17%)
  local copies, waits for them, and re-layouts  7.68 us (3%)
  other arithmetic  3.43 us (2%)
    all_to_all x1, waiting for transfers between devices, local(): kv = lax.all_to_all(send, 'dp', 0, 0, tiled=True)  34.4 us
    all_to_all x1, waiting for transfers between devices, local(): parts = lax.all_to_all(parts, 'dp', 0, 0, tiled=True)  28.2 us
    ppermute x15, starting transfers between devices, shift_y(): return lax.ppermute(x, 'dp', pairs)  20.8 us
    ppermute x14, starting transfers between devices, shift_z(): return lax.ppermute(x, 'dp', pairs)  20.4 us
    ppermute x3, waiting for transfers between devices, local(): terms[s] = lax.ppermute(terms[s], 'tensor', pairs)  16.2 us
    ppermute x15, waiting for transfers between devices, shift_y(): return lax.ppermute(x, 'dp', pairs)  14.4 us
    ppermute x14, waiting for transfers between devices, shift_z(): return lax.ppermute(x, 'dp', pairs)  13 us
    all_to_all x1, starting transfers between devices, local(): kv = lax.all_to_all(send, 'dp', 0, 0, tiled=True)  8.89 us
  transfers between devices with their start and end apart: 39, of which 17 were waited for; matrix products, arithmetic and copies ran while one was open for 3% of the time, Pallas kernels for 13%

profile of v12, /device:TPU:32, one launch (start us, length us, event | category | flops | bytes accessed | tf_op | source)
XLA Modules:
  0.0 222.7 jit_solution(8519783619188823024)
XLA Ops:
  0.6 2.0 collective-permute-start
  2.7 3.2 %collective-permute-start.5 = (bf16[256,128]{1,0:T(8,128)(2,1)}, bf16[256,128]{1,0:T(8,128)(2,1)S(1)}, u32[]{:S(2)}, u32[]{:S(2)}) collective-permute-start(bf16[256,128]{1,0:T(8,128)(2,1)} %param.12), channel_id=1, source_target_pairs={{0,128},{8,136},{16,144},{24,152},{32,160},{40,168},{48,176},{56,1... | collective-permute-start | bytes 196616 | tf_op jit(solution)/shard_map/ppermute | solution.py:456
  5.9 1.1 collective-permute-start.4
  10.6 2.1 collective-permute-done.6
  12.7 4.1 %collective-permute-start.8 = (bf16[1024,128]{1,0:T(8,128)(2,1)S(1)}, bf16[1024,128]{1,0:T(8,128)(2,1)S(1)}, u32[]{:S(2)}, u32[]{:S(2)}) collective-permute-start(bf16[1024,128]{1,0:T(8,128)(2,1)S(1)} %constant_dynamic-update-slice_fusion.refs_8_), channel_id=1, source_target_pairs={{0,56},{8,0},{16,8},{24,16},{32,24},{40,32},{48,40},{56,48},{64,12... | collective-permute-start | bytes 786440 | tf_op jit(solution)/shard_map/ppermute | solution.py:461
  16.9 1.0 collective-permute-start.2
  17.9 1.1 collective-permute-start.3
  19.1 4.9 %collective-permute-done.2 = bf16[256,128]{1,0:T(8,128)(2,1)S(1)} collective-permute-done((bf16[256,128]{1,0:T(8,128)(2,1)S(1)}, bf16[256,128]{1,0:T(8,128)(2,1)S(1)}, u32[]{:S(2)}, u32[]{:S(2)}) %collective-permute-start.2) | collective-permute-done | bytes 65568 | tf_op jit(solution)/shard_map/ppermute | solution.py:461
  24.0 1.4 collective-permute-start.12
  25.5 3.2 %collective-permute-start.9 = (bf16[1024,128]{1,0:T(8,128)(2,1)S(1)}, bf16[1024,128]{1,0:T(8,128)(2,1)S(1)}, u32[]{:S(2)}, u32[]{:S(2)}) collective-permute-start(bf16[1024,128]{1,0:T(8,128)(2,1)S(1)} %constant_dynamic-update-slice_fusion.4.refs_0_), channel_id=1, source_target_pairs={{0,192},{8,200},{16,208},{24,216},{32,224},{40,232},{48,240},{56,2... | collective-permute-start | bytes 786440 | tf_op jit(solution)/shard_map/ppermute | solution.py:456
  28.7 1.7 collective-permute-start.13
  30.4 1.4 collective-permute-start.18
  31.9 1.9 collective-permute-start.19
  34.1 2.0 collective-permute-start.14
  36.2 4.1 %collective-permute-done.14 = bf16[256,128]{1,0:T(8,128)(2,1)S(1)} collective-permute-done((bf16[256,128]{1,0:T(8,128)(2,1)S(1)}, bf16[256,128]{1,0:T(8,128)(2,1)S(1)}, u32[]{:S(2)}, u32[]{:S(2)}) %collective-permute-start.14) | collective-permute-done | bytes 65568 | tf_op jit(solution)/shard_map/ppermute | solution.py:461
  40.4 1.1 collective-permute-start.20
  41.6 3.2 %collective-permute-start.15 = (bf16[1024,128]{1,0:T(8,128)(2,1)S(1)}, bf16[1024,128]{1,0:T(8,128)(2,1)S(1)}, u32[]{:S(2)}, u32[]{:S(2)}) collective-permute-start(bf16[1024,128]{1,0:T(8,128)(2,1)S(1)} %constant_dynamic-update-slice_fusion.8.refs_4_), channel_id=1, source_target_pairs={{0,192},{8,200},{16,208},{24,216},{32,224},{40,232},{48,240},{56,2... | collective-permute-start | bytes 786440 | tf_op jit(solution)/shard_map/ppermute | solution.py:456
  44.9 2.5 %collective-permute-start.21 = (bf16[1024,128]{1,0:T(8,128)(2,1)S(1)}, bf16[1024,128]{1,0:T(8,128)(2,1)}, u32[]{:S(2)}, u32[]{:S(2)}) collective-permute-start(bf16[1024,128]{1,0:T(8,128)(2,1)S(1)} %collective-permute-done.19.refs_12_), channel_id=1, source_target_pairs={{0,56},{8,0},{16,8},{24,16},{32,24},{40,32},{48,40},{56,48},{64,12... | collective-permute-start | bytes 786440 | tf_op jit(solution)/shard_map/ppermute | solution.py:461
  47.4 1.7 collective-permute-done.16.refs_6_
  49.4 1.7 collective-permute-done.20.refs_13_
  51.9 5.0 %collective-permute-done.17.refs_7_ = bf16[1024,128]{1,0:T(8,128)(2,1)} collective-permute-done((bf16[1024,128]{1,0:T(8,128)(2,1)S(1)}, bf16[1024,128]{1,0:T(8,128)(2,1)}, u32[]{:S(2)}, u32[]{:S(2)}) %collective-permute-start.17) | collective-permute-done | bytes 262176 | tf_op jit(solution)/shard_map/ppermute | solution.py:456
  56.8 1.6 collective-permute-done.22.refs_15_
  59.1 6.0 %project.1 = (bf16[32,128,256]{2,1,0:T(8,128)(2,1)}, f32[256,128]{1,0:T(8,128)}) custom-call(s32[5,32]{1,0:T(8,128)S(1)} %stack.41.table_ref, bf16[256,8192]{1,0:T(8,128)(2,1)} %bitcast.24, bf16[1024,128]{1,0:T(8,128)(2,1)S(1)} %constant_dynamic-update-slice_fusion.4.refs_0_, bf16[1024,128]{1,0:T(8,128)(2,1)S(1)} %collective-permute-done.9.refs_1_, ...), custom_call_target="tpu_custom_call" | custom-call | flops 1073741824 | bytes 10485760 | tf_op jit(solution)/shard_map/project/pallas_call | solution.py:92
  65.2 8.9 %all-to-all-start = ((bf16[32,128,256]{2,1,0:T(8,128)(2,1)}), bf16[32,128,256]{2,1,0:T(8,128)(2,1)S(1)}, u32[]{:S(2)}, u32[]{:S(2)}) async-start(bf16[32,128,256]{2,1,0:T(8,128)(2,1)} %get-tuple-element.66), calls=%async_computation | async-start | bytes 4194304 | tf_op jit(solution)/shard_map/all_to_all | solution.py:524
  74.2 2.9 %dynamic-slice_bitcast_fusion = (bf16[128,2048]{1,0:T(8,128)(2,1)}, bf16[128,2048]{1,0:T(8,128)(2,1)}, bf16[128,2048]{1,0:T(8,128)(2,1)}, bf16[128,2048]{1,0:T(8,128)(2,1)}) fusion(bf16[2,128,8192]{2,1,0:T(8,128)(2,1)} %param.10, s32[]{:T(128)S(6)} %select_n.86, s32[]{:T(128)S(6)} %select_n.94, s32[]{:T(128)S(6)} %select_n.92, s32[]{:T(128)S(6)} %select_n.90, ...), kind=kLoop, calls=%fused_computation.2 | loop fusion | bytes 4194324 | tf_op jit(solution)/shard_map/squeeze | solution.py:530
  77.1 2.7 %collective-permute-start.25 = (bf16[128,2048]{1,0:T(8,128)(2,1)}, bf16[128,2048]{1,0:T(8,128)(2,1)}, u32[]{:S(2)}, u32[]{:S(2)}) collective-permute-start(bf16[128,2048]{1,0:T(8,128)(2,1)} %get-tuple-element.123), channel_id=1, source_target_pairs={{0,192},{8,200},{16,208},{24,216},{32,224},{40,232},{48,240},{56,2... | collective-permute-start | bytes 1572872 | tf_op jit(solution)/shard_map/ppermute | solution.py:456
  81.5 34.4 %all-to-all-done.kv_ref = bf16[32,128,256]{2,1,0:T(8,128)(2,1)S(1)} async-done(((bf16[32,128,256]{2,1,0:T(8,128)(2,1)}), bf16[32,128,256]{2,1,0:T(8,128)(2,1)S(1)}, u32[]{:S(2)}, u32[]{:S(2)}) %all-to-all-start) | async-done | bytes 2097184 | tf_op jit(solution)/shard_map/all_to_all | solution.py:524
  115.9 7.9 %attend.1 = (bf16[32,128,256]{2,1,0:T(8,128)(2,1)}, bf16[32,128,128]{2,1,0:T(8,128)(2,1)}, bf16[32,128,128]{2,1,0:T(8,128)(2,1)}) custom-call(s32[5,32]{1,0:T(8,128)S(1)} %stack.41.table_ref, bf16[512,1024]{1,0:T(8,128)(2,1)} %q_hbm.1, bf16[512,1024]{1,0:T(8,128)(2,1)} %ct_hbm.1, bf16[32,128,256]{2,1,0:T(8,128)(2,1)S(1)} %all-to-all-done.kv_ref), custom_call_target="tpu_custom_call" | custom-call | flops 536870912 | bytes 8388608 | tf_op jit(solution)/shard_map/attend/pallas_call | solution.py:213
  123.9 5.7 %all-to-all-start.1 = ((bf16[32,128,256]{2,1,0:T(8,128)(2,1)}), bf16[32,128,256]{2,1,0:T(8,128)(2,1)}, u32[]{:S(2)}, u32[]{:S(2)}) async-start(bf16[32,128,256]{2,1,0:T(8,128)(2,1)} %get-tuple-element.70), calls=%async_computation.1 | async-start | bytes 4194304 | tf_op jit(solution)/shard_map/all_to_all | solution.py:540
  129.6 2.2 %transpose_pieces.1.own_ref = bf16[2048,512]{1,0:T(8,128)(2,1)S(1)} custom-call(bf16[128,2048]{1,0:T(8,128)(2,1)} %get-tuple-element.71.refs_0_, bf16[128,2048]{1,0:T(8,128)(2,1)} %collective-permute-done.23.refs_1_, bf16[128,2048]{1,0:T(8,128)(2,1)} %collective-permute-done.24.refs_2_, bf16[128,2048]{1,0:T(8,128)(2,1)} %collective-permute-done.25.refs_3_), custom_call_target="tpu_custom_call" | custom-call | bytes 4194304 | tf_op jit(solution)/shard_map/transpose_pieces/pallas_call | solution.py:326
  132.3 4.1 %assemble.1 = (bf16[8192,128]{1,0:T(8,128)(2,1)}, bf16[8192,128]{1,0:T(8,128)(2,1)}) custom-call(s32[5,32]{1,0:T(8,128)S(1)} %stack.41.table_ref, bf16[1024,128]{1,0:T(8,128)(2,1)S(1)} %constant_dynamic-update-slice_fusion.4.refs_0_, bf16[1024,128]{1,0:T(8,128)(2,1)S(1)} %copy-done.6, bf16[1024,128]{1,0:T(8,128)(2,1)S(1)} %copy-done.4, ...), custom_call_target="tpu_custom_call" | custom-call | bytes 1048576 | tf_op jit(solution)/shard_map/assemble/pallas_call | solution.py:371
  136.9 6.2 %apply.1 = (bf16[512,1024]{1,0:T(8,128)(2,1)}, bf16[512,1024]{1,0:T(8,128)(2,1)}) custom-call(s32[5,32]{1,0:T(8,128)S(1)} %stack.41.table_ref, bf16[32,128,256]{2,1,0:T(8,128)(2,1)} %copy-done, bf16[32,128,128]{2,1,0:T(8,128)(2,1)} %get-tuple-element.75.probs_ref, bf16[32,128,128]{2,1,0:T(8,128)(2,1)} %get-tuple-element.76.ds_ref), custom_call_target="tpu_custom_call" | custom-call | flops 268435456 | bytes 6291456 | tf_op jit(solution)/shard_map/apply/pallas_call | solution.py:255
  143.1 1.4 copy-done.1
  144.4 28.2 %all-to-all-done.1.part_ref = bf16[32,128,256]{2,1,0:T(8,128)(2,1)} async-done(((bf16[32,128,256]{2,1,0:T(8,128)(2,1)}), bf16[32,128,256]{2,1,0:T(8,128)(2,1)}, u32[]{:S(2)}, u32[]{:S(2)}) %all-to-all-start.1) | async-done | bytes 2097184 | tf_op jit(solution)/shard_map/all_to_all | solution.py:540
  172.6 3.0 %owner_grads.1 = (bf16[256,256]{1,0:T(8,128)(2,1)S(1)}, bf16[256,256]{1,0:T(8,128)(2,1)S(1)}) custom-call(s32[5,32]{1,0:T(8,128)S(1)} %stack.41.table_ref, bf16[32,128,256]{2,1,0:T(8,128)(2,1)} %all-to-all-done.1.part_ref, f32[256,128]{1,0:T(8,128)} %get-tuple-element.68.raw_ref, f32[1,128]{1,0:T(1,128)S(1)} %bitcast.23), custom_call_target="tpu_custom_call" | custom-call | bytes 3145728 | tf_op jit(solution)/shard_map/owner_grads/pallas_call | solution.py:301
  175.7 1.8 collective-permute-start.31
  177.4 1.8 collective-permute-start.30
  180.7 3.2 %collective-permute-done.30.refs_2_ = bf16[256,256]{1,0:T(8,128)(2,1)S(1)} collective-permute-done((bf16[256,256]{1,0:T(8,128)(2,1)S(1)}, bf16[256,256]{1,0:T(8,128)(2,1)S(1)}, u32[]{:S(2)}, u32[]{:S(2)}) %collective-permute-start.30) | collective-permute-done | bytes 131104 | tf_op jit(solution)/shard_map/ppermute | solution.py:456
  183.9 1.5 collective-permute-done.29.refs_1_
  185.4 2.3 %weight_terms.1 = bf16[8,256,256]{2,1,0:T(8,128)(2,1)} custom-call(bf16[2048,512]{1,0:T(8,128)(2,1)S(1)} %transpose_pieces.1.own_ref, bf16[2048,512]{1,0:T(8,128)(2,1)S(1)} %copy-done.2, bf16[256,256]{1,0:T(8,128)(2,1)S(1)} %get-tuple-element.101.refs_0_, bf16[256,256]{1,0:T(8,128)(2,1)S(1)} %collective-permute-done.29.refs_1_, ...), custom_call_target="tpu_custom_call" | custom-call | flops 1073741824 | bytes 6291456 | tf_op jit(solution)/shard_map/weight_terms/pallas_call | solution.py:352
  187.7 4.0 %all-to-all-start.2 = ((bf16[8,256,256]{2,1,0:T(8,128)(2,1)}), bf16[8,256,256]{2,1,0:T(8,128)(2,1)S(1)}, u32[]{:S(2)}, u32[]{:S(2)}) async-start(bf16[8,256,256]{2,1,0:T(8,128)(2,1)} %weight_terms.1), calls=%async_computation.2 | async-start | bytes 2097152 | tf_op jit(solution)/shard_map/all_to_all | solution.py:555
  191.6 6.2 %feature_terms.1 = (bf16[32,8192]{1,0:T(8,128)(2,1)S(1)}, bf16[32,8192]{1,0:T(8,128)(2,1)S(1)}, bf16[32,8192]{1,0:T(8,128)(2,1)S(1)}, bf16[32,8192]{1,0:T(8,128)(2,1)S(1)}) custom-call(s32[5,32]{1,0:T(8,128)S(1)} %stack.41.table_ref, bf16[256,256]{1,0:T(8,128)(2,1)S(1)} %get-tuple-element.104.own_ref, ...), custom_call_target="tpu_custom_call" | custom-call | flops 2147483648 | bytes 10485760 | tf_op jit(solution)/shard_map/feature_terms/pallas_call | solution.py:432
  197.8 1.6 collective-permute-start.33
  199.4 2.7 %collective-permute-start.34 = (bf16[32,8192]{1,0:T(8,128)(2,1)S(1)}, bf16[32,8192]{1,0:T(8,128)(2,1)S(1)}, u32[]{:S(2)}, u32[]{:S(2)}) collective-permute-start(bf16[32,8192]{1,0:T(8,128)(2,1)S(1)} %get-tuple-element.112), channel_id=1, source_target_pairs={{0,4},{1,5},{2,6},{3,7},{4,0},{5,1},{6,2},{7,3},{8,12},{9,13},{10,... | collective-permute-start | bytes 1572872 | tf_op jit(solution)/shard_map/ppermute | solution.py:560
  202.1 1.4 collective-permute-start.35
  203.5 10.4 %collective-permute-done.33 = bf16[32,8192]{1,0:T(8,128)(2,1)S(1)} collective-permute-done((bf16[32,8192]{1,0:T(8,128)(2,1)S(1)}, bf16[32,8192]{1,0:T(8,128)(2,1)S(1)}, u32[]{:S(2)}, u32[]{:S(2)}) %collective-permute-start.33) | collective-permute-done | bytes 524320 | tf_op jit(solution)/shard_map/ppermute | solution.py:560
  213.9 5.9 %collective-permute-done.34 = bf16[32,8192]{1,0:T(8,128)(2,1)S(1)} collective-permute-done((bf16[32,8192]{1,0:T(8,128)(2,1)S(1)}, bf16[32,8192]{1,0:T(8,128)(2,1)S(1)}, u32[]{:S(2)}, u32[]{:S(2)}) %collective-permute-start.34) | collective-permute-done | bytes 524320 | tf_op jit(solution)/shard_map/ppermute | solution.py:560
  220.6 2.1 add_convert_fusion
  (107 shorter events, 11.3 us)
Async XLA Ops:
  0.6 16.2 %collective-permute-start = (bf16[256,128]{1,0:T(8,128)(2,1)}, bf16[256,128]{1,0:T(8,128)(2,1)S(1)}, u32[]{:S(2)}, u32[]{:S(2)}) collective-permute-start(bf16[256,128]{1,0:T(8,128)(2,1)} %param.11), channel_id=1, source_target_pairs={{0,8},{8,16},{16,24},{24,32},{32,40},{40,48},{48,56},{56,0},{64,72... | collective-permute-start | bytes 196616 | tf_op jit(solution)/shard_map/ppermute | solution.py:461
  2.6 15.3 %collective-permute-start.1 = (bf16[256,128]{1,0:T(8,128)(2,1)}, bf16[256,128]{1,0:T(8,128)(2,1)S(1)}, u32[]{:S(2)}, u32[]{:S(2)}) collective-permute-start(bf16[256,128]{1,0:T(8,128)(2,1)} %param.11), channel_id=1, source_target_pairs={{0,56},{8,0},{16,8},{24,16},{32,24},{40,32},{48,40},{56,48},{64,12... | collective-permute-start | bytes 196616 | tf_op jit(solution)/shard_map/ppermute | solution.py:461
  2.7 7.8 %collective-permute-start.5 = (bf16[256,128]{1,0:T(8,128)(2,1)}, bf16[256,128]{1,0:T(8,128)(2,1)S(1)}, u32[]{:S(2)}, u32[]{:S(2)}) collective-permute-start(bf16[256,128]{1,0:T(8,128)(2,1)} %param.12), channel_id=1, source_target_pairs={{0,128},{8,136},{16,144},{24,152},{32,160},{40,168},{48,176},{56,1... | collective-permute-start | bytes 196616 | tf_op jit(solution)/shard_map/ppermute | solution.py:456
  5.9 4.6 %collective-permute-start.4 = (bf16[256,128]{1,0:T(8,128)(2,1)}, bf16[256,128]{1,0:T(8,128)(2,1)S(1)}, u32[]{:S(2)}, u32[]{:S(2)}) collective-permute-start(bf16[256,128]{1,0:T(8,128)(2,1)} %param.12), channel_id=1, source_target_pairs={{0,192},{8,200},{16,208},{24,216},{32,224},{40,232},{48,240},{56,2... | collective-permute-start | bytes 196616 | tf_op jit(solution)/shard_map/ppermute | solution.py:456
  7.0 5.7 %collective-permute-start.6 = (bf16[256,128]{1,0:T(8,128)(2,1)}, bf16[256,128]{1,0:T(8,128)(2,1)S(1)}, u32[]{:S(2)}, u32[]{:S(2)}) collective-permute-start(bf16[256,128]{1,0:T(8,128)(2,1)} %param.12), channel_id=1, source_target_pairs={{0,64},{8,72},{16,80},{24,88},{32,96},{40,104},{48,112},{56,120},{... | collective-permute-start | bytes 196616 | tf_op jit(solution)/shard_map/ppermute | solution.py:456
  12.7 11.3 %collective-permute-start.8 = (bf16[1024,128]{1,0:T(8,128)(2,1)S(1)}, bf16[1024,128]{1,0:T(8,128)(2,1)S(1)}, u32[]{:S(2)}, u32[]{:S(2)}) collective-permute-start(bf16[1024,128]{1,0:T(8,128)(2,1)S(1)} %constant_dynamic-update-slice_fusion.refs_8_), channel_id=1, source_target_pairs={{0,56},{8,0},{16,8},{24,16},{32,24},{40,32},{48,40},{56,48},{64,12... | collective-permute-start | bytes 786440 | tf_op jit(solution)/shard_map/ppermute | solution.py:461
  16.8 7.2 %collective-permute-start.7 = (bf16[1024,128]{1,0:T(8,128)(2,1)S(1)}, bf16[1024,128]{1,0:T(8,128)(2,1)S(1)}, u32[]{:S(2)}, u32[]{:S(2)}) collective-permute-start(bf16[1024,128]{1,0:T(8,128)(2,1)S(1)} %constant_dynamic-update-slice_fusion.refs_8_), channel_id=1, source_target_pairs={{0,8},{8,16},{16,24},{24,32},{32,40},{40,48},{48,56},{56,0},{64,72... | collective-permute-start | bytes 786440 | tf_op jit(solution)/shard_map/ppermute | solution.py:461
  16.9 7.1 %collective-permute-start.2 = (bf16[256,128]{1,0:T(8,128)(2,1)S(1)}, bf16[256,128]{1,0:T(8,128)(2,1)S(1)}, u32[]{:S(2)}, u32[]{:S(2)}) collective-permute-start(bf16[256,128]{1,0:T(8,128)(2,1)S(1)} %collective-permute-done), channel_id=1, source_target_pairs={{0,8},{8,16},{16,24},{24,32},{32,40},{40,48},{48,56},{56,0},{64,72... | collective-permute-start | bytes 196616 | tf_op jit(solution)/shard_map/ppermute | solution.py:461
  17.9 6.1 %collective-permute-start.3 = (bf16[256,128]{1,0:T(8,128)(2,1)S(1)}, bf16[256,128]{1,0:T(8,128)(2,1)S(1)}, u32[]{:S(2)}, u32[]{:S(2)}) collective-permute-start(bf16[256,128]{1,0:T(8,128)(2,1)S(1)} %collective-permute-done.1), channel_id=1, source_target_pairs={{0,56},{8,0},{16,8},{24,16},{32,24},{40,32},{48,40},{56,48},{64,12... | collective-permute-start | bytes 196616 | tf_op jit(solution)/shard_map/ppermute | solution.py:461
  24.0 7.9 %collective-permute-start.12 = (bf16[256,128]{1,0:T(8,128)(2,1)S(1)}, bf16[256,128]{1,0:T(8,128)(2,1)S(1)}, u32[]{:S(2)}, u32[]{:S(2)}) collective-permute-start(bf16[256,128]{1,0:T(8,128)(2,1)S(1)} %collective-permute-done.2), channel_id=1, source_target_pairs={{0,8},{8,16},{16,24},{24,32},{32,40},{40,48},{48,56},{56,0},{64,72... | collective-permute-start | bytes 196616 | tf_op jit(solution)/shard_map/ppermute | solution.py:461
  25.4 16.2 %collective-permute-start.10 = (bf16[1024,128]{1,0:T(8,128)(2,1)S(1)}, bf16[1024,128]{1,0:T(8,128)(2,1)S(1)}, u32[]{:S(2)}, u32[]{:S(2)}) collective-permute-start(bf16[1024,128]{1,0:T(8,128)(2,1)S(1)} %constant_dynamic-update-slice_fusion.4.refs_0_), channel_id=1, source_target_pairs={{0,64},{8,72},{16,80},{24,88},{32,96},{40,104},{48,112},{56,120},{... | collective-permute-start | bytes 786440 | tf_op jit(solution)/shard_map/ppermute | solution.py:456
  25.5 19.3 %collective-permute-start.9 = (bf16[1024,128]{1,0:T(8,128)(2,1)S(1)}, bf16[1024,128]{1,0:T(8,128)(2,1)S(1)}, u32[]{:S(2)}, u32[]{:S(2)}) collective-permute-start(bf16[1024,128]{1,0:T(8,128)(2,1)S(1)} %constant_dynamic-update-slice_fusion.4.refs_0_), channel_id=1, source_target_pairs={{0,192},{8,200},{16,208},{24,216},{32,224},{40,232},{48,240},{56,2... | collective-permute-start | bytes 786440 | tf_op jit(solution)/shard_map/ppermute | solution.py:456
  28.7 5.4 %collective-permute-start.13 = (bf16[256,128]{1,0:T(8,128)(2,1)S(1)}, bf16[256,128]{1,0:T(8,128)(2,1)S(1)}, u32[]{:S(2)}, u32[]{:S(2)}) collective-permute-start(bf16[256,128]{1,0:T(8,128)(2,1)S(1)} %collective-permute-done.3), channel_id=1, source_target_pairs={{0,56},{8,0},{16,8},{24,16},{32,24},{40,32},{48,40},{56,48},{64,12... | collective-permute-start | bytes 196616 | tf_op jit(solution)/shard_map/ppermute | solution.py:461
  30.4 9.9 %collective-permute-start.18 = (bf16[1024,128]{1,0:T(8,128)(2,1)S(1)}, bf16[1024,128]{1,0:T(8,128)(2,1)S(1)}, u32[]{:S(2)}, u32[]{:S(2)}) collective-permute-start(bf16[1024,128]{1,0:T(8,128)(2,1)S(1)} %collective-permute-done.7.refs_9_), channel_id=1, source_target_pairs={{0,8},{8,16},{16,24},{24,32},{32,40},{40,48},{48,56},{56,0},{64,72... | collective-permute-start | bytes 786440 | tf_op jit(solution)/shard_map/ppermute | solution.py:461
  31.9 13.0 %collective-permute-start.19 = (bf16[1024,128]{1,0:T(8,128)(2,1)S(1)}, bf16[1024,128]{1,0:T(8,128)(2,1)S(1)}, u32[]{:S(2)}, u32[]{:S(2)}) collective-permute-start(bf16[1024,128]{1,0:T(8,128)(2,1)S(1)} %collective-permute-done.8.refs_10_), channel_id=1, source_target_pairs={{0,56},{8,0},{16,8},{24,16},{32,24},{40,32},{48,40},{56,48},{64,12... | collective-permute-start | bytes 786440 | tf_op jit(solution)/shard_map/ppermute | solution.py:461
  34.1 6.1 %collective-permute-start.14 = (bf16[256,128]{1,0:T(8,128)(2,1)S(1)}, bf16[256,128]{1,0:T(8,128)(2,1)S(1)}, u32[]{:S(2)}, u32[]{:S(2)}) collective-permute-start(bf16[256,128]{1,0:T(8,128)(2,1)S(1)} %collective-permute-done.12), channel_id=1, source_target_pairs={{0,8},{8,16},{16,24},{24,32},{32,40},{40,48},{48,56},{56,0},{64,72... | collective-permute-start | bytes 196616 | tf_op jit(solution)/shard_map/ppermute | solution.py:461
  40.3 8.9 %collective-permute-start.16 = (bf16[1024,128]{1,0:T(8,128)(2,1)S(1)}, bf16[1024,128]{1,0:T(8,128)(2,1)S(1)}, u32[]{:S(2)}, u32[]{:S(2)}) collective-permute-start(bf16[1024,128]{1,0:T(8,128)(2,1)S(1)} %constant_dynamic-update-slice_fusion.8.refs_4_), channel_id=1, source_target_pairs={{0,64},{8,72},{16,80},{24,88},{32,96},{40,104},{48,112},{56,120},{... | collective-permute-start | bytes 786440 | tf_op jit(solution)/shard_map/ppermute | solution.py:456
  40.4 24.7 %copy-start.7 = (bf16[1024,128]{1,0:T(8,128)(2,1)}, bf16[1024,128]{1,0:T(8,128)(2,1)S(1)}, u32[]{:S(2)}) copy-start(bf16[1024,128]{1,0:T(8,128)(2,1)S(1)} %collective-permute-done.18.refs_11_) | copy-start | bytes 786436
  40.4 10.7 %collective-permute-start.20 = (bf16[1024,128]{1,0:T(8,128)(2,1)S(1)}, bf16[1024,128]{1,0:T(8,128)(2,1)S(1)}, u32[]{:S(2)}, u32[]{:S(2)}) collective-permute-start(bf16[1024,128]{1,0:T(8,128)(2,1)S(1)} %collective-permute-done.18.refs_11_), channel_id=1, source_target_pairs={{0,8},{8,16},{16,24},{24,32},{32,40},{40,48},{48,56},{56,0},{64,72... | collective-permute-start | bytes 786440 | tf_op jit(solution)/shard_map/ppermute | solution.py:461
  41.6 23.5 %copy-start.3 = (bf16[1024,128]{1,0:T(8,128)(2,1)}, bf16[1024,128]{1,0:T(8,128)(2,1)S(1)}, u32[]{:S(2)}) copy-start(bf16[1024,128]{1,0:T(8,128)(2,1)S(1)} %collective-permute-done.10.refs_2_) | copy-start | bytes 786436
  41.6 9.7 %collective-permute-start.15 = (bf16[1024,128]{1,0:T(8,128)(2,1)S(1)}, bf16[1024,128]{1,0:T(8,128)(2,1)S(1)}, u32[]{:S(2)}, u32[]{:S(2)}) collective-permute-start(bf16[1024,128]{1,0:T(8,128)(2,1)S(1)} %constant_dynamic-update-slice_fusion.8.refs_4_), channel_id=1, source_target_pairs={{0,192},{8,200},{16,208},{24,216},{32,224},{40,232},{48,240},{56,2... | collective-permute-start | bytes 786440 | tf_op jit(solution)/shard_map/ppermute | solution.py:456
  44.8 20.3 %copy-start.5 = (bf16[1024,128]{1,0:T(8,128)(2,1)}, bf16[1024,128]{1,0:T(8,128)(2,1)S(1)}, u32[]{:S(2)}) copy-start(bf16[1024,128]{1,0:T(8,128)(2,1)S(1)} %collective-permute-done.9.refs_1_) | copy-start | bytes 786436
  44.8 6.7 %collective-permute-start.11 = (bf16[1024,128]{1,0:T(8,128)(2,1)S(1)}, bf16[1024,128]{1,0:T(8,128)(2,1)S(1)}, u32[]{:S(2)}, u32[]{:S(2)}) collective-permute-start(bf16[1024,128]{1,0:T(8,128)(2,1)S(1)} %collective-permute-done.9.refs_1_), channel_id=1, source_target_pairs={{0,192},{8,200},{16,208},{24,216},{32,224},{40,232},{48,240},{56,2... | collective-permute-start | bytes 786440 | tf_op jit(solution)/shard_map/ppermute | solution.py:456
  44.9 20.2 %copy-start.9 = (bf16[1024,128]{1,0:T(8,128)(2,1)}, bf16[1024,128]{1,0:T(8,128)(2,1)S(1)}, u32[]{:S(2)}) copy-start(bf16[1024,128]{1,0:T(8,128)(2,1)S(1)} %collective-permute-done.19.refs_12_) | copy-start | bytes 786436
  44.9 6.9 %collective-permute-start.21 = (bf16[1024,128]{1,0:T(8,128)(2,1)S(1)}, bf16[1024,128]{1,0:T(8,128)(2,1)}, u32[]{:S(2)}, u32[]{:S(2)}) collective-permute-start(bf16[1024,128]{1,0:T(8,128)(2,1)S(1)} %collective-permute-done.19.refs_12_), channel_id=1, source_target_pairs={{0,56},{8,0},{16,8},{24,16},{32,24},{40,32},{48,40},{56,48},{64,12... | collective-permute-start | bytes 786440 | tf_op jit(solution)/shard_map/ppermute | solution.py:461
  49.1 16.0 %copy-start.11 = (bf16[1024,128]{1,0:T(8,128)(2,1)}, bf16[1024,128]{1,0:T(8,128)(2,1)S(1)}, u32[]{:S(2)}) copy-start(bf16[1024,128]{1,0:T(8,128)(2,1)S(1)} %collective-permute-done.16.refs_6_) | copy-start | bytes 786436
  49.1 7.7 %collective-permute-start.17 = (bf16[1024,128]{1,0:T(8,128)(2,1)S(1)}, bf16[1024,128]{1,0:T(8,128)(2,1)}, u32[]{:S(2)}, u32[]{:S(2)}) collective-permute-start(bf16[1024,128]{1,0:T(8,128)(2,1)S(1)} %collective-permute-done.16.refs_6_), channel_id=1, source_target_pairs={{0,64},{8,72},{16,80},{24,88},{32,96},{40,104},{48,112},{56,120},{... | collective-permute-start | bytes 786440 | tf_op jit(solution)/shard_map/ppermute | solution.py:456
  51.1 14.1 %copy-start.13 = (bf16[1024,128]{1,0:T(8,128)(2,1)}, bf16[1024,128]{1,0:T(8,128)(2,1)S(1)}, u32[]{:S(2)}) copy-start(bf16[1024,128]{1,0:T(8,128)(2,1)S(1)} %collective-permute-done.20.refs_13_) | copy-start | bytes 786436
  51.1 7.4 %collective-permute-start.22 = (bf16[1024,128]{1,0:T(8,128)(2,1)S(1)}, bf16[1024,128]{1,0:T(8,128)(2,1)}, u32[]{:S(2)}, u32[]{:S(2)}) collective-permute-start(bf16[1024,128]{1,0:T(8,128)(2,1)S(1)} %collective-permute-done.20.refs_13_), channel_id=1, source_target_pairs={{0,8},{8,16},{16,24},{24,32},{32,40},{40,48},{48,56},{56,0},{64,72... | collective-permute-start | bytes 786440 | tf_op jit(solution)/shard_map/ppermute | solution.py:461
  51.3 13.8 %copy-start.15 = (bf16[1024,128]{1,0:T(8,128)(2,1)}, bf16[1024,128]{1,0:T(8,128)(2,1)S(1)}, u32[]{:S(2)}) copy-start(bf16[1024,128]{1,0:T(8,128)(2,1)S(1)} %collective-permute-done.15.refs_5_) | copy-start | bytes 786436
  51.5 13.7 %copy-start.17 = (bf16[1024,128]{1,0:T(8,128)(2,1)}, bf16[1024,128]{1,0:T(8,128)(2,1)S(1)}, u32[]{:S(2)}) copy-start(bf16[1024,128]{1,0:T(8,128)(2,1)S(1)} %collective-permute-done.11.refs_3_) | copy-start | bytes 786436
  65.2 50.7 %all-to-all-start = ((bf16[32,128,256]{2,1,0:T(8,128)(2,1)}), bf16[32,128,256]{2,1,0:T(8,128)(2,1)S(1)}, u32[]{:S(2)}, u32[]{:S(2)}) async-start(bf16[32,128,256]{2,1,0:T(8,128)(2,1)} %get-tuple-element.66), calls=%async_computation | async-start | bytes 4194304 | tf_op jit(solution)/shard_map/all_to_all | solution.py:524
  77.1 46.8 %collective-permute-start.25 = (bf16[128,2048]{1,0:T(8,128)(2,1)}, bf16[128,2048]{1,0:T(8,128)(2,1)}, u32[]{:S(2)}, u32[]{:S(2)}) collective-permute-start(bf16[128,2048]{1,0:T(8,128)(2,1)} %get-tuple-element.123), channel_id=1, source_target_pairs={{0,192},{8,200},{16,208},{24,216},{32,224},{40,232},{48,240},{56,2... | collective-permute-start | bytes 1572872 | tf_op jit(solution)/shard_map/ppermute | solution.py:456
  79.8 44.1 %collective-permute-start.24 = (bf16[128,2048]{1,0:T(8,128)(2,1)}, bf16[128,2048]{1,0:T(8,128)(2,1)}, u32[]{:S(2)}, u32[]{:S(2)}) collective-permute-start(bf16[128,2048]{1,0:T(8,128)(2,1)} %get-tuple-element.124), channel_id=1, source_target_pairs={{0,128},{8,136},{16,144},{24,152},{32,160},{40,168},{48,176},{56,1... | collective-permute-start | bytes 1572872 | tf_op jit(solution)/shard_map/ppermute | solution.py:456
  80.6 43.3 %collective-permute-start.23 = (bf16[128,2048]{1,0:T(8,128)(2,1)}, bf16[128,2048]{1,0:T(8,128)(2,1)}, u32[]{:S(2)}, u32[]{:S(2)}) collective-permute-start(bf16[128,2048]{1,0:T(8,128)(2,1)} %get-tuple-element.125), channel_id=1, source_target_pairs={{0,64},{8,72},{16,80},{24,88},{32,96},{40,104},{48,112},{56,120},{... | collective-permute-start | bytes 1572872 | tf_op jit(solution)/shard_map/ppermute | solution.py:456
  123.9 48.8 %all-to-all-start.1 = ((bf16[32,128,256]{2,1,0:T(8,128)(2,1)}), bf16[32,128,256]{2,1,0:T(8,128)(2,1)}, u32[]{:S(2)}, u32[]{:S(2)}) async-start(bf16[32,128,256]{2,1,0:T(8,128)(2,1)} %get-tuple-element.70), calls=%async_computation.1 | async-start | bytes 4194304 | tf_op jit(solution)/shard_map/all_to_all | solution.py:540
  131.9 11.2 %collective-permute-start.26 = (bf16[2048,512]{1,0:T(8,128)(2,1)S(1)}, bf16[2048,512]{1,0:T(8,128)(2,1)S(1)}, u32[]{:S(2)}, u32[]{:S(2)}) collective-permute-start(bf16[2048,512]{1,0:T(8,128)(2,1)S(1)} %transpose_pieces.1.own_ref), channel_id=1, source_target_pairs={{0,1},{1,0},{2,3},{3,2},{4,5},{5,4},{6,7},{7,6},{8,9},{9,8},{10,11... | collective-permute-start | bytes 6291464 | tf_op jit(solution)/shard_map/ppermute | solution.py:465
  136.4 8.0 %collective-permute-start.27 = (bf16[8192,128]{1,0:T(8,128)(2,1)}, bf16[8192,128]{1,0:T(8,128)(2,1)}, u32[]{:S(2)}, u32[]{:S(2)}) collective-permute-start(bf16[8192,128]{1,0:T(8,128)(2,1)} %get-tuple-element.106.refs_0_), channel_id=1, source_target_pairs={{0,1},{1,0},{2,3},{3,2},{4,5},{5,4},{6,7},{7,6},{8,9},{9,8},{10,11... | collective-permute-start | bytes 6291464 | tf_op jit(solution)/shard_map/ppermute | solution.py:465
  136.8 7.6 %collective-permute-start.28 = (bf16[8192,128]{1,0:T(8,128)(2,1)}, bf16[8192,128]{1,0:T(8,128)(2,1)}, u32[]{:S(2)}, u32[]{:S(2)}) collective-permute-start(bf16[8192,128]{1,0:T(8,128)(2,1)} %get-tuple-element.107.refs_1_), channel_id=1, source_target_pairs={{0,1},{1,0},{2,3},{3,2},{4,5},{5,4},{6,7},{7,6},{8,9},{9,8},{10,11... | collective-permute-start | bytes 6291464 | tf_op jit(solution)/shard_map/ppermute | solution.py:465
  136.9 35.8 %copy-start.20 = (f32[128]{0:T(128)S(1)}, f32[128]{0:T(128)}, u32[]{:S(2)}) copy-start(f32[128]{0:T(128)} %param.13) | copy-start | bytes 1540
  175.7 5.0 %collective-permute-start.31 = (bf16[256,256]{1,0:T(8,128)(2,1)S(1)}, bf16[256,256]{1,0:T(8,128)(2,1)S(1)}, u32[]{:S(2)}, u32[]{:S(2)}) collective-permute-start(bf16[256,256]{1,0:T(8,128)(2,1)S(1)} %get-tuple-element.101.refs_0_), channel_id=1, source_target_pairs={{0,192},{8,200},{16,208},{24,216},{32,224},{40,232},{48,240},{56,2... | collective-permute-start | bytes 393224 | tf_op jit(solution)/shard_map/ppermute | solution.py:456
  177.4 6.5 %collective-permute-start.30 = (bf16[256,256]{1,0:T(8,128)(2,1)S(1)}, bf16[256,256]{1,0:T(8,128)(2,1)S(1)}, u32[]{:S(2)}, u32[]{:S(2)}) collective-permute-start(bf16[256,256]{1,0:T(8,128)(2,1)S(1)} %get-tuple-element.101.refs_0_), channel_id=1, source_target_pairs={{0,128},{8,136},{16,144},{24,152},{32,160},{40,168},{48,176},{56,1... | collective-permute-start | bytes 393224 | tf_op jit(solution)/shard_map/ppermute | solution.py:456
  179.2 6.2 %collective-permute-start.29 = (bf16[256,256]{1,0:T(8,128)(2,1)S(1)}, bf16[256,256]{1,0:T(8,128)(2,1)S(1)}, u32[]{:S(2)}, u32[]{:S(2)}) collective-permute-start(bf16[256,256]{1,0:T(8,128)(2,1)S(1)} %get-tuple-element.101.refs_0_), channel_id=1, source_target_pairs={{0,64},{8,72},{16,80},{24,88},{32,96},{40,104},{48,112},{56,120},{... | collective-permute-start | bytes 393224 | tf_op jit(solution)/shard_map/ppermute | solution.py:456
  179.9 7.8 %collective-permute-start.32 = (bf16[256,256]{1,0:T(8,128)(2,1)S(1)}, bf16[256,256]{1,0:T(8,128)(2,1)S(1)}, u32[]{:S(2)}, u32[]{:S(2)}) collective-permute-start(bf16[256,256]{1,0:T(8,128)(2,1)S(1)} %get-tuple-element.104.own_ref), channel_id=1, source_target_pairs={{0,1},{1,0},{2,3},{3,2},{4,5},{5,4},{6,7},{7,6},{8,9},{9,8},{10,11... | collective-permute-start | bytes 393224 | tf_op jit(solution)/shard_map/ppermute | solution.py:465
  187.7 32.1 %all-to-all-start.2 = ((bf16[8,256,256]{2,1,0:T(8,128)(2,1)}), bf16[8,256,256]{2,1,0:T(8,128)(2,1)S(1)}, u32[]{:S(2)}, u32[]{:S(2)}) async-start(bf16[8,256,256]{2,1,0:T(8,128)(2,1)} %weight_terms.1), calls=%async_computation.2 | async-start | bytes 2097152 | tf_op jit(solution)/shard_map/all_to_all | solution.py:555
  197.8 16.1 %collective-permute-start.33 = (bf16[32,8192]{1,0:T(8,128)(2,1)S(1)}, bf16[32,8192]{1,0:T(8,128)(2,1)S(1)}, u32[]{:S(2)}, u32[]{:S(2)}) collective-permute-start(bf16[32,8192]{1,0:T(8,128)(2,1)S(1)} %get-tuple-element.111), channel_id=1, source_target_pairs={{0,2},{1,3},{2,4},{3,5},{4,6},{5,7},{6,0},{7,1},{8,10},{9,11},{10,... | collective-permute-start | bytes 1572872 | tf_op jit(solution)/shard_map/ppermute | solution.py:560
  199.4 20.4 %collective-permute-start.34 = (bf16[32,8192]{1,0:T(8,128)(2,1)S(1)}, bf16[32,8192]{1,0:T(8,128)(2,1)S(1)}, u32[]{:S(2)}, u32[]{:S(2)}) collective-permute-start(bf16[32,8192]{1,0:T(8,128)(2,1)S(1)} %get-tuple-element.112), channel_id=1, source_target_pairs={{0,4},{1,5},{2,6},{3,7},{4,0},{5,1},{6,2},{7,3},{8,12},{9,13},{10,... | collective-permute-start | bytes 1572872 | tf_op jit(solution)/shard_map/ppermute | solution.py:560
  202.1 17.7 %collective-permute-start.35 = (bf16[32,8192]{1,0:T(8,128)(2,1)S(1)}, bf16[32,8192]{1,0:T(8,128)(2,1)}, u32[]{:S(2)}, u32[]{:S(2)}) collective-permute-start(bf16[32,8192]{1,0:T(8,128)(2,1)S(1)} %get-tuple-element.113), channel_id=1, source_target_pairs={{0,6},{1,7},{2,0},{3,1},{4,2},{5,3},{6,4},{7,5},{8,14},{9,15},{10,... | collective-permute-start | bytes 1572872 | tf_op jit(solution)/shard_map/ppermute | solution.py:560
  (12 other events, 43.9 us)

commit v13 on v12

--- a/solution.py
+++ b/solution.py
@@ -449,6 +449,37 @@
     )(table, own, other, *hold(*weights))
 
 
+def finish_kernel(share_ref, *refs):
+    terms, (features_ref, key_ref, value_ref) = refs[:-3], refs[-3:]
+    head_dim = key_ref.shape[1]
+    total = share_ref[0].astype(F32)
+    for i in range(1, share_ref.shape[0]):
+        total = total + share_ref[i].astype(F32)
+    key_ref[...] = total[:, :head_dim]
+    value_ref[...] = total[:, head_dim:]
+    block = features_ref.shape[1] // NZ
+    for i in range(NZ):
+        here = slice(i * block, (i + 1) * block)
+        total = terms[0][:, here].astype(F32)
+        for term in terms[1:]:
+            total = total + term[:, here].astype(F32)
+        features_ref[:, here] = total.astype(BF16)
+
+
+def finish(shares, terms):
+    rows, cols = shares.shape[1:]
+    weights = pltpu.HBM((rows, cols // 2), F32)
+    return pl.pallas_call(
+        finish_kernel,
+        in_specs=[in_vmem()] * (1 + len(terms)),
+        out_specs=[in_vmem()] * 3,
+        out_shape=[pltpu.HBM(terms[0].shape, BF16), weights, weights],
+        compiler_params=limit(6),
+        cost_estimate=cost(0, 3),
+        name="finish",
+    )(shares, *terms)
+
+
 def shift_y(x, by):
     if by == 0:
         return x
@@ -555,20 +586,12 @@
     shares = lax.all_to_all(shares, "dp", 0, 0, tiled=True, axis_index_groups=Z_GROUPS)
 
     terms = list(feature_terms(table, grads, other_grads, weights, tensor_count))
-    for s in (2, 1, 3):
+    for s in range(1, tensor_count // 2):
         pairs = [(t, (t + 2 * s) % tensor_count) for t in range(tensor_count)]
         terms[s] = lax.ppermute(terms[s], "tensor", pairs)
-    shares, terms = lax.optimization_barrier((shares, terms))
-    grad_features = sum(term.astype(F32) for term in terms).astype(BF16)
+    grad_features, grad_k, grad_v = finish(shares, terms)
     grad_features = grad_features.reshape(images, tokens // tensor_count, width)
-    weight_grads = jnp.sum(shares.astype(F32), axis=0)
-    return (
-        attended,
-        grad_queries,
-        grad_features,
-        weight_grads[:, :head_dim],
-        weight_grads[:, head_dim:],
-    )
+    return attended, grad_queries, grad_features, grad_k, grad_v
 
 
 def solution(mesh):

time: 223 us -> 221 us (level)
  other arithmetic: 3.43 us -> 1.19 us
where the time goes in v13:
time: 221 us
  waiting for transfers between devices  106 us (48%)
  starting transfers between devices  66.3 us (30%)
  Pallas kernels  39.1 us (18%)
  local copies, waits for them, and re-layouts  6.95 us (3%)
    all_to_all x1, waiting for transfers between devices, local(): kv = lax.all_to_all(send, 'dp', 0, 0, tiled=True)  34.4 us
    all_to_all x1, waiting for transfers between devices, local(): parts = lax.all_to_all(parts, 'dp', 0, 0, tiled=True)  28.1 us
    ppermute x15, starting transfers between devices, shift_y(): return lax.ppermute(x, 'dp', pairs)  20.7 us
    ppermute x14, starting transfers between devices, shift_z(): return lax.ppermute(x, 'dp', pairs)  20.4 us
    ppermute x3, waiting for transfers between devices, local(): terms[s] = lax.ppermute(terms[s], 'tensor', pairs)  16.1 us
    ppermute x15, waiting for transfers between devices, shift_y(): return lax.ppermute(x, 'dp', pairs)  14.5 us
    ppermute x14, waiting for transfers between devices, shift_z(): return lax.ppermute(x, 'dp', pairs)  13 us
    all_to_all x1, starting transfers between devices, local(): kv = lax.all_to_all(send, 'dp', 0, 0, tiled=True)  8.9 us
  transfers between devices with their start and end apart: 39, of which 17 were waited for; matrix products, arithmetic and copies ran while one was open for 3% of the time, Pallas kernels for 13%

profile of v13, /device:TPU:32, one launch (start us, length us, event | category | flops | bytes accessed | tf_op | source)
XLA Modules:
  0.0 220.9 jit_solution(2692589457831808488)
XLA Ops:
  0.6 2.0 collective-permute-start
  2.7 3.2 %collective-permute-start.5 = (bf16[256,128]{1,0:T(8,128)(2,1)}, bf16[256,128]{1,0:T(8,128)(2,1)S(1)}, u32[]{:S(2)}, u32[]{:S(2)}) collective-permute-start(bf16[256,128]{1,0:T(8,128)(2,1)} %param.12), channel_id=1, source_target_pairs={{0,128},{8,136},{16,144},{24,152},{32,160},{40,168},{48,176},{56,1... | collective-permute-start | bytes 196616 | tf_op jit(solution)/shard_map/ppermute | solution.py:487
  5.9 1.1 collective-permute-start.4
  10.6 2.1 collective-permute-done.6
  12.7 4.1 %collective-permute-start.8 = (bf16[1024,128]{1,0:T(8,128)(2,1)S(1)}, bf16[1024,128]{1,0:T(8,128)(2,1)S(1)}, u32[]{:S(2)}, u32[]{:S(2)}) collective-permute-start(bf16[1024,128]{1,0:T(8,128)(2,1)S(1)} %constant_dynamic-update-slice_fusion.refs_8_), channel_id=1, source_target_pairs={{0,56},{8,0},{16,8},{24,16},{32,24},{40,32},{48,40},{56,48},{64,12... | collective-permute-start | bytes 786440 | tf_op jit(solution)/shard_map/ppermute | solution.py:492
  16.9 1.0 collective-permute-start.2
  17.9 1.1 collective-permute-start.3
  19.1 4.9 %collective-permute-done.2 = bf16[256,128]{1,0:T(8,128)(2,1)S(1)} collective-permute-done((bf16[256,128]{1,0:T(8,128)(2,1)S(1)}, bf16[256,128]{1,0:T(8,128)(2,1)S(1)}, u32[]{:S(2)}, u32[]{:S(2)}) %collective-permute-start.2) | collective-permute-done | bytes 65568 | tf_op jit(solution)/shard_map/ppermute | solution.py:492
  24.0 1.4 collective-permute-start.12
  25.5 3.2 %collective-permute-start.9 = (bf16[1024,128]{1,0:T(8,128)(2,1)S(1)}, bf16[1024,128]{1,0:T(8,128)(2,1)S(1)}, u32[]{:S(2)}, u32[]{:S(2)}) collective-permute-start(bf16[1024,128]{1,0:T(8,128)(2,1)S(1)} %constant_dynamic-update-slice_fusion.4.refs_0_), channel_id=1, source_target_pairs={{0,192},{8,200},{16,208},{24,216},{32,224},{40,232},{48,240},{56,2... | collective-permute-start | bytes 786440 | tf_op jit(solution)/shard_map/ppermute | solution.py:487
  28.7 1.7 collective-permute-start.13
  30.4 1.4 collective-permute-start.18
  31.9 1.9 collective-permute-start.19
  34.1 2.0 collective-permute-start.14
  36.2 4.1 %collective-permute-done.14 = bf16[256,128]{1,0:T(8,128)(2,1)S(1)} collective-permute-done((bf16[256,128]{1,0:T(8,128)(2,1)S(1)}, bf16[256,128]{1,0:T(8,128)(2,1)S(1)}, u32[]{:S(2)}, u32[]{:S(2)}) %collective-permute-start.14) | collective-permute-done | bytes 65568 | tf_op jit(solution)/shard_map/ppermute | solution.py:492
  40.4 1.1 collective-permute-start.20
  41.6 3.2 %collective-permute-start.15 = (bf16[1024,128]{1,0:T(8,128)(2,1)S(1)}, bf16[1024,128]{1,0:T(8,128)(2,1)S(1)}, u32[]{:S(2)}, u32[]{:S(2)}) collective-permute-start(bf16[1024,128]{1,0:T(8,128)(2,1)S(1)} %constant_dynamic-update-slice_fusion.8.refs_4_), channel_id=1, source_target_pairs={{0,192},{8,200},{16,208},{24,216},{32,224},{40,232},{48,240},{56,2... | collective-permute-start | bytes 786440 | tf_op jit(solution)/shard_map/ppermute | solution.py:487
  44.9 2.5 %collective-permute-start.21 = (bf16[1024,128]{1,0:T(8,128)(2,1)S(1)}, bf16[1024,128]{1,0:T(8,128)(2,1)}, u32[]{:S(2)}, u32[]{:S(2)}) collective-permute-start(bf16[1024,128]{1,0:T(8,128)(2,1)S(1)} %collective-permute-done.19.refs_12_), channel_id=1, source_target_pairs={{0,56},{8,0},{16,8},{24,16},{32,24},{40,32},{48,40},{56,48},{64,12... | collective-permute-start | bytes 786440 | tf_op jit(solution)/shard_map/ppermute | solution.py:492
  47.4 1.7 collective-permute-done.16.refs_6_
  49.4 1.7 collective-permute-done.20.refs_13_
  51.9 5.0 %collective-permute-done.17.refs_7_ = bf16[1024,128]{1,0:T(8,128)(2,1)} collective-permute-done((bf16[1024,128]{1,0:T(8,128)(2,1)S(1)}, bf16[1024,128]{1,0:T(8,128)(2,1)}, u32[]{:S(2)}, u32[]{:S(2)}) %collective-permute-start.17) | collective-permute-done | bytes 262176 | tf_op jit(solution)/shard_map/ppermute | solution.py:487
  56.8 1.6 collective-permute-done.22.refs_15_
  59.1 6.0 %project.1 = (bf16[32,128,256]{2,1,0:T(8,128)(2,1)}, f32[256,128]{1,0:T(8,128)}) custom-call(s32[5,32]{1,0:T(8,128)S(1)} %stack.41.table_ref, bf16[256,8192]{1,0:T(8,128)(2,1)} %bitcast.24, bf16[1024,128]{1,0:T(8,128)(2,1)S(1)} %constant_dynamic-update-slice_fusion.4.refs_0_, bf16[1024,128]{1,0:T(8,128)(2,1)S(1)} %collective-permute-done.9.refs_1_, ...), custom_call_target="tpu_custom_call" | custom-call | flops 1073741824 | bytes 10485760 | tf_op jit(solution)/shard_map/project/pallas_call | solution.py:92
  65.2 8.9 %all-to-all-start = ((bf16[32,128,256]{2,1,0:T(8,128)(2,1)}), bf16[32,128,256]{2,1,0:T(8,128)(2,1)S(1)}, u32[]{:S(2)}, u32[]{:S(2)}) async-start(bf16[32,128,256]{2,1,0:T(8,128)(2,1)} %get-tuple-element.64), calls=%async_computation | async-start | bytes 4194304 | tf_op jit(solution)/shard_map/all_to_all | solution.py:555
  74.1 2.9 %dynamic-slice_bitcast_fusion = (bf16[128,2048]{1,0:T(8,128)(2,1)}, bf16[128,2048]{1,0:T(8,128)(2,1)}, bf16[128,2048]{1,0:T(8,128)(2,1)}, bf16[128,2048]{1,0:T(8,128)(2,1)}) fusion(bf16[2,128,8192]{2,1,0:T(8,128)(2,1)} %param.10, s32[]{:T(128)S(6)} %select_n.86, s32[]{:T(128)S(6)} %select_n.94, s32[]{:T(128)S(6)} %select_n.92, s32[]{:T(128)S(6)} %select_n.90, ...), kind=kLoop, calls=%fused_computation | loop fusion | bytes 4194324 | tf_op jit(solution)/shard_map/squeeze | solution.py:561
  77.0 2.7 %collective-permute-start.25 = (bf16[128,2048]{1,0:T(8,128)(2,1)}, bf16[128,2048]{1,0:T(8,128)(2,1)}, u32[]{:S(2)}, u32[]{:S(2)}) collective-permute-start(bf16[128,2048]{1,0:T(8,128)(2,1)} %get-tuple-element.119), channel_id=1, source_target_pairs={{0,192},{8,200},{16,208},{24,216},{32,224},{40,232},{48,240},{56,2... | collective-permute-start | bytes 1572872 | tf_op jit(solution)/shard_map/ppermute | solution.py:487
  81.4 34.4 %all-to-all-done.kv_ref = bf16[32,128,256]{2,1,0:T(8,128)(2,1)S(1)} async-done(((bf16[32,128,256]{2,1,0:T(8,128)(2,1)}), bf16[32,128,256]{2,1,0:T(8,128)(2,1)S(1)}, u32[]{:S(2)}, u32[]{:S(2)}) %all-to-all-start) | async-done | bytes 2097184 | tf_op jit(solution)/shard_map/all_to_all | solution.py:555
  115.9 8.0 %attend.1 = (bf16[32,128,256]{2,1,0:T(8,128)(2,1)}, bf16[32,128,128]{2,1,0:T(8,128)(2,1)}, bf16[32,128,128]{2,1,0:T(8,128)(2,1)}) custom-call(s32[5,32]{1,0:T(8,128)S(1)} %stack.41.table_ref, bf16[512,1024]{1,0:T(8,128)(2,1)} %q_hbm.1, bf16[512,1024]{1,0:T(8,128)(2,1)} %ct_hbm.1, bf16[32,128,256]{2,1,0:T(8,128)(2,1)S(1)} %all-to-all-done.kv_ref), custom_call_target="tpu_custom_call" | custom-call | flops 536870912 | bytes 8388608 | tf_op jit(solution)/shard_map/attend/pallas_call | solution.py:213
  123.9 5.7 %all-to-all-start.1 = ((bf16[32,128,256]{2,1,0:T(8,128)(2,1)}), bf16[32,128,256]{2,1,0:T(8,128)(2,1)}, u32[]{:S(2)}, u32[]{:S(2)}) async-start(bf16[32,128,256]{2,1,0:T(8,128)(2,1)} %get-tuple-element.68), calls=%async_computation.1 | async-start | bytes 4194304 | tf_op jit(solution)/shard_map/all_to_all | solution.py:571
  129.7 2.2 %transpose_pieces.1.own_ref = bf16[2048,512]{1,0:T(8,128)(2,1)S(1)} custom-call(bf16[128,2048]{1,0:T(8,128)(2,1)} %get-tuple-element.69.refs_0_, bf16[128,2048]{1,0:T(8,128)(2,1)} %collective-permute-done.23.refs_1_, bf16[128,2048]{1,0:T(8,128)(2,1)} %collective-permute-done.24.refs_2_, bf16[128,2048]{1,0:T(8,128)(2,1)} %collective-permute-done.25.refs_3_), custom_call_target="tpu_custom_call" | custom-call | bytes 4194304 | tf_op jit(solution)/shard_map/transpose_pieces/pallas_call | solution.py:326
  132.3 4.1 %assemble.1 = (bf16[8192,128]{1,0:T(8,128)(2,1)}, bf16[8192,128]{1,0:T(8,128)(2,1)}) custom-call(s32[5,32]{1,0:T(8,128)S(1)} %stack.41.table_ref, bf16[1024,128]{1,0:T(8,128)(2,1)S(1)} %constant_dynamic-update-slice_fusion.4.refs_0_, bf16[1024,128]{1,0:T(8,128)(2,1)S(1)} %copy-done.6, bf16[1024,128]{1,0:T(8,128)(2,1)S(1)} %copy-done.4, ...), custom_call_target="tpu_custom_call" | custom-call | bytes 1048576 | tf_op jit(solution)/shard_map/assemble/pallas_call | solution.py:371
  136.9 6.2 %apply.1 = (bf16[512,1024]{1,0:T(8,128)(2,1)}, bf16[512,1024]{1,0:T(8,128)(2,1)}) custom-call(s32[5,32]{1,0:T(8,128)S(1)} %stack.41.table_ref, bf16[32,128,256]{2,1,0:T(8,128)(2,1)} %copy-done, bf16[32,128,128]{2,1,0:T(8,128)(2,1)} %get-tuple-element.73.probs_ref, bf16[32,128,128]{2,1,0:T(8,128)(2,1)} %get-tuple-element.74.ds_ref), custom_call_target="tpu_custom_call" | custom-call | flops 268435456 | bytes 6291456 | tf_op jit(solution)/shard_map/apply/pallas_call | solution.py:255
  143.1 1.4 copy-done.1
  144.5 28.1 %all-to-all-done.1.part_ref = bf16[32,128,256]{2,1,0:T(8,128)(2,1)} async-done(((bf16[32,128,256]{2,1,0:T(8,128)(2,1)}), bf16[32,128,256]{2,1,0:T(8,128)(2,1)}, u32[]{:S(2)}, u32[]{:S(2)}) %all-to-all-start.1) | async-done | bytes 2097184 | tf_op jit(solution)/shard_map/all_to_all | solution.py:571
  172.6 3.0 %owner_grads.1 = (bf16[256,256]{1,0:T(8,128)(2,1)S(1)}, bf16[256,256]{1,0:T(8,128)(2,1)S(1)}) custom-call(s32[5,32]{1,0:T(8,128)S(1)} %stack.41.table_ref, bf16[32,128,256]{2,1,0:T(8,128)(2,1)} %all-to-all-done.1.part_ref, f32[256,128]{1,0:T(8,128)} %get-tuple-element.66.raw_ref, f32[1,128]{1,0:T(1,128)S(1)} %bitcast.23), custom_call_target="tpu_custom_call" | custom-call | bytes 3145728 | tf_op jit(solution)/shard_map/owner_grads/pallas_call | solution.py:301
  175.6 1.7 collective-permute-start.31
  177.3 1.9 collective-permute-start.30
  180.7 3.2 %collective-permute-done.30.refs_2_ = bf16[256,256]{1,0:T(8,128)(2,1)S(1)} collective-permute-done((bf16[256,256]{1,0:T(8,128)(2,1)S(1)}, bf16[256,256]{1,0:T(8,128)(2,1)S(1)}, u32[]{:S(2)}, u32[]{:S(2)}) %collective-permute-start.30) | collective-permute-done | bytes 131104 | tf_op jit(solution)/shard_map/ppermute | solution.py:487
  183.8 1.6 collective-permute-done.29.refs_1_
  185.4 2.3 %weight_terms.1 = bf16[8,256,256]{2,1,0:T(8,128)(2,1)} custom-call(bf16[2048,512]{1,0:T(8,128)(2,1)S(1)} %transpose_pieces.1.own_ref, bf16[2048,512]{1,0:T(8,128)(2,1)S(1)} %copy-done.2, bf16[256,256]{1,0:T(8,128)(2,1)S(1)} %get-tuple-element.99.refs_0_, bf16[256,256]{1,0:T(8,128)(2,1)S(1)} %collective-permute-done.29.refs_1_, ...), custom_call_target="tpu_custom_call" | custom-call | flops 1073741824 | bytes 6291456 | tf_op jit(solution)/shard_map/weight_terms/pallas_call | solution.py:352
  187.7 4.1 %all-to-all-start.2 = ((bf16[8,256,256]{2,1,0:T(8,128)(2,1)}), bf16[8,256,256]{2,1,0:T(8,128)(2,1)S(1)}, u32[]{:S(2)}, u32[]{:S(2)}) async-start(bf16[8,256,256]{2,1,0:T(8,128)(2,1)} %weight_terms.1), calls=%async_computation.2 | async-start | bytes 2097152 | tf_op jit(solution)/shard_map/all_to_all | solution.py:586
  191.8 6.2 %feature_terms.1 = (bf16[32,8192]{1,0:T(8,128)(2,1)S(1)}, bf16[32,8192]{1,0:T(8,128)(2,1)S(1)}, bf16[32,8192]{1,0:T(8,128)(2,1)S(1)}, bf16[32,8192]{1,0:T(8,128)(2,1)S(1)}) custom-call(s32[5,32]{1,0:T(8,128)S(1)} %stack.41.table_ref, bf16[256,256]{1,0:T(8,128)(2,1)S(1)} %get-tuple-element.102.own_ref, ...), custom_call_target="tpu_custom_call" | custom-call | flops 2147483648 | bytes 10485760 | tf_op jit(solution)/shard_map/feature_terms/pallas_call | solution.py:432
  197.9 1.6 collective-permute-start.33
  199.5 2.7 %collective-permute-start.34 = (bf16[32,8192]{1,0:T(8,128)(2,1)S(1)}, bf16[32,8192]{1,0:T(8,128)(2,1)S(1)}, u32[]{:S(2)}, u32[]{:S(2)}) collective-permute-start(bf16[32,8192]{1,0:T(8,128)(2,1)S(1)} %get-tuple-element.110), channel_id=1, source_target_pairs={{0,4},{1,5},{2,6},{3,7},{4,0},{5,1},{6,2},{7,3},{8,12},{9,13},{10,... | collective-permute-start | bytes 1572872 | tf_op jit(solution)/shard_map/ppermute | solution.py:591
  202.2 1.4 collective-permute-start.35
  203.6 10.4 %collective-permute-done.33.refs_1_ = bf16[32,8192]{1,0:T(8,128)(2,1)S(1)} collective-permute-done((bf16[32,8192]{1,0:T(8,128)(2,1)S(1)}, bf16[32,8192]{1,0:T(8,128)(2,1)S(1)}, u32[]{:S(2)}, u32[]{:S(2)}) %collective-permute-start.33) | collective-permute-done | bytes 524320 | tf_op jit(solution)/shard_map/ppermute | solution.py:591
  214.0 5.7 %collective-permute-done.34.refs_2_ = bf16[32,8192]{1,0:T(8,128)(2,1)S(1)} collective-permute-done((bf16[32,8192]{1,0:T(8,128)(2,1)S(1)}, bf16[32,8192]{1,0:T(8,128)(2,1)S(1)}, u32[]{:S(2)}, u32[]{:S(2)}) %collective-permute-start.34) | collective-permute-done | bytes 524320 | tf_op jit(solution)/shard_map/ppermute | solution.py:591
  219.7 1.2 finish.1
  (105 shorter events, 10.3 us)
Async XLA Ops:
  0.6 16.2 %collective-permute-start = (bf16[256,128]{1,0:T(8,128)(2,1)}, bf16[256,128]{1,0:T(8,128)(2,1)S(1)}, u32[]{:S(2)}, u32[]{:S(2)}) collective-permute-start(bf16[256,128]{1,0:T(8,128)(2,1)} %param.11), channel_id=1, source_target_pairs={{0,8},{8,16},{16,24},{24,32},{32,40},{40,48},{48,56},{56,0},{64,72... | collective-permute-start | bytes 196616 | tf_op jit(solution)/shard_map/ppermute | solution.py:492
  2.6 15.3 %collective-permute-start.1 = (bf16[256,128]{1,0:T(8,128)(2,1)}, bf16[256,128]{1,0:T(8,128)(2,1)S(1)}, u32[]{:S(2)}, u32[]{:S(2)}) collective-permute-start(bf16[256,128]{1,0:T(8,128)(2,1)} %param.11), channel_id=1, source_target_pairs={{0,56},{8,0},{16,8},{24,16},{32,24},{40,32},{48,40},{56,48},{64,12... | collective-permute-start | bytes 196616 | tf_op jit(solution)/shard_map/ppermute | solution.py:492
  2.7 7.8 %collective-permute-start.5 = (bf16[256,128]{1,0:T(8,128)(2,1)}, bf16[256,128]{1,0:T(8,128)(2,1)S(1)}, u32[]{:S(2)}, u32[]{:S(2)}) collective-permute-start(bf16[256,128]{1,0:T(8,128)(2,1)} %param.12), channel_id=1, source_target_pairs={{0,128},{8,136},{16,144},{24,152},{32,160},{40,168},{48,176},{56,1... | collective-permute-start | bytes 196616 | tf_op jit(solution)/shard_map/ppermute | solution.py:487
  5.9 4.6 %collective-permute-start.4 = (bf16[256,128]{1,0:T(8,128)(2,1)}, bf16[256,128]{1,0:T(8,128)(2,1)S(1)}, u32[]{:S(2)}, u32[]{:S(2)}) collective-permute-start(bf16[256,128]{1,0:T(8,128)(2,1)} %param.12), channel_id=1, source_target_pairs={{0,192},{8,200},{16,208},{24,216},{32,224},{40,232},{48,240},{56,2... | collective-permute-start | bytes 196616 | tf_op jit(solution)/shard_map/ppermute | solution.py:487
  7.0 5.7 %collective-permute-start.6 = (bf16[256,128]{1,0:T(8,128)(2,1)}, bf16[256,128]{1,0:T(8,128)(2,1)S(1)}, u32[]{:S(2)}, u32[]{:S(2)}) collective-permute-start(bf16[256,128]{1,0:T(8,128)(2,1)} %param.12), channel_id=1, source_target_pairs={{0,64},{8,72},{16,80},{24,88},{32,96},{40,104},{48,112},{56,120},{... | collective-permute-start | bytes 196616 | tf_op jit(solution)/shard_map/ppermute | solution.py:487
  12.7 11.3 %collective-permute-start.8 = (bf16[1024,128]{1,0:T(8,128)(2,1)S(1)}, bf16[1024,128]{1,0:T(8,128)(2,1)S(1)}, u32[]{:S(2)}, u32[]{:S(2)}) collective-permute-start(bf16[1024,128]{1,0:T(8,128)(2,1)S(1)} %constant_dynamic-update-slice_fusion.refs_8_), channel_id=1, source_target_pairs={{0,56},{8,0},{16,8},{24,16},{32,24},{40,32},{48,40},{56,48},{64,12... | collective-permute-start | bytes 786440 | tf_op jit(solution)/shard_map/ppermute | solution.py:492
  16.8 7.2 %collective-permute-start.7 = (bf16[1024,128]{1,0:T(8,128)(2,1)S(1)}, bf16[1024,128]{1,0:T(8,128)(2,1)S(1)}, u32[]{:S(2)}, u32[]{:S(2)}) collective-permute-start(bf16[1024,128]{1,0:T(8,128)(2,1)S(1)} %constant_dynamic-update-slice_fusion.refs_8_), channel_id=1, source_target_pairs={{0,8},{8,16},{16,24},{24,32},{32,40},{40,48},{48,56},{56,0},{64,72... | collective-permute-start | bytes 786440 | tf_op jit(solution)/shard_map/ppermute | solution.py:492
  16.9 7.1 %collective-permute-start.2 = (bf16[256,128]{1,0:T(8,128)(2,1)S(1)}, bf16[256,128]{1,0:T(8,128)(2,1)S(1)}, u32[]{:S(2)}, u32[]{:S(2)}) collective-permute-start(bf16[256,128]{1,0:T(8,128)(2,1)S(1)} %collective-permute-done), channel_id=1, source_target_pairs={{0,8},{8,16},{16,24},{24,32},{32,40},{40,48},{48,56},{56,0},{64,72... | collective-permute-start | bytes 196616 | tf_op jit(solution)/shard_map/ppermute | solution.py:492
  17.9 6.1 %collective-permute-start.3 = (bf16[256,128]{1,0:T(8,128)(2,1)S(1)}, bf16[256,128]{1,0:T(8,128)(2,1)S(1)}, u32[]{:S(2)}, u32[]{:S(2)}) collective-permute-start(bf16[256,128]{1,0:T(8,128)(2,1)S(1)} %collective-permute-done.1), channel_id=1, source_target_pairs={{0,56},{8,0},{16,8},{24,16},{32,24},{40,32},{48,40},{56,48},{64,12... | collective-permute-start | bytes 196616 | tf_op jit(solution)/shard_map/ppermute | solution.py:492
  24.0 7.9 %collective-permute-start.12 = (bf16[256,128]{1,0:T(8,128)(2,1)S(1)}, bf16[256,128]{1,0:T(8,128)(2,1)S(1)}, u32[]{:S(2)}, u32[]{:S(2)}) collective-permute-start(bf16[256,128]{1,0:T(8,128)(2,1)S(1)} %collective-permute-done.2), channel_id=1, source_target_pairs={{0,8},{8,16},{16,24},{24,32},{32,40},{40,48},{48,56},{56,0},{64,72... | collective-permute-start | bytes 196616 | tf_op jit(solution)/shard_map/ppermute | solution.py:492
  25.4 16.2 %collective-permute-start.10 = (bf16[1024,128]{1,0:T(8,128)(2,1)S(1)}, bf16[1024,128]{1,0:T(8,128)(2,1)S(1)}, u32[]{:S(2)}, u32[]{:S(2)}) collective-permute-start(bf16[1024,128]{1,0:T(8,128)(2,1)S(1)} %constant_dynamic-update-slice_fusion.4.refs_0_), channel_id=1, source_target_pairs={{0,64},{8,72},{16,80},{24,88},{32,96},{40,104},{48,112},{56,120},{... | collective-permute-start | bytes 786440 | tf_op jit(solution)/shard_map/ppermute | solution.py:487
  25.5 19.3 %collective-permute-start.9 = (bf16[1024,128]{1,0:T(8,128)(2,1)S(1)}, bf16[1024,128]{1,0:T(8,128)(2,1)S(1)}, u32[]{:S(2)}, u32[]{:S(2)}) collective-permute-start(bf16[1024,128]{1,0:T(8,128)(2,1)S(1)} %constant_dynamic-update-slice_fusion.4.refs_0_), channel_id=1, source_target_pairs={{0,192},{8,200},{16,208},{24,216},{32,224},{40,232},{48,240},{56,2... | collective-permute-start | bytes 786440 | tf_op jit(solution)/shard_map/ppermute | solution.py:487
  28.7 5.4 %collective-permute-start.13 = (bf16[256,128]{1,0:T(8,128)(2,1)S(1)}, bf16[256,128]{1,0:T(8,128)(2,1)S(1)}, u32[]{:S(2)}, u32[]{:S(2)}) collective-permute-start(bf16[256,128]{1,0:T(8,128)(2,1)S(1)} %collective-permute-done.3), channel_id=1, source_target_pairs={{0,56},{8,0},{16,8},{24,16},{32,24},{40,32},{48,40},{56,48},{64,12... | collective-permute-start | bytes 196616 | tf_op jit(solution)/shard_map/ppermute | solution.py:492
  30.4 9.9 %collective-permute-start.18 = (bf16[1024,128]{1,0:T(8,128)(2,1)S(1)}, bf16[1024,128]{1,0:T(8,128)(2,1)S(1)}, u32[]{:S(2)}, u32[]{:S(2)}) collective-permute-start(bf16[1024,128]{1,0:T(8,128)(2,1)S(1)} %collective-permute-done.7.refs_9_), channel_id=1, source_target_pairs={{0,8},{8,16},{16,24},{24,32},{32,40},{40,48},{48,56},{56,0},{64,72... | collective-permute-start | bytes 786440 | tf_op jit(solution)/shard_map/ppermute | solution.py:492
  31.9 13.0 %collective-permute-start.19 = (bf16[1024,128]{1,0:T(8,128)(2,1)S(1)}, bf16[1024,128]{1,0:T(8,128)(2,1)S(1)}, u32[]{:S(2)}, u32[]{:S(2)}) collective-permute-start(bf16[1024,128]{1,0:T(8,128)(2,1)S(1)} %collective-permute-done.8.refs_10_), channel_id=1, source_target_pairs={{0,56},{8,0},{16,8},{24,16},{32,24},{40,32},{48,40},{56,48},{64,12... | collective-permute-start | bytes 786440 | tf_op jit(solution)/shard_map/ppermute | solution.py:492
  34.1 6.1 %collective-permute-start.14 = (bf16[256,128]{1,0:T(8,128)(2,1)S(1)}, bf16[256,128]{1,0:T(8,128)(2,1)S(1)}, u32[]{:S(2)}, u32[]{:S(2)}) collective-permute-start(bf16[256,128]{1,0:T(8,128)(2,1)S(1)} %collective-permute-done.12), channel_id=1, source_target_pairs={{0,8},{8,16},{16,24},{24,32},{32,40},{40,48},{48,56},{56,0},{64,72... | collective-permute-start | bytes 196616 | tf_op jit(solution)/shard_map/ppermute | solution.py:492
  40.3 8.9 %collective-permute-start.16 = (bf16[1024,128]{1,0:T(8,128)(2,1)S(1)}, bf16[1024,128]{1,0:T(8,128)(2,1)S(1)}, u32[]{:S(2)}, u32[]{:S(2)}) collective-permute-start(bf16[1024,128]{1,0:T(8,128)(2,1)S(1)} %constant_dynamic-update-slice_fusion.8.refs_4_), channel_id=1, source_target_pairs={{0,64},{8,72},{16,80},{24,88},{32,96},{40,104},{48,112},{56,120},{... | collective-permute-start | bytes 786440 | tf_op jit(solution)/shard_map/ppermute | solution.py:487
  40.4 24.7 %copy-start.7 = (bf16[1024,128]{1,0:T(8,128)(2,1)}, bf16[1024,128]{1,0:T(8,128)(2,1)S(1)}, u32[]{:S(2)}) copy-start(bf16[1024,128]{1,0:T(8,128)(2,1)S(1)} %collective-permute-done.18.refs_11_) | copy-start | bytes 786436
  40.4 10.7 %collective-permute-start.20 = (bf16[1024,128]{1,0:T(8,128)(2,1)S(1)}, bf16[1024,128]{1,0:T(8,128)(2,1)S(1)}, u32[]{:S(2)}, u32[]{:S(2)}) collective-permute-start(bf16[1024,128]{1,0:T(8,128)(2,1)S(1)} %collective-permute-done.18.refs_11_), channel_id=1, source_target_pairs={{0,8},{8,16},{16,24},{24,32},{32,40},{40,48},{48,56},{56,0},{64,72... | collective-permute-start | bytes 786440 | tf_op jit(solution)/shard_map/ppermute | solution.py:492
  41.6 23.5 %copy-start.3 = (bf16[1024,128]{1,0:T(8,128)(2,1)}, bf16[1024,128]{1,0:T(8,128)(2,1)S(1)}, u32[]{:S(2)}) copy-start(bf16[1024,128]{1,0:T(8,128)(2,1)S(1)} %collective-permute-done.10.refs_2_) | copy-start | bytes 786436
  41.6 9.7 %collective-permute-start.15 = (bf16[1024,128]{1,0:T(8,128)(2,1)S(1)}, bf16[1024,128]{1,0:T(8,128)(2,1)S(1)}, u32[]{:S(2)}, u32[]{:S(2)}) collective-permute-start(bf16[1024,128]{1,0:T(8,128)(2,1)S(1)} %constant_dynamic-update-slice_fusion.8.refs_4_), channel_id=1, source_target_pairs={{0,192},{8,200},{16,208},{24,216},{32,224},{40,232},{48,240},{56,2... | collective-permute-start | bytes 786440 | tf_op jit(solution)/shard_map/ppermute | solution.py:487
  44.8 20.3 %copy-start.5 = (bf16[1024,128]{1,0:T(8,128)(2,1)}, bf16[1024,128]{1,0:T(8,128)(2,1)S(1)}, u32[]{:S(2)}) copy-start(bf16[1024,128]{1,0:T(8,128)(2,1)S(1)} %collective-permute-done.9.refs_1_) | copy-start | bytes 786436
  44.8 6.7 %collective-permute-start.11 = (bf16[1024,128]{1,0:T(8,128)(2,1)S(1)}, bf16[1024,128]{1,0:T(8,128)(2,1)S(1)}, u32[]{:S(2)}, u32[]{:S(2)}) collective-permute-start(bf16[1024,128]{1,0:T(8,128)(2,1)S(1)} %collective-permute-done.9.refs_1_), channel_id=1, source_target_pairs={{0,192},{8,200},{16,208},{24,216},{32,224},{40,232},{48,240},{56,2... | collective-permute-start | bytes 786440 | tf_op jit(solution)/shard_map/ppermute | solution.py:487
  44.9 20.2 %copy-start.9 = (bf16[1024,128]{1,0:T(8,128)(2,1)}, bf16[1024,128]{1,0:T(8,128)(2,1)S(1)}, u32[]{:S(2)}) copy-start(bf16[1024,128]{1,0:T(8,128)(2,1)S(1)} %collective-permute-done.19.refs_12_) | copy-start | bytes 786436
  44.9 6.9 %collective-permute-start.21 = (bf16[1024,128]{1,0:T(8,128)(2,1)S(1)}, bf16[1024,128]{1,0:T(8,128)(2,1)}, u32[]{:S(2)}, u32[]{:S(2)}) collective-permute-start(bf16[1024,128]{1,0:T(8,128)(2,1)S(1)} %collective-permute-done.19.refs_12_), channel_id=1, source_target_pairs={{0,56},{8,0},{16,8},{24,16},{32,24},{40,32},{48,40},{56,48},{64,12... | collective-permute-start | bytes 786440 | tf_op jit(solution)/shard_map/ppermute | solution.py:492
  49.1 16.0 %copy-start.11 = (bf16[1024,128]{1,0:T(8,128)(2,1)}, bf16[1024,128]{1,0:T(8,128)(2,1)S(1)}, u32[]{:S(2)}) copy-start(bf16[1024,128]{1,0:T(8,128)(2,1)S(1)} %collective-permute-done.16.refs_6_) | copy-start | bytes 786436
  49.1 7.7 %collective-permute-start.17 = (bf16[1024,128]{1,0:T(8,128)(2,1)S(1)}, bf16[1024,128]{1,0:T(8,128)(2,1)}, u32[]{:S(2)}, u32[]{:S(2)}) collective-permute-start(bf16[1024,128]{1,0:T(8,128)(2,1)S(1)} %collective-permute-done.16.refs_6_), channel_id=1, source_target_pairs={{0,64},{8,72},{16,80},{24,88},{32,96},{40,104},{48,112},{56,120},{... | collective-permute-start | bytes 786440 | tf_op jit(solution)/shard_map/ppermute | solution.py:487
  51.1 14.1 %copy-start.13 = (bf16[1024,128]{1,0:T(8,128)(2,1)}, bf16[1024,128]{1,0:T(8,128)(2,1)S(1)}, u32[]{:S(2)}) copy-start(bf16[1024,128]{1,0:T(8,128)(2,1)S(1)} %collective-permute-done.20.refs_13_) | copy-start | bytes 786436
  51.1 7.4 %collective-permute-start.22 = (bf16[1024,128]{1,0:T(8,128)(2,1)S(1)}, bf16[1024,128]{1,0:T(8,128)(2,1)}, u32[]{:S(2)}, u32[]{:S(2)}) collective-permute-start(bf16[1024,128]{1,0:T(8,128)(2,1)S(1)} %collective-permute-done.20.refs_13_), channel_id=1, source_target_pairs={{0,8},{8,16},{16,24},{24,32},{32,40},{40,48},{48,56},{56,0},{64,72... | collective-permute-start | bytes 786440 | tf_op jit(solution)/shard_map/ppermute | solution.py:492
  51.3 13.8 %copy-start.15 = (bf16[1024,128]{1,0:T(8,128)(2,1)}, bf16[1024,128]{1,0:T(8,128)(2,1)S(1)}, u32[]{:S(2)}) copy-start(bf16[1024,128]{1,0:T(8,128)(2,1)S(1)} %collective-permute-done.15.refs_5_) | copy-start | bytes 786436
  51.5 13.6 %copy-start.17 = (bf16[1024,128]{1,0:T(8,128)(2,1)}, bf16[1024,128]{1,0:T(8,128)(2,1)S(1)}, u32[]{:S(2)}) copy-start(bf16[1024,128]{1,0:T(8,128)(2,1)S(1)} %collective-permute-done.11.refs_3_) | copy-start | bytes 786436
  65.2 50.7 %all-to-all-start = ((bf16[32,128,256]{2,1,0:T(8,128)(2,1)}), bf16[32,128,256]{2,1,0:T(8,128)(2,1)S(1)}, u32[]{:S(2)}, u32[]{:S(2)}) async-start(bf16[32,128,256]{2,1,0:T(8,128)(2,1)} %get-tuple-element.64), calls=%async_computation | async-start | bytes 4194304 | tf_op jit(solution)/shard_map/all_to_all | solution.py:555
  77.0 46.8 %collective-permute-start.25 = (bf16[128,2048]{1,0:T(8,128)(2,1)}, bf16[128,2048]{1,0:T(8,128)(2,1)}, u32[]{:S(2)}, u32[]{:S(2)}) collective-permute-start(bf16[128,2048]{1,0:T(8,128)(2,1)} %get-tuple-element.119), channel_id=1, source_target_pairs={{0,192},{8,200},{16,208},{24,216},{32,224},{40,232},{48,240},{56,2... | collective-permute-start | bytes 1572872 | tf_op jit(solution)/shard_map/ppermute | solution.py:487
  79.8 44.1 %collective-permute-start.24 = (bf16[128,2048]{1,0:T(8,128)(2,1)}, bf16[128,2048]{1,0:T(8,128)(2,1)}, u32[]{:S(2)}, u32[]{:S(2)}) collective-permute-start(bf16[128,2048]{1,0:T(8,128)(2,1)} %get-tuple-element.120), channel_id=1, source_target_pairs={{0,128},{8,136},{16,144},{24,152},{32,160},{40,168},{48,176},{56,1... | collective-permute-start | bytes 1572872 | tf_op jit(solution)/shard_map/ppermute | solution.py:487
  80.6 43.3 %collective-permute-start.23 = (bf16[128,2048]{1,0:T(8,128)(2,1)}, bf16[128,2048]{1,0:T(8,128)(2,1)}, u32[]{:S(2)}, u32[]{:S(2)}) collective-permute-start(bf16[128,2048]{1,0:T(8,128)(2,1)} %get-tuple-element.121), channel_id=1, source_target_pairs={{0,64},{8,72},{16,80},{24,88},{32,96},{40,104},{48,112},{56,120},{... | collective-permute-start | bytes 1572872 | tf_op jit(solution)/shard_map/ppermute | solution.py:487
  123.9 48.7 %all-to-all-start.1 = ((bf16[32,128,256]{2,1,0:T(8,128)(2,1)}), bf16[32,128,256]{2,1,0:T(8,128)(2,1)}, u32[]{:S(2)}, u32[]{:S(2)}) async-start(bf16[32,128,256]{2,1,0:T(8,128)(2,1)} %get-tuple-element.68), calls=%async_computation.1 | async-start | bytes 4194304 | tf_op jit(solution)/shard_map/all_to_all | solution.py:571
  131.9 11.2 %collective-permute-start.26 = (bf16[2048,512]{1,0:T(8,128)(2,1)S(1)}, bf16[2048,512]{1,0:T(8,128)(2,1)S(1)}, u32[]{:S(2)}, u32[]{:S(2)}) collective-permute-start(bf16[2048,512]{1,0:T(8,128)(2,1)S(1)} %transpose_pieces.1.own_ref), channel_id=1, source_target_pairs={{0,1},{1,0},{2,3},{3,2},{4,5},{5,4},{6,7},{7,6},{8,9},{9,8},{10,11... | collective-permute-start | bytes 6291464 | tf_op jit(solution)/shard_map/ppermute | solution.py:496
  136.4 8.0 %collective-permute-start.27 = (bf16[8192,128]{1,0:T(8,128)(2,1)}, bf16[8192,128]{1,0:T(8,128)(2,1)}, u32[]{:S(2)}, u32[]{:S(2)}) collective-permute-start(bf16[8192,128]{1,0:T(8,128)(2,1)} %get-tuple-element.104.refs_0_), channel_id=1, source_target_pairs={{0,1},{1,0},{2,3},{3,2},{4,5},{5,4},{6,7},{7,6},{8,9},{9,8},{10,11... | collective-permute-start | bytes 6291464 | tf_op jit(solution)/shard_map/ppermute | solution.py:496
  136.9 7.6 %collective-permute-start.28 = (bf16[8192,128]{1,0:T(8,128)(2,1)}, bf16[8192,128]{1,0:T(8,128)(2,1)}, u32[]{:S(2)}, u32[]{:S(2)}) collective-permute-start(bf16[8192,128]{1,0:T(8,128)(2,1)} %get-tuple-element.105.refs_1_), channel_id=1, source_target_pairs={{0,1},{1,0},{2,3},{3,2},{4,5},{5,4},{6,7},{7,6},{8,9},{9,8},{10,11... | collective-permute-start | bytes 6291464 | tf_op jit(solution)/shard_map/ppermute | solution.py:496
  136.9 35.7 %copy-start.20 = (f32[128]{0:T(128)S(1)}, f32[128]{0:T(128)}, u32[]{:S(2)}) copy-start(f32[128]{0:T(128)} %param.13) | copy-start | bytes 1540
  175.6 5.0 %collective-permute-start.31 = (bf16[256,256]{1,0:T(8,128)(2,1)S(1)}, bf16[256,256]{1,0:T(8,128)(2,1)S(1)}, u32[]{:S(2)}, u32[]{:S(2)}) collective-permute-start(bf16[256,256]{1,0:T(8,128)(2,1)S(1)} %get-tuple-element.99.refs_0_), channel_id=1, source_target_pairs={{0,192},{8,200},{16,208},{24,216},{32,224},{40,232},{48,240},{56,2... | collective-permute-start | bytes 393224 | tf_op jit(solution)/shard_map/ppermute | solution.py:487
  177.3 6.5 %collective-permute-start.30 = (bf16[256,256]{1,0:T(8,128)(2,1)S(1)}, bf16[256,256]{1,0:T(8,128)(2,1)S(1)}, u32[]{:S(2)}, u32[]{:S(2)}) collective-permute-start(bf16[256,256]{1,0:T(8,128)(2,1)S(1)} %get-tuple-element.99.refs_0_), channel_id=1, source_target_pairs={{0,128},{8,136},{16,144},{24,152},{32,160},{40,168},{48,176},{56,1... | collective-permute-start | bytes 393224 | tf_op jit(solution)/shard_map/ppermute | solution.py:487
  179.2 6.2 %collective-permute-start.29 = (bf16[256,256]{1,0:T(8,128)(2,1)S(1)}, bf16[256,256]{1,0:T(8,128)(2,1)S(1)}, u32[]{:S(2)}, u32[]{:S(2)}) collective-permute-start(bf16[256,256]{1,0:T(8,128)(2,1)S(1)} %get-tuple-element.99.refs_0_), channel_id=1, source_target_pairs={{0,64},{8,72},{16,80},{24,88},{32,96},{40,104},{48,112},{56,120},{... | collective-permute-start | bytes 393224 | tf_op jit(solution)/shard_map/ppermute | solution.py:487
  179.8 7.8 %collective-permute-start.32 = (bf16[256,256]{1,0:T(8,128)(2,1)S(1)}, bf16[256,256]{1,0:T(8,128)(2,1)S(1)}, u32[]{:S(2)}, u32[]{:S(2)}) collective-permute-start(bf16[256,256]{1,0:T(8,128)(2,1)S(1)} %get-tuple-element.102.own_ref), channel_id=1, source_target_pairs={{0,1},{1,0},{2,3},{3,2},{4,5},{5,4},{6,7},{7,6},{8,9},{9,8},{10,11... | collective-permute-start | bytes 393224 | tf_op jit(solution)/shard_map/ppermute | solution.py:496
  187.7 32.0 %all-to-all-start.2 = ((bf16[8,256,256]{2,1,0:T(8,128)(2,1)}), bf16[8,256,256]{2,1,0:T(8,128)(2,1)S(1)}, u32[]{:S(2)}, u32[]{:S(2)}) async-start(bf16[8,256,256]{2,1,0:T(8,128)(2,1)} %weight_terms.1), calls=%async_computation.2 | async-start | bytes 2097152 | tf_op jit(solution)/shard_map/all_to_all | solution.py:586
  197.9 16.1 %collective-permute-start.33 = (bf16[32,8192]{1,0:T(8,128)(2,1)S(1)}, bf16[32,8192]{1,0:T(8,128)(2,1)S(1)}, u32[]{:S(2)}, u32[]{:S(2)}) collective-permute-start(bf16[32,8192]{1,0:T(8,128)(2,1)S(1)} %get-tuple-element.109), channel_id=1, source_target_pairs={{0,2},{1,3},{2,4},{3,5},{4,6},{5,7},{6,0},{7,1},{8,10},{9,11},{10,... | collective-permute-start | bytes 1572872 | tf_op jit(solution)/shard_map/ppermute | solution.py:591
  199.5 20.2 %collective-permute-start.34 = (bf16[32,8192]{1,0:T(8,128)(2,1)S(1)}, bf16[32,8192]{1,0:T(8,128)(2,1)S(1)}, u32[]{:S(2)}, u32[]{:S(2)}) collective-permute-start(bf16[32,8192]{1,0:T(8,128)(2,1)S(1)} %get-tuple-element.110), channel_id=1, source_target_pairs={{0,4},{1,5},{2,6},{3,7},{4,0},{5,1},{6,2},{7,3},{8,12},{9,13},{10,... | collective-permute-start | bytes 1572872 | tf_op jit(solution)/shard_map/ppermute | solution.py:591
  202.2 17.5 %collective-permute-start.35 = (bf16[32,8192]{1,0:T(8,128)(2,1)S(1)}, bf16[32,8192]{1,0:T(8,128)(2,1)S(1)}, u32[]{:S(2)}, u32[]{:S(2)}) collective-permute-start(bf16[32,8192]{1,0:T(8,128)(2,1)S(1)} %get-tuple-element.111), channel_id=1, source_target_pairs={{0,6},{1,7},{2,0},{3,1},{4,2},{5,3},{6,4},{7,5},{8,14},{9,15},{10,... | collective-permute-start | bytes 1572872 | tf_op jit(solution)/shard_map/ppermute | solution.py:591
  (12 other events, 44.0 us)

commit v14 on v13

--- a/solution.py
+++ b/solution.py
@@ -267,9 +267,20 @@
     )(table, *hold(kv, probs, d_scores))
 
 
-def owner_kernel(table_ref, part_ref, raw_ref, gain_ref, grad_ref, by_core_ref, acc):
+def owner_kernel(table_ref, part_hbm, raw_ref, gain_ref, grad_ref, by_core_ref, *scratch):
+    acc, part_ref, sems = scratch
     head_dim = gain_ref.shape[1]
     tokens = part_ref.shape[1]
+    steps = sems.shape[0]
+    count = part_ref.shape[0] // steps
+    copies = []
+    for step in range(steps):
+        here = pl.ds(step * count, count)
+        copies.append(
+            pltpu.make_async_copy(part_hbm.at[here], part_ref.at[here], sems.at[step])
+        )
+    for copy in copies:
+        copy.start()
     acc[...] = jnp.zeros_like(acc)
 
     def add(d, carry):
@@ -279,7 +290,9 @@
 
         return carry
 
-    lax.fori_loop(0, part_ref.shape[0], add, 0)
+    for step in range(steps):
+        copies[step].wait()
+        lax.fori_loop(step * count, (step + 1) * count, add, 0)
     gain = gain_ref[...]
     for i in range(acc.shape[0]):
         here = slice(i * tokens, (i + 1) * tokens)
@@ -303,9 +316,13 @@
         grid_spec=pltpu.PrefetchScalarGridSpec(
             num_scalar_prefetch=1,
             grid=(),
-            in_specs=[in_vmem()] * 3,
+            in_specs=[in_hbm()] + [in_vmem()] * 2,
             out_specs=[in_vmem()] * 2,
-            scratch_shapes=[pltpu.VMEM((images, tokens, cols), F32)],
+            scratch_shapes=[
+                pltpu.VMEM((images, tokens, cols), F32),
+                pltpu.VMEM(parts.shape, BF16),
+                pltpu.SemaphoreType.DMA((4,)),
+            ],
         ),
         out_shape=[grads, grads],
         compiler_params=limit(6),

time: 221 us -> 222 us (level)
  no operation moved by 1% of the time
where the time goes in v14:
time: 222 us; the launch traced here: 221 us
  waiting for transfers between devices  106 us (48%)
  starting transfers between devices  66.2 us (30%)
  Pallas kernels  39.4 us (18%)
  local copies, waits for them, and re-layouts  6.95 us (3%)
    all_to_all x1, waiting for transfers between devices, local(): kv = lax.all_to_all(send, 'dp', 0, 0, tiled=True)  34.4 us
    all_to_all x1, waiting for transfers between devices, local(): parts = lax.all_to_all(parts, 'dp', 0, 0, tiled=True)  28.1 us
    ppermute x15, starting transfers between devices, shift_y(): return lax.ppermute(x, 'dp', pairs)  20.8 us
    ppermute x14, starting transfers between devices, shift_z(): return lax.ppermute(x, 'dp', pairs)  20.4 us
    ppermute x3, waiting for transfers between devices, local(): terms[s] = lax.ppermute(terms[s], 'tensor', pairs)  16.3 us
    ppermute x15, waiting for transfers between devices, shift_y(): return lax.ppermute(x, 'dp', pairs)  14.5 us
    ppermute x14, waiting for transfers between devices, shift_z(): return lax.ppermute(x, 'dp', pairs)  13 us
    all_to_all x1, starting transfers between devices, local(): kv = lax.all_to_all(send, 'dp', 0, 0, tiled=True)  8.9 us
  transfers between devices with their start and end apart: 39, of which 17 were waited for; matrix products, arithmetic and copies ran while one was open for 3% of the time, Pallas kernels for 13%

profile of v14, /device:TPU:32, one launch (start us, length us, event | category | flops | bytes accessed | tf_op | source)
XLA Modules:
  0.0 221.2 jit_solution(9136209092509830262)
XLA Ops:
  0.6 2.0 collective-permute-start
  2.7 3.2 %collective-permute-start.5 = (bf16[256,128]{1,0:T(8,128)(2,1)}, bf16[256,128]{1,0:T(8,128)(2,1)S(1)}, u32[]{:S(2)}, u32[]{:S(2)}) collective-permute-start(bf16[256,128]{1,0:T(8,128)(2,1)} %param.12), channel_id=1, source_target_pairs={{0,128},{8,136},{16,144},{24,152},{32,160},{40,168},{48,176},{56,1... | collective-permute-start | bytes 196616 | tf_op jit(solution)/shard_map/ppermute | solution.py:504
  5.9 1.1 collective-permute-start.4
  10.6 2.1 collective-permute-done.6
  12.7 4.1 %collective-permute-start.8 = (bf16[1024,128]{1,0:T(8,128)(2,1)S(1)}, bf16[1024,128]{1,0:T(8,128)(2,1)S(1)}, u32[]{:S(2)}, u32[]{:S(2)}) collective-permute-start(bf16[1024,128]{1,0:T(8,128)(2,1)S(1)} %constant_dynamic-update-slice_fusion.refs_8_), channel_id=1, source_target_pairs={{0,56},{8,0},{16,8},{24,16},{32,24},{40,32},{48,40},{56,48},{64,12... | collective-permute-start | bytes 786440 | tf_op jit(solution)/shard_map/ppermute | solution.py:509
  16.9 1.0 collective-permute-start.2
  17.9 1.1 collective-permute-start.3
  19.1 4.9 %collective-permute-done.2 = bf16[256,128]{1,0:T(8,128)(2,1)S(1)} collective-permute-done((bf16[256,128]{1,0:T(8,128)(2,1)S(1)}, bf16[256,128]{1,0:T(8,128)(2,1)S(1)}, u32[]{:S(2)}, u32[]{:S(2)}) %collective-permute-start.2) | collective-permute-done | bytes 65568 | tf_op jit(solution)/shard_map/ppermute | solution.py:509
  24.0 1.4 collective-permute-start.12
  25.5 3.2 %collective-permute-start.9 = (bf16[1024,128]{1,0:T(8,128)(2,1)S(1)}, bf16[1024,128]{1,0:T(8,128)(2,1)S(1)}, u32[]{:S(2)}, u32[]{:S(2)}) collective-permute-start(bf16[1024,128]{1,0:T(8,128)(2,1)S(1)} %constant_dynamic-update-slice_fusion.4.refs_0_), channel_id=1, source_target_pairs={{0,192},{8,200},{16,208},{24,216},{32,224},{40,232},{48,240},{56,2... | collective-permute-start | bytes 786440 | tf_op jit(solution)/shard_map/ppermute | solution.py:504
  28.7 1.7 collective-permute-start.13
  30.4 1.4 collective-permute-start.18
  31.9 1.9 collective-permute-start.19
  34.1 2.0 collective-permute-start.14
  36.2 4.1 %collective-permute-done.14 = bf16[256,128]{1,0:T(8,128)(2,1)S(1)} collective-permute-done((bf16[256,128]{1,0:T(8,128)(2,1)S(1)}, bf16[256,128]{1,0:T(8,128)(2,1)S(1)}, u32[]{:S(2)}, u32[]{:S(2)}) %collective-permute-start.14) | collective-permute-done | bytes 65568 | tf_op jit(solution)/shard_map/ppermute | solution.py:509
  40.4 1.1 collective-permute-start.20
  41.6 3.2 %collective-permute-start.15 = (bf16[1024,128]{1,0:T(8,128)(2,1)S(1)}, bf16[1024,128]{1,0:T(8,128)(2,1)S(1)}, u32[]{:S(2)}, u32[]{:S(2)}) collective-permute-start(bf16[1024,128]{1,0:T(8,128)(2,1)S(1)} %constant_dynamic-update-slice_fusion.8.refs_4_), channel_id=1, source_target_pairs={{0,192},{8,200},{16,208},{24,216},{32,224},{40,232},{48,240},{56,2... | collective-permute-start | bytes 786440 | tf_op jit(solution)/shard_map/ppermute | solution.py:504
  44.9 2.5 %collective-permute-start.21 = (bf16[1024,128]{1,0:T(8,128)(2,1)S(1)}, bf16[1024,128]{1,0:T(8,128)(2,1)}, u32[]{:S(2)}, u32[]{:S(2)}) collective-permute-start(bf16[1024,128]{1,0:T(8,128)(2,1)S(1)} %collective-permute-done.19.refs_12_), channel_id=1, source_target_pairs={{0,56},{8,0},{16,8},{24,16},{32,24},{40,32},{48,40},{56,48},{64,12... | collective-permute-start | bytes 786440 | tf_op jit(solution)/shard_map/ppermute | solution.py:509
  47.4 1.7 collective-permute-done.16.refs_6_
  49.4 1.7 collective-permute-done.20.refs_13_
  51.9 5.0 %collective-permute-done.17.refs_7_ = bf16[1024,128]{1,0:T(8,128)(2,1)} collective-permute-done((bf16[1024,128]{1,0:T(8,128)(2,1)S(1)}, bf16[1024,128]{1,0:T(8,128)(2,1)}, u32[]{:S(2)}, u32[]{:S(2)}) %collective-permute-start.17) | collective-permute-done | bytes 262176 | tf_op jit(solution)/shard_map/ppermute | solution.py:504
  56.8 1.6 collective-permute-done.22.refs_15_
  59.1 6.0 %project.1 = (bf16[32,128,256]{2,1,0:T(8,128)(2,1)}, f32[256,128]{1,0:T(8,128)}) custom-call(s32[5,32]{1,0:T(8,128)S(1)} %stack.41.table_ref, bf16[256,8192]{1,0:T(8,128)(2,1)} %bitcast.24, bf16[1024,128]{1,0:T(8,128)(2,1)S(1)} %constant_dynamic-update-slice_fusion.4.refs_0_, bf16[1024,128]{1,0:T(8,128)(2,1)S(1)} %collective-permute-done.9.refs_1_, ...), custom_call_target="tpu_custom_call" | custom-call | flops 1073741824 | bytes 10485760 | tf_op jit(solution)/shard_map/project/pallas_call | solution.py:92
  65.2 8.9 %all-to-all-start = ((bf16[32,128,256]{2,1,0:T(8,128)(2,1)}), bf16[32,128,256]{2,1,0:T(8,128)(2,1)S(1)}, u32[]{:S(2)}, u32[]{:S(2)}) async-start(bf16[32,128,256]{2,1,0:T(8,128)(2,1)} %get-tuple-element.64), calls=%async_computation | async-start | bytes 4194304 | tf_op jit(solution)/shard_map/all_to_all | solution.py:572
  74.1 2.9 %dynamic-slice_bitcast_fusion = (bf16[128,2048]{1,0:T(8,128)(2,1)}, bf16[128,2048]{1,0:T(8,128)(2,1)}, bf16[128,2048]{1,0:T(8,128)(2,1)}, bf16[128,2048]{1,0:T(8,128)(2,1)}) fusion(bf16[2,128,8192]{2,1,0:T(8,128)(2,1)} %param.10, s32[]{:T(128)S(6)} %select_n.86, s32[]{:T(128)S(6)} %select_n.94, s32[]{:T(128)S(6)} %select_n.92, s32[]{:T(128)S(6)} %select_n.90, ...), kind=kLoop, calls=%fused_computation | loop fusion | bytes 4194324 | tf_op jit(solution)/shard_map/squeeze | solution.py:578
  77.0 2.7 %collective-permute-start.25 = (bf16[128,2048]{1,0:T(8,128)(2,1)}, bf16[128,2048]{1,0:T(8,128)(2,1)}, u32[]{:S(2)}, u32[]{:S(2)}) collective-permute-start(bf16[128,2048]{1,0:T(8,128)(2,1)} %get-tuple-element.119), channel_id=1, source_target_pairs={{0,192},{8,200},{16,208},{24,216},{32,224},{40,232},{48,240},{56,2... | collective-permute-start | bytes 1572872 | tf_op jit(solution)/shard_map/ppermute | solution.py:504
  81.4 34.4 %all-to-all-done.kv_ref = bf16[32,128,256]{2,1,0:T(8,128)(2,1)S(1)} async-done(((bf16[32,128,256]{2,1,0:T(8,128)(2,1)}), bf16[32,128,256]{2,1,0:T(8,128)(2,1)S(1)}, u32[]{:S(2)}, u32[]{:S(2)}) %all-to-all-start) | async-done | bytes 2097184 | tf_op jit(solution)/shard_map/all_to_all | solution.py:572
  115.9 8.0 %attend.1 = (bf16[32,128,256]{2,1,0:T(8,128)(2,1)}, bf16[32,128,128]{2,1,0:T(8,128)(2,1)}, bf16[32,128,128]{2,1,0:T(8,128)(2,1)}) custom-call(s32[5,32]{1,0:T(8,128)S(1)} %stack.41.table_ref, bf16[512,1024]{1,0:T(8,128)(2,1)} %q_hbm.1, bf16[512,1024]{1,0:T(8,128)(2,1)} %ct_hbm.1, bf16[32,128,256]{2,1,0:T(8,128)(2,1)S(1)} %all-to-all-done.kv_ref), custom_call_target="tpu_custom_call" | custom-call | flops 536870912 | bytes 8388608 | tf_op jit(solution)/shard_map/attend/pallas_call | solution.py:213
  123.9 5.7 %all-to-all-start.1 = ((bf16[32,128,256]{2,1,0:T(8,128)(2,1)}), bf16[32,128,256]{2,1,0:T(8,128)(2,1)}, u32[]{:S(2)}, u32[]{:S(2)}) async-start(bf16[32,128,256]{2,1,0:T(8,128)(2,1)} %get-tuple-element.68), calls=%async_computation.1 | async-start | bytes 4194304 | tf_op jit(solution)/shard_map/all_to_all | solution.py:588
  129.7 2.2 %transpose_pieces.1.own_ref = bf16[2048,512]{1,0:T(8,128)(2,1)S(1)} custom-call(bf16[128,2048]{1,0:T(8,128)(2,1)} %get-tuple-element.69.refs_0_, bf16[128,2048]{1,0:T(8,128)(2,1)} %collective-permute-done.23.refs_1_, bf16[128,2048]{1,0:T(8,128)(2,1)} %collective-permute-done.24.refs_2_, bf16[128,2048]{1,0:T(8,128)(2,1)} %collective-permute-done.25.refs_3_), custom_call_target="tpu_custom_call" | custom-call | bytes 4194304 | tf_op jit(solution)/shard_map/transpose_pieces/pallas_call | solution.py:343
  132.3 4.1 %assemble.1 = (bf16[8192,128]{1,0:T(8,128)(2,1)}, bf16[8192,128]{1,0:T(8,128)(2,1)}) custom-call(s32[5,32]{1,0:T(8,128)S(1)} %stack.41.table_ref, bf16[1024,128]{1,0:T(8,128)(2,1)S(1)} %constant_dynamic-update-slice_fusion.4.refs_0_, bf16[1024,128]{1,0:T(8,128)(2,1)S(1)} %copy-done.6, bf16[1024,128]{1,0:T(8,128)(2,1)S(1)} %copy-done.4, ...), custom_call_target="tpu_custom_call" | custom-call | bytes 1048576 | tf_op jit(solution)/shard_map/assemble/pallas_call | solution.py:388
  136.9 6.2 %apply.1 = (bf16[512,1024]{1,0:T(8,128)(2,1)}, bf16[512,1024]{1,0:T(8,128)(2,1)}) custom-call(s32[5,32]{1,0:T(8,128)S(1)} %stack.41.table_ref, bf16[32,128,256]{2,1,0:T(8,128)(2,1)} %copy-done, bf16[32,128,128]{2,1,0:T(8,128)(2,1)} %get-tuple-element.73.probs_ref, bf16[32,128,128]{2,1,0:T(8,128)(2,1)} %get-tuple-element.74.ds_ref), custom_call_target="tpu_custom_call" | custom-call | flops 268435456 | bytes 6291456 | tf_op jit(solution)/shard_map/apply/pallas_call | solution.py:255
  143.1 1.4 copy-done.1
  144.5 28.1 %all-to-all-done.1.part_hbm = bf16[32,128,256]{2,1,0:T(8,128)(2,1)} async-done(((bf16[32,128,256]{2,1,0:T(8,128)(2,1)}), bf16[32,128,256]{2,1,0:T(8,128)(2,1)}, u32[]{:S(2)}, u32[]{:S(2)}) %all-to-all-start.1) | async-done | bytes 2097184 | tf_op jit(solution)/shard_map/all_to_all | solution.py:588
  172.6 3.4 %owner_grads.1 = (bf16[256,256]{1,0:T(8,128)(2,1)S(1)}, bf16[256,256]{1,0:T(8,128)(2,1)S(1)}) custom-call(s32[5,32]{1,0:T(8,128)S(1)} %stack.41.table_ref, bf16[32,128,256]{2,1,0:T(8,128)(2,1)} %all-to-all-done.1.part_hbm, f32[256,128]{1,0:T(8,128)} %get-tuple-element.66.raw_ref, f32[1,128]{1,0:T(1,128)S(1)} %bitcast.23), custom_call_target="tpu_custom_call" | custom-call | bytes 3145728 | tf_op jit(solution)/shard_map/owner_grads/pallas_call | solution.py:314
  176.0 1.8 collective-permute-start.31
  177.8 1.9 collective-permute-start.30
  181.0 3.2 %collective-permute-done.30.refs_2_ = bf16[256,256]{1,0:T(8,128)(2,1)S(1)} collective-permute-done((bf16[256,256]{1,0:T(8,128)(2,1)S(1)}, bf16[256,256]{1,0:T(8,128)(2,1)S(1)}, u32[]{:S(2)}, u32[]{:S(2)}) %collective-permute-start.30) | collective-permute-done | bytes 131104 | tf_op jit(solution)/shard_map/ppermute | solution.py:504
  184.2 1.6 collective-permute-done.29.refs_1_
  185.8 2.3 %weight_terms.1 = bf16[8,256,256]{2,1,0:T(8,128)(2,1)} custom-call(bf16[2048,512]{1,0:T(8,128)(2,1)S(1)} %transpose_pieces.1.own_ref, bf16[2048,512]{1,0:T(8,128)(2,1)S(1)} %copy-done.2, bf16[256,256]{1,0:T(8,128)(2,1)S(1)} %get-tuple-element.99.refs_0_, bf16[256,256]{1,0:T(8,128)(2,1)S(1)} %collective-permute-done.29.refs_1_, ...), custom_call_target="tpu_custom_call" | custom-call | flops 1073741824 | bytes 6291456 | tf_op jit(solution)/shard_map/weight_terms/pallas_call | solution.py:369
  188.1 3.8 %all-to-all-start.2 = ((bf16[8,256,256]{2,1,0:T(8,128)(2,1)}), bf16[8,256,256]{2,1,0:T(8,128)(2,1)S(1)}, u32[]{:S(2)}, u32[]{:S(2)}) async-start(bf16[8,256,256]{2,1,0:T(8,128)(2,1)} %weight_terms.1), calls=%async_computation.2 | async-start | bytes 2097152 | tf_op jit(solution)/shard_map/all_to_all | solution.py:603
  191.9 6.1 %feature_terms.1 = (bf16[32,8192]{1,0:T(8,128)(2,1)S(1)}, bf16[32,8192]{1,0:T(8,128)(2,1)S(1)}, bf16[32,8192]{1,0:T(8,128)(2,1)S(1)}, bf16[32,8192]{1,0:T(8,128)(2,1)S(1)}) custom-call(s32[5,32]{1,0:T(8,128)S(1)} %stack.41.table_ref, bf16[256,256]{1,0:T(8,128)(2,1)S(1)} %get-tuple-element.102.own_ref, ...), custom_call_target="tpu_custom_call" | custom-call | flops 2147483648 | bytes 10485760 | tf_op jit(solution)/shard_map/feature_terms/pallas_call | solution.py:449
  198.1 1.6 collective-permute-start.33
  199.7 2.7 %collective-permute-start.34 = (bf16[32,8192]{1,0:T(8,128)(2,1)S(1)}, bf16[32,8192]{1,0:T(8,128)(2,1)S(1)}, u32[]{:S(2)}, u32[]{:S(2)}) collective-permute-start(bf16[32,8192]{1,0:T(8,128)(2,1)S(1)} %get-tuple-element.110), channel_id=1, source_target_pairs={{0,4},{1,5},{2,6},{3,7},{4,0},{5,1},{6,2},{7,3},{8,12},{9,13},{10,... | collective-permute-start | bytes 1572872 | tf_op jit(solution)/shard_map/ppermute | solution.py:608
  202.4 1.4 collective-permute-start.35
  203.8 10.4 %collective-permute-done.33.refs_1_ = bf16[32,8192]{1,0:T(8,128)(2,1)S(1)} collective-permute-done((bf16[32,8192]{1,0:T(8,128)(2,1)S(1)}, bf16[32,8192]{1,0:T(8,128)(2,1)S(1)}, u32[]{:S(2)}, u32[]{:S(2)}) %collective-permute-start.33) | collective-permute-done | bytes 524320 | tf_op jit(solution)/shard_map/ppermute | solution.py:608
  214.2 5.9 %collective-permute-done.34.refs_2_ = bf16[32,8192]{1,0:T(8,128)(2,1)S(1)} collective-permute-done((bf16[32,8192]{1,0:T(8,128)(2,1)S(1)}, bf16[32,8192]{1,0:T(8,128)(2,1)S(1)}, u32[]{:S(2)}, u32[]{:S(2)}) %collective-permute-start.34) | collective-permute-done | bytes 524320 | tf_op jit(solution)/shard_map/ppermute | solution.py:608
  220.1 1.2 finish.1
  (105 shorter events, 10.3 us)
Async XLA Ops:
  0.6 16.2 %collective-permute-start = (bf16[256,128]{1,0:T(8,128)(2,1)}, bf16[256,128]{1,0:T(8,128)(2,1)S(1)}, u32[]{:S(2)}, u32[]{:S(2)}) collective-permute-start(bf16[256,128]{1,0:T(8,128)(2,1)} %param.11), channel_id=1, source_target_pairs={{0,8},{8,16},{16,24},{24,32},{32,40},{40,48},{48,56},{56,0},{64,72... | collective-permute-start | bytes 196616 | tf_op jit(solution)/shard_map/ppermute | solution.py:509
  2.6 15.3 %collective-permute-start.1 = (bf16[256,128]{1,0:T(8,128)(2,1)}, bf16[256,128]{1,0:T(8,128)(2,1)S(1)}, u32[]{:S(2)}, u32[]{:S(2)}) collective-permute-start(bf16[256,128]{1,0:T(8,128)(2,1)} %param.11), channel_id=1, source_target_pairs={{0,56},{8,0},{16,8},{24,16},{32,24},{40,32},{48,40},{56,48},{64,12... | collective-permute-start | bytes 196616 | tf_op jit(solution)/shard_map/ppermute | solution.py:509
  2.7 7.8 %collective-permute-start.5 = (bf16[256,128]{1,0:T(8,128)(2,1)}, bf16[256,128]{1,0:T(8,128)(2,1)S(1)}, u32[]{:S(2)}, u32[]{:S(2)}) collective-permute-start(bf16[256,128]{1,0:T(8,128)(2,1)} %param.12), channel_id=1, source_target_pairs={{0,128},{8,136},{16,144},{24,152},{32,160},{40,168},{48,176},{56,1... | collective-permute-start | bytes 196616 | tf_op jit(solution)/shard_map/ppermute | solution.py:504
  5.9 4.6 %collective-permute-start.4 = (bf16[256,128]{1,0:T(8,128)(2,1)}, bf16[256,128]{1,0:T(8,128)(2,1)S(1)}, u32[]{:S(2)}, u32[]{:S(2)}) collective-permute-start(bf16[256,128]{1,0:T(8,128)(2,1)} %param.12), channel_id=1, source_target_pairs={{0,192},{8,200},{16,208},{24,216},{32,224},{40,232},{48,240},{56,2... | collective-permute-start | bytes 196616 | tf_op jit(solution)/shard_map/ppermute | solution.py:504
  7.0 5.7 %collective-permute-start.6 = (bf16[256,128]{1,0:T(8,128)(2,1)}, bf16[256,128]{1,0:T(8,128)(2,1)S(1)}, u32[]{:S(2)}, u32[]{:S(2)}) collective-permute-start(bf16[256,128]{1,0:T(8,128)(2,1)} %param.12), channel_id=1, source_target_pairs={{0,64},{8,72},{16,80},{24,88},{32,96},{40,104},{48,112},{56,120},{... | collective-permute-start | bytes 196616 | tf_op jit(solution)/shard_map/ppermute | solution.py:504
  12.7 11.3 %collective-permute-start.8 = (bf16[1024,128]{1,0:T(8,128)(2,1)S(1)}, bf16[1024,128]{1,0:T(8,128)(2,1)S(1)}, u32[]{:S(2)}, u32[]{:S(2)}) collective-permute-start(bf16[1024,128]{1,0:T(8,128)(2,1)S(1)} %constant_dynamic-update-slice_fusion.refs_8_), channel_id=1, source_target_pairs={{0,56},{8,0},{16,8},{24,16},{32,24},{40,32},{48,40},{56,48},{64,12... | collective-permute-start | bytes 786440 | tf_op jit(solution)/shard_map/ppermute | solution.py:509
  16.8 7.2 %collective-permute-start.7 = (bf16[1024,128]{1,0:T(8,128)(2,1)S(1)}, bf16[1024,128]{1,0:T(8,128)(2,1)S(1)}, u32[]{:S(2)}, u32[]{:S(2)}) collective-permute-start(bf16[1024,128]{1,0:T(8,128)(2,1)S(1)} %constant_dynamic-update-slice_fusion.refs_8_), channel_id=1, source_target_pairs={{0,8},{8,16},{16,24},{24,32},{32,40},{40,48},{48,56},{56,0},{64,72... | collective-permute-start | bytes 786440 | tf_op jit(solution)/shard_map/ppermute | solution.py:509
  16.9 7.1 %collective-permute-start.2 = (bf16[256,128]{1,0:T(8,128)(2,1)S(1)}, bf16[256,128]{1,0:T(8,128)(2,1)S(1)}, u32[]{:S(2)}, u32[]{:S(2)}) collective-permute-start(bf16[256,128]{1,0:T(8,128)(2,1)S(1)} %collective-permute-done), channel_id=1, source_target_pairs={{0,8},{8,16},{16,24},{24,32},{32,40},{40,48},{48,56},{56,0},{64,72... | collective-permute-start | bytes 196616 | tf_op jit(solution)/shard_map/ppermute | solution.py:509
  17.9 6.1 %collective-permute-start.3 = (bf16[256,128]{1,0:T(8,128)(2,1)S(1)}, bf16[256,128]{1,0:T(8,128)(2,1)S(1)}, u32[]{:S(2)}, u32[]{:S(2)}) collective-permute-start(bf16[256,128]{1,0:T(8,128)(2,1)S(1)} %collective-permute-done.1), channel_id=1, source_target_pairs={{0,56},{8,0},{16,8},{24,16},{32,24},{40,32},{48,40},{56,48},{64,12... | collective-permute-start | bytes 196616 | tf_op jit(solution)/shard_map/ppermute | solution.py:509
  24.0 7.9 %collective-permute-start.12 = (bf16[256,128]{1,0:T(8,128)(2,1)S(1)}, bf16[256,128]{1,0:T(8,128)(2,1)S(1)}, u32[]{:S(2)}, u32[]{:S(2)}) collective-permute-start(bf16[256,128]{1,0:T(8,128)(2,1)S(1)} %collective-permute-done.2), channel_id=1, source_target_pairs={{0,8},{8,16},{16,24},{24,32},{32,40},{40,48},{48,56},{56,0},{64,72... | collective-permute-start | bytes 196616 | tf_op jit(solution)/shard_map/ppermute | solution.py:509
  25.4 16.2 %collective-permute-start.10 = (bf16[1024,128]{1,0:T(8,128)(2,1)S(1)}, bf16[1024,128]{1,0:T(8,128)(2,1)S(1)}, u32[]{:S(2)}, u32[]{:S(2)}) collective-permute-start(bf16[1024,128]{1,0:T(8,128)(2,1)S(1)} %constant_dynamic-update-slice_fusion.4.refs_0_), channel_id=1, source_target_pairs={{0,64},{8,72},{16,80},{24,88},{32,96},{40,104},{48,112},{56,120},{... | collective-permute-start | bytes 786440 | tf_op jit(solution)/shard_map/ppermute | solution.py:504
  25.5 19.3 %collective-permute-start.9 = (bf16[1024,128]{1,0:T(8,128)(2,1)S(1)}, bf16[1024,128]{1,0:T(8,128)(2,1)S(1)}, u32[]{:S(2)}, u32[]{:S(2)}) collective-permute-start(bf16[1024,128]{1,0:T(8,128)(2,1)S(1)} %constant_dynamic-update-slice_fusion.4.refs_0_), channel_id=1, source_target_pairs={{0,192},{8,200},{16,208},{24,216},{32,224},{40,232},{48,240},{56,2... | collective-permute-start | bytes 786440 | tf_op jit(solution)/shard_map/ppermute | solution.py:504
  28.7 5.4 %collective-permute-start.13 = (bf16[256,128]{1,0:T(8,128)(2,1)S(1)}, bf16[256,128]{1,0:T(8,128)(2,1)S(1)}, u32[]{:S(2)}, u32[]{:S(2)}) collective-permute-start(bf16[256,128]{1,0:T(8,128)(2,1)S(1)} %collective-permute-done.3), channel_id=1, source_target_pairs={{0,56},{8,0},{16,8},{24,16},{32,24},{40,32},{48,40},{56,48},{64,12... | collective-permute-start | bytes 196616 | tf_op jit(solution)/shard_map/ppermute | solution.py:509
  30.4 9.9 %collective-permute-start.18 = (bf16[1024,128]{1,0:T(8,128)(2,1)S(1)}, bf16[1024,128]{1,0:T(8,128)(2,1)S(1)}, u32[]{:S(2)}, u32[]{:S(2)}) collective-permute-start(bf16[1024,128]{1,0:T(8,128)(2,1)S(1)} %collective-permute-done.7.refs_9_), channel_id=1, source_target_pairs={{0,8},{8,16},{16,24},{24,32},{32,40},{40,48},{48,56},{56,0},{64,72... | collective-permute-start | bytes 786440 | tf_op jit(solution)/shard_map/ppermute | solution.py:509
  31.9 13.0 %collective-permute-start.19 = (bf16[1024,128]{1,0:T(8,128)(2,1)S(1)}, bf16[1024,128]{1,0:T(8,128)(2,1)S(1)}, u32[]{:S(2)}, u32[]{:S(2)}) collective-permute-start(bf16[1024,128]{1,0:T(8,128)(2,1)S(1)} %collective-permute-done.8.refs_10_), channel_id=1, source_target_pairs={{0,56},{8,0},{16,8},{24,16},{32,24},{40,32},{48,40},{56,48},{64,12... | collective-permute-start | bytes 786440 | tf_op jit(solution)/shard_map/ppermute | solution.py:509
  34.1 6.1 %collective-permute-start.14 = (bf16[256,128]{1,0:T(8,128)(2,1)S(1)}, bf16[256,128]{1,0:T(8,128)(2,1)S(1)}, u32[]{:S(2)}, u32[]{:S(2)}) collective-permute-start(bf16[256,128]{1,0:T(8,128)(2,1)S(1)} %collective-permute-done.12), channel_id=1, source_target_pairs={{0,8},{8,16},{16,24},{24,32},{32,40},{40,48},{48,56},{56,0},{64,72... | collective-permute-start | bytes 196616 | tf_op jit(solution)/shard_map/ppermute | solution.py:509
  40.3 8.9 %collective-permute-start.16 = (bf16[1024,128]{1,0:T(8,128)(2,1)S(1)}, bf16[1024,128]{1,0:T(8,128)(2,1)S(1)}, u32[]{:S(2)}, u32[]{:S(2)}) collective-permute-start(bf16[1024,128]{1,0:T(8,128)(2,1)S(1)} %constant_dynamic-update-slice_fusion.8.refs_4_), channel_id=1, source_target_pairs={{0,64},{8,72},{16,80},{24,88},{32,96},{40,104},{48,112},{56,120},{... | collective-permute-start | bytes 786440 | tf_op jit(solution)/shard_map/ppermute | solution.py:504
  40.4 24.7 %copy-start.7 = (bf16[1024,128]{1,0:T(8,128)(2,1)}, bf16[1024,128]{1,0:T(8,128)(2,1)S(1)}, u32[]{:S(2)}) copy-start(bf16[1024,128]{1,0:T(8,128)(2,1)S(1)} %collective-permute-done.18.refs_11_) | copy-start | bytes 786436
  40.4 10.7 %collective-permute-start.20 = (bf16[1024,128]{1,0:T(8,128)(2,1)S(1)}, bf16[1024,128]{1,0:T(8,128)(2,1)S(1)}, u32[]{:S(2)}, u32[]{:S(2)}) collective-permute-start(bf16[1024,128]{1,0:T(8,128)(2,1)S(1)} %collective-permute-done.18.refs_11_), channel_id=1, source_target_pairs={{0,8},{8,16},{16,24},{24,32},{32,40},{40,48},{48,56},{56,0},{64,72... | collective-permute-start | bytes 786440 | tf_op jit(solution)/shard_map/ppermute | solution.py:509
  41.6 23.5 %copy-start.3 = (bf16[1024,128]{1,0:T(8,128)(2,1)}, bf16[1024,128]{1,0:T(8,128)(2,1)S(1)}, u32[]{:S(2)}) copy-start(bf16[1024,128]{1,0:T(8,128)(2,1)S(1)} %collective-permute-done.10.refs_2_) | copy-start | bytes 786436
  41.6 9.7 %collective-permute-start.15 = (bf16[1024,128]{1,0:T(8,128)(2,1)S(1)}, bf16[1024,128]{1,0:T(8,128)(2,1)S(1)}, u32[]{:S(2)}, u32[]{:S(2)}) collective-permute-start(bf16[1024,128]{1,0:T(8,128)(2,1)S(1)} %constant_dynamic-update-slice_fusion.8.refs_4_), channel_id=1, source_target_pairs={{0,192},{8,200},{16,208},{24,216},{32,224},{40,232},{48,240},{56,2... | collective-permute-start | bytes 786440 | tf_op jit(solution)/shard_map/ppermute | solution.py:504
  44.8 20.3 %copy-start.5 = (bf16[1024,128]{1,0:T(8,128)(2,1)}, bf16[1024,128]{1,0:T(8,128)(2,1)S(1)}, u32[]{:S(2)}) copy-start(bf16[1024,128]{1,0:T(8,128)(2,1)S(1)} %collective-permute-done.9.refs_1_) | copy-start | bytes 786436
  44.8 6.7 %collective-permute-start.11 = (bf16[1024,128]{1,0:T(8,128)(2,1)S(1)}, bf16[1024,128]{1,0:T(8,128)(2,1)S(1)}, u32[]{:S(2)}, u32[]{:S(2)}) collective-permute-start(bf16[1024,128]{1,0:T(8,128)(2,1)S(1)} %collective-permute-done.9.refs_1_), channel_id=1, source_target_pairs={{0,192},{8,200},{16,208},{24,216},{32,224},{40,232},{48,240},{56,2... | collective-permute-start | bytes 786440 | tf_op jit(solution)/shard_map/ppermute | solution.py:504
  44.9 20.2 %copy-start.9 = (bf16[1024,128]{1,0:T(8,128)(2,1)}, bf16[1024,128]{1,0:T(8,128)(2,1)S(1)}, u32[]{:S(2)}) copy-start(bf16[1024,128]{1,0:T(8,128)(2,1)S(1)} %collective-permute-done.19.refs_12_) | copy-start | bytes 786436
  44.9 6.9 %collective-permute-start.21 = (bf16[1024,128]{1,0:T(8,128)(2,1)S(1)}, bf16[1024,128]{1,0:T(8,128)(2,1)}, u32[]{:S(2)}, u32[]{:S(2)}) collective-permute-start(bf16[1024,128]{1,0:T(8,128)(2,1)S(1)} %collective-permute-done.19.refs_12_), channel_id=1, source_target_pairs={{0,56},{8,0},{16,8},{24,16},{32,24},{40,32},{48,40},{56,48},{64,12... | collective-permute-start | bytes 786440 | tf_op jit(solution)/shard_map/ppermute | solution.py:509
  49.1 16.0 %copy-start.11 = (bf16[1024,128]{1,0:T(8,128)(2,1)}, bf16[1024,128]{1,0:T(8,128)(2,1)S(1)}, u32[]{:S(2)}) copy-start(bf16[1024,128]{1,0:T(8,128)(2,1)S(1)} %collective-permute-done.16.refs_6_) | copy-start | bytes 786436
  49.1 7.7 %collective-permute-start.17 = (bf16[1024,128]{1,0:T(8,128)(2,1)S(1)}, bf16[1024,128]{1,0:T(8,128)(2,1)}, u32[]{:S(2)}, u32[]{:S(2)}) collective-permute-start(bf16[1024,128]{1,0:T(8,128)(2,1)S(1)} %collective-permute-done.16.refs_6_), channel_id=1, source_target_pairs={{0,64},{8,72},{16,80},{24,88},{32,96},{40,104},{48,112},{56,120},{... | collective-permute-start | bytes 786440 | tf_op jit(solution)/shard_map/ppermute | solution.py:504
  51.1 14.1 %copy-start.13 = (bf16[1024,128]{1,0:T(8,128)(2,1)}, bf16[1024,128]{1,0:T(8,128)(2,1)S(1)}, u32[]{:S(2)}) copy-start(bf16[1024,128]{1,0:T(8,128)(2,1)S(1)} %collective-permute-done.20.refs_13_) | copy-start | bytes 786436
  51.1 7.4 %collective-permute-start.22 = (bf16[1024,128]{1,0:T(8,128)(2,1)S(1)}, bf16[1024,128]{1,0:T(8,128)(2,1)}, u32[]{:S(2)}, u32[]{:S(2)}) collective-permute-start(bf16[1024,128]{1,0:T(8,128)(2,1)S(1)} %collective-permute-done.20.refs_13_), channel_id=1, source_target_pairs={{0,8},{8,16},{16,24},{24,32},{32,40},{40,48},{48,56},{56,0},{64,72... | collective-permute-start | bytes 786440 | tf_op jit(solution)/shard_map/ppermute | solution.py:509
  51.3 13.8 %copy-start.15 = (bf16[1024,128]{1,0:T(8,128)(2,1)}, bf16[1024,128]{1,0:T(8,128)(2,1)S(1)}, u32[]{:S(2)}) copy-start(bf16[1024,128]{1,0:T(8,128)(2,1)S(1)} %collective-permute-done.15.refs_5_) | copy-start | bytes 786436
  51.5 13.6 %copy-start.17 = (bf16[1024,128]{1,0:T(8,128)(2,1)}, bf16[1024,128]{1,0:T(8,128)(2,1)S(1)}, u32[]{:S(2)}) copy-start(bf16[1024,128]{1,0:T(8,128)(2,1)S(1)} %collective-permute-done.11.refs_3_) | copy-start | bytes 786436
  65.2 50.7 %all-to-all-start = ((bf16[32,128,256]{2,1,0:T(8,128)(2,1)}), bf16[32,128,256]{2,1,0:T(8,128)(2,1)S(1)}, u32[]{:S(2)}, u32[]{:S(2)}) async-start(bf16[32,128,256]{2,1,0:T(8,128)(2,1)} %get-tuple-element.64), calls=%async_computation | async-start | bytes 4194304 | tf_op jit(solution)/shard_map/all_to_all | solution.py:572
  77.0 46.8 %collective-permute-start.25 = (bf16[128,2048]{1,0:T(8,128)(2,1)}, bf16[128,2048]{1,0:T(8,128)(2,1)}, u32[]{:S(2)}, u32[]{:S(2)}) collective-permute-start(bf16[128,2048]{1,0:T(8,128)(2,1)} %get-tuple-element.119), channel_id=1, source_target_pairs={{0,192},{8,200},{16,208},{24,216},{32,224},{40,232},{48,240},{56,2... | collective-permute-start | bytes 1572872 | tf_op jit(solution)/shard_map/ppermute | solution.py:504
  79.8 44.1 %collective-permute-start.24 = (bf16[128,2048]{1,0:T(8,128)(2,1)}, bf16[128,2048]{1,0:T(8,128)(2,1)}, u32[]{:S(2)}, u32[]{:S(2)}) collective-permute-start(bf16[128,2048]{1,0:T(8,128)(2,1)} %get-tuple-element.120), channel_id=1, source_target_pairs={{0,128},{8,136},{16,144},{24,152},{32,160},{40,168},{48,176},{56,1... | collective-permute-start | bytes 1572872 | tf_op jit(solution)/shard_map/ppermute | solution.py:504
  80.6 43.3 %collective-permute-start.23 = (bf16[128,2048]{1,0:T(8,128)(2,1)}, bf16[128,2048]{1,0:T(8,128)(2,1)}, u32[]{:S(2)}, u32[]{:S(2)}) collective-permute-start(bf16[128,2048]{1,0:T(8,128)(2,1)} %get-tuple-element.121), channel_id=1, source_target_pairs={{0,64},{8,72},{16,80},{24,88},{32,96},{40,104},{48,112},{56,120},{... | collective-permute-start | bytes 1572872 | tf_op jit(solution)/shard_map/ppermute | solution.py:504
  123.9 48.7 %all-to-all-start.1 = ((bf16[32,128,256]{2,1,0:T(8,128)(2,1)}), bf16[32,128,256]{2,1,0:T(8,128)(2,1)}, u32[]{:S(2)}, u32[]{:S(2)}) async-start(bf16[32,128,256]{2,1,0:T(8,128)(2,1)} %get-tuple-element.68), calls=%async_computation.1 | async-start | bytes 4194304 | tf_op jit(solution)/shard_map/all_to_all | solution.py:588
  131.9 11.2 %collective-permute-start.26 = (bf16[2048,512]{1,0:T(8,128)(2,1)S(1)}, bf16[2048,512]{1,0:T(8,128)(2,1)S(1)}, u32[]{:S(2)}, u32[]{:S(2)}) collective-permute-start(bf16[2048,512]{1,0:T(8,128)(2,1)S(1)} %transpose_pieces.1.own_ref), channel_id=1, source_target_pairs={{0,1},{1,0},{2,3},{3,2},{4,5},{5,4},{6,7},{7,6},{8,9},{9,8},{10,11... | collective-permute-start | bytes 6291464 | tf_op jit(solution)/shard_map/ppermute | solution.py:513
  136.4 8.0 %collective-permute-start.27 = (bf16[8192,128]{1,0:T(8,128)(2,1)}, bf16[8192,128]{1,0:T(8,128)(2,1)}, u32[]{:S(2)}, u32[]{:S(2)}) collective-permute-start(bf16[8192,128]{1,0:T(8,128)(2,1)} %get-tuple-element.104.refs_0_), channel_id=1, source_target_pairs={{0,1},{1,0},{2,3},{3,2},{4,5},{5,4},{6,7},{7,6},{8,9},{9,8},{10,11... | collective-permute-start | bytes 6291464 | tf_op jit(solution)/shard_map/ppermute | solution.py:513
  136.9 7.6 %collective-permute-start.28 = (bf16[8192,128]{1,0:T(8,128)(2,1)}, bf16[8192,128]{1,0:T(8,128)(2,1)}, u32[]{:S(2)}, u32[]{:S(2)}) collective-permute-start(bf16[8192,128]{1,0:T(8,128)(2,1)} %get-tuple-element.105.refs_1_), channel_id=1, source_target_pairs={{0,1},{1,0},{2,3},{3,2},{4,5},{5,4},{6,7},{7,6},{8,9},{9,8},{10,11... | collective-permute-start | bytes 6291464 | tf_op jit(solution)/shard_map/ppermute | solution.py:513
  136.9 35.7 %copy-start.20 = (f32[128]{0:T(128)S(1)}, f32[128]{0:T(128)}, u32[]{:S(2)}) copy-start(f32[128]{0:T(128)} %param.13) | copy-start | bytes 1540
  176.0 5.0 %collective-permute-start.31 = (bf16[256,256]{1,0:T(8,128)(2,1)S(1)}, bf16[256,256]{1,0:T(8,128)(2,1)S(1)}, u32[]{:S(2)}, u32[]{:S(2)}) collective-permute-start(bf16[256,256]{1,0:T(8,128)(2,1)S(1)} %get-tuple-element.99.refs_0_), channel_id=1, source_target_pairs={{0,192},{8,200},{16,208},{24,216},{32,224},{40,232},{48,240},{56,2... | collective-permute-start | bytes 393224 | tf_op jit(solution)/shard_map/ppermute | solution.py:504
  177.8 6.5 %collective-permute-start.30 = (bf16[256,256]{1,0:T(8,128)(2,1)S(1)}, bf16[256,256]{1,0:T(8,128)(2,1)S(1)}, u32[]{:S(2)}, u32[]{:S(2)}) collective-permute-start(bf16[256,256]{1,0:T(8,128)(2,1)S(1)} %get-tuple-element.99.refs_0_), channel_id=1, source_target_pairs={{0,128},{8,136},{16,144},{24,152},{32,160},{40,168},{48,176},{56,1... | collective-permute-start | bytes 393224 | tf_op jit(solution)/shard_map/ppermute | solution.py:504
  179.6 6.2 %collective-permute-start.29 = (bf16[256,256]{1,0:T(8,128)(2,1)S(1)}, bf16[256,256]{1,0:T(8,128)(2,1)S(1)}, u32[]{:S(2)}, u32[]{:S(2)}) collective-permute-start(bf16[256,256]{1,0:T(8,128)(2,1)S(1)} %get-tuple-element.99.refs_0_), channel_id=1, source_target_pairs={{0,64},{8,72},{16,80},{24,88},{32,96},{40,104},{48,112},{56,120},{... | collective-permute-start | bytes 393224 | tf_op jit(solution)/shard_map/ppermute | solution.py:504
  180.2 7.9 %collective-permute-start.32 = (bf16[256,256]{1,0:T(8,128)(2,1)S(1)}, bf16[256,256]{1,0:T(8,128)(2,1)S(1)}, u32[]{:S(2)}, u32[]{:S(2)}) collective-permute-start(bf16[256,256]{1,0:T(8,128)(2,1)S(1)} %get-tuple-element.102.own_ref), channel_id=1, source_target_pairs={{0,1},{1,0},{2,3},{3,2},{4,5},{5,4},{6,7},{7,6},{8,9},{9,8},{10,11... | collective-permute-start | bytes 393224 | tf_op jit(solution)/shard_map/ppermute | solution.py:513
  188.1 32.0 %all-to-all-start.2 = ((bf16[8,256,256]{2,1,0:T(8,128)(2,1)}), bf16[8,256,256]{2,1,0:T(8,128)(2,1)S(1)}, u32[]{:S(2)}, u32[]{:S(2)}) async-start(bf16[8,256,256]{2,1,0:T(8,128)(2,1)} %weight_terms.1), calls=%async_computation.2 | async-start | bytes 2097152 | tf_op jit(solution)/shard_map/all_to_all | solution.py:603
  198.1 16.1 %collective-permute-start.33 = (bf16[32,8192]{1,0:T(8,128)(2,1)S(1)}, bf16[32,8192]{1,0:T(8,128)(2,1)S(1)}, u32[]{:S(2)}, u32[]{:S(2)}) collective-permute-start(bf16[32,8192]{1,0:T(8,128)(2,1)S(1)} %get-tuple-element.109), channel_id=1, source_target_pairs={{0,2},{1,3},{2,4},{3,5},{4,6},{5,7},{6,0},{7,1},{8,10},{9,11},{10,... | collective-permute-start | bytes 1572872 | tf_op jit(solution)/shard_map/ppermute | solution.py:608
  199.7 20.4 %collective-permute-start.34 = (bf16[32,8192]{1,0:T(8,128)(2,1)S(1)}, bf16[32,8192]{1,0:T(8,128)(2,1)S(1)}, u32[]{:S(2)}, u32[]{:S(2)}) collective-permute-start(bf16[32,8192]{1,0:T(8,128)(2,1)S(1)} %get-tuple-element.110), channel_id=1, source_target_pairs={{0,4},{1,5},{2,6},{3,7},{4,0},{5,1},{6,2},{7,3},{8,12},{9,13},{10,... | collective-permute-start | bytes 1572872 | tf_op jit(solution)/shard_map/ppermute | solution.py:608
  202.4 17.7 %collective-permute-start.35 = (bf16[32,8192]{1,0:T(8,128)(2,1)S(1)}, bf16[32,8192]{1,0:T(8,128)(2,1)S(1)}, u32[]{:S(2)}, u32[]{:S(2)}) collective-permute-start(bf16[32,8192]{1,0:T(8,128)(2,1)S(1)} %get-tuple-element.111), channel_id=1, source_target_pairs={{0,6},{1,7},{2,0},{3,1},{4,2},{5,3},{6,4},{7,5},{8,14},{9,15},{10,... | collective-permute-start | bytes 1572872 | tf_op jit(solution)/shard_map/ppermute | solution.py:608
  (12 other events, 44.4 us)
